TPU v7x, 32 devices: a whole 2x2x4 slice. The times are simulated.
32 devices in a mesh: section: 4 (over y, x), ctx: 8 (over z, core).
Axes of the slice: x: 2, y: 2, z: 4, core: 2. Of those that a mesh axis runs over, the one named last changes fastest.
Arguments:
- incoming: bfloat16 [4, 1024, 4096], P('section', 'ctx'), may hold values from -6 to 6
- layer_input: bfloat16 [4, 1024, 4096], P('section', 'ctx'), may hold values from -6 to 6
- pre_gate: bfloat16 [4, 1024, 4096], P('section', 'ctx'), may hold values from -6 to 6
- mid_gate: bfloat16 [4, 1024, 4096], P('section', 'ctx'), may hold values from -6 to 6
- long_gate: bfloat16 [4, 1024, 4096], P('section', 'ctx'), may hold values from -6 to 6
- out_gate: bfloat16 [4, 1024, 4096], P('section', 'ctx'), may hold values from -6 to 6
- long_filter: bfloat16 [4, 4096, 1024], P('section', 'ctx'), may hold values from -0.1875 to 0.1875
- mid_filter: bfloat16 [4, 128, 4096], P('section'), may hold values from -0.5 to 0.5
Outputs:
- input_grad: bfloat16 [4, 1024, 4096], P('section', 'ctx')
- long_grad: bfloat16 [4, 4096, 1024], P('section', 'ctx')
- mid_grad: bfloat16 [4, 128, 4096], P('section', None, 'ctx')
All inputs are finite; a program needn't handle non-finite values.
Results may differ from a plain program's by a relative error of at most 0.008.
Values may be sent and summed in bfloat16 or wider, within the bound.
No kernel may reach another device: no remote copies, remote signals or barrier semaphores. Data moves between devices by JAX's collectives and lax.ppermute only.
A program may use at most 192 MiB of HBM per device.

v0:
```python
import math

import jax
import jax.numpy as jnp
from jax import lax
from jax.sharding import PartitionSpec as P


def passed_along(value, axis, steps):
    count = lax.axis_size(axis)
    pairs = [(source, (source + steps) % count) for source in range(count)]
    return lax.ppermute(value, axis, pairs)


def shifted(array, axis, by):
    devices = lax.axis_size(axis)
    pairs = [(i, i + by) for i in range(devices) if 0 <= i + by < devices]
    return lax.ppermute(array, axis, pairs)


def unit_roots(rows, cols, period):
    row_ids = jnp.arange(rows, dtype=jnp.int32)[:, None]
    col_ids = jnp.arange(cols, dtype=jnp.int32)[None, :]
    angle = (row_ids * col_ids % period).astype(jnp.float32) * (-2.0 * math.pi / period)
    return (jnp.cos(angle), jnp.sin(angle))


def contract(form, left, right):
    return jnp.einsum(
        form, left, right, precision=lax.Precision.HIGH, preferred_element_type=jnp.float32
    )


def to_spectrum(parts, factor_a, factor_b):
    channels = parts.shape[0]
    inputs_count = parts.shape[1]
    half = factor_a // 2
    period = factor_a * factor_b
    fa_cos, fa_sin = unit_roots(factor_a, half, factor_a)
    first_table = jnp.stack([jnp.stack([fa_cos, -fa_sin]), jnp.stack([fa_sin, fa_cos])])[
        :, :inputs_count
    ]
    tw_cos, tw_sin = unit_roots(factor_a, factor_b, period)
    fb_cos, fb_sin = unit_roots(factor_b, factor_b, factor_b)
    second_table = jnp.stack([jnp.stack([fb_cos, fb_sin]), jnp.stack([-fb_sin, fb_cos])])
    shaped = parts.reshape(channels, inputs_count, half, factor_b)
    first = contract("qrca,nrab->nqcb", first_table, shaped)
    first_re = first[:, 0]
    first_im = first[:, 1]
    turned = jnp.stack(
        [first_re * tw_cos - first_im * tw_sin, first_re * tw_sin + first_im * tw_cos], 1
    )
    return contract("nqcb,qpbd->npcd", turned, second_table)


def from_spectrum(spectrum, factor_a, factor_b, scale):
    channels = spectrum.shape[0]
    half = factor_a // 2
    period = factor_a * factor_b
    fb_cos, fb_sin = unit_roots(factor_b, factor_b, factor_b)
    back_table = jnp.stack([jnp.stack([fb_cos, -fb_sin]), jnp.stack([fb_sin, fb_cos])])
    tw_cos, tw_sin = unit_roots(factor_a, factor_b, period)
    fa_cos, fa_sin = unit_roots(half, factor_a, factor_a)
    last_table = jnp.stack(
        [
            jnp.stack([fa_cos, fa_sin]) * (scale / period),
            jnp.stack([-fa_sin, fa_cos]) * (1.0 / period),
        ]
    )
    middle = contract("npcd,pqdb->nqcb", spectrum, back_table)
    middle_re = middle[:, 0]
    middle_im = middle[:, 1]
    turned = jnp.stack(
        [middle_re * tw_cos + middle_im * tw_sin, middle_im * tw_cos - middle_re * tw_sin], 1
    )
    result = contract("rqac,nqcb->nrab", last_table, turned)
    length = half * factor_b
    return (result[:, 0].reshape(channels, length), result[:, 1].reshape(channels, length))


def depthwise(extended, kernel):
    result = lax.conv_general_dilated(
        extended[None],
        kernel[:, None, :],
        (1,),
        "VALID",
        dimension_numbers=("NWC", "WIO", "NWC"),
        feature_group_count=extended.shape[1],
        preferred_element_type=jnp.float32,
    )
    return result[0]


def per_device(
    incoming, layer_input, pre_gate, mid_gate, long_gate, out_gate, long_filter, mid_filter
):
    sections = lax.axis_size("section")
    beta = (2.0 * sections) ** (-0.5)
    adjoint = passed_along(incoming[0], "section", -1).astype(jnp.float32)
    inputs = layer_input[0].astype(jnp.float32)
    tokens = inputs.shape[0]
    gate_pre = pre_gate[0].astype(jnp.float32)
    gate_mid = mid_gate[0].astype(jnp.float32)
    gate_long = long_gate[0].astype(jnp.float32)
    gate_out = out_gate[0].astype(jnp.float32)
    filter_taps = mid_filter[0]
    reach = filter_taps.shape[0] - 1
    seq_len = tokens * lax.axis_size("ctx")
    scale = float(seq_len) ** (-0.5)
    mixed_in = (inputs * gate_pre).astype(jnp.bfloat16)
    earlier = shifted(mixed_in[tokens - reach :], "ctx", 1)
    extended = jnp.concatenate([earlier, mixed_in], 0)
    branch = depthwise(extended, filter_taps[::-1])
    resid = inputs + beta * branch * gate_mid
    long_in = (resid * gate_long).astype(jnp.bfloat16)
    grad_z = (beta * adjoint * gate_out).astype(jnp.bfloat16)
    channel_z, channel_w = (
        lax.all_to_all(grad_z.T, "ctx", split_axis=0, concat_axis=1, tiled=True),
        lax.all_to_all(long_in.T, "ctx", split_axis=0, concat_axis=1, tiled=True),
    )
    factor_b = math.gcd(seq_len, 128)
    factor_a = 2 * seq_len // factor_b
    zspec = to_spectrum(channel_z[:, None], factor_a, factor_b)
    zspec_re = zspec[:, 0]
    zspec_im = zspec[:, 1]
    pair = to_spectrum(jnp.stack([channel_w, -long_filter[0]], 1), factor_a, factor_b)
    pair_re = pair[:, 0]
    pair_im = pair[:, 1]
    joint_re = zspec_re * pair_re + zspec_im * pair_im
    joint_im = zspec_im * pair_re - zspec_re * pair_im
    lag_grad, input_part = from_spectrum(
        jnp.stack([joint_re, joint_im], 1), factor_a, factor_b, scale
    )
    long_grad = lag_grad.astype(jnp.bfloat16)[None]
    returned = lax.all_to_all(
        input_part.astype(jnp.bfloat16), "ctx", split_axis=1, concat_axis=0, tiled=True
    ).T
    grad_u = adjoint + returned.astype(jnp.float32) * gate_long
    grad_b = (beta * grad_u * gate_mid).astype(jnp.bfloat16)
    later = shifted(grad_b[:reach], "ctx", -1)
    grad_act = depthwise(jnp.concatenate([grad_b, later], 0), filter_taps)
    input_grad = (grad_u + grad_act * gate_pre).astype(jnp.bfloat16)[None]
    tap_part = depthwise(extended, grad_b)[::-1]
    total_taps = lax.psum(tap_part, "ctx")
    columns = tap_part.shape[1] // lax.axis_size("ctx")
    own_taps = lax.dynamic_slice_in_dim(total_taps, lax.axis_index("ctx") * columns, columns, 1)
    mid_grad = (own_taps * scale).astype(jnp.bfloat16)[None]
    return (input_grad, long_grad, mid_grad)


def solution(mesh):
    placed = (
        P("section", "ctx", None),
        P("section", "ctx", None),
        P("section", "ctx", None),
        P("section", "ctx", None),
        P("section", "ctx", None),
        P("section", "ctx", None),
        P("section", "ctx", None),
        P("section", None, None),
    )
    return jax.shard_map(
        per_device,
        mesh=mesh,
        in_specs=placed,
        out_specs=(P("section", "ctx", None), P("section", "ctx", None), P("section", None, "ctx")),
        check_vma=False,
    )
```

profile of v0, /device:TPU:0, one launch (start us, length us, event | category | flops | bytes accessed | tf_op | source)
XLA Modules:
  0.0 348.7 jit_solution(218762235483841021)
XLA Ops:
  7.2 1.9 fusion.23
  9.1 1.2 slice.67
  10.3 3.4 collective-permute-start.1
  13.6 3.3 collective-permute-start
  16.9 10.2 %rev.6 = bf16[128,4096]{1,0:T(8,128)(2,1)} reverse(bf16[128,4096]{1,0:T(8,128)(2,1)S(1)} %bitcast.185), dimensions={0} | reverse | bytes 2097152 | tf_op jit(solution)/shard_map/rev | solution.py:113
  27.1 1.6 maximum_bitcast_fusion.5
  28.8 27.4 %convolution_multiply_fusion = f32[1,128,4096]{2,0,1:T(1,128)S(1)} fusion(bf16[1,255,4096]{2,1,0:T(8,128)(2,1)S(1)} %maximum_bitcast_fusion.5, bf16[128,1,4096]{2,0,1:T(8,128)(2,1)S(1)} %bitcast.187), kind=kOutput, calls=%fused_computation.13 | convolution fusion | flops 134742016 | bytes 5234688 | tf_op jit(solution)/shard_map/conv_general_dilated | solution.py:82
  56.3 2.1 fusion.33
  58.4 1.3 copy.74
  59.7 5.8 %all-to-all-start.1 = ((bf16[8,512,128]{2,1,0:T(8,128)(2,1)}), bf16[8,512,128]{2,1,0:T(8,128)(2,1)S(1)}, u32[]{:S(2)}, u32[]{:S(2)}) async-start(bf16[8,512,128]{2,1,0:T(8,128)(2,1)} %bitcast.35), calls=%async_computation.1 | async-start | bytes 2097152 | tf_op jit(solution)/shard_map/all_to_all | solution.py:119
  65.5 1.9 fusion.35
  67.4 1.3 copy.45
  68.8 23.4 %all-to-all-done.1 = bf16[8,512,128]{2,1,0:T(8,128)(2,1)S(1)} async-done(((bf16[8,512,128]{2,1,0:T(8,128)(2,1)}), bf16[8,512,128]{2,1,0:T(8,128)(2,1)S(1)}, u32[]{:S(2)}, u32[]{:S(2)}) %all-to-all-start.1) | async-done | bytes 1048608 | tf_op jit(solution)/shard_map/all_to_all | solution.py:119
  92.1 3.7 %all-to-all-start = ((bf16[8,512,128]{2,1,0:T(8,128)(2,1)}), bf16[8,512,128]{2,1,0:T(8,128)(2,1)S(1)}, u32[]{:S(2)}, u32[]{:S(2)}) async-start(bf16[8,512,128]{2,1,0:T(8,128)(2,1)} %bitcast.184), calls=%async_computation | async-start | bytes 2097152 | tf_op jit(solution)/shard_map/all_to_all | solution.py:118
  95.9 1.4 negate_bitcast_fusion
  99.5 0.7 fusion.42
  100.2 1.9 copy.128
  102.1 5.7 %convolution_bitcast_fusion = f32[512,2,16,128]{3,2,1,0:T(8,128)} fusion(bf16[512,1,8,128]{3,2,1,0:T(8,128)(2,1)S(1)} %bitcast.182, bf16[512,1,8,128]{3,2,1,0:T(8,128)(2,1)S(1)} %bitcast.183, f32[1,2,16,8]{2,3,0,1:T(8,128)S(1)} %get-tuple-element.24, f32[1,2,16,8]{2,3,0,1:T(8,128)S(1)} %get-tuple-element.23), kind=kOutput, calls=%fused_computation.28 | convolution fusion | flops 205521408 | bytes 10487808 | tf_op jit(solution)/shard_map/qrca,nrab->nqcb/dot_general | solution.py:29
  107.8 14.6 %all-to-all-done = bf16[8,512,128]{2,1,0:T(8,128)(2,1)S(1)} async-done(((bf16[8,512,128]{2,1,0:T(8,128)(2,1)}), bf16[8,512,128]{2,1,0:T(8,128)(2,1)S(1)}, u32[]{:S(2)}, u32[]{:S(2)}) %all-to-all-start) | async-done | bytes 1048608 | tf_op jit(solution)/shard_map/all_to_all | solution.py:118
  122.4 2.4 convolution_bitcast_fusion.1
  124.8 1.0 copy-done.1
  125.7 5.6 %multiply_subtract_fusion.3 = (f32[512,1,16,128]{3,2,1,0:T(8,128)}, f32[512,1,16,128]{3,2,1,0:T(8,128)}, f32[512,1,16,128]{3,2,1,0:T(8,128)S(1)}, f32[512,1,16,128]{3,2,1,0:T(8,128)}) fusion(f32[512,2,16,128]{3,2,1,0:T(8,128)S(1)} %convolution_bitcast_fusion.1, f32[16,128]{1,0:T(8,128)S(1)} %copy-done.18, f32[16,128]{1,0:T(8,128)S(1)} %copy-done.19, ...), kind=kLoop, calls=%fused_computation.22 | loop fusion | flops 12582912 | bytes 33570816 | tf_op jit(solution)/shard_map/sub | solution.py:51
  131.3 4.0 %pad_maximum_fusion = f32[512,2,16,128]{3,2,1,0:T(8,128)S(1)} fusion(f32[512,1,16,128]{3,2,1,0:T(8,128)} %get-tuple-element.8, f32[512,1,16,128]{3,2,1,0:T(8,128)} %get-tuple-element.7), kind=kLoop, calls=%fused_computation | loop fusion | flops 2097152 | bytes 16777216 | tf_op jit(solution)/shard_map/stack | solution.py:50
  135.3 2.9 pad_maximum_fusion.1
  138.2 9.7 %fusion.14 = f32[512,2,16,128]{0,3,2,1:T(8,128)} fusion(f32[512,2,16,128]{3,2,1,0:T(8,128)S(1)} %pad_maximum_fusion, f32[1,2,128,128]{2,3,0,1:T(8,128)S(1)} %get-tuple-element.14, f32[1,2,128,128]{2,3,0,1:T(8,128)S(1)} %get-tuple-element.17), kind=kOutput, calls=%fused_computation.30 | convolution fusion | flops 3221291008 | bytes 17039360 | tf_op jit(solution)/shard_map/nqcb,qpbd->npcd/dot_general | solution.py:29
  147.9 9.6 %fusion.17 = f32[512,2,16,128]{0,3,2,1:T(8,128)} fusion(f32[512,2,16,128]{3,2,1,0:T(8,128)S(1)} %pad_maximum_fusion.1, f32[1,2,128,128]{2,3,0,1:T(8,128)S(1)} %get-tuple-element.14, f32[1,2,128,128]{2,3,0,1:T(8,128)S(1)} %get-tuple-element.17), kind=kOutput, calls=%fused_computation.31 | convolution fusion | flops 3221291008 | bytes 17039360 | tf_op jit(solution)/shard_map/nqcb,qpbd->npcd/dot_general | solution.py:29
  157.5 4.5 %multiply_add_fusion.1 = (f32[512,1,16,128]{0,3,2,1:T(8,128)S(1)}, f32[512,1,16,128]{0,3,2,1:T(8,128)S(1)}) fusion(f32[512,2,16,128]{0,3,2,1:T(8,128)} %fusion.17, f32[512,2,16,128]{0,3,2,1:T(8,128)S(1)} %copy-done), kind=kLoop, calls=%fused_computation.18 | loop fusion | flops 6291456 | bytes 25165824 | tf_op jit(solution)/shard_map/add | solution.py:129
  162.1 4.3 %maximum_bitcast_fusion = f32[512,2,16,128,1]{0,3,2,1,4:T(8,128)} fusion(f32[512,1,16,128]{0,3,2,1:T(8,128)S(1)} %get-tuple-element.4, f32[512,1,16,128]{0,3,2,1:T(8,128)S(1)} %get-tuple-element.3), kind=kLoop, calls=%fused_computation.2 | loop fusion | flops 2097152 | bytes 16777216 | tf_op jit(solution)/shard_map/stack | solution.py:132
  166.4 10.3 %copy.70 = f32[512,2,16,128,1]{3,2,1,4,0:T(8,128)} copy(f32[512,2,16,128,1]{0,3,2,1,4:T(8,128)} %maximum_bitcast_fusion) | data formatting | bytes 16777216 | tf_op jit(solution)/shard_map/stack | solution.py:132
  176.7 6.2 %convolution_bitcast_fusion.2 = f32[512,2,16,128]{3,2,1,0:T(8,128)S(1)} fusion(f32[512,2,16,128,1]{3,2,1,4,0:T(8,128)} %copy.70, f32[1,2,128,128]{2,3,1,0:T(8,128)S(1)} %copy-done.17, f32[1,2,128,128]{2,3,1,0:T(8,128)S(1)} %get-tuple-element.13), kind=kOutput, calls=%fused_computation.32 | convolution fusion | flops 3221291008 | bytes 17039360 | tf_op jit(solution)/shard_map/npcd,pqdb->nqcb/dot_general | solution.py:29
  182.9 0.9 multiply_add_fusion
  183.8 2.6 fusion.32
  186.6 1.1 copy.58
  187.8 3.6 %all-to-all-start.2 = ((bf16[512,8,128]{2,0,1:T(8,128)(2,1)}), bf16[512,8,128]{2,0,1:T(8,128)(2,1)S(1)}, u32[]{:S(2)}, u32[]{:S(2)}) async-start(bf16[512,8,128]{2,0,1:T(8,128)(2,1)} %copy.58), calls=%async_computation.2 | async-start | bytes 2097152 | tf_op jit(solution)/shard_map/all_to_all | solution.py:135
  191.4 1.3 convert_element_type.242
  192.6 25.2 %all-to-all-done.2 = bf16[512,8,128]{2,0,1:T(8,128)(2,1)S(1)} async-done(((bf16[512,8,128]{2,0,1:T(8,128)(2,1)}), bf16[512,8,128]{2,0,1:T(8,128)(2,1)S(1)}, u32[]{:S(2)}, u32[]{:S(2)}) %all-to-all-start.2) | async-done | bytes 1048608 | tf_op jit(solution)/shard_map/all_to_all | solution.py:135
  217.8 1.5 convert_element_type.251
  219.3 1.9 copy.78
  221.3 3.9 %fusion.22 = bf16[128,4096]{1,0:T(8,128)(2,1)} fusion(bf16[1,128,4096]{2,1,0:T(8,128)(2,1)} %param.11, bf16[1,128,4096]{2,1,0:T(8,128)(2,1)} %param.12, f32[4096,128]{0,1:T(8,128)S(1)} %copy.78, bf16[128,4096]{1,0:T(8,128)(2,1)S(1)} %collective-permute-done), kind=kLoop, calls=%fused_computation.44 | loop fusion | flops 4194304 | bytes 6291456 | tf_op jit(solution)/shard_map/convert_element_type | solution.py:139
  225.2 1.3 collective-permute-start.2
  226.5 28.8 %fusion.11 = f32[1,128,4096]{2,0,1:T(1,128)S(1)} fusion(bf16[1,255,4096]{2,1,0:T(8,128)(2,1)S(1)} %copy-done.13, bf16[128,1,4096]{2,0,1:T(8,128)(2,1)} %bitcast.73), kind=kOutput, calls=%fused_computation.25 | convolution fusion | flops 134217728 | bytes 5234688 | tf_op jit(solution)/shard_map/conv_general_dilated | solution.py:82
  255.3 3.0 copy.127
  258.3 16.6 %rev.7 = f32[128,4096]{1,0:T(8,128)} reverse(f32[128,4096]{1,0:T(8,128)} %bitcast.181), dimensions={0} | reverse | bytes 4194304 | tf_op jit(solution)/shard_map/rev | solution.py:143
  274.9 1.5 maximum_bitcast_fusion.8
  276.5 30.1 %fusion.9 = f32[1,128,4096]{2,0,1:T(1,128)S(1)} fusion(bf16[1,255,4096]{2,1,0:T(8,128)(2,1)S(1)} %maximum_bitcast_fusion.8, bf16[128,1,4096]{2,0,1:T(8,128)(2,1)S(1)} %bitcast.186), kind=kOutput, calls=%fused_computation.23 | convolution fusion | flops 134217728 | bytes 5234688 | tf_op jit(solution)/shard_map/conv_general_dilated | solution.py:82
  306.6 2.8 fusion.34
  309.4 30.3 %all-reduce.2.cloned.1.call-done = f32[128,4096]{1,0:T(8,128)} async-done(((f32[128,4096]{1,0:T(8,128)}), f32[128,4096]{1,0:T(8,128)}) %all-reduce.2.cloned.1.call-update) | async-done | bytes 2097168 | tf_op jit(solution)/shard_map/psum | solution.py:144
  339.8 1.6 fusion.44
  (59 shorter events, 2.6 us)
Async XLA Ops:
  7.2 9.8 %copy-start.14 = (bf16[1,128,4096]{2,1,0:T(8,128)(2,1)S(1)}, bf16[1,128,4096]{2,1,0:T(8,128)(2,1)}, u32[]{:S(2)}) copy-start(bf16[1,128,4096]{2,1,0:T(8,128)(2,1)} %param.15) | copy-start | bytes 3145732
  10.3 16.9 %collective-permute-start.1 = (bf16[127,4096]{1,0:T(8,128)(2,1)}, bf16[127,4096]{1,0:T(8,128)(2,1)}, u32[]{:S(2)}, u32[]{:S(2)}) collective-permute-start(bf16[127,4096]{1,0:T(8,128)(2,1)} %slice.67), channel_id=1, source_target_pairs={{0,1},{1,2},{2,3},{3,4},{4,5},{5,6},{6,7},{8,9},{9,10},{10,11},{11... | collective-permute-start | bytes 3121160 | tf_op jit(solution)/shard_map/ppermute | solution.py:18
  13.6 51.9 %collective-permute-start = (bf16[128,4096]{1,0:T(8,128)(2,1)}, bf16[128,4096]{1,0:T(8,128)(2,1)S(1)}, u32[]{:S(2)}, u32[]{:S(2)}) collective-permute-start(bf16[128,4096]{1,0:T(8,128)(2,1)} %bitcast), channel_id=1, source_target_pairs={{0,24},{8,0},{16,8},{24,16},{1,25},{9,1},{17,9},{25,17},{2,26},{10... | collective-permute-start | bytes 3145736 | tf_op jit(solution)/shard_map/ppermute | solution.py:12
  27.1 1.6 copy-start.16
  28.8 27.5 %copy-start.12 = (bf16[1,255,4096]{2,1,0:T(8,128)(2,1)}, bf16[1,255,4096]{2,1,0:T(8,128)(2,1)S(1)}, u32[]{:S(2)}) copy-start(bf16[1,255,4096]{2,1,0:T(8,128)(2,1)S(1)} %maximum_bitcast_fusion.5) | copy-start | bytes 6266884
  28.8 27.5 %copy-start.6 = (bf16[1,128,4096]{2,1,0:T(8,128)(2,1)S(1)}, bf16[1,128,4096]{2,1,0:T(8,128)(2,1)}, u32[]{:S(2)}) copy-start(bf16[1,128,4096]{2,1,0:T(8,128)(2,1)} %param.12) | copy-start | bytes 3145732
  28.8 27.5 %copy-start.8 = (bf16[1,128,4096]{2,1,0:T(8,128)(2,1)S(1)}, bf16[1,128,4096]{2,1,0:T(8,128)(2,1)}, u32[]{:S(2)}) copy-start(bf16[1,128,4096]{2,1,0:T(8,128)(2,1)} %param.9) | copy-start | bytes 3145732
  28.8 27.5 %copy-start.10 = (bf16[1,128,4096]{2,1,0:T(8,128)(2,1)S(1)}, bf16[1,128,4096]{2,1,0:T(8,128)(2,1)}, u32[]{:S(2)}) copy-start(bf16[1,128,4096]{2,1,0:T(8,128)(2,1)} %param.11) | copy-start | bytes 3145732
  59.7 32.4 %all-to-all-start.1 = ((bf16[8,512,128]{2,1,0:T(8,128)(2,1)}), bf16[8,512,128]{2,1,0:T(8,128)(2,1)S(1)}, u32[]{:S(2)}, u32[]{:S(2)}) async-start(bf16[8,512,128]{2,1,0:T(8,128)(2,1)} %bitcast.35), calls=%async_computation.1 | async-start | bytes 2097152 | tf_op jit(solution)/shard_map/all_to_all | solution.py:119
  65.5 155.8 %copy-start.4 = (bf16[128,4096]{1,0:T(8,128)(2,1)}, bf16[128,4096]{1,0:T(8,128)(2,1)S(1)}, u32[]{:S(2)}) copy-start(bf16[128,4096]{1,0:T(8,128)(2,1)S(1)} %collective-permute-done) | copy-start | bytes 3145732
  92.1 3.7 %copy-start.9 = (bf16[8,512,128]{2,1,0:T(8,128)(2,1)}, bf16[8,512,128]{2,1,0:T(8,128)(2,1)S(1)}, u32[]{:S(2)}) copy-start(bf16[8,512,128]{2,1,0:T(8,128)(2,1)S(1)} %all-to-all-done.1) | copy-start | bytes 3145732
  92.1 30.2 %all-to-all-start = ((bf16[8,512,128]{2,1,0:T(8,128)(2,1)}), bf16[8,512,128]{2,1,0:T(8,128)(2,1)S(1)}, u32[]{:S(2)}, u32[]{:S(2)}) async-start(bf16[8,512,128]{2,1,0:T(8,128)(2,1)} %bitcast.184), calls=%async_computation | async-start | bytes 2097152 | tf_op jit(solution)/shard_map/all_to_all | solution.py:118
  107.8 16.9 %copy-start.18 = (f32[16,128]{1,0:T(8,128)S(1)}, f32[16,128]{1,0:T(8,128)}, u32[]{:S(2)}) copy-start(f32[16,128]{1,0:T(8,128)} %get-tuple-element.27) | copy-start | bytes 24580
  107.8 17.0 %copy-start.19 = (f32[16,128]{1,0:T(8,128)S(1)}, f32[16,128]{1,0:T(8,128)}, u32[]{:S(2)}) copy-start(f32[16,128]{1,0:T(8,128)} %get-tuple-element.28) | copy-start | bytes 24580
  122.4 3.4 copy-start.1
  147.9 9.6 %copy-start = (f32[512,2,16,128]{0,3,2,1:T(8,128)S(1)}, f32[512,2,16,128]{0,3,2,1:T(8,128)}, u32[]{:S(2)}) copy-start(f32[512,2,16,128]{0,3,2,1:T(8,128)} %fusion.14) | copy-start | bytes 25165828
  166.4 10.3 %copy-start.17 = (f32[1,2,128,128]{2,3,1,0:T(8,128)S(1)}, f32[1,2,128,128]{2,3,1,0:T(8,128)}, u32[]{:S(2)}) copy-start(f32[1,2,128,128]{2,3,1,0:T(8,128)} %get-tuple-element.18) | copy-start | bytes 393220
  182.9 0.9 copy-start.20
  182.9 0.9 copy-start.21
  187.8 30.1 %all-to-all-start.2 = ((bf16[512,8,128]{2,0,1:T(8,128)(2,1)}), bf16[512,8,128]{2,0,1:T(8,128)(2,1)S(1)}, u32[]{:S(2)}, u32[]{:S(2)}) async-start(bf16[512,8,128]{2,0,1:T(8,128)(2,1)} %copy.58), calls=%async_computation.2 | async-start | bytes 2097152 | tf_op jit(solution)/shard_map/all_to_all | solution.py:135
  191.3 148.4 %all-reduce.2.cloned.1.call-start = ((), (), s32[]{:S(2)}) async-start(), calls=%async_computation.3 | async-start | bytes 4194304 | tf_op jit(solution)/shard_map/psum | solution.py:144
  221.3 34.0 %copy-start.2 = (f32[4096,128]{0,1:T(8,128)}, f32[4096,128]{0,1:T(8,128)S(1)}, u32[]{:S(2)}) copy-start(f32[4096,128]{0,1:T(8,128)S(1)} %copy.78) | copy-start | bytes 6291460
  221.3 5.2 %copy-start.13 = (bf16[1,255,4096]{2,1,0:T(8,128)(2,1)S(1)}, bf16[1,255,4096]{2,1,0:T(8,128)(2,1)}, u32[]{:S(2)}) copy-start(bf16[1,255,4096]{2,1,0:T(8,128)(2,1)} %copy-done.12) | copy-start | bytes 6266884
  225.2 49.7 %collective-permute-start.2 = (bf16[127,4096]{1,0:T(8,128)(2,1)}, bf16[127,4096]{1,0:T(8,128)(2,1)S(1)}, u32[]{:S(2)}, u32[]{:S(2)}) collective-permute-start(bf16[127,4096]{1,0:T(8,128)(2,1)} %bitcast.179), channel_id=1, source_target_pairs={{1,0},{2,1},{3,2},{4,3},{5,4},{6,5},{7,6},{9,8},{10,9},{11,10},{12... | collective-permute-start | bytes 3121160 | tf_op jit(solution)/shard_map/ppermute | solution.py:18
  274.9 1.5 copy-start.15
  276.4 30.2 %copy-start.3 = (f32[4096,128]{0,1:T(8,128)S(1)}, f32[4096,128]{0,1:T(8,128)}, u32[]{:S(2)}) copy-start(f32[4096,128]{0,1:T(8,128)} %copy-done.2) | copy-start | bytes 6291460
  276.4 30.2 %copy-start.5 = (bf16[128,4096]{1,0:T(8,128)(2,1)S(1)}, bf16[128,4096]{1,0:T(8,128)(2,1)}, u32[]{:S(2)}) copy-start(bf16[128,4096]{1,0:T(8,128)(2,1)} %copy-done.4) | copy-start | bytes 3145732
  276.4 30.2 %copy-start.7 = (bf16[1,128,4096]{2,1,0:T(8,128)(2,1)S(1)}, bf16[1,128,4096]{2,1,0:T(8,128)(2,1)}, u32[]{:S(2)}) copy-start(bf16[1,128,4096]{2,1,0:T(8,128)(2,1)} %param.12) | copy-start | bytes 3145732
  276.4 30.2 %copy-start.11 = (bf16[1,128,4096]{2,1,0:T(8,128)(2,1)S(1)}, bf16[1,128,4096]{2,1,0:T(8,128)(2,1)}, u32[]{:S(2)}) copy-start(bf16[1,128,4096]{2,1,0:T(8,128)(2,1)} %param.10) | copy-start | bytes 3145732
Sparse Core Ops, SparseCore 0:
  275.0 64.7 all-reduce.1
where the time goes:
time: 355 us; the launch traced here: 349 us
  matrix products  122 us (34%)
  waiting for transfers between devices  93.4 us (26%)
  local copies, waits for them, and re-layouts  51.7 us (15%)
  other arithmetic  45.1 us (13%)
  starting transfers between devices  21 us (6%)
  between operations  14.9 us (4%)
    conv_general_dilated x3, matrix products, depthwise(): lax.conv_general_dilated(extended[None], kernel[:, None, :], (1,), 'VALID...  86.3 us
    dot_general x6, matrix products, contract(): jnp.einsum(form, left, right, precision=lax.Precision.HIGH, preferred_ele...  36.2 us
    psum x1, waiting for transfers between devices, per_device(): total_taps = lax.psum(tap_part, 'ctx')  30.3 us
    all_to_all x1, waiting for transfers between devices, per_device(): lax.all_to_all(input_part.astype(jnp.bfloat16), 'ctx', split_axis=1, conc...  25.2 us
    all_to_all x1, waiting for transfers between devices, per_device(): lax.all_to_all(long_in.T, 'ctx', split_axis=0, concat_axis=1, tiled=True)  23.4 us
    rev x1, local copies, waits for them, and re-layouts, per_device(): tap_part = depthwise(extended, grad_b)[::-1]  16.6 us
    all_to_all x1, waiting for transfers between devices, per_device(): lax.all_to_all(grad_z.T, 'ctx', split_axis=0, concat_axis=1, tiled=True)  14.6 us
    another operation x1, local copies, waits for them, and re-layouts, per_device(): jnp.stack([joint_re, joint_im], 1)  10.3 us
  transfers between devices with their start and end apart: 7, of which 4 were waited for; matrix products, arithmetic and copies ran while one was open for 41% of the time, Pallas kernels for 0%

commit v1 on v0

v1 whole, which is shorter than its diff:
```python
import functools
import math

import jax
import jax.numpy as jnp
import numpy as np
from jax import lax
from jax.experimental import pallas as pl
from jax.experimental.pallas import tpu as pltpu
from jax.sharding import PartitionSpec as P

BF16 = jnp.bfloat16
F32 = jnp.float32
VMEM_BYTES = 48 * 1024 * 1024


def passed_along(value, axis, steps):
    count = lax.axis_size(axis)
    pairs = [(source, (source + steps) % count) for source in range(count)]
    return lax.ppermute(value, axis, pairs)


def shifted(array, axis, by):
    devices = lax.axis_size(axis)
    pairs = [(i, i + by) for i in range(devices) if 0 <= i + by < devices]
    return lax.ppermute(array, axis, pairs)


def forward_table(period, positions):
    angle = np.pi * np.outer(2 * np.arange(period // 2) + 1, positions) / period
    return np.concatenate([np.cos(angle), -np.sin(angle)], 0).astype(BF16)


def inverse_table(period, positions):
    angle = np.pi * np.outer(positions, 2 * np.arange(period // 2) + 1) / period
    return (np.concatenate([np.cos(angle), -np.sin(angle)], 1) * (2.0 / period)).astype(BF16)


def dot(left, right):
    return jnp.dot(left, right, preferred_element_type=F32)


def dot_nt(left, right):
    return lax.dot_general(left, right, (((1,), (1,)), ((), ())), preferred_element_type=F32)


def times(left, right):
    half = left.shape[0] // 2
    l_re, l_im, r_re, r_im = left[:half], left[half:], right[:half], right[half:]
    return jnp.concatenate(
        [(l_re * r_re - l_im * r_im).astype(BF16), (l_re * r_im + l_im * r_re).astype(BF16)], 0
    )


def times_conj(left, right):
    half = left.shape[0] // 2
    l_re, l_im, r_re, r_im = left[:half], left[half:], right[:half], right[half:]
    return jnp.concatenate(
        [(l_re * r_re + l_im * r_im).astype(BF16), (l_im * r_re - l_re * r_im).astype(BF16)], 0
    )


def put_columns(out_ref, value, start):
    owned = out_ref.shape[2]
    width = value.shape[1]
    if owned >= width:
        out_ref[start // owned, :, start % owned : start % owned + width] = value
    else:
        for j in range(width // owned):
            out_ref[start // owned + j] = value[:, j * owned : (j + 1) * owned]


def get_columns(in_ref, start, width):
    owned = in_ref.shape[2]
    if owned >= width:
        return in_ref[start // owned, :, start % owned : start % owned + width]
    return jnp.concatenate([in_ref[start // owned + j] for j in range(width // owned)], 1)


def mix_kernel(inputs_ref, gate_ref, out_ref):
    out_ref[...] = (inputs_ref[...].astype(F32) * gate_ref[...].astype(F32)).astype(BF16)


def grad_z_kernel(beta, adjoint_ref, gate_ref, out_ref):
    value = beta * adjoint_ref[...].astype(F32) * gate_ref[...].astype(F32)
    put_columns(out_ref, value.astype(BF16), 0)


def branch_kernel(
    beta, step, fwd_ref, inv_ref, earlier_ref, mixed_ref, taps_ref, inputs_ref, mid_ref, long_ref, out_ref
):
    tokens = mixed_ref.shape[0]
    taps = taps_ref.shape[0]
    for start in range(0, mixed_ref.shape[1], step):
        cols = slice(start, start + step)
        signal = dot(fwd_ref[:, :tokens], earlier_ref[:, cols]) + dot(
            fwd_ref[:, tokens:], mixed_ref[:, cols]
        )
        filt = dot(fwd_ref[:, :taps], taps_ref[:, cols])
        branch = dot(inv_ref[...], times(signal, filt))
        resid = inputs_ref[:, cols].astype(F32) + beta * branch * mid_ref[:, cols].astype(F32)
        value = (resid * long_ref[:, cols].astype(F32)).astype(BF16)
        put_columns(out_ref, value, start)


def taps_kernel(
    beta, step, fwd_ref, inv_ref, earlier_ref, mixed_ref, adjoint_ref, grad_w_ref, long_ref, mid_ref,
    grad_b_ref, part_ref,
):
    tokens = mixed_ref.shape[0]
    for start in range(0, mixed_ref.shape[1], step):
        cols = slice(start, start + step)
        grad_w = get_columns(grad_w_ref, start, step).astype(F32)
        grad_u = adjoint_ref[:, cols].astype(F32) + grad_w * long_ref[:, cols].astype(F32)
        grad_b = (beta * grad_u * mid_ref[:, cols].astype(F32)).astype(BF16)
        grad_b_ref[:, cols] = grad_b
        signal = dot(fwd_ref[:, :tokens], earlier_ref[:, cols]) + dot(
            fwd_ref[:, tokens:], mixed_ref[:, cols]
        )
        grad = dot(fwd_ref[:, :tokens], grad_b)
        part = dot(inv_ref[...], times_conj(signal, grad))
        put_columns(part_ref, part.astype(BF16), start)


def input_grad_kernel(
    step, fwd_ref, inv_ref, grad_b_ref, later_ref, taps_ref, adjoint_ref, grad_w_ref, long_ref, pre_ref,
    out_ref,
):
    tokens = grad_b_ref.shape[0]
    taps = taps_ref.shape[0]
    for start in range(0, grad_b_ref.shape[1], step):
        cols = slice(start, start + step)
        grad_w = get_columns(grad_w_ref, start, step).astype(F32)
        grad_u = adjoint_ref[:, cols].astype(F32) + grad_w * long_ref[:, cols].astype(F32)
        signal = dot(fwd_ref[:, :tokens], grad_b_ref[:, cols]) + dot(
            fwd_ref[:, tokens:], later_ref[:, cols]
        )
        filt = dot(fwd_ref[:, :taps], taps_ref[:, cols])
        act = dot(inv_ref[...], times_conj(signal, filt))
        out_ref[:, cols] = (grad_u + act * pre_ref[:, cols].astype(F32)).astype(BF16)


def filter_kernel(blocks, fwd_ref, filt_ref, out_ref):
    size = filt_ref.shape[1] // blocks
    for d in range(blocks):
        piece = dot_nt(fwd_ref[:, size:], filt_ref[:, d * size : (d + 1) * size])
        if d:
            piece += dot_nt(fwd_ref[:, :size], filt_ref[:, (d - 1) * size : d * size])
        out_ref[d] = piece


def correlate(blocks, own_ref, other, joint_ref):
    period, width = joint_ref.shape[1:]
    half = period // 2
    rows, lanes = 16, math.gcd(width, 128) if width % 128 == 0 else width

    def chunk(i, _):
        at = pl.multiple_of(i * rows, rows)
        re, im = pl.ds(at, rows), pl.ds(pl.multiple_of(half + at, rows), rows)
        for start in range(0, width, lanes):
            cols = slice(start, start + lanes)
            own = [(own_ref[q, re, cols], own_ref[q, im, cols]) for q in range(blocks)]
            oth = [(other[d, re, cols], other[d, im, cols]) for d in range(blocks)]
            for p in range(blocks):
                sum_re = sum_im = None
                for q in range(p, blocks):
                    a_re, a_im = own[q]
                    b_re, b_im = oth[q - p]
                    new_re = a_re * b_re + a_im * b_im
                    new_im = a_im * b_re - a_re * b_im
                    sum_re = new_re if sum_re is None else sum_re + new_re
                    sum_im = new_im if sum_im is None else sum_im + new_im
                joint_ref[p, re, cols] = sum_re.astype(BF16)
                joint_ref[p, im, cols] = sum_im.astype(BF16)
        return 0

    lax.fori_loop(0, half // rows, chunk, 0)


def grad_w_kernel(blocks, fwd_ref, inv_ref, grad_ref, filt_ref, out_ref, own_ref, joint_ref):
    size = grad_ref.shape[0] // blocks
    for q in range(blocks):
        own_ref[q] = dot(fwd_ref[:, size:], grad_ref[q * size : (q + 1) * size])
    correlate(blocks, own_ref, filt_ref, joint_ref)
    for p in range(blocks):
        out_ref[p * size : (p + 1) * size] = dot(inv_ref[...], joint_ref[p]).astype(BF16)


def long_grad_kernel(
    blocks, scale, fwd_ref, inv_ref, grad_ref, long_ref, out_ref, own_ref, other_ref, joint_ref
):
    size = grad_ref.shape[0] // blocks
    for q in range(blocks):
        own_ref[q] = dot(fwd_ref[:, size:], grad_ref[q * size : (q + 1) * size])
        other = dot(fwd_ref[:, size:], long_ref[q * size : (q + 1) * size])
        if q:
            other += dot(fwd_ref[:, :size], long_ref[(q - 1) * size : q * size])
        other_ref[q] = other
    correlate(blocks, own_ref, other_ref, joint_ref)
    for p in range(blocks):
        lags = (dot(inv_ref[...], joint_ref[p]) * scale).T
        out_ref[:, p * size : (p + 1) * size] = lags.astype(BF16)


def total_kernel(scale, parts_ref, out_ref):
    total = parts_ref[0].astype(F32)
    for i in range(1, parts_ref.shape[0]):
        total += parts_ref[i].astype(F32)
    out_ref[...] = (total * scale).astype(BF16)


def call(body, grid, ins, outs, args, flops, scratch=(), name=None):
    moved = sum(a.size * a.dtype.itemsize for a in args)
    moved += sum(math.prod(shape) * jnp.dtype(kind).itemsize for shape, kind, _ in outs)
    result = pl.pallas_call(
        body,
        grid=grid,
        in_specs=ins,
        out_specs=[spec for _, _, spec in outs],
        out_shape=[jax.ShapeDtypeStruct(shape, kind) for shape, kind, _ in outs],
        scratch_shapes=list(scratch),
        compiler_params=pltpu.CompilerParams(vmem_limit_bytes=VMEM_BYTES),
        cost_estimate=pl.CostEstimate(flops=flops, bytes_accessed=moved, transcendentals=0),
        name=name,
    )(*args)
    return result[0] if len(result) == 1 else result


def whole_spec(array):
    return pl.BlockSpec(array.shape, lambda i: (0,) * array.ndim)


def per_device(
    incoming, layer_input, pre_gate, mid_gate, long_gate, out_gate, long_filter, mid_filter
):
    sections = lax.axis_size("section")
    devices = lax.axis_size("ctx")
    beta = (2.0 * sections) ** (-0.5)
    tokens, channels = layer_input.shape[1:]
    taps = mid_filter.shape[1]
    seq_len = tokens * devices
    scale = float(seq_len) ** (-0.5)
    owned = channels // devices

    span = tokens + max(tokens, taps)
    fwd = jnp.asarray(forward_table(span, np.arange(span)))
    inv_conv = jnp.asarray(inverse_table(span, tokens + np.arange(tokens)))
    inv_corr = jnp.asarray(inverse_table(span, np.arange(tokens)))
    inv_taps = jnp.asarray(inverse_table(span, tokens - np.arange(taps)))
    size = max(math.gcd(seq_len, 256), seq_len // 8)
    blocks = seq_len // size
    period = 2 * size
    long_fwd = jnp.asarray(forward_table(period, np.arange(-size, size)))
    long_inv = jnp.asarray(inverse_table(period, np.arange(size)))

    wide = max(512, owned)
    step = min(256, wide)
    grid = (channels // wide,)
    rows_spec = pl.BlockSpec((tokens, wide), lambda i: (0, i))
    taps_spec = pl.BlockSpec((taps, wide), lambda i: (0, i))
    major_spec = pl.BlockSpec((wide // owned, tokens, owned), lambda i: (i, 0, 0))
    taps_major = pl.BlockSpec((wide // owned, taps, owned), lambda i: (i, 0, 0))
    rows_shape = (tokens, channels)
    major_shape = (devices, tokens, owned)
    mid_flops = 8 * span * tokens * channels

    tile = math.gcd(owned, 256)
    long_grid = (owned // tile,)
    long_spec = pl.BlockSpec((seq_len, tile), lambda i: (0, i))
    lag_spec = pl.BlockSpec((tile, seq_len), lambda i: (i, 0))
    spectrum_spec = pl.BlockSpec((blocks, period, tile), lambda i: (0, 0, i))
    spectrum = pltpu.VMEM((blocks, period, tile), F32)
    joint = pltpu.VMEM((blocks, period, tile), BF16)
    long_flops = 4 * period * seq_len * owned

    inputs, gate_pre, gate_mid, gate_long, gate_out = (
        array[0] for array in (layer_input, pre_gate, mid_gate, long_gate, out_gate)
    )
    filter_taps = mid_filter[0]

    adjoint = passed_along(incoming[0], "section", -1)
    mixed_in = call(
        mix_kernel, grid, [rows_spec] * 2, [(rows_shape, BF16, rows_spec)], [inputs, gate_pre],
        2 * tokens * channels, name="mix",
    )
    earlier = shifted(mixed_in, "ctx", 1)
    filter_spectrum = call(
        functools.partial(filter_kernel, blocks), long_grid, [whole_spec(long_fwd), lag_spec],
        [((blocks, period, owned), F32, spectrum_spec)], [long_fwd, long_filter[0]], long_flops,
        name="filter",
    )
    grad_z = call(
        functools.partial(grad_z_kernel, beta), grid, [rows_spec] * 2,
        [(major_shape, BF16, major_spec)], [adjoint, gate_out], 2 * tokens * channels, name="gradz",
    )
    long_in = call(
        functools.partial(branch_kernel, beta, step), grid,
        [whole_spec(fwd), whole_spec(inv_conv)] + [rows_spec] * 2 + [taps_spec] + [rows_spec] * 3,
        [(major_shape, BF16, major_spec)],
        [fwd, inv_conv, earlier, mixed_in, filter_taps, inputs, gate_mid, gate_long], mid_flops,
        name="branch",
    )
    channel_z = lax.all_to_all(grad_z, "ctx", split_axis=0, concat_axis=0, tiled=True)
    channel_w = lax.all_to_all(long_in, "ctx", split_axis=0, concat_axis=0, tiled=True)
    channel_z = channel_z.reshape(seq_len, owned)
    channel_w = channel_w.reshape(seq_len, owned)
    grad_w = call(
        functools.partial(grad_w_kernel, blocks), long_grid,
        [whole_spec(long_fwd), whole_spec(long_inv), long_spec, spectrum_spec],
        [((seq_len, owned), BF16, long_spec)], [long_fwd, long_inv, channel_z, filter_spectrum],
        long_flops, [spectrum, joint], name="gradw",
    )
    returned = lax.all_to_all(
        grad_w.reshape(major_shape), "ctx", split_axis=0, concat_axis=0, tiled=True
    )
    long_grad = call(
        functools.partial(long_grad_kernel, blocks, scale), long_grid,
        [whole_spec(long_fwd), whole_spec(long_inv), long_spec, long_spec],
        [((owned, seq_len), BF16, lag_spec)], [long_fwd, long_inv, channel_z, channel_w],
        2 * long_flops, [spectrum, spectrum, joint], name="longgrad",
    )
    grad_b, tap_parts = call(
        functools.partial(taps_kernel, beta, step), grid,
        [whole_spec(fwd), whole_spec(inv_taps)] + [rows_spec] * 3 + [major_spec] + [rows_spec] * 2,
        [(rows_shape, BF16, rows_spec), ((devices, taps, owned), BF16, taps_major)],
        [fwd, inv_taps, earlier, mixed_in, adjoint, returned, gate_long, gate_mid], mid_flops,
        name="taps",
    )
    later = shifted(grad_b, "ctx", -1)
    gathered = lax.all_to_all(tap_parts, "ctx", split_axis=0, concat_axis=0, tiled=True)
    input_grad = call(
        functools.partial(input_grad_kernel, step), grid,
        [whole_spec(fwd), whole_spec(inv_corr)] + [rows_spec] * 2 + [taps_spec, rows_spec, major_spec]
        + [rows_spec] * 2,
        [(rows_shape, BF16, rows_spec)],
        [fwd, inv_corr, grad_b, later, filter_taps, adjoint, returned, gate_long, gate_pre],
        mid_flops, name="inputgrad",
    )
    mid_grad = call(
        functools.partial(total_kernel, scale), (1,), [whole_spec(gathered)],
        [((taps, owned), BF16, pl.BlockSpec((taps, owned), lambda i: (0, 0)))], [gathered],
        devices * taps * owned, name="midgrad",
    )
    return (input_grad[None], long_grad[None], mid_grad[None])


def solution(mesh):
    placed = (
        P("section", "ctx", None),
        P("section", "ctx", None),
        P("section", "ctx", None),
        P("section", "ctx", None),
        P("section", "ctx", None),
        P("section", "ctx", None),
        P("section", "ctx", None),
        P("section", None, None),
    )
    return jax.shard_map(
        per_device,
        mesh=mesh,
        in_specs=placed,
        out_specs=(P("section", "ctx", None), P("section", "ctx", None), P("section", None, "ctx")),
        check_vma=False,
    )
```

time: 355 us -> 203 us (0.57)
  the two profiles are of different devices: /device:TPU:0 before, /device:TPU:11 now
where the time goes in v1:
time: 203 us; the launch traced here: 202 us
  waiting for transfers between devices  106 us (52%)
  Pallas kernels  43.4 us (21%)
  starting transfers between devices  32.4 us (16%)
  local copies, waits for them, and re-layouts  19.4 us (10%)
    ppermute x2, waiting for transfers between devices, shifted(): return lax.ppermute(array, axis, pairs)  52.3 us
    pallas_call x9, Pallas kernels, call(): pl.pallas_call(body, grid=grid, in_specs=ins, out_specs=[spec for _, _, s...  43.4 us
    ppermute x1, waiting for transfers between devices, passed_along(): return lax.ppermute(value, axis, pairs)  24.9 us
    unnamed x52, local copies, waits for them, and re-layouts  19.4 us
    all_to_all x1, waiting for transfers between devices, per_device(): lax.all_to_all(grad_z, 'ctx', split_axis=0, concat_axis=0, tiled=True)  18.3 us
    all_to_all x1, waiting for transfers between devices, per_device(): lax.all_to_all(long_in, 'ctx', split_axis=0, concat_axis=0, tiled=True)  10.7 us
    all_to_all x1, starting transfers between devices, per_device(): lax.all_to_all(tap_parts, 'ctx', split_axis=0, concat_axis=0, tiled=True)  7.26 us
    all_to_all x1, starting transfers between devices, per_device(): lax.all_to_all(grad_w.reshape(major_shape), 'ctx', split_axis=0, concat_a...  7.16 us
  transfers between devices with their start and end apart: 7, of which 5 were waited for; matrix products, arithmetic and copies ran while one was open for 0% of the time, Pallas kernels for 17%

profile of v1, /device:TPU:11, one launch (start us, length us, event | category | flops | bytes accessed | tf_op | source)
XLA Modules:
  0.0 202.1 jit_solution(14271621353327792874)
XLA Ops:
  0.6 0.3 collective-permute-start.1
  0.9 24.9 %collective-permute-done.1.adjoint_ref = bf16[128,4096]{1,0:T(8,128)(2,1)S(1)} collective-permute-done((bf16[128,4096]{1,0:T(8,128)(2,1)}, bf16[128,4096]{1,0:T(8,128)(2,1)S(1)}, u32[]{:S(2)}, u32[]{:S(2)}) %collective-permute-start.1) | collective-permute-done | bytes 1048608 | tf_op jit(solution)/shard_map/ppermute | solution.py:20
  25.8 1.2 copy-done.17
  27.0 3.0 %gradz.1 = bf16[8,128,512]{2,1,0:T(8,128)(2,1)} custom-call(bf16[128,4096]{1,0:T(8,128)(2,1)S(1)} %collective-permute-done.1.adjoint_ref, bf16[128,4096]{1,0:T(8,128)(2,1)S(1)} %bitcast.23), custom_call_target="tpu_custom_call" | custom-call | flops 1048576 | bytes 3145728 | tf_op jit(solution)/shard_map/gradz/pallas_call | solution.py:215
  30.0 6.6 %all-to-all-start = ((bf16[8,128,512]{2,1,0:T(8,128)(2,1)}), bf16[8,128,512]{2,1,0:T(8,128)(2,1)S(1)}, u32[]{:S(2)}, u32[]{:S(2)}) async-start(bf16[8,128,512]{2,1,0:T(8,128)(2,1)} %gradz.1), calls=%async_computation | async-start | bytes 2097152 | tf_op jit(solution)/shard_map/all_to_all | solution.py:303
  36.6 0.0 copy-done.19
  36.7 1.0 copy-done.13
  37.7 1.7 filter.1.filt_ref
  39.4 0.0 copy-start
  39.4 2.0 copy-done
  41.4 18.3 %all-to-all-done = bf16[8,128,512]{2,1,0:T(8,128)(2,1)S(1)} async-done(((bf16[8,128,512]{2,1,0:T(8,128)(2,1)}), bf16[8,128,512]{2,1,0:T(8,128)(2,1)S(1)}, u32[]{:S(2)}, u32[]{:S(2)}) %all-to-all-start) | async-done | bytes 1048608 | tf_op jit(solution)/shard_map/all_to_all | solution.py:303
  59.7 0.0 copy-done.22
  59.7 1.4 copy-done.14
  61.1 5.1 %gradw.1 = bf16[1024,512]{1,0:T(8,128)(2,1)S(1)} custom-call(bf16[512,512]{1,0:T(8,128)(2,1)S(1)} %copy-done.14, bf16[256,512]{1,0:T(8,128)(2,1)S(1)} %copy-done.22, bf16[1024,512]{1,0:T(8,128)(2,1)S(1)} %bitcast.16, f32[4,512,512]{2,1,0:T(8,128)} %copy-done), custom_call_target="tpu_custom_call" | custom-call | flops 1073741824 | bytes 7077888 | tf_op jit(solution)/shard_map/gradw/pallas_call | solution.py:215
  66.2 0.0 copy-start.9
  66.2 1.0 copy-done.9
  67.2 0.0 copy-done.6
  67.2 7.2 %all-to-all-start.1 = ((bf16[8,128,512]{2,1,0:T(8,128)(2,1)}), bf16[8,128,512]{2,1,0:T(8,128)(2,1)S(1)}, u32[]{:S(2)}, u32[]{:S(2)}) async-start(bf16[8,128,512]{2,1,0:T(8,128)(2,1)} %bitcast.18), calls=%async_computation.1 | async-start | bytes 2097152 | tf_op jit(solution)/shard_map/all_to_all | solution.py:313
  74.4 1.2 copy-done.3
  75.6 1.2 copy-done.10
  76.8 0.6 mix.1.mixed_ref
  77.4 3.4 %collective-permute-start = (bf16[128,4096]{1,0:T(8,128)(2,1)S(1)}, bf16[128,4096]{1,0:T(8,128)(2,1)S(1)}, u32[]{:S(2)}, u32[]{:S(2)}) collective-permute-start(bf16[128,4096]{1,0:T(8,128)(2,1)S(1)} %mix.1.mixed_ref), channel_id=1, source_target_pairs={{0,1},{1,2},{2,3},{3,4},{4,5},{5,6},{6,7},{8,9},{9,10},{10,11},{11... | collective-permute-start | bytes 3145736 | tf_op jit(solution)/shard_map/ppermute | solution.py:26
  80.8 27.8 %collective-permute-done.earlier_ref = bf16[128,4096]{1,0:T(8,128)(2,1)S(1)} collective-permute-done((bf16[128,4096]{1,0:T(8,128)(2,1)S(1)}, bf16[128,4096]{1,0:T(8,128)(2,1)S(1)}, u32[]{:S(2)}, u32[]{:S(2)}) %collective-permute-start) | collective-permute-done | bytes 1048608 | tf_op jit(solution)/shard_map/ppermute | solution.py:26
  108.6 1.2 copy-done.11
  109.8 0.8 copy-done.25
  110.7 8.2 %branch.1 = bf16[8,128,512]{2,1,0:T(8,128)(2,1)S(1)} custom-call(bf16[256,256]{1,0:T(8,128)(2,1)S(1)} %copy-done.16, bf16[128,256]{1,0:T(8,128)(2,1)S(1)} %copy-done.25, bf16[128,4096]{1,0:T(8,128)(2,1)S(1)} %collective-permute-done.earlier_ref, bf16[128,4096]{1,0:T(8,128)(2,1)S(1)} %mix.1.mixed_ref, bf16[128,4096]{1,0:T(8,128)(2,1)S(1)} %bitcast.21, ...), custom_call_target="tpu_custom_call" | custom-call | flops 1073741824 | bytes 7536640 | tf_op jit(solution)/shard_map/branch/pallas_call | solution.py:215
  118.8 0.0 copy-start.4
  118.9 1.0 copy-done.4
  119.8 1.0 copy-done.8
  120.8 0.0 all-to-all-done.1.grad_w_ref
  120.8 5.2 %all-to-all-start.2 = ((bf16[8,128,512]{2,1,0:T(8,128)(2,1)}), bf16[8,128,512]{2,1,0:T(8,128)(2,1)}, u32[]{:S(2)}, u32[]{:S(2)}) async-start(bf16[8,128,512]{2,1,0:T(8,128)(2,1)} %copy-done.8), calls=%async_computation.2 | async-start | bytes 2097152 | tf_op jit(solution)/shard_map/all_to_all | solution.py:304
  126.1 1.2 copy-done.5
  127.3 0.8 copy-done.24
  128.1 8.3 %taps.1 = (bf16[128,4096]{1,0:T(8,128)(2,1)S(1)}, bf16[8,128,512]{2,1,0:T(8,128)(2,1)S(1)}) custom-call(bf16[256,256]{1,0:T(8,128)(2,1)S(1)} %copy-done.16, bf16[128,256]{1,0:T(8,128)(2,1)S(1)} %copy-done.24, bf16[128,4096]{1,0:T(8,128)(2,1)S(1)} %copy-done.5, bf16[128,4096]{1,0:T(8,128)(2,1)S(1)} %mix.1.mixed_ref, ...), custom_call_target="tpu_custom_call" | custom-call | flops 1073741824 | bytes 8585216 | tf_op jit(solution)/shard_map/taps/pallas_call | solution.py:215
  136.4 1.0 copy-done.18
  137.4 1.0 copy-done.20
  138.4 10.7 %all-to-all-done.2 = bf16[8,128,512]{2,1,0:T(8,128)(2,1)} async-done(((bf16[8,128,512]{2,1,0:T(8,128)(2,1)}), bf16[8,128,512]{2,1,0:T(8,128)(2,1)}, u32[]{:S(2)}, u32[]{:S(2)}) %all-to-all-start.2) | async-done | bytes 1048608 | tf_op jit(solution)/shard_map/all_to_all | solution.py:304
  149.1 7.3 %all-to-all-start.3 = ((bf16[8,128,512]{2,1,0:T(8,128)(2,1)}), bf16[8,128,512]{2,1,0:T(8,128)(2,1)S(1)}, u32[]{:S(2)}, u32[]{:S(2)}) async-start(bf16[8,128,512]{2,1,0:T(8,128)(2,1)} %copy-done.18), calls=%async_computation.3 | async-start | bytes 2097152 | tf_op jit(solution)/shard_map/all_to_all | solution.py:330
  156.4 2.4 %collective-permute-start.2 = (bf16[128,4096]{1,0:T(8,128)(2,1)}, bf16[128,4096]{1,0:T(8,128)(2,1)S(1)}, u32[]{:S(2)}, u32[]{:S(2)}) collective-permute-start(bf16[128,4096]{1,0:T(8,128)(2,1)} %copy-done.20), channel_id=1, source_target_pairs={{1,0},{2,1},{3,2},{4,3},{5,4},{6,5},{7,6},{9,8},{10,9},{11,10},{12... | collective-permute-start | bytes 3145736 | tf_op jit(solution)/shard_map/ppermute | solution.py:26
  158.8 0.0 copy-start.7
  158.8 1.2 copy-done.7
  160.0 1.0 copy-done.15
  161.0 7.0 %longgrad.1 = bf16[512,1024]{1,0:T(8,128)(2,1)} custom-call(bf16[512,512]{1,0:T(8,128)(2,1)S(1)} %copy-done.15, bf16[256,512]{1,0:T(8,128)(2,1)S(1)} %copy-done.22, bf16[1024,512]{1,0:T(8,128)(2,1)S(1)} %bitcast.17, bf16[1024,512]{1,0:T(8,128)(2,1)} %bitcast.11.long_ref), custom_call_target="tpu_custom_call" | custom-call | flops 2147483648 | bytes 3932160 | tf_op jit(solution)/shard_map/longgrad/pallas_call | solution.py:215
  168.1 24.4 %collective-permute-done.2.later_ref = bf16[128,4096]{1,0:T(8,128)(2,1)S(1)} collective-permute-done((bf16[128,4096]{1,0:T(8,128)(2,1)}, bf16[128,4096]{1,0:T(8,128)(2,1)S(1)}, u32[]{:S(2)}, u32[]{:S(2)}) %collective-permute-start.2) | collective-permute-done | bytes 1048608 | tf_op jit(solution)/shard_map/ppermute | solution.py:26
  192.5 0.0 copy-done.2
  192.5 8.8 %inputgrad.1 = bf16[128,4096]{1,0:T(8,128)(2,1)} custom-call(bf16[256,256]{1,0:T(8,128)(2,1)S(1)} %copy-done.16, bf16[128,256]{1,0:T(8,128)(2,1)S(1)} %copy-done.23, bf16[128,4096]{1,0:T(8,128)(2,1)S(1)} %copy-done.21, bf16[128,4096]{1,0:T(8,128)(2,1)S(1)} %collective-permute-done.2.later_ref, bf16[128,4096]{1,0:T(8,128)(2,1)S(1)} %bitcast.22, ...), custom_call_target="tpu_custom_call" | custom-call | flops 1073741824 | bytes 8585216 | tf_op jit(solution)/shard_map/inputgrad/pallas_call | solution.py:215
  201.3 0.0 all-to-all-done.3.parts_ref
  201.3 0.8 midgrad.1
  (27 shorter events, 0.0 us)
Async XLA Ops:
  0.6 25.2 %collective-permute-start.1 = (bf16[128,4096]{1,0:T(8,128)(2,1)}, bf16[128,4096]{1,0:T(8,128)(2,1)S(1)}, u32[]{:S(2)}, u32[]{:S(2)}) collective-permute-start(bf16[128,4096]{1,0:T(8,128)(2,1)} %bitcast.32), channel_id=1, source_target_pairs={{0,24},{8,0},{16,8},{24,16},{1,25},{9,1},{17,9},{25,17},{2,26},{10... | collective-permute-start | bytes 3145736 | tf_op jit(solution)/shard_map/ppermute | solution.py:20
  25.8 1.2 copy-start.17
  27.0 9.6 %copy-start.19 = (bf16[1,512,1024]{2,1,0:T(8,128)(2,1)S(1)}, bf16[1,512,1024]{2,1,0:T(8,128)(2,1)}, u32[]{:S(2)}) copy-start(bf16[1,512,1024]{2,1,0:T(8,128)(2,1)} %param.20) | copy-start | bytes 3145732
  30.0 29.7 %copy-start.22 = (bf16[256,512]{1,0:T(8,128)(2,1)S(1)}, bf16[256,512]{1,0:T(8,128)(2,1)}, u32[]{:S(2)}) copy-start(bf16[256,512]{1,0:T(8,128)(2,1)} %constant.17.clone.inv_ref) | copy-start | bytes 786436
  30.0 29.7 %all-to-all-start = ((bf16[8,128,512]{2,1,0:T(8,128)(2,1)}), bf16[8,128,512]{2,1,0:T(8,128)(2,1)S(1)}, u32[]{:S(2)}, u32[]{:S(2)}) async-start(bf16[8,128,512]{2,1,0:T(8,128)(2,1)} %gradz.1), calls=%async_computation | async-start | bytes 2097152 | tf_op jit(solution)/shard_map/all_to_all | solution.py:303
  36.7 1.0 copy-start.13
  39.4 2.0 copy-start
  59.7 7.5 %copy-start.6 = (bf16[8,128,512]{2,1,0:T(8,128)(2,1)}, bf16[8,128,512]{2,1,0:T(8,128)(2,1)S(1)}, u32[]{:S(2)}) copy-start(bf16[8,128,512]{2,1,0:T(8,128)(2,1)S(1)} %all-to-all-done) | copy-start | bytes 3145732
  59.7 1.4 copy-start.14
  66.2 1.0 copy-start.9
  67.2 41.4 %copy-start.16 = (bf16[256,256]{1,0:T(8,128)(2,1)S(1)}, bf16[256,256]{1,0:T(8,128)(2,1)}, u32[]{:S(2)}) copy-start(bf16[256,256]{1,0:T(8,128)(2,1)} %constant.12.clone.fwd_ref) | copy-start | bytes 393220
  67.2 53.6 %all-to-all-start.1 = ((bf16[8,128,512]{2,1,0:T(8,128)(2,1)}), bf16[8,128,512]{2,1,0:T(8,128)(2,1)S(1)}, u32[]{:S(2)}, u32[]{:S(2)}) async-start(bf16[8,128,512]{2,1,0:T(8,128)(2,1)} %bitcast.18), calls=%async_computation.1 | async-start | bytes 2097152 | tf_op jit(solution)/shard_map/all_to_all | solution.py:313
  74.4 1.2 copy-start.3
  75.6 1.2 copy-start.10
  77.4 31.2 %collective-permute-start = (bf16[128,4096]{1,0:T(8,128)(2,1)S(1)}, bf16[128,4096]{1,0:T(8,128)(2,1)S(1)}, u32[]{:S(2)}, u32[]{:S(2)}) collective-permute-start(bf16[128,4096]{1,0:T(8,128)(2,1)S(1)} %mix.1.mixed_ref), channel_id=1, source_target_pairs={{0,1},{1,2},{2,3},{3,4},{4,5},{5,6},{6,7},{8,9},{9,10},{10,11},{11... | collective-permute-start | bytes 3145736 | tf_op jit(solution)/shard_map/ppermute | solution.py:26
  108.6 1.2 copy-start.11
  109.8 0.8 copy-start.25
  118.8 1.0 copy-start.4
  119.8 1.0 copy-start.8
  120.8 5.3 %copy-start.1 = (bf16[8,128,512]{2,1,0:T(8,128)(2,1)}, bf16[8,128,512]{2,1,0:T(8,128)(2,1)S(1)}, u32[]{:S(2)}) copy-start(bf16[8,128,512]{2,1,0:T(8,128)(2,1)S(1)} %all-to-all-done.1.grad_w_ref) | copy-start | bytes 3145732
  120.8 28.3 %all-to-all-start.2 = ((bf16[8,128,512]{2,1,0:T(8,128)(2,1)}), bf16[8,128,512]{2,1,0:T(8,128)(2,1)}, u32[]{:S(2)}, u32[]{:S(2)}) async-start(bf16[8,128,512]{2,1,0:T(8,128)(2,1)} %copy-done.8), calls=%async_computation.2 | async-start | bytes 2097152 | tf_op jit(solution)/shard_map/all_to_all | solution.py:304
  126.1 1.2 copy-start.5
  127.3 0.8 copy-start.24
  136.4 1.0 copy-start.18
  137.4 1.0 copy-start.20
  149.1 43.4 %copy-start.12 = (bf16[1,128,4096]{2,1,0:T(8,128)(2,1)S(1)}, bf16[1,128,4096]{2,1,0:T(8,128)(2,1)}, u32[]{:S(2)}) copy-start(bf16[1,128,4096]{2,1,0:T(8,128)(2,1)} %param.21) | copy-start | bytes 3145732
  149.1 52.2 %all-to-all-start.3 = ((bf16[8,128,512]{2,1,0:T(8,128)(2,1)}), bf16[8,128,512]{2,1,0:T(8,128)(2,1)S(1)}, u32[]{:S(2)}, u32[]{:S(2)}) async-start(bf16[8,128,512]{2,1,0:T(8,128)(2,1)} %copy-done.18), calls=%async_computation.3 | async-start | bytes 2097152 | tf_op jit(solution)/shard_map/all_to_all | solution.py:330
  156.4 36.1 %copy-start.2 = (bf16[8,128,512]{2,1,0:T(8,128)(2,1)S(1)}, bf16[8,128,512]{2,1,0:T(8,128)(2,1)}, u32[]{:S(2)}) copy-start(bf16[8,128,512]{2,1,0:T(8,128)(2,1)} %copy-done.1) | copy-start | bytes 3145732
  156.4 36.1 %collective-permute-start.2 = (bf16[128,4096]{1,0:T(8,128)(2,1)}, bf16[128,4096]{1,0:T(8,128)(2,1)S(1)}, u32[]{:S(2)}, u32[]{:S(2)}) collective-permute-start(bf16[128,4096]{1,0:T(8,128)(2,1)} %copy-done.20), channel_id=1, source_target_pairs={{1,0},{2,1},{3,2},{4,3},{5,4},{6,5},{7,6},{9,8},{10,9},{11,10},{12... | collective-permute-start | bytes 3145736 | tf_op jit(solution)/shard_map/ppermute | solution.py:26
  158.8 1.2 copy-start.7
  160.0 1.0 copy-start.15
  161.0 31.4 %copy-start.21 = (bf16[128,4096]{1,0:T(8,128)(2,1)S(1)}, bf16[128,4096]{1,0:T(8,128)(2,1)}, u32[]{:S(2)}) copy-start(bf16[128,4096]{1,0:T(8,128)(2,1)} %copy-done.20) | copy-start | bytes 3145732
  161.0 31.4 %copy-start.23 = (bf16[128,256]{1,0:T(8,128)(2,1)S(1)}, bf16[128,256]{1,0:T(8,128)(2,1)}, u32[]{:S(2)}) copy-start(bf16[128,256]{1,0:T(8,128)(2,1)} %constant.14.clone.inv_ref) | copy-start | bytes 196612

commit v2 on v1

--- a/solution.py
+++ b/solution.py
@@ -11,7 +11,7 @@
 
 BF16 = jnp.bfloat16
 F32 = jnp.float32
-VMEM_BYTES = 48 * 1024 * 1024
+VMEM_BYTES = 60 * 1024 * 1024
 
 
 def passed_along(value, axis, steps):
@@ -104,10 +104,12 @@
 
 
 def taps_kernel(
-    beta, step, fwd_ref, inv_ref, earlier_ref, mixed_ref, adjoint_ref, grad_w_ref, long_ref, mid_ref,
-    grad_b_ref, part_ref,
+    beta, step, core_ref, fwd_ref, inv_ref, earlier_ref, mixed_ref, adjoint_ref, grad_w_ref, long_ref,
+    mid_ref, grad_b_ref, part_ref,
 ):
     tokens = mixed_ref.shape[0]
+    owned = part_ref.shape[3]
+    core = core_ref[0]
     for start in range(0, mixed_ref.shape[1], step):
         cols = slice(start, start + step)
         grad_w = get_columns(grad_w_ref, start, step).astype(F32)
@@ -118,8 +120,12 @@
             fwd_ref[:, tokens:], mixed_ref[:, cols]
         )
         grad = dot(fwd_ref[:, :tokens], grad_b)
-        part = dot(inv_ref[...], times_conj(signal, grad))
-        put_columns(part_ref, part.astype(BF16), start)
+        part = dot(inv_ref[...], times_conj(signal, grad)).astype(BF16)
+        width = min(owned, step)
+        for j in range(0, step, width):
+            owner, at = divmod(start + j, owned)
+            slot = core if owner % 2 == 0 else 1 - core
+            part_ref[slot, owner // 2, :, at : at + width] = part[:, j : j + width]
 
 
 def input_grad_kernel(
@@ -253,13 +259,13 @@
     long_fwd = jnp.asarray(forward_table(period, np.arange(-size, size)))
     long_inv = jnp.asarray(inverse_table(period, np.arange(size)))
 
-    wide = max(512, owned)
+    wide = max(1024, 2 * owned)
     step = min(256, wide)
     grid = (channels // wide,)
     rows_spec = pl.BlockSpec((tokens, wide), lambda i: (0, i))
     taps_spec = pl.BlockSpec((taps, wide), lambda i: (0, i))
     major_spec = pl.BlockSpec((wide // owned, tokens, owned), lambda i: (i, 0, 0))
-    taps_major = pl.BlockSpec((wide // owned, taps, owned), lambda i: (i, 0, 0))
+    taps_major = pl.BlockSpec((2, wide // owned // 2, taps, owned), lambda i: (0, i, 0, 0))
     rows_shape = (tokens, channels)
     major_shape = (devices, tokens, owned)
     mid_flops = 8 * span * tokens * channels
@@ -278,21 +284,13 @@
     )
     filter_taps = mid_filter[0]
 
-    adjoint = passed_along(incoming[0], "section", -1)
     mixed_in = call(
         mix_kernel, grid, [rows_spec] * 2, [(rows_shape, BF16, rows_spec)], [inputs, gate_pre],
         2 * tokens * channels, name="mix",
     )
+    sent, mixed_in = lax.optimization_barrier((incoming[0], mixed_in))
     earlier = shifted(mixed_in, "ctx", 1)
-    filter_spectrum = call(
-        functools.partial(filter_kernel, blocks), long_grid, [whole_spec(long_fwd), lag_spec],
-        [((blocks, period, owned), F32, spectrum_spec)], [long_fwd, long_filter[0]], long_flops,
-        name="filter",
-    )
-    grad_z = call(
-        functools.partial(grad_z_kernel, beta), grid, [rows_spec] * 2,
-        [(major_shape, BF16, major_spec)], [adjoint, gate_out], 2 * tokens * channels, name="gradz",
-    )
+    adjoint = passed_along(sent, "section", -1)
     long_in = call(
         functools.partial(branch_kernel, beta, step), grid,
         [whole_spec(fwd), whole_spec(inv_conv)] + [rows_spec] * 2 + [taps_spec] + [rows_spec] * 3,
@@ -300,8 +298,19 @@
         [fwd, inv_conv, earlier, mixed_in, filter_taps, inputs, gate_mid, gate_long], mid_flops,
         name="branch",
     )
+    channel_w = lax.all_to_all(long_in, "ctx", split_axis=0, concat_axis=0, tiled=True)
+    adjoint, long_lags, _ = lax.optimization_barrier((adjoint, long_filter[0], long_in))
+    grad_z = call(
+        functools.partial(grad_z_kernel, beta), grid, [rows_spec] * 2,
+        [(major_shape, BF16, major_spec)], [adjoint, gate_out], 2 * tokens * channels, name="gradz",
+    )
+    filter_spectrum = call(
+        functools.partial(filter_kernel, blocks), long_grid, [whole_spec(long_fwd), lag_spec],
+        [((blocks, period, owned), F32, spectrum_spec)], [long_fwd, long_lags], long_flops,
+        name="filter",
+    )
+    grad_z, channel_w, filter_spectrum = lax.optimization_barrier((grad_z, channel_w, filter_spectrum))
     channel_z = lax.all_to_all(grad_z, "ctx", split_axis=0, concat_axis=0, tiled=True)
-    channel_w = lax.all_to_all(long_in, "ctx", split_axis=0, concat_axis=0, tiled=True)
     channel_z = channel_z.reshape(seq_len, owned)
     channel_w = channel_w.reshape(seq_len, owned)
     grad_w = call(
@@ -313,21 +322,31 @@
     returned = lax.all_to_all(
         grad_w.reshape(major_shape), "ctx", split_axis=0, concat_axis=0, tiled=True
     )
+    channel_z, channel_w, _ = lax.optimization_barrier((channel_z, channel_w, grad_w))
     long_grad = call(
         functools.partial(long_grad_kernel, blocks, scale), long_grid,
         [whole_spec(long_fwd), whole_spec(long_inv), long_spec, long_spec],
         [((owned, seq_len), BF16, lag_spec)], [long_fwd, long_inv, channel_z, channel_w],
         2 * long_flops, [spectrum, spectrum, joint], name="longgrad",
     )
+    returned, long_grad = lax.optimization_barrier((returned, long_grad))
+    core = (lax.axis_index("ctx") % 2).astype(jnp.int32)[None]
     grad_b, tap_parts = call(
         functools.partial(taps_kernel, beta, step), grid,
-        [whole_spec(fwd), whole_spec(inv_taps)] + [rows_spec] * 3 + [major_spec] + [rows_spec] * 2,
-        [(rows_shape, BF16, rows_spec), ((devices, taps, owned), BF16, taps_major)],
-        [fwd, inv_taps, earlier, mixed_in, adjoint, returned, gate_long, gate_mid], mid_flops,
+        [pl.BlockSpec(memory_space=pltpu.SMEM), whole_spec(fwd), whole_spec(inv_taps)]
+        + [rows_spec] * 3 + [major_spec] + [rows_spec] * 2,
+        [(rows_shape, BF16, rows_spec), ((2, devices // 2, taps, owned), BF16, taps_major)],
+        [core, fwd, inv_taps, earlier, mixed_in, adjoint, returned, gate_long, gate_mid], mid_flops,
         name="taps",
     )
+    partner = lax.ppermute(tap_parts[1], "ctx", [(i, i ^ 1) for i in range(devices)])
     later = shifted(grad_b, "ctx", -1)
-    gathered = lax.all_to_all(tap_parts, "ctx", split_axis=0, concat_axis=0, tiled=True)
+    chip_parts = (tap_parts[0].astype(F32) + partner.astype(F32)).astype(BF16)
+    gathered = lax.all_to_all(
+        chip_parts, "ctx", split_axis=0, concat_axis=0, tiled=True,
+        axis_index_groups=[list(range(c, devices, 2)) for c in range(2)],
+    )
+    later, _ = lax.optimization_barrier((later, chip_parts))
     input_grad = call(
         functools.partial(input_grad_kernel, step), grid,
         [whole_spec(fwd), whole_spec(inv_corr)] + [rows_spec] * 2 + [taps_spec, rows_spec, major_spec]

time: 203 us -> 183 us (0.901)
  the two profiles are of different devices: /device:TPU:11 before, /device:TPU:7 now
where the time goes in v2:
time: 183 us; the launch traced here: 182 us
  waiting for transfers between devices  70.4 us (38%)
  Pallas kernels  51 us (28%)
  blocking collectives  31 us (17%)
  starting transfers between devices  20.9 us (11%)
  local copies, waits for them, and re-layouts  5.83 us (3%)
  other arithmetic  1.97 us (1%)
    pallas_call x9, Pallas kernels, call(): pl.pallas_call(body, grid=grid, in_specs=ins, out_specs=[spec for _, _, s...  51 us
    all_to_all x1, blocking collectives, per_device(): lax.all_to_all(grad_z, 'ctx', split_axis=0, concat_axis=0, tiled=True)  31 us
    ppermute x2, waiting for transfers between devices, shifted(): return lax.ppermute(array, axis, pairs)  26.6 us
    ppermute x1, waiting for transfers between devices, passed_along(): return lax.ppermute(value, axis, pairs)  25.4 us
    all_to_all x1, waiting for transfers between devices, per_device(): lax.all_to_all(grad_w.reshape(major_shape), 'ctx', split_axis=0, concat_a...  18.4 us
    all_to_all x1, starting transfers between devices, per_device(): lax.all_to_all(long_in, 'ctx', split_axis=0, concat_axis=0, tiled=True)  6.07 us
    ppermute x2, starting transfers between devices, shifted(): return lax.ppermute(array, axis, pairs)  5.67 us
    unnamed x16, local copies, waits for them, and re-layouts  4.75 us
  transfers between devices with their start and end apart: 7, of which 4 were waited for; matrix products, arithmetic and copies ran while one was open for 1% of the time, Pallas kernels for 13%

profile of v2, /device:TPU:7, one launch (start us, length us, event | category | flops | bytes accessed | tf_op | source)
XLA Modules:
  0.0 181.9 jit_solution(8961508109526753771)
XLA Ops:
  0.6 3.6 %mix.1.mixed_ref = bf16[128,4096]{1,0:T(8,128)(2,1)} custom-call(bf16[128,4096]{1,0:T(8,128)(2,1)} %bitcast.23, bf16[128,4096]{1,0:T(8,128)(2,1)} %bitcast.30), custom_call_target="tpu_custom_call" | custom-call | flops 1048576 | bytes 3145728 | tf_op jit(solution)/shard_map/mix/pallas_call | solution.py:221
  4.3 3.8 %collective-permute-start = (bf16[128,4096]{1,0:T(8,128)(2,1)}, bf16[128,4096]{1,0:T(8,128)(2,1)S(1)}, u32[]{:S(2)}, u32[]{:S(2)}) collective-permute-start(bf16[128,4096]{1,0:T(8,128)(2,1)} %mix.1.mixed_ref), channel_id=1, source_target_pairs={{0,1},{1,2},{2,3},{3,4},{4,5},{5,6},{6,7},{8,9},{9,10},{10,11},{11... | collective-permute-start | bytes 3145736 | tf_op jit(solution)/shard_map/ppermute | solution.py:26
  8.0 12.0 %collective-permute-done.earlier_ref = bf16[128,4096]{1,0:T(8,128)(2,1)S(1)} collective-permute-done((bf16[128,4096]{1,0:T(8,128)(2,1)}, bf16[128,4096]{1,0:T(8,128)(2,1)S(1)}, u32[]{:S(2)}, u32[]{:S(2)}) %collective-permute-start) | collective-permute-done | bytes 1048608 | tf_op jit(solution)/shard_map/ppermute | solution.py:26
  20.1 0.0 copy-start.2
  20.1 1.0 copy-done.2
  21.1 0.0 copy-start.7
  21.1 8.1 %branch.1 = bf16[8,128,512]{2,1,0:T(8,128)(2,1)} custom-call(bf16[256,256]{1,0:T(8,128)(2,1)} %constant.29.clone.fwd_ref, bf16[128,256]{1,0:T(8,128)(2,1)} %constant.30.clone.inv_ref, bf16[128,4096]{1,0:T(8,128)(2,1)} %copy-done.2, bf16[128,4096]{1,0:T(8,128)(2,1)} %mix.1.mixed_ref, bf16[128,4096]{1,0:T(8,128)(2,1)} %bitcast.32, bf16[128,4096]{1,0:T(8,128)(2,1)} %bitcast.24, ...), custom_call_target="tpu_custom_call" | custom-call | flops 1073741824 | bytes 7536640 | tf_op jit(solution)/shard_map/branch/pallas_call | solution.py:221
  29.2 6.1 %all-to-all-start = ((bf16[8,128,512]{2,1,0:T(8,128)(2,1)}), bf16[8,128,512]{2,1,0:T(8,128)(2,1)S(1)}, u32[]{:S(2)}, u32[]{:S(2)}) async-start(bf16[8,128,512]{2,1,0:T(8,128)(2,1)} %branch.1), calls=%async_computation | async-start | bytes 2097152 | tf_op jit(solution)/shard_map/all_to_all | solution.py:301
  35.3 0.0 copy-done.7
  35.3 0.2 collective-permute-start.1
  35.6 25.4 %collective-permute-done.1.adjoint_ref = bf16[128,4096]{1,0:T(8,128)(2,1)S(1)} collective-permute-done((bf16[128,4096]{1,0:T(8,128)(2,1)S(1)}, bf16[128,4096]{1,0:T(8,128)(2,1)S(1)}, u32[]{:S(2)}, u32[]{:S(2)}) %collective-permute-start.1) | collective-permute-done | bytes 1048608 | tf_op jit(solution)/shard_map/ppermute | solution.py:20
  60.9 0.0 copy-start
  60.9 1.0 copy-done
  61.9 3.7 %gradz.1 = bf16[8,128,512]{2,1,0:T(8,128)(2,1)} custom-call(bf16[128,4096]{1,0:T(8,128)(2,1)} %copy-done, bf16[128,4096]{1,0:T(8,128)(2,1)} %bitcast.34), custom_call_target="tpu_custom_call" | custom-call | flops 1048576 | bytes 3145728 | tf_op jit(solution)/shard_map/gradz/pallas_call | solution.py:221
  65.6 0.0 copy-start.3
  65.6 4.1 %filter.1.filt_ref = f32[4,512,512]{2,1,0:T(8,128)} custom-call(bf16[512,512]{1,0:T(8,128)(2,1)} %constant.33.clone.fwd_ref, bf16[512,1024]{1,0:T(8,128)(2,1)} %bitcast.36), custom_call_target="tpu_custom_call" | custom-call | flops 1073741824 | bytes 5767168 | tf_op jit(solution)/shard_map/filter/pallas_call | solution.py:221
  69.6 0.0 all-to-all-done
  69.6 0.0 copy-done.3
  69.7 0.0 copy-start.5
  69.7 31.0 %all_to_all.20 = bf16[8,128,512]{2,1,0:T(8,128)(2,1)} all-to-all(bf16[8,128,512]{2,1,0:T(8,128)(2,1)S(1)} %copy-done.3), channel_id=1, replica_groups=mesh['section'=4,'ctx'=8] {'ctx'}, dimensions={0} | all-to-all | bytes 2097152 | tf_op jit(solution)/shard_map/all_to_all | solution.py:313
  100.7 6.2 %gradw.1 = bf16[1024,512]{1,0:T(8,128)(2,1)} custom-call(bf16[512,512]{1,0:T(8,128)(2,1)} %constant.33.clone.fwd_ref, bf16[256,512]{1,0:T(8,128)(2,1)} %constant.34.clone.inv_ref, bf16[1024,512]{1,0:T(8,128)(2,1)} %bitcast.27, f32[4,512,512]{2,1,0:T(8,128)} %filter.1.filt_ref), custom_call_target="tpu_custom_call" | custom-call | flops 1073741824 | bytes 7077888 | tf_op jit(solution)/shard_map/gradw/pallas_call | solution.py:221
  106.9 0.0 copy-done.5
  106.9 4.5 %all-to-all-start.2 = ((bf16[8,128,512]{2,1,0:T(8,128)(2,1)}), bf16[8,128,512]{2,1,0:T(8,128)(2,1)S(1)}, u32[]{:S(2)}, u32[]{:S(2)}) async-start(bf16[8,128,512]{2,1,0:T(8,128)(2,1)} %bitcast.29), calls=%async_computation.2 | async-start | bytes 2097152 | tf_op jit(solution)/shard_map/all_to_all | solution.py:322
  111.4 7.3 %longgrad.1 = bf16[512,1024]{1,0:T(8,128)(2,1)} custom-call(bf16[512,512]{1,0:T(8,128)(2,1)} %constant.33.clone.fwd_ref, bf16[256,512]{1,0:T(8,128)(2,1)} %constant.34.clone.inv_ref, bf16[1024,512]{1,0:T(8,128)(2,1)} %bitcast.28, bf16[1024,512]{1,0:T(8,128)(2,1)} %bitcast.35), custom_call_target="tpu_custom_call" | custom-call | flops 2147483648 | bytes 3932160 | tf_op jit(solution)/shard_map/longgrad/pallas_call | solution.py:221
  118.7 18.4 %all-to-all-done.2.grad_w_ref = bf16[8,128,512]{2,1,0:T(8,128)(2,1)S(1)} async-done(((bf16[8,128,512]{2,1,0:T(8,128)(2,1)}), bf16[8,128,512]{2,1,0:T(8,128)(2,1)S(1)}, u32[]{:S(2)}, u32[]{:S(2)}) %all-to-all-start.2) | async-done | bytes 1048608 | tf_op jit(solution)/shard_map/all_to_all | solution.py:322
  137.2 0.0 copy-start.1
  137.2 1.0 copy-done.1
  138.1 8.0 %taps.1 = (bf16[128,4096]{1,0:T(8,128)(2,1)}, bf16[2,4,128,512]{3,2,1,0:T(8,128)(2,1)}) custom-call(s32[1]{0:T(128)} %bitcast.core_ref, bf16[256,256]{1,0:T(8,128)(2,1)} %constant.29.clone.fwd_ref, bf16[128,256]{1,0:T(8,128)(2,1)} %constant.32.clone.inv_ref, bf16[128,4096]{1,0:T(8,128)(2,1)} %copy-done.2, bf16[128,4096]{1,0:T(8,128)(2,1)} %mix.1.mixed_ref, ...), custom_call_target="tpu_custom_call" | custom-call | flops 1073741824 | bytes 8585220 | tf_op jit(solution)/shard_map/taps/pallas_call | solution.py:221
  146.1 1.1 slice_bitcast_fusion
  147.2 0.9 collective-permute-start.3
  148.1 1.9 %collective-permute-start.2 = (bf16[128,4096]{1,0:T(8,128)(2,1)}, bf16[128,4096]{1,0:T(8,128)(2,1)S(1)}, u32[]{:S(2)}, u32[]{:S(2)}) collective-permute-start(bf16[128,4096]{1,0:T(8,128)(2,1)} %get-tuple-element.27.grad_b_ref), channel_id=1, source_target_pairs={{1,0},{2,1},{3,2},{4,3},{5,4},{6,5},{7,6},{9,8},{10,9},{11,10},{12... | collective-permute-start | bytes 3145736 | tf_op jit(solution)/shard_map/ppermute | solution.py:26
  150.0 0.0 collective-permute-done.3
  150.1 2.0 %fusion = bf16[4,128,512]{2,1,0:T(8,128)(2,1)} fusion(bf16[4,128,512]{2,1,0:T(8,128)(2,1)S(1)} %collective-permute-done.3, bf16[2,4,128,512]{3,2,1,0:T(8,128)(2,1)} %get-tuple-element.28), kind=kLoop, calls=%fused_computation.1 | loop fusion | flops 1048576 | bytes 1572864 | tf_op jit(solution)/shard_map/convert_element_type | solution.py:344
  152.0 3.5 %all-to-all-start.3 = ((bf16[4,128,512]{2,1,0:T(8,128)(2,1)}), bf16[4,128,512]{2,1,0:T(8,128)(2,1)S(1)}, u32[]{:S(2)}, u32[]{:S(2)}) async-start(bf16[4,128,512]{2,1,0:T(8,128)(2,1)} %fusion), calls=%async_computation.3 | async-start | bytes 1048576 | tf_op jit(solution)/shard_map/all_to_all | solution.py:345
  155.5 14.5 %collective-permute-done.2.later_ref = bf16[128,4096]{1,0:T(8,128)(2,1)S(1)} collective-permute-done((bf16[128,4096]{1,0:T(8,128)(2,1)}, bf16[128,4096]{1,0:T(8,128)(2,1)S(1)}, u32[]{:S(2)}, u32[]{:S(2)}) %collective-permute-start.2) | collective-permute-done | bytes 1048608 | tf_op jit(solution)/shard_map/ppermute | solution.py:26
  170.0 0.0 copy-start.6
  170.0 1.0 copy-done.6
  171.0 8.3 %inputgrad.1 = bf16[128,4096]{1,0:T(8,128)(2,1)} custom-call(bf16[256,256]{1,0:T(8,128)(2,1)} %constant.29.clone.fwd_ref, bf16[128,256]{1,0:T(8,128)(2,1)} %constant.31.clone.inv_ref, bf16[128,4096]{1,0:T(8,128)(2,1)} %get-tuple-element.27.grad_b_ref, bf16[128,4096]{1,0:T(8,128)(2,1)} %copy-done.6, bf16[128,4096]{1,0:T(8,128)(2,1)} %bitcast.33, ...), custom_call_target="tpu_custom_call" | custom-call | flops 1073741824 | bytes 8585216 | tf_op jit(solution)/shard_map/inputgrad/pallas_call | solution.py:221
  179.3 0.0 all-to-all-done.3.parts_ref
  179.3 0.0 copy-start.4
  179.3 0.8 copy-done.4
  180.1 1.8 midgrad.1
Async XLA Ops:
  4.3 15.8 %collective-permute-start = (bf16[128,4096]{1,0:T(8,128)(2,1)}, bf16[128,4096]{1,0:T(8,128)(2,1)S(1)}, u32[]{:S(2)}, u32[]{:S(2)}) collective-permute-start(bf16[128,4096]{1,0:T(8,128)(2,1)} %mix.1.mixed_ref), channel_id=1, source_target_pairs={{0,1},{1,2},{2,3},{3,4},{4,5},{5,6},{6,7},{8,9},{9,10},{10,11},{11... | collective-permute-start | bytes 3145736 | tf_op jit(solution)/shard_map/ppermute | solution.py:26
  20.1 1.0 copy-start.2
  21.1 14.2 %copy-start.7 = (bf16[1,128,4096]{2,1,0:T(8,128)(2,1)S(1)}, bf16[1,128,4096]{2,1,0:T(8,128)(2,1)}, u32[]{:S(2)}) copy-start(bf16[1,128,4096]{2,1,0:T(8,128)(2,1)} %param.14) | copy-start | bytes 3145732
  29.2 40.4 %all-to-all-start = ((bf16[8,128,512]{2,1,0:T(8,128)(2,1)}), bf16[8,128,512]{2,1,0:T(8,128)(2,1)S(1)}, u32[]{:S(2)}, u32[]{:S(2)}) async-start(bf16[8,128,512]{2,1,0:T(8,128)(2,1)} %branch.1), calls=%async_computation | async-start | bytes 2097152 | tf_op jit(solution)/shard_map/all_to_all | solution.py:301
  35.3 25.6 %collective-permute-start.1 = (bf16[128,4096]{1,0:T(8,128)(2,1)S(1)}, bf16[128,4096]{1,0:T(8,128)(2,1)S(1)}, u32[]{:S(2)}, u32[]{:S(2)}) collective-permute-start(bf16[128,4096]{1,0:T(8,128)(2,1)S(1)} %bitcast.39), channel_id=1, source_target_pairs={{0,24},{8,0},{16,8},{24,16},{1,25},{9,1},{17,9},{25,17},{2,26},{10... | collective-permute-start | bytes 3145736 | tf_op jit(solution)/shard_map/ppermute | solution.py:20
  60.9 1.0 copy-start
  65.6 4.1 %copy-start.3 = (bf16[8,128,512]{2,1,0:T(8,128)(2,1)S(1)}, bf16[8,128,512]{2,1,0:T(8,128)(2,1)}, u32[]{:S(2)}) copy-start(bf16[8,128,512]{2,1,0:T(8,128)(2,1)} %gradz.1) | copy-start | bytes 3145732
  69.7 37.3 %copy-start.5 = (bf16[8,128,512]{2,1,0:T(8,128)(2,1)}, bf16[8,128,512]{2,1,0:T(8,128)(2,1)S(1)}, u32[]{:S(2)}) copy-start(bf16[8,128,512]{2,1,0:T(8,128)(2,1)S(1)} %all-to-all-done) | copy-start | bytes 3145732
  106.9 30.2 %all-to-all-start.2 = ((bf16[8,128,512]{2,1,0:T(8,128)(2,1)}), bf16[8,128,512]{2,1,0:T(8,128)(2,1)S(1)}, u32[]{:S(2)}, u32[]{:S(2)}) async-start(bf16[8,128,512]{2,1,0:T(8,128)(2,1)} %bitcast.29), calls=%async_computation.2 | async-start | bytes 2097152 | tf_op jit(solution)/shard_map/all_to_all | solution.py:322
  137.2 1.0 copy-start.1
  147.2 2.9 %collective-permute-start.3 = (bf16[4,128,512]{2,1,0:T(8,128)(2,1)S(1)}, bf16[4,128,512]{2,1,0:T(8,128)(2,1)S(1)}, u32[]{:S(2)}, u32[]{:S(2)}) collective-permute-start(bf16[4,128,512]{2,1,0:T(8,128)(2,1)S(1)} %slice_bitcast_fusion), channel_id=1, source_target_pairs={{0,1},{1,0},{2,3},{3,2},{4,5},{5,4},{6,7},{7,6},{8,9},{9,8},{10,11... | collective-permute-start | bytes 1572872 | tf_op jit(solution)/shard_map/ppermute | solution.py:342
  148.1 21.9 %collective-permute-start.2 = (bf16[128,4096]{1,0:T(8,128)(2,1)}, bf16[128,4096]{1,0:T(8,128)(2,1)S(1)}, u32[]{:S(2)}, u32[]{:S(2)}) collective-permute-start(bf16[128,4096]{1,0:T(8,128)(2,1)} %get-tuple-element.27.grad_b_ref), channel_id=1, source_target_pairs={{1,0},{2,1},{3,2},{4,3},{5,4},{6,5},{7,6},{9,8},{10,9},{11,10},{12... | collective-permute-start | bytes 3145736 | tf_op jit(solution)/shard_map/ppermute | solution.py:26
  152.0 27.3 %all-to-all-start.3 = ((bf16[4,128,512]{2,1,0:T(8,128)(2,1)}), bf16[4,128,512]{2,1,0:T(8,128)(2,1)S(1)}, u32[]{:S(2)}, u32[]{:S(2)}) async-start(bf16[4,128,512]{2,1,0:T(8,128)(2,1)} %fusion), calls=%async_computation.3 | async-start | bytes 1048576 | tf_op jit(solution)/shard_map/all_to_all | solution.py:345
  170.0 1.0 copy-start.6
  179.3 0.8 copy-start.4

commit v3 on v1

--- a/solution.py
+++ b/solution.py
@@ -11,7 +11,7 @@
 
 BF16 = jnp.bfloat16
 F32 = jnp.float32
-VMEM_BYTES = 48 * 1024 * 1024
+MIB = 1024 * 1024
 
 
 def passed_along(value, axis, steps):
@@ -42,6 +42,10 @@
 
 def dot_nt(left, right):
     return lax.dot_general(left, right, (((1,), (1,)), ((), ())), preferred_element_type=F32)
+
+
+def stacked(*rows):
+    return jnp.concatenate(rows, 0)
 
 
 def times(left, right):
@@ -93,9 +97,7 @@
     taps = taps_ref.shape[0]
     for start in range(0, mixed_ref.shape[1], step):
         cols = slice(start, start + step)
-        signal = dot(fwd_ref[:, :tokens], earlier_ref[:, cols]) + dot(
-            fwd_ref[:, tokens:], mixed_ref[:, cols]
-        )
+        signal = dot(fwd_ref[...], stacked(earlier_ref[:, cols], mixed_ref[:, cols]))
         filt = dot(fwd_ref[:, :taps], taps_ref[:, cols])
         branch = dot(inv_ref[...], times(signal, filt))
         resid = inputs_ref[:, cols].astype(F32) + beta * branch * mid_ref[:, cols].astype(F32)
@@ -103,23 +105,33 @@
         put_columns(out_ref, value, start)
 
 
+def grad_b_kernel(beta, adjoint_ref, grad_w_ref, long_ref, mid_ref, out_ref):
+    grad_w = get_columns(grad_w_ref, 0, out_ref.shape[1]).astype(F32)
+    grad_u = adjoint_ref[...].astype(F32) + grad_w * long_ref[...].astype(F32)
+    out_ref[...] = (beta * grad_u * mid_ref[...].astype(F32)).astype(BF16)
+
+
 def taps_kernel(
-    beta, step, fwd_ref, inv_ref, earlier_ref, mixed_ref, adjoint_ref, grad_w_ref, long_ref, mid_ref,
-    grad_b_ref, part_ref,
+    step, core_ref, fwd_ref, inv_ref, earlier_ref, mixed_ref, grad_b_ref, keep_ref, send_ref
 ):
     tokens = mixed_ref.shape[0]
+    owned = keep_ref.shape[2]
+    width = min(owned, step)
+
+    def put(even_ref, odd_ref, owner, at, value):
+        ref = even_ref if owner % 2 == 0 else odd_ref
+        ref[owner // 2, :, at : at + width] = value
+
     for start in range(0, mixed_ref.shape[1], step):
         cols = slice(start, start + step)
-        grad_w = get_columns(grad_w_ref, start, step).astype(F32)
-        grad_u = adjoint_ref[:, cols].astype(F32) + grad_w * long_ref[:, cols].astype(F32)
-        grad_b = (beta * grad_u * mid_ref[:, cols].astype(F32)).astype(BF16)
-        grad_b_ref[:, cols] = grad_b
-        signal = dot(fwd_ref[:, :tokens], earlier_ref[:, cols]) + dot(
-            fwd_ref[:, tokens:], mixed_ref[:, cols]
-        )
-        grad = dot(fwd_ref[:, :tokens], grad_b)
-        part = dot(inv_ref[...], times_conj(signal, grad))
-        put_columns(part_ref, part.astype(BF16), start)
+        signal = dot(fwd_ref[...], stacked(earlier_ref[:, cols], mixed_ref[:, cols]))
+        grad = dot(fwd_ref[:, :tokens], grad_b_ref[:, cols])
+        part = dot(inv_ref[...], times_conj(signal, grad)).astype(BF16)
+        for j in range(0, step, width):
+            owner, at = divmod(start + j, owned)
+            value = part[:, j : j + width]
+            pl.when(core_ref[0] == 0)(functools.partial(put, keep_ref, send_ref, owner, at, value))
+            pl.when(core_ref[0] == 1)(functools.partial(put, send_ref, keep_ref, owner, at, value))
 
 
 def input_grad_kernel(
@@ -132,21 +144,10 @@
         cols = slice(start, start + step)
         grad_w = get_columns(grad_w_ref, start, step).astype(F32)
         grad_u = adjoint_ref[:, cols].astype(F32) + grad_w * long_ref[:, cols].astype(F32)
-        signal = dot(fwd_ref[:, :tokens], grad_b_ref[:, cols]) + dot(
-            fwd_ref[:, tokens:], later_ref[:, cols]
-        )
+        signal = dot(fwd_ref[...], stacked(grad_b_ref[:, cols], later_ref[:, cols]))
         filt = dot(fwd_ref[:, :taps], taps_ref[:, cols])
         act = dot(inv_ref[...], times_conj(signal, filt))
         out_ref[:, cols] = (grad_u + act * pre_ref[:, cols].astype(F32)).astype(BF16)
-
-
-def filter_kernel(blocks, fwd_ref, filt_ref, out_ref):
-    size = filt_ref.shape[1] // blocks
-    for d in range(blocks):
-        piece = dot_nt(fwd_ref[:, size:], filt_ref[:, d * size : (d + 1) * size])
-        if d:
-            piece += dot_nt(fwd_ref[:, :size], filt_ref[:, (d - 1) * size : d * size])
-        out_ref[d] = piece
 
 
 def correlate(blocks, own_ref, other, joint_ref):
@@ -177,11 +178,17 @@
     lax.fori_loop(0, half // rows, chunk, 0)
 
 
-def grad_w_kernel(blocks, fwd_ref, inv_ref, grad_ref, filt_ref, out_ref, own_ref, joint_ref):
+def grad_w_kernel(
+    blocks, fwd_ref, inv_ref, grad_ref, filt_ref, out_ref, own_ref, other_ref, joint_ref
+):
     size = grad_ref.shape[0] // blocks
     for q in range(blocks):
         own_ref[q] = dot(fwd_ref[:, size:], grad_ref[q * size : (q + 1) * size])
-    correlate(blocks, own_ref, filt_ref, joint_ref)
+        other = dot_nt(fwd_ref[:, size:], filt_ref[:, q * size : (q + 1) * size])
+        if q:
+            other += dot_nt(fwd_ref[:, :size], filt_ref[:, (q - 1) * size : q * size])
+        other_ref[q] = other
+    correlate(blocks, own_ref, other_ref, joint_ref)
     for p in range(blocks):
         out_ref[p * size : (p + 1) * size] = dot(inv_ref[...], joint_ref[p]).astype(BF16)
 
@@ -209,7 +216,7 @@
     out_ref[...] = (total * scale).astype(BF16)
 
 
-def call(body, grid, ins, outs, args, flops, scratch=(), name=None):
+def call(body, grid, ins, outs, args, flops, scratch=(), vmem=16, name=None):
     moved = sum(a.size * a.dtype.itemsize for a in args)
     moved += sum(math.prod(shape) * jnp.dtype(kind).itemsize for shape, kind, _ in outs)
     result = pl.pallas_call(
@@ -219,7 +226,7 @@
         out_specs=[spec for _, _, spec in outs],
         out_shape=[jax.ShapeDtypeStruct(shape, kind) for shape, kind, _ in outs],
         scratch_shapes=list(scratch),
-        compiler_params=pltpu.CompilerParams(vmem_limit_bytes=VMEM_BYTES),
+        compiler_params=pltpu.CompilerParams(vmem_limit_bytes=vmem * MIB),
         cost_estimate=pl.CostEstimate(flops=flops, bytes_accessed=moved, transcendentals=0),
         name=name,
     )(*args)
@@ -253,13 +260,14 @@
     long_fwd = jnp.asarray(forward_table(period, np.arange(-size, size)))
     long_inv = jnp.asarray(inverse_table(period, np.arange(size)))
 
-    wide = max(512, owned)
+    wide = max(1024, 2 * owned)
     step = min(256, wide)
     grid = (channels // wide,)
     rows_spec = pl.BlockSpec((tokens, wide), lambda i: (0, i))
     taps_spec = pl.BlockSpec((taps, wide), lambda i: (0, i))
     major_spec = pl.BlockSpec((wide // owned, tokens, owned), lambda i: (i, 0, 0))
-    taps_major = pl.BlockSpec((wide // owned, taps, owned), lambda i: (i, 0, 0))
+    half_major = pl.BlockSpec((wide // owned // 2, taps, owned), lambda i: (i, 0, 0))
+    half_shape = (devices // 2, taps, owned)
     rows_shape = (tokens, channels)
     major_shape = (devices, tokens, owned)
     mid_flops = 8 * span * tokens * channels
@@ -268,9 +276,11 @@
     long_grid = (owned // tile,)
     long_spec = pl.BlockSpec((seq_len, tile), lambda i: (0, i))
     lag_spec = pl.BlockSpec((tile, seq_len), lambda i: (i, 0))
-    spectrum_spec = pl.BlockSpec((blocks, period, tile), lambda i: (0, 0, i))
     spectrum = pltpu.VMEM((blocks, period, tile), F32)
     joint = pltpu.VMEM((blocks, period, tile), BF16)
+    lanes = -(-tile // 128) * 128
+    long_vmem = 2 * (long_fwd.size + long_inv.size) * 2 + 20 * blocks * period * lanes
+    long_vmem = -(-long_vmem // MIB) + 6
     long_flops = 4 * period * seq_len * owned
 
     inputs, gate_pre, gate_mid, gate_long, gate_out = (
@@ -284,15 +294,13 @@
         2 * tokens * channels, name="mix",
     )
     earlier = shifted(mixed_in, "ctx", 1)
-    filter_spectrum = call(
-        functools.partial(filter_kernel, blocks), long_grid, [whole_spec(long_fwd), lag_spec],
-        [((blocks, period, owned), F32, spectrum_spec)], [long_fwd, long_filter[0]], long_flops,
-        name="filter",
-    )
+    adjoint, earlier = lax.optimization_barrier((adjoint, earlier))
     grad_z = call(
         functools.partial(grad_z_kernel, beta), grid, [rows_spec] * 2,
         [(major_shape, BF16, major_spec)], [adjoint, gate_out], 2 * tokens * channels, name="gradz",
     )
+    grad_z, earlier = lax.optimization_barrier((grad_z, earlier))
+    channel_z = lax.all_to_all(grad_z, "ctx", split_axis=0, concat_axis=0, tiled=True)
     long_in = call(
         functools.partial(branch_kernel, beta, step), grid,
         [whole_spec(fwd), whole_spec(inv_conv)] + [rows_spec] * 2 + [taps_spec] + [rows_spec] * 3,
@@ -300,34 +308,48 @@
         [fwd, inv_conv, earlier, mixed_in, filter_taps, inputs, gate_mid, gate_long], mid_flops,
         name="branch",
     )
-    channel_z = lax.all_to_all(grad_z, "ctx", split_axis=0, concat_axis=0, tiled=True)
+    channel_z, long_in = lax.optimization_barrier((channel_z, long_in))
     channel_w = lax.all_to_all(long_in, "ctx", split_axis=0, concat_axis=0, tiled=True)
     channel_z = channel_z.reshape(seq_len, owned)
-    channel_w = channel_w.reshape(seq_len, owned)
     grad_w = call(
         functools.partial(grad_w_kernel, blocks), long_grid,
-        [whole_spec(long_fwd), whole_spec(long_inv), long_spec, spectrum_spec],
-        [((seq_len, owned), BF16, long_spec)], [long_fwd, long_inv, channel_z, filter_spectrum],
-        long_flops, [spectrum, joint], name="gradw",
-    )
+        [whole_spec(long_fwd), whole_spec(long_inv), long_spec, lag_spec],
+        [((seq_len, owned), BF16, long_spec)], [long_fwd, long_inv, channel_z, long_filter[0]],
+        2 * long_flops, [spectrum, spectrum, joint], long_vmem, "gradw",
+    )
+    grad_w, channel_w = lax.optimization_barrier((grad_w, channel_w))
     returned = lax.all_to_all(
         grad_w.reshape(major_shape), "ctx", split_axis=0, concat_axis=0, tiled=True
     )
+    channel_w = channel_w.reshape(seq_len, owned)
     long_grad = call(
         functools.partial(long_grad_kernel, blocks, scale), long_grid,
         [whole_spec(long_fwd), whole_spec(long_inv), long_spec, long_spec],
         [((owned, seq_len), BF16, lag_spec)], [long_fwd, long_inv, channel_z, channel_w],
-        2 * long_flops, [spectrum, spectrum, joint], name="longgrad",
-    )
-    grad_b, tap_parts = call(
-        functools.partial(taps_kernel, beta, step), grid,
-        [whole_spec(fwd), whole_spec(inv_taps)] + [rows_spec] * 3 + [major_spec] + [rows_spec] * 2,
-        [(rows_shape, BF16, rows_spec), ((devices, taps, owned), BF16, taps_major)],
-        [fwd, inv_taps, earlier, mixed_in, adjoint, returned, gate_long, gate_mid], mid_flops,
-        name="taps",
+        2 * long_flops, [spectrum, spectrum, joint], long_vmem, "longgrad",
+    )
+    returned, long_grad = lax.optimization_barrier((returned, long_grad))
+    grad_b = call(
+        functools.partial(grad_b_kernel, beta), grid,
+        [rows_spec, major_spec] + [rows_spec] * 2, [(rows_shape, BF16, rows_spec)],
+        [adjoint, returned, gate_long, gate_mid], 4 * tokens * channels, name="gradb",
     )
     later = shifted(grad_b, "ctx", -1)
-    gathered = lax.all_to_all(tap_parts, "ctx", split_axis=0, concat_axis=0, tiled=True)
+    core = (lax.axis_index("ctx") % 2).astype(jnp.int32)[None]
+    keep, send = call(
+        functools.partial(taps_kernel, step), grid,
+        [pl.BlockSpec(memory_space=pltpu.SMEM), whole_spec(fwd), whole_spec(inv_taps)]
+        + [rows_spec] * 3,
+        [(half_shape, BF16, half_major)] * 2,
+        [core, fwd, inv_taps, earlier, mixed_in, grad_b], mid_flops, name="taps",
+    )
+    partner = lax.ppermute(send, "ctx", [(i, i ^ 1) for i in range(devices)])
+    chip_parts = (keep.astype(F32) + partner.astype(F32)).astype(BF16)
+    gathered = lax.all_to_all(
+        chip_parts, "ctx", split_axis=0, concat_axis=0, tiled=True,
+        axis_index_groups=[list(range(c, devices, 2)) for c in range(2)],
+    )
+    later, _ = lax.optimization_barrier((later, chip_parts))
     input_grad = call(
         functools.partial(input_grad_kernel, step), grid,
         [whole_spec(fwd), whole_spec(inv_corr)] + [rows_spec] * 2 + [taps_spec, rows_spec, major_spec]

time: 203 us -> 172 us (0.85)
  the two profiles are of different devices: /device:TPU:11 before, /device:TPU:1 now
where the time goes in v3:
time: 172 us; the launch traced here: 171 us
  waiting for transfers between devices  84.3 us (49%)
  Pallas kernels  36.6 us (21%)
  starting transfers between devices  26.8 us (16%)
  local copies, waits for them, and re-layouts  21.4 us (12%)
    pallas_call x9, Pallas kernels, call(): pl.pallas_call(body, grid=grid, in_specs=ins, out_specs=[spec for _, _, s...  36.6 us
    ppermute x2, waiting for transfers between devices, shifted(): return lax.ppermute(array, axis, pairs)  23.4 us
    unnamed x60, local copies, waits for them, and re-layouts  21.4 us
    all_to_all x1, waiting for transfers between devices, per_device(): lax.all_to_all(grad_w.reshape(major_shape), 'ctx', split_axis=0, concat_a...  16.6 us
    all_to_all x1, waiting for transfers between devices, per_device(): lax.all_to_all(long_in, 'ctx', split_axis=0, concat_axis=0, tiled=True)  16.6 us
    all_to_all x1, waiting for transfers between devices, per_device(): lax.all_to_all(grad_z, 'ctx', split_axis=0, concat_axis=0, tiled=True)  15.1 us
    ppermute x1, waiting for transfers between devices, passed_along(): return lax.ppermute(value, axis, pairs)  12.6 us
    ppermute x2, starting transfers between devices, shifted(): return lax.ppermute(array, axis, pairs)  6.65 us
  transfers between devices with their start and end apart: 8, of which 6 were waited for; matrix products, arithmetic and copies ran while one was open for 1% of the time, Pallas kernels for 14%

profile of v3, /device:TPU:1, one launch (start us, length us, event | category | flops | bytes accessed | tf_op | source)
XLA Modules:
  0.0 171.0 jit_solution(16651222624836009708)
XLA Ops:
  0.6 0.0 copy-start.1
  0.6 1.2 copy-done.1
  1.9 1.2 copy-done.12
  3.1 0.5 mix.1.mixed_ref
  3.6 4.7 %collective-permute-start.1 = (bf16[128,4096]{1,0:T(8,128)(2,1)S(1)}, bf16[128,4096]{1,0:T(8,128)(2,1)S(1)}, u32[]{:S(2)}, u32[]{:S(2)}) collective-permute-start(bf16[128,4096]{1,0:T(8,128)(2,1)S(1)} %mix.1.mixed_ref), channel_id=1, source_target_pairs={{0,1},{1,2},{2,3},{3,4},{4,5},{5,6},{6,7},{8,9},{9,10},{10,11},{11... | collective-permute-start | bytes 3145736 | tf_op jit(solution)/shard_map/ppermute | solution.py:26
  8.4 1.0 copy-done.5
  9.3 2.2 %collective-permute-start = (bf16[128,4096]{1,0:T(8,128)(2,1)S(1)}, bf16[128,4096]{1,0:T(8,128)(2,1)S(1)}, u32[]{:S(2)}, u32[]{:S(2)}) collective-permute-start(bf16[128,4096]{1,0:T(8,128)(2,1)S(1)} %bitcast.32), channel_id=1, source_target_pairs={{0,24},{8,0},{16,8},{24,16},{1,25},{9,1},{17,9},{25,17},{2,26},{10... | collective-permute-start | bytes 3145736 | tf_op jit(solution)/shard_map/ppermute | solution.py:20
  11.5 8.6 %collective-permute-done.1.earlier_ref = bf16[128,4096]{1,0:T(8,128)(2,1)S(1)} collective-permute-done((bf16[128,4096]{1,0:T(8,128)(2,1)S(1)}, bf16[128,4096]{1,0:T(8,128)(2,1)S(1)}, u32[]{:S(2)}, u32[]{:S(2)}) %collective-permute-start.1) | collective-permute-done | bytes 1048608 | tf_op jit(solution)/shard_map/ppermute | solution.py:26
  20.1 1.0 copy-done.15
  21.1 12.6 %collective-permute-done.adjoint_ref = bf16[128,4096]{1,0:T(8,128)(2,1)S(1)} collective-permute-done((bf16[128,4096]{1,0:T(8,128)(2,1)S(1)}, bf16[128,4096]{1,0:T(8,128)(2,1)S(1)}, u32[]{:S(2)}, u32[]{:S(2)}) %collective-permute-start) | collective-permute-done | bytes 1048608 | tf_op jit(solution)/shard_map/ppermute | solution.py:20
  33.7 0.5 gradz.1
  34.2 0.0 copy-start.9
  34.2 1.0 copy-done.9
  35.2 4.3 %all-to-all-start = ((bf16[8,128,512]{2,1,0:T(8,128)(2,1)}), bf16[8,128,512]{2,1,0:T(8,128)(2,1)}, u32[]{:S(2)}, u32[]{:S(2)}) async-start(bf16[8,128,512]{2,1,0:T(8,128)(2,1)} %copy-done.9), calls=%async_computation | async-start | bytes 2097152 | tf_op jit(solution)/shard_map/all_to_all | solution.py:303
  39.6 0.0 copy-start.3
  39.6 1.2 copy-done.3
  40.8 1.2 copy-done.6
  42.0 1.2 copy-done.10
  43.2 1.2 copy-done.16
  44.5 5.0 %branch.1 = bf16[8,128,512]{2,1,0:T(8,128)(2,1)S(1)} custom-call(bf16[256,256]{1,0:T(8,128)(2,1)S(1)} %copy-done.21, bf16[128,256]{1,0:T(8,128)(2,1)S(1)} %copy-done.23, bf16[128,4096]{1,0:T(8,128)(2,1)S(1)} %copy-done.16, bf16[128,4096]{1,0:T(8,128)(2,1)S(1)} %copy-done.6, bf16[128,4096]{1,0:T(8,128)(2,1)S(1)} %bitcast.22, bf16[128,4096]{1,0:T(8,128)(2,1)S(1)} %bitcast.19, ...), custom_call_target="tpu_custom_call" | custom-call | flops 1073741824 | bytes 7536640 | tf_op jit(solution)/shard_map/branch/pallas_call | solution.py:222
  49.5 1.0 copy-done.8
  50.4 15.1 %all-to-all-done = bf16[8,128,512]{2,1,0:T(8,128)(2,1)} async-done(((bf16[8,128,512]{2,1,0:T(8,128)(2,1)}), bf16[8,128,512]{2,1,0:T(8,128)(2,1)}, u32[]{:S(2)}, u32[]{:S(2)}) %all-to-all-start) | async-done | bytes 1048608 | tf_op jit(solution)/shard_map/all_to_all | solution.py:303
  65.6 4.2 %all-to-all-start.1 = ((bf16[8,128,512]{2,1,0:T(8,128)(2,1)}), bf16[8,128,512]{2,1,0:T(8,128)(2,1)S(1)}, u32[]{:S(2)}, u32[]{:S(2)}) async-start(bf16[8,128,512]{2,1,0:T(8,128)(2,1)} %copy-done.8), calls=%async_computation.1 | async-start | bytes 2097152 | tf_op jit(solution)/shard_map/all_to_all | solution.py:312
  69.8 1.2 copy-done.24
  71.0 1.0 copy-done.25
  72.0 5.9 %gradw.1 = bf16[1024,512]{1,0:T(8,128)(2,1)S(1)} custom-call(bf16[512,512]{1,0:T(8,128)(2,1)S(1)} %copy-done.25, bf16[256,512]{1,0:T(8,128)(2,1)S(1)} %copy-done.27, bf16[1024,512]{1,0:T(8,128)(2,1)} %bitcast.7.grad_ref, bf16[512,1024]{1,0:T(8,128)(2,1)S(1)} %bitcast.29), custom_call_target="tpu_custom_call" | custom-call | flops 2147483648 | bytes 3932160 | tf_op jit(solution)/shard_map/gradw/pallas_call | solution.py:222
  78.0 0.0 copy-start.20
  78.0 1.0 copy-done.20
  79.0 16.6 %all-to-all-done.1 = bf16[8,128,512]{2,1,0:T(8,128)(2,1)S(1)} async-done(((bf16[8,128,512]{2,1,0:T(8,128)(2,1)}), bf16[8,128,512]{2,1,0:T(8,128)(2,1)S(1)}, u32[]{:S(2)}, u32[]{:S(2)}) %all-to-all-start.1) | async-done | bytes 1048608 | tf_op jit(solution)/shard_map/all_to_all | solution.py:312
  95.5 1.0 copy-done.18
  96.5 4.3 %all-to-all-start.2 = ((bf16[8,128,512]{2,1,0:T(8,128)(2,1)}), bf16[8,128,512]{2,1,0:T(8,128)(2,1)S(1)}, u32[]{:S(2)}, u32[]{:S(2)}) async-start(bf16[8,128,512]{2,1,0:T(8,128)(2,1)} %bitcast.28), calls=%async_computation.2 | async-start | bytes 2097152 | tf_op jit(solution)/shard_map/all_to_all | solution.py:321
  100.8 1.2 copy-done.19
  102.1 1.0 copy-done.26
  103.1 6.9 %longgrad.1 = bf16[512,1024]{1,0:T(8,128)(2,1)} custom-call(bf16[512,512]{1,0:T(8,128)(2,1)S(1)} %copy-done.26, bf16[256,512]{1,0:T(8,128)(2,1)S(1)} %copy-done.27, bf16[1024,512]{1,0:T(8,128)(2,1)} %bitcast.7.grad_ref, bf16[1024,512]{1,0:T(8,128)(2,1)S(1)} %bitcast.27), custom_call_target="tpu_custom_call" | custom-call | flops 2147483648 | bytes 3932160 | tf_op jit(solution)/shard_map/longgrad/pallas_call | solution.py:222
  110.0 16.6 %all-to-all-done.2.grad_w_ref = bf16[8,128,512]{2,1,0:T(8,128)(2,1)S(1)} async-done(((bf16[8,128,512]{2,1,0:T(8,128)(2,1)}), bf16[8,128,512]{2,1,0:T(8,128)(2,1)S(1)}, u32[]{:S(2)}, u32[]{:S(2)}) %all-to-all-start.2) | async-done | bytes 1048608 | tf_op jit(solution)/shard_map/all_to_all | solution.py:321
  126.6 1.2 copy-done.4
  127.8 2.1 %gradb.1.grad_b_ref = bf16[128,4096]{1,0:T(8,128)(2,1)} custom-call(bf16[128,4096]{1,0:T(8,128)(2,1)S(1)} %collective-permute-done.adjoint_ref, bf16[8,128,512]{2,1,0:T(8,128)(2,1)S(1)} %all-to-all-done.2.grad_w_ref, bf16[128,4096]{1,0:T(8,128)(2,1)S(1)} %bitcast.16, bf16[128,4096]{1,0:T(8,128)(2,1)S(1)} %bitcast.21), custom_call_target="tpu_custom_call" | custom-call | flops 2097152 | bytes 5242880 | tf_op jit(solution)/shard_map/gradb/pallas_call | solution.py:222
  129.9 7.5 %taps.1 = (bf16[4,128,512]{2,1,0:T(8,128)(2,1)S(1)}, bf16[4,128,512]{2,1,0:T(8,128)(2,1)S(1)}) custom-call(s32[1]{0:T(128)} %bitcast.11.core_ref, bf16[256,256]{1,0:T(8,128)(2,1)S(1)} %copy-done.21, bf16[128,256]{1,0:T(8,128)(2,1)S(1)} %copy-done.28, bf16[128,4096]{1,0:T(8,128)(2,1)S(1)} %copy-done.17, bf16[128,4096]{1,0:T(8,128)(2,1)S(1)} %copy-done.7, ...), custom_call_target="tpu_custom_call" | custom-call | flops 1073741824 | bytes 4390916 | tf_op jit(solution)/shard_map/taps/pallas_call | solution.py:222
  137.4 0.9 collective-permute-start.3
  138.3 1.9 %collective-permute-start.2 = (bf16[128,4096]{1,0:T(8,128)(2,1)}, bf16[128,4096]{1,0:T(8,128)(2,1)}, u32[]{:S(2)}, u32[]{:S(2)}) collective-permute-start(bf16[128,4096]{1,0:T(8,128)(2,1)} %gradb.1.grad_b_ref), channel_id=1, source_target_pairs={{1,0},{2,1},{3,2},{4,3},{5,4},{6,5},{7,6},{9,8},{10,9},{11,10},{12... | collective-permute-start | bytes 3145736 | tf_op jit(solution)/shard_map/ppermute | solution.py:26
  140.2 0.0 collective-permute-done.3
  140.2 0.9 add_convert_fusion
  141.2 4.3 %all-to-all-start.3 = ((bf16[4,128,512]{2,1,0:T(8,128)(2,1)}), bf16[4,128,512]{2,1,0:T(8,128)(2,1)}, u32[]{:S(2)}, u32[]{:S(2)}) async-start(bf16[4,128,512]{2,1,0:T(8,128)(2,1)} %add_convert_fusion), calls=%async_computation.3 | async-start | bytes 1048576 | tf_op jit(solution)/shard_map/all_to_all | solution.py:348
  145.5 14.9 %collective-permute-done.2.later_ref = bf16[128,4096]{1,0:T(8,128)(2,1)} collective-permute-done((bf16[128,4096]{1,0:T(8,128)(2,1)}, bf16[128,4096]{1,0:T(8,128)(2,1)}, u32[]{:S(2)}, u32[]{:S(2)}) %collective-permute-start.2) | collective-permute-done | bytes 1048608 | tf_op jit(solution)/shard_map/ppermute | solution.py:26
  160.3 1.2 copy-done.11
  161.6 1.2 copy-done.13
  162.8 6.4 %inputgrad.1 = bf16[128,4096]{1,0:T(8,128)(2,1)} custom-call(bf16[256,256]{1,0:T(8,128)(2,1)S(1)} %copy-done.21, bf16[128,256]{1,0:T(8,128)(2,1)S(1)} %copy-done.22, bf16[128,4096]{1,0:T(8,128)(2,1)} %gradb.1.grad_b_ref, bf16[128,4096]{1,0:T(8,128)(2,1)} %collective-permute-done.2.later_ref, bf16[128,4096]{1,0:T(8,128)(2,1)S(1)} %bitcast.23, ...), custom_call_target="tpu_custom_call" | custom-call | flops 1073741824 | bytes 8585216 | tf_op jit(solution)/shard_map/inputgrad/pallas_call | solution.py:222
  169.2 1.8 %midgrad.1 = bf16[128,512]{1,0:T(8,128)(2,1)} custom-call(bf16[4,128,512]{2,1,0:T(8,128)(2,1)} %all-to-all-done.3.parts_ref), custom_call_target="tpu_custom_call" | custom-call | flops 524288 | bytes 655360 | tf_op jit(solution)/shard_map/midgrad/pallas_call | solution.py:222
  (38 shorter events, 0.1 us)
Async XLA Ops:
  0.6 1.2 copy-start.1
  1.9 1.2 copy-start.12
  3.1 6.3 %copy-start.29 = (bf16[1,128,4096]{2,1,0:T(8,128)(2,1)S(1)}, bf16[1,128,4096]{2,1,0:T(8,128)(2,1)}, u32[]{:S(2)}) copy-start(bf16[1,128,4096]{2,1,0:T(8,128)(2,1)} %param.14) | copy-start | bytes 3145732
  3.1 30.6 %copy-start.14 = (bf16[1,128,4096]{2,1,0:T(8,128)(2,1)S(1)}, bf16[1,128,4096]{2,1,0:T(8,128)(2,1)}, u32[]{:S(2)}) copy-start(bf16[1,128,4096]{2,1,0:T(8,128)(2,1)} %param.19) | copy-start | bytes 3145732
  3.6 16.5 %collective-permute-start.1 = (bf16[128,4096]{1,0:T(8,128)(2,1)S(1)}, bf16[128,4096]{1,0:T(8,128)(2,1)S(1)}, u32[]{:S(2)}, u32[]{:S(2)}) collective-permute-start(bf16[128,4096]{1,0:T(8,128)(2,1)S(1)} %mix.1.mixed_ref), channel_id=1, source_target_pairs={{0,1},{1,2},{2,3},{3,4},{4,5},{5,6},{6,7},{8,9},{9,10},{10,11},{11... | collective-permute-start | bytes 3145736 | tf_op jit(solution)/shard_map/ppermute | solution.py:26
  8.4 1.0 copy-start.5
  9.3 24.3 %collective-permute-start = (bf16[128,4096]{1,0:T(8,128)(2,1)S(1)}, bf16[128,4096]{1,0:T(8,128)(2,1)S(1)}, u32[]{:S(2)}, u32[]{:S(2)}) collective-permute-start(bf16[128,4096]{1,0:T(8,128)(2,1)S(1)} %bitcast.32), channel_id=1, source_target_pairs={{0,24},{8,0},{16,8},{24,16},{1,25},{9,1},{17,9},{25,17},{2,26},{10... | collective-permute-start | bytes 3145736 | tf_op jit(solution)/shard_map/ppermute | solution.py:20
  20.1 1.0 copy-start.15
  33.7 5.9 %copy-start.21 = (bf16[256,256]{1,0:T(8,128)(2,1)S(1)}, bf16[256,256]{1,0:T(8,128)(2,1)}, u32[]{:S(2)}) copy-start(bf16[256,256]{1,0:T(8,128)(2,1)} %constant.29.clone.fwd_ref) | copy-start | bytes 393220
  33.7 5.9 %copy-start.23 = (bf16[128,256]{1,0:T(8,128)(2,1)S(1)}, bf16[128,256]{1,0:T(8,128)(2,1)}, u32[]{:S(2)}) copy-start(bf16[128,256]{1,0:T(8,128)(2,1)} %constant.30.clone.inv_ref) | copy-start | bytes 196612
  34.2 1.0 copy-start.9
  35.2 4.4 %copy-start = (bf16[1,128,4096]{2,1,0:T(8,128)(2,1)S(1)}, bf16[1,128,4096]{2,1,0:T(8,128)(2,1)}, u32[]{:S(2)}) copy-start(bf16[1,128,4096]{2,1,0:T(8,128)(2,1)} %param.18) | copy-start | bytes 3145732
  35.2 4.4 %copy-start.2 = (bf16[1,128,4096]{2,1,0:T(8,128)(2,1)S(1)}, bf16[1,128,4096]{2,1,0:T(8,128)(2,1)}, u32[]{:S(2)}) copy-start(bf16[1,128,4096]{2,1,0:T(8,128)(2,1)} %param.15) | copy-start | bytes 3145732
  35.2 30.4 %all-to-all-start = ((bf16[8,128,512]{2,1,0:T(8,128)(2,1)}), bf16[8,128,512]{2,1,0:T(8,128)(2,1)}, u32[]{:S(2)}, u32[]{:S(2)}) async-start(bf16[8,128,512]{2,1,0:T(8,128)(2,1)} %copy-done.9), calls=%async_computation | async-start | bytes 2097152 | tf_op jit(solution)/shard_map/all_to_all | solution.py:303
  39.6 1.2 copy-start.3
  40.8 1.2 copy-start.6
  42.0 1.2 copy-start.10
  43.2 1.2 copy-start.16
  49.4 1.0 copy-start.8
  50.4 19.3 %copy-start.27 = (bf16[256,512]{1,0:T(8,128)(2,1)S(1)}, bf16[256,512]{1,0:T(8,128)(2,1)}, u32[]{:S(2)}) copy-start(bf16[256,512]{1,0:T(8,128)(2,1)} %constant.34.clone.inv_ref) | copy-start | bytes 786436
  65.6 29.9 %all-to-all-start.1 = ((bf16[8,128,512]{2,1,0:T(8,128)(2,1)}), bf16[8,128,512]{2,1,0:T(8,128)(2,1)S(1)}, u32[]{:S(2)}, u32[]{:S(2)}) async-start(bf16[8,128,512]{2,1,0:T(8,128)(2,1)} %copy-done.8), calls=%async_computation.1 | async-start | bytes 2097152 | tf_op jit(solution)/shard_map/all_to_all | solution.py:312
  69.8 1.2 copy-start.24
  71.0 1.0 copy-start.25
  78.0 1.0 copy-start.20
  95.5 1.0 copy-start.18
  96.5 30.1 %all-to-all-start.2 = ((bf16[8,128,512]{2,1,0:T(8,128)(2,1)}), bf16[8,128,512]{2,1,0:T(8,128)(2,1)S(1)}, u32[]{:S(2)}, u32[]{:S(2)}) async-start(bf16[8,128,512]{2,1,0:T(8,128)(2,1)} %bitcast.28), calls=%async_computation.2 | async-start | bytes 2097152 | tf_op jit(solution)/shard_map/all_to_all | solution.py:321
  100.8 1.2 copy-start.19
  102.1 1.0 copy-start.26
  126.6 1.2 copy-start.4
  127.8 2.1 %copy-start.7 = (bf16[128,4096]{1,0:T(8,128)(2,1)S(1)}, bf16[128,4096]{1,0:T(8,128)(2,1)}, u32[]{:S(2)}) copy-start(bf16[128,4096]{1,0:T(8,128)(2,1)} %copy-done.5) | copy-start | bytes 3145732
  127.8 2.1 %copy-start.17 = (bf16[128,4096]{1,0:T(8,128)(2,1)S(1)}, bf16[128,4096]{1,0:T(8,128)(2,1)}, u32[]{:S(2)}) copy-start(bf16[128,4096]{1,0:T(8,128)(2,1)} %copy-done.15) | copy-start | bytes 3145732
  127.8 2.1 %copy-start.28 = (bf16[128,256]{1,0:T(8,128)(2,1)S(1)}, bf16[128,256]{1,0:T(8,128)(2,1)}, u32[]{:S(2)}) copy-start(bf16[128,256]{1,0:T(8,128)(2,1)} %constant.32.clone.inv_ref) | copy-start | bytes 196612
  137.4 2.8 %collective-permute-start.3 = (bf16[4,128,512]{2,1,0:T(8,128)(2,1)S(1)}, bf16[4,128,512]{2,1,0:T(8,128)(2,1)S(1)}, u32[]{:S(2)}, u32[]{:S(2)}) collective-permute-start(bf16[4,128,512]{2,1,0:T(8,128)(2,1)S(1)} %get-tuple-element.26), channel_id=1, source_target_pairs={{0,1},{1,0},{2,3},{3,2},{4,5},{5,4},{6,7},{7,6},{8,9},{9,8},{10,11... | collective-permute-start | bytes 1572872 | tf_op jit(solution)/shard_map/ppermute | solution.py:346
  138.3 22.0 %collective-permute-start.2 = (bf16[128,4096]{1,0:T(8,128)(2,1)}, bf16[128,4096]{1,0:T(8,128)(2,1)}, u32[]{:S(2)}, u32[]{:S(2)}) collective-permute-start(bf16[128,4096]{1,0:T(8,128)(2,1)} %gradb.1.grad_b_ref), channel_id=1, source_target_pairs={{1,0},{2,1},{3,2},{4,3},{5,4},{6,5},{7,6},{9,8},{10,9},{11,10},{12... | collective-permute-start | bytes 3145736 | tf_op jit(solution)/shard_map/ppermute | solution.py:26
  141.2 19.2 %copy-start.22 = (bf16[128,256]{1,0:T(8,128)(2,1)S(1)}, bf16[128,256]{1,0:T(8,128)(2,1)}, u32[]{:S(2)}) copy-start(bf16[128,256]{1,0:T(8,128)(2,1)} %constant.31.clone.inv_ref) | copy-start | bytes 196612
  141.2 28.0 %all-to-all-start.3 = ((bf16[4,128,512]{2,1,0:T(8,128)(2,1)}), bf16[4,128,512]{2,1,0:T(8,128)(2,1)}, u32[]{:S(2)}, u32[]{:S(2)}) async-start(bf16[4,128,512]{2,1,0:T(8,128)(2,1)} %add_convert_fusion), calls=%async_computation.3 | async-start | bytes 1048576 | tf_op jit(solution)/shard_map/all_to_all | solution.py:348
  160.3 1.2 copy-start.11
  161.6 1.2 copy-start.13

commit v4 on v3

--- a/solution.py
+++ b/solution.py
@@ -237,7 +237,7 @@
     return pl.BlockSpec(array.shape, lambda i: (0,) * array.ndim)
 
 
-def per_device(
+def by_all_to_all(
     incoming, layer_input, pre_gate, mid_gate, long_gate, out_gate, long_filter, mid_filter
 ):
     sections = lax.axis_size("section")
@@ -366,6 +366,283 @@
     return (input_grad[None], long_grad[None], mid_grad[None])
 
 
+def columns(index, width):
+    return pl.ds(pl.multiple_of(index * width, width), width)
+
+
+def pick_kernel(me_ref, in_ref, near_ref, far_ref):
+    half, width = me_ref[1], near_ref.shape[1]
+    near_ref[...] = in_ref[:, columns(half, width)]
+    far_ref[...] = in_ref[:, columns(1 - half, width)]
+
+
+def pieces_z_kernel(beta, first, me_ref, adjoint_ref, gate_ref, *out_refs):
+    count = len(out_refs)
+    width = out_refs[0].shape[1]
+    me = me_ref[0]
+    for k in range(count):
+        owner = me ^ (first + k)
+        part = adjoint_ref[:, columns(owner & (count - 1), width)].astype(F32)
+        gate = gate_ref[:, columns(owner, width)].astype(F32)
+        out_refs[k][...] = (beta * part * gate).astype(BF16)
+
+
+def pieces_branch_kernel(
+    beta, me_ref, fwd_ref, inv_ref, earlier_ref, mixed_ref, taps_ref, inputs_ref, mid_ref, long_ref,
+    signal_ref, filt_ref, *out_refs,
+):
+    taps = taps_ref.shape[0]
+    width = out_refs[0].shape[1]
+    me = me_ref[0]
+    count = len(out_refs)
+    for k in list(range(count // 2, count)) + list(range(count // 2)):
+        cols = columns(me ^ k, width)
+        signal = dot(fwd_ref[...], stacked(earlier_ref[:, cols], mixed_ref[:, cols]))
+        filt = dot(fwd_ref[:, :taps], taps_ref[:, cols])
+        signal_ref[:, cols] = signal.astype(BF16)
+        filt_ref[:, cols] = filt.astype(BF16)
+        branch = dot(inv_ref[...], times(signal, filt))
+        resid = inputs_ref[:, cols].astype(F32) + beta * branch * mid_ref[:, cols].astype(F32)
+        out_refs[k][...] = (resid * long_ref[:, cols].astype(F32)).astype(BF16)
+
+
+def spectra(blocks, fwd_ref, array_ref, cols, out_ref):
+    size = array_ref.shape[0] // blocks
+    for q in range(blocks):
+        out_ref[q] = dot(fwd_ref[:, size:], array_ref[q * size : (q + 1) * size, cols])
+
+
+def extended_spectra(blocks, fwd_ref, array_ref, cols, out_ref):
+    size = array_ref.shape[0] // blocks
+    out_ref[0] = dot(fwd_ref[:, size:], array_ref[:size, cols])
+    for q in range(1, blocks):
+        out_ref[q] = dot(fwd_ref[...], array_ref[(q - 1) * size : (q + 1) * size, cols])
+
+
+def pieces_grad_w_kernel(blocks, count, me_ref, fwd_ref, inv_ref, filt_ref, *refs):
+    piece_refs, out_refs = refs[:count], refs[count : 2 * count]
+    whole_ref, own_ref, other_ref, joint_ref, result_ref = refs[2 * count :]
+    rows = piece_refs[0].shape[0]
+    size = whole_ref.shape[0] // blocks
+    tile = joint_ref.shape[2]
+    me = me_ref[0]
+    for k in range(count):
+        whole_ref[columns(me ^ k, rows), :] = piece_refs[k][...]
+    for start in range(0, whole_ref.shape[1], tile):
+        cols = slice(start, start + tile)
+        spectra(blocks, fwd_ref, whole_ref, cols, own_ref)
+        other_ref[0] = dot_nt(fwd_ref[:, size:], filt_ref[cols, :size])
+        for q in range(1, blocks):
+            other_ref[q] = dot_nt(fwd_ref[...], filt_ref[cols, (q - 1) * size : (q + 1) * size])
+        correlate(blocks, own_ref, other_ref, joint_ref)
+        for p in range(blocks):
+            result_ref[p * size : (p + 1) * size, cols] = dot(inv_ref[...], joint_ref[p]).astype(BF16)
+    for k in range(count):
+        out_refs[k][...] = result_ref[columns(me ^ k, rows), :]
+
+
+def pieces_long_grad_kernel(blocks, scale, count, me_ref, fwd_ref, inv_ref, grad_ref, *refs):
+    piece_refs, out_ref = refs[:count], refs[count]
+    own_ref, other_ref, joint_ref, whole_ref = refs[count + 1 :]
+    rows = piece_refs[0].shape[0]
+    size = whole_ref.shape[0] // blocks
+    tile = joint_ref.shape[2]
+    me = me_ref[0]
+    for k in range(count):
+        whole_ref[columns(me ^ k, rows), :] = piece_refs[k][...]
+    for start in range(0, whole_ref.shape[1], tile):
+        cols = slice(start, start + tile)
+        spectra(blocks, fwd_ref, grad_ref, cols, own_ref)
+        extended_spectra(blocks, fwd_ref, whole_ref, cols, other_ref)
+        correlate(blocks, own_ref, other_ref, joint_ref)
+        for p in range(blocks):
+            lags = (dot(inv_ref[...], joint_ref[p]) * scale).T
+            out_ref[cols, p * size : (p + 1) * size] = lags.astype(BF16)
+
+
+def pieces_grad_b_kernel(beta, count, me_ref, near_ref, far_ref, long_ref, mid_ref, *refs):
+    piece_refs, (grad_u_ref, grad_b_ref) = refs[:count], refs[count:]
+    width = piece_refs[0].shape[1]
+    half = count // 2
+    me = me_ref[0]
+    for k in range(count):
+        owner = me ^ k
+        cols = columns(owner, width)
+        adjoint_ref = near_ref if k < half else far_ref
+        adjoint = adjoint_ref[:, columns(owner & (half - 1), width)].astype(F32)
+        grad_u = adjoint + piece_refs[k][...].astype(F32) * long_ref[:, cols].astype(F32)
+        grad_u_ref[:, cols] = grad_u
+        grad_b_ref[:, cols] = (beta * grad_u * mid_ref[:, cols].astype(F32)).astype(BF16)
+
+
+def pieces_taps_kernel(me_ref, fwd_ref, inv_ref, signal_ref, grad_b_ref, keep_ref, send_ref):
+    tokens = grad_b_ref.shape[0]
+    width = keep_ref.shape[2]
+    me = me_ref[0]
+    for k in range(2 * keep_ref.shape[0]):
+        cols = columns(me ^ k, width)
+        grad = dot(fwd_ref[:, :tokens], grad_b_ref[:, cols])
+        part = dot(inv_ref[...], times_conj(signal_ref[:, cols].astype(F32), grad)).astype(BF16)
+        (send_ref if k % 2 else keep_ref)[k // 2] = part
+
+
+def pair_kernel(keep_ref, came_ref, *out_refs):
+    for m, out_ref in enumerate(out_refs):
+        out_ref[...] = (keep_ref[m].astype(F32) + came_ref[m].astype(F32)).astype(BF16)
+
+
+def pieces_total_kernel(scale, *refs):
+    total = refs[0][...].astype(F32)
+    for ref in refs[1:-1]:
+        total += ref[...].astype(F32)
+    refs[-1][...] = (total * scale).astype(BF16)
+
+
+def pieces_input_grad_kernel(
+    step, fwd_ref, inv_ref, grad_b_ref, later_ref, filt_ref, grad_u_ref, pre_ref, out_ref
+):
+    for start in range(0, grad_b_ref.shape[1], step):
+        cols = slice(start, start + step)
+        signal = dot(fwd_ref[...], stacked(grad_b_ref[:, cols], later_ref[:, cols]))
+        act = dot(inv_ref[...], times_conj(signal, filt_ref[:, cols].astype(F32)))
+        value = grad_u_ref[:, cols] + act * pre_ref[:, cols].astype(F32)
+        out_ref[:, cols] = value.astype(BF16)
+
+
+def local(body, outs, args, flops, scratch=(), vmem=24, name=None):
+    moved = sum(a.size * a.dtype.itemsize for a in args)
+    moved += sum(math.prod(shape) * jnp.dtype(kind).itemsize for shape, kind in outs)
+    specs = [
+        pl.BlockSpec(memory_space=pltpu.SMEM if a.dtype == jnp.int32 else pltpu.VMEM) for a in args
+    ]
+    result = pl.pallas_call(
+        body,
+        in_specs=specs,
+        out_specs=[pl.BlockSpec(memory_space=pltpu.VMEM) for _ in outs],
+        out_shape=[jax.ShapeDtypeStruct(shape, kind) for shape, kind in outs],
+        scratch_shapes=list(scratch),
+        compiler_params=pltpu.CompilerParams(vmem_limit_bytes=vmem * MIB),
+        cost_estimate=pl.CostEstimate(flops=flops, bytes_accessed=moved, transcendentals=0),
+        name=name,
+    )(*args)
+    return result[0] if len(result) == 1 else result
+
+
+def swapped(array, k):
+    count = lax.axis_size("ctx")
+    return lax.ppermute(array, "ctx", [(i, i ^ k) for i in range(count)])
+
+
+def exchanged(pieces, step=1):
+    came = [pieces[0]] + [None] * (len(pieces) - 1)
+    for k in range(len(pieces) - 1, 0, -1):
+        came[k] = swapped(pieces[k], k * step)
+    return came
+
+
+def by_permutes(
+    incoming, layer_input, pre_gate, mid_gate, long_gate, out_gate, long_filter, mid_filter
+):
+    sections = lax.axis_size("section")
+    devices = lax.axis_size("ctx")
+    half = devices // 2
+    beta = (2.0 * sections) ** (-0.5)
+    tokens, channels = layer_input.shape[1:]
+    taps = mid_filter.shape[1]
+    seq_len = tokens * devices
+    scale = float(seq_len) ** (-0.5)
+    owned = channels // devices
+
+    span = tokens + max(tokens, taps)
+    fwd = jnp.asarray(forward_table(span, np.arange(span)))
+    inv_conv = jnp.asarray(inverse_table(span, tokens + np.arange(tokens)))
+    inv_corr = jnp.asarray(inverse_table(span, np.arange(tokens)))
+    inv_taps = jnp.asarray(inverse_table(span, tokens - np.arange(taps)))
+    size = max(math.gcd(seq_len, 256), seq_len // 8)
+    blocks = seq_len // size
+    period = 2 * size
+    long_fwd = jnp.asarray(forward_table(period, np.arange(-size, size)))
+    long_inv = jnp.asarray(inverse_table(period, np.arange(size)))
+    tile = math.gcd(owned, 256)
+    spectrum = pltpu.VMEM((blocks, period, tile), F32)
+    joint = pltpu.VMEM((blocks, period, tile), BF16)
+    staged = pltpu.VMEM((seq_len, owned), BF16)
+
+    rows_shape = ((tokens, channels), BF16)
+    half_shape = ((tokens, channels // 2), BF16)
+    piece = ((tokens, owned), BF16)
+    tap_piece = ((taps, owned), BF16)
+    mid_flops = 8 * span * tokens * channels
+    long_flops = 12 * period * seq_len * owned
+    few = 4 * tokens * channels
+
+    index = lax.axis_index("ctx")
+    me = jnp.stack([index, index // half]).astype(jnp.int32)
+    inputs, gate_pre, gate_mid, gate_long, gate_out = (
+        array[0] for array in (layer_input, pre_gate, mid_gate, long_gate, out_gate)
+    )
+    filter_taps = mid_filter[0]
+
+    near, far = local(pick_kernel, [half_shape] * 2, [me, incoming[0]], few, name="pick")
+    far = passed_along(far, "section", -1)
+    near = passed_along(near, "section", -1)
+    mixed_in = local(mix_kernel, [rows_shape], [inputs, gate_pre], few, name="mix")
+    earlier = shifted(mixed_in, "ctx", 1)
+    far_z = local(
+        functools.partial(pieces_z_kernel, beta, half), [piece] * half, [me, far, gate_out], few, name="farz"
+    )
+    near_z = local(
+        functools.partial(pieces_z_kernel, beta, 0), [piece] * half, [me, near, gate_out], few, name="nearz"
+    )
+    signal, filt, *pieces_w = local(
+        functools.partial(pieces_branch_kernel, beta),
+        [((span, channels), BF16)] * 2 + [piece] * devices,
+        [me, fwd, inv_conv, earlier, mixed_in, filter_taps, inputs, gate_mid, gate_long], mid_flops,
+        name="branch",
+    )
+    pieces_z = exchanged(list(near_z) + list(far_z))
+    pieces_w = exchanged(pieces_w)
+    *pieces_g, channel_z = local(
+        functools.partial(pieces_grad_w_kernel, blocks, devices),
+        [piece] * devices + [((seq_len, owned), BF16)],
+        [me, long_fwd, long_inv, long_filter[0], *pieces_z], long_flops,
+        [spectrum, spectrum, joint, staged], name="gradw",
+    )
+    pieces_g = exchanged(pieces_g)
+    long_grad = local(
+        functools.partial(pieces_long_grad_kernel, blocks, scale, devices), [((owned, seq_len), BF16)],
+        [me, long_fwd, long_inv, channel_z, *pieces_w], long_flops,
+        [spectrum, spectrum, joint, staged], name="longgrad",
+    )
+    pieces_g, long_grad = lax.optimization_barrier((pieces_g, long_grad))
+    grad_u, grad_b = local(
+        functools.partial(pieces_grad_b_kernel, beta, devices), [((tokens, channels), F32), rows_shape],
+        [me, near, far, gate_long, gate_mid, *pieces_g], few, name="gradb",
+    )
+    later = shifted(grad_b, "ctx", -1)
+    keep, send = local(
+        pieces_taps_kernel, [((half, taps, owned), BF16)] * 2, [me, fwd, inv_taps, signal, grad_b],
+        mid_flops, name="taps",
+    )
+    sums = local(pair_kernel, [tap_piece] * half, [keep, swapped(send, 1)], few, name="pair")
+    sums = exchanged(list(sums), 2)
+    later, _ = lax.optimization_barrier((later, sums[0]))
+    input_grad = local(
+        functools.partial(pieces_input_grad_kernel, 512), [rows_shape],
+        [fwd, inv_corr, grad_b, later, filt, grad_u, gate_pre], mid_flops, name="inputgrad",
+    )
+    mid_grad = local(functools.partial(pieces_total_kernel, scale), [tap_piece], sums, few, name="midgrad")
+    return (input_grad[None], long_grad[None], mid_grad[None])
+
+
+def per_device(*arrays):
+    devices = lax.axis_size("ctx")
+    owned = arrays[0].shape[2] // devices
+    if owned % 128 == 0 and devices in (2, 4, 8, 16):
+        return by_permutes(*arrays)
+    return by_all_to_all(*arrays)
+
+
 def solution(mesh):
     placed = (
         P("section", "ctx", None),

time: 172 us -> 147 us (0.85)
  the two profiles are of different devices: /device:TPU:1 before, /device:TPU:0 now
where the time goes in v4:
time: 147 us
  waiting for transfers between devices  63 us (43%)
  starting transfers between devices  53.5 us (36%)
  Pallas kernels  25.8 us (18%)
  local copies, waits for them, and re-layouts  3.75 us (3%)
    ppermute x25, waiting for transfers between devices, swapped(): return lax.ppermute(array, 'ctx', [(i, i ^ k) for i in range(count)])  48.2 us
    ppermute x25, starting transfers between devices, swapped(): return lax.ppermute(array, 'ctx', [(i, i ^ k) for i in range(count)])  45.8 us
    pallas_call x12, Pallas kernels, local(): pl.pallas_call(body, in_specs=specs, out_specs=[pl.BlockSpec(memory_space...  25.8 us
    ppermute x2, waiting for transfers between devices, passed_along(): return lax.ppermute(value, axis, pairs)  14.8 us
    ppermute x2, starting transfers between devices, passed_along(): return lax.ppermute(value, axis, pairs)  4.53 us
    unnamed x32, local copies, waits for them, and re-layouts  3.75 us
    ppermute x2, starting transfers between devices, shifted(): return lax.ppermute(array, axis, pairs)  3.13 us
  transfers between devices with their start and end apart: 29, of which 13 were waited for; matrix products, arithmetic and copies ran while one was open for 0% of the time, Pallas kernels for 14%

profile of v4, /device:TPU:0, one launch (start us, length us, event | category | flops | bytes accessed | tf_op | source)
XLA Modules:
  0.0 147.0 jit_solution(12874047063425258407)
XLA Ops:
  0.7 1.2 copy-done.8
  1.9 0.6 pick.1
  2.6 3.9 %collective-permute-start = (bf16[128,2048]{1,0:T(8,128)(2,1)S(1)}, bf16[128,2048]{1,0:T(8,128)(2,1)S(1)}, u32[]{:S(2)}, u32[]{:S(2)}) collective-permute-start(bf16[128,2048]{1,0:T(8,128)(2,1)S(1)} %get-tuple-element.50), channel_id=1, source_target_pairs={{0,24},{8,0},{16,8},{24,16},{1,25},{9,1},{17,9},{25,17},{2,26},{10... | collective-permute-start | bytes 1572872 | tf_op jit(solution)/shard_map/ppermute | solution.py:20
  6.5 1.2 copy-done
  7.7 1.2 copy-done.5
  9.0 0.2 mix.1.mixed_ref
  9.2 1.7 %collective-permute-start.16 = (bf16[128,4096]{1,0:T(8,128)(2,1)S(1)}, bf16[128,4096]{1,0:T(8,128)(2,1)S(1)}, u32[]{:S(2)}, u32[]{:S(2)}) collective-permute-start(bf16[128,4096]{1,0:T(8,128)(2,1)S(1)} %mix.1.mixed_ref), channel_id=1, source_target_pairs={{0,1},{1,2},{2,3},{3,4},{4,5},{5,6},{6,7},{8,9},{9,10},{10,11},{11... | collective-permute-start | bytes 3145736 | tf_op jit(solution)/shard_map/ppermute | solution.py:26
  10.9 0.6 collective-permute-start.1
  11.5 7.3 %collective-permute-done.adjoint_ref.near_ref = bf16[128,2048]{1,0:T(8,128)(2,1)S(1)} collective-permute-done((bf16[128,2048]{1,0:T(8,128)(2,1)S(1)}, bf16[128,2048]{1,0:T(8,128)(2,1)S(1)}, u32[]{:S(2)}, u32[]{:S(2)}) %collective-permute-start) | collective-permute-done | bytes 524320 | tf_op jit(solution)/shard_map/ppermute | solution.py:20
  18.8 0.7 nearz.1
  19.6 1.7 %collective-permute-start.3 = (bf16[128,512]{1,0:T(8,128)(2,1)S(1)}, bf16[128,512]{1,0:T(8,128)(2,1)S(1)}, u32[]{:S(2)}, u32[]{:S(2)}) collective-permute-start(bf16[128,512]{1,0:T(8,128)(2,1)S(1)} %get-tuple-element.54), channel_id=1, source_target_pairs={{0,2},{1,3},{2,0},{3,1},{4,6},{5,7},{6,4},{7,5},{8,10},{9,11},{10,... | collective-permute-start | bytes 393224 | tf_op jit(solution)/shard_map/ppermute | solution.py:533
  21.5 7.4 %collective-permute-done.1.adjoint_ref.far_ref = bf16[128,2048]{1,0:T(8,128)(2,1)S(1)} collective-permute-done((bf16[128,2048]{1,0:T(8,128)(2,1)S(1)}, bf16[128,2048]{1,0:T(8,128)(2,1)S(1)}, u32[]{:S(2)}, u32[]{:S(2)}) %collective-permute-start.1) | collective-permute-done | bytes 524320 | tf_op jit(solution)/shard_map/ppermute | solution.py:20
  28.9 0.7 farz.1
  29.6 2.7 %collective-permute-start.5 = (bf16[128,512]{1,0:T(8,128)(2,1)S(1)}, bf16[128,512]{1,0:T(8,128)(2,1)S(1)}, u32[]{:S(2)}, u32[]{:S(2)}) collective-permute-start(bf16[128,512]{1,0:T(8,128)(2,1)S(1)} %get-tuple-element.56), channel_id=1, source_target_pairs={{0,4},{1,5},{2,6},{3,7},{4,0},{5,1},{6,2},{7,3},{8,12},{9,13},{10,... | collective-permute-start | bytes 393224 | tf_op jit(solution)/shard_map/ppermute | solution.py:533
  32.3 2.2 %collective-permute-start.7 = (bf16[128,512]{1,0:T(8,128)(2,1)S(1)}, bf16[128,512]{1,0:T(8,128)(2,1)S(1)}, u32[]{:S(2)}, u32[]{:S(2)}) collective-permute-start(bf16[128,512]{1,0:T(8,128)(2,1)S(1)} %get-tuple-element.58), channel_id=1, source_target_pairs={{0,6},{1,7},{2,4},{3,5},{4,2},{5,3},{6,0},{7,1},{8,14},{9,15},{10,... | collective-permute-start | bytes 393224 | tf_op jit(solution)/shard_map/ppermute | solution.py:533
  34.6 1.5 %collective-permute-start.8 = (bf16[128,512]{1,0:T(8,128)(2,1)S(1)}, bf16[128,512]{1,0:T(8,128)(2,1)S(1)}, u32[]{:S(2)}, u32[]{:S(2)}) collective-permute-start(bf16[128,512]{1,0:T(8,128)(2,1)S(1)} %get-tuple-element.59), channel_id=1, source_target_pairs={{0,7},{1,6},{2,5},{3,4},{4,3},{5,2},{6,1},{7,0},{8,15},{9,14},{10,... | collective-permute-start | bytes 393224 | tf_op jit(solution)/shard_map/ppermute | solution.py:533
  36.1 11.3 %collective-permute-done.5.refs_4_ = bf16[128,512]{1,0:T(8,128)(2,1)S(1)} collective-permute-done((bf16[128,512]{1,0:T(8,128)(2,1)S(1)}, bf16[128,512]{1,0:T(8,128)(2,1)S(1)}, u32[]{:S(2)}, u32[]{:S(2)}) %collective-permute-start.5) | collective-permute-done | bytes 131104 | tf_op jit(solution)/shard_map/ppermute | solution.py:533
  47.4 0.6 collective-permute-done.6.refs_5_
  48.1 5.3 %gradw.1 = (bf16[128,512]{1,0:T(8,128)(2,1)S(1)}, bf16[128,512]{1,0:T(8,128)(2,1)S(1)}, bf16[128,512]{1,0:T(8,128)(2,1)S(1)}, bf16[128,512]{1,0:T(8,128)(2,1)S(1...) custom-call(s32[2]{0:T(128)S(1)} %pad_add_fusion.me_ref, ...), custom_call_target="tpu_custom_call" | custom-call | flops 3221225472 | bytes 4980744 | tf_op jit(solution)/shard_map/gradw/pallas_call | solution.py:518
  53.4 2.1 %collective-permute-start.9 = (bf16[128,512]{1,0:T(8,128)(2,1)S(1)}, bf16[128,512]{1,0:T(8,128)(2,1)S(1)}, u32[]{:S(2)}, u32[]{:S(2)}) collective-permute-start(bf16[128,512]{1,0:T(8,128)(2,1)S(1)} %get-tuple-element.61), channel_id=1, source_target_pairs={{0,1},{1,0},{2,3},{3,2},{4,5},{5,4},{6,7},{7,6},{8,9},{9,8},{10,11... | collective-permute-start | bytes 393224 | tf_op jit(solution)/shard_map/ppermute | solution.py:533
  55.5 5.3 %collective-permute-start.10 = (bf16[128,512]{1,0:T(8,128)(2,1)S(1)}, bf16[128,512]{1,0:T(8,128)(2,1)S(1)}, u32[]{:S(2)}, u32[]{:S(2)}) collective-permute-start(bf16[128,512]{1,0:T(8,128)(2,1)S(1)} %get-tuple-element.62), channel_id=1, source_target_pairs={{0,2},{1,3},{2,0},{3,1},{4,6},{5,7},{6,4},{7,5},{8,10},{9,11},{10,... | collective-permute-start | bytes 393224 | tf_op jit(solution)/shard_map/ppermute | solution.py:533
  60.9 3.6 %branch.1 = (bf16[256,4096]{1,0:T(8,128)(2,1)S(1)}, bf16[256,4096]{1,0:T(8,128)(2,1)S(1)}, bf16[128,512]{1,0:T(8,128)(2,1)S(1)}, bf16[128,512]{1,0:T(8,128)(2,1)...) custom-call(s32[2]{0:T(128)S(1)} %pad_add_fusion.me_ref, ...), custom_call_target="tpu_custom_call" | custom-call | flops 1073741824 | bytes 11730952 | tf_op jit(solution)/shard_map/branch/pallas_call | solution.py:518
  64.7 0.3 collective-permute-start.18
  65.0 1.4 collective-permute-start.19
  66.4 2.0 %collective-permute-start.20 = (bf16[128,512]{1,0:T(8,128)(2,1)S(1)}, bf16[128,512]{1,0:T(8,128)(2,1)S(1)}, u32[]{:S(2)}, u32[]{:S(2)}) collective-permute-start(bf16[128,512]{1,0:T(8,128)(2,1)S(1)} %get-tuple-element.73), channel_id=1, source_target_pairs={{0,4},{1,5},{2,6},{3,7},{4,0},{5,1},{6,2},{7,3},{8,12},{9,13},{10,... | collective-permute-start | bytes 393224 | tf_op jit(solution)/shard_map/ppermute | solution.py:533
  68.4 0.7 collective-permute-start.21
  69.1 3.0 %collective-permute-start.22 = (bf16[128,512]{1,0:T(8,128)(2,1)S(1)}, bf16[128,512]{1,0:T(8,128)(2,1)S(1)}, u32[]{:S(2)}, u32[]{:S(2)}) collective-permute-start(bf16[128,512]{1,0:T(8,128)(2,1)S(1)} %get-tuple-element.75), channel_id=1, source_target_pairs={{0,6},{1,7},{2,4},{3,5},{4,2},{5,3},{6,0},{7,1},{8,14},{9,15},{10,... | collective-permute-start | bytes 393224 | tf_op jit(solution)/shard_map/ppermute | solution.py:533
  72.2 3.2 %collective-permute-done.18.refs_2_ = bf16[128,512]{1,0:T(8,128)(2,1)S(1)} collective-permute-done((bf16[128,512]{1,0:T(8,128)(2,1)S(1)}, bf16[128,512]{1,0:T(8,128)(2,1)S(1)}, u32[]{:S(2)}, u32[]{:S(2)}) %collective-permute-start.18) | collective-permute-done | bytes 131104 | tf_op jit(solution)/shard_map/ppermute | solution.py:533
  75.4 1.7 %collective-permute-done.19.refs_3_ = bf16[128,512]{1,0:T(8,128)(2,1)S(1)} collective-permute-done((bf16[128,512]{1,0:T(8,128)(2,1)S(1)}, bf16[128,512]{1,0:T(8,128)(2,1)S(1)}, u32[]{:S(2)}, u32[]{:S(2)}) %collective-permute-start.19) | collective-permute-done | bytes 131104 | tf_op jit(solution)/shard_map/ppermute | solution.py:533
  77.1 2.4 %collective-permute-start.12 = (bf16[128,512]{1,0:T(8,128)(2,1)S(1)}, bf16[128,512]{1,0:T(8,128)(2,1)S(1)}, u32[]{:S(2)}, u32[]{:S(2)}) collective-permute-start(bf16[128,512]{1,0:T(8,128)(2,1)S(1)} %get-tuple-element.64), channel_id=1, source_target_pairs={{0,4},{1,5},{2,6},{3,7},{4,0},{5,1},{6,2},{7,3},{8,12},{9,13},{10,... | collective-permute-start | bytes 393224 | tf_op jit(solution)/shard_map/ppermute | solution.py:533
  79.5 7.4 %collective-permute-done.21.refs_5_ = bf16[128,512]{1,0:T(8,128)(2,1)S(1)} collective-permute-done((bf16[128,512]{1,0:T(8,128)(2,1)S(1)}, bf16[128,512]{1,0:T(8,128)(2,1)S(1)}, u32[]{:S(2)}, u32[]{:S(2)}) %collective-permute-start.21) | collective-permute-done | bytes 131104 | tf_op jit(solution)/shard_map/ppermute | solution.py:533
  86.9 8.5 %collective-permute-start.14 = (bf16[128,512]{1,0:T(8,128)(2,1)S(1)}, bf16[128,512]{1,0:T(8,128)(2,1)S(1)}, u32[]{:S(2)}, u32[]{:S(2)}) collective-permute-start(bf16[128,512]{1,0:T(8,128)(2,1)S(1)} %get-tuple-element.66), channel_id=1, source_target_pairs={{0,6},{1,7},{2,4},{3,5},{4,2},{5,3},{6,0},{7,1},{8,14},{9,15},{10,... | collective-permute-start | bytes 393224 | tf_op jit(solution)/shard_map/ppermute | solution.py:533
  95.4 0.6 collective-permute-start.15
  96.0 6.2 %longgrad.1 = bf16[512,1024]{1,0:T(8,128)(2,1)} custom-call(s32[2]{0:T(128)S(1)} %pad_add_fusion.me_ref, bf16[512,512]{1,0:T(8,128)(2,1)S(1)} %copy-done.13, bf16[256,512]{1,0:T(8,128)(2,1)S(1)} %copy-done.14, bf16[1024,512]{1,0:T(8,128)(2,1)S(1)} %get-tuple-element.68.grad_ref, bf16[128,512]{1,0:T(8,128)(2,1)S(1)} %get-tuple-element.69.refs_0_, ...), custom_call_target="tpu_custom_call" | custom-call | flops 3221225472 | bytes 3932168 | tf_op jit(solution)/shard_map/longgrad/pallas_call | solution.py:518
  102.2 5.2 %collective-permute-done.12.refs_4_ = bf16[128,512]{1,0:T(8,128)(2,1)S(1)} collective-permute-done((bf16[128,512]{1,0:T(8,128)(2,1)S(1)}, bf16[128,512]{1,0:T(8,128)(2,1)S(1)}, u32[]{:S(2)}, u32[]{:S(2)}) %collective-permute-start.12) | collective-permute-done | bytes 131104 | tf_op jit(solution)/shard_map/ppermute | solution.py:533
  107.4 1.9 %collective-permute-done.13.refs_5_ = bf16[128,512]{1,0:T(8,128)(2,1)S(1)} collective-permute-done((bf16[128,512]{1,0:T(8,128)(2,1)S(1)}, bf16[128,512]{1,0:T(8,128)(2,1)S(1)}, u32[]{:S(2)}, u32[]{:S(2)}) %collective-permute-start.13) | collective-permute-done | bytes 131104 | tf_op jit(solution)/shard_map/ppermute | solution.py:533
  109.3 1.2 gradb.1
  110.5 1.5 %collective-permute-start.24 = (bf16[128,4096]{1,0:T(8,128)(2,1)S(1)}, bf16[128,4096]{1,0:T(8,128)(2,1)S(1)}, u32[]{:S(2)}, u32[]{:S(2)}) collective-permute-start(bf16[128,4096]{1,0:T(8,128)(2,1)S(1)} %get-tuple-element.85.grad_b_ref), channel_id=1, source_target_pairs={{1,0},{2,1},{3,2},{4,3},{5,4},{6,5},{7,6},{9,8},{10,9},{11,10},{12... | collective-permute-start | bytes 3145736 | tf_op jit(solution)/shard_map/ppermute | solution.py:26
  112.0 3.0 %taps.1 = (bf16[4,128,512]{2,1,0:T(8,128)(2,1)S(1)}, bf16[4,128,512]{2,1,0:T(8,128)(2,1)S(1)}) custom-call(s32[2]{0:T(128)S(1)} %pad_add_fusion.me_ref, bf16[256,256]{1,0:T(8,128)(2,1)S(1)} %copy-done.9, bf16[128,256]{1,0:T(8,128)(2,1)S(1)} %copy-done.15, bf16[256,4096]{1,0:T(8,128)(2,1)S(1)} %get-tuple-element.86.signal_ref, ...), custom_call_target="tpu_custom_call" | custom-call | flops 1073741824 | bytes 4390920 | tf_op jit(solution)/shard_map/taps/pallas_call | solution.py:518
  115.0 1.4 collective-permute-start.25
  116.4 1.5 %collective-permute-done.25.came_ref = bf16[4,128,512]{2,1,0:T(8,128)(2,1)S(1)} collective-permute-done((bf16[4,128,512]{2,1,0:T(8,128)(2,1)S(1)}, bf16[4,128,512]{2,1,0:T(8,128)(2,1)S(1)}, u32[]{:S(2)}, u32[]{:S(2)}) %collective-permute-start.25) | collective-permute-done | bytes 524320 | tf_op jit(solution)/shard_map/ppermute | solution.py:533
  118.0 6.1 %collective-permute-start.26 = (bf16[128,512]{1,0:T(8,128)(2,1)S(1)}, bf16[128,512]{1,0:T(8,128)(2,1)S(1)}, u32[]{:S(2)}, u32[]{:S(2)}) collective-permute-start(bf16[128,512]{1,0:T(8,128)(2,1)S(1)} %get-tuple-element.94), channel_id=1, source_target_pairs={{0,2},{1,3},{2,0},{3,1},{4,6},{5,7},{6,4},{7,5},{8,10},{9,11},{10,... | collective-permute-start | bytes 393224 | tf_op jit(solution)/shard_map/ppermute | solution.py:533
  124.2 3.2 %collective-permute-start.27 = (bf16[128,512]{1,0:T(8,128)(2,1)S(1)}, bf16[128,512]{1,0:T(8,128)(2,1)S(1)}, u32[]{:S(2)}, u32[]{:S(2)}) collective-permute-start(bf16[128,512]{1,0:T(8,128)(2,1)S(1)} %get-tuple-element.95), channel_id=1, source_target_pairs={{0,4},{1,5},{2,6},{3,7},{4,0},{5,1},{6,2},{7,3},{8,12},{9,13},{10,... | collective-permute-start | bytes 393224 | tf_op jit(solution)/shard_map/ppermute | solution.py:533
  127.4 9.7 %collective-permute-done.26.refs_1_ = bf16[128,512]{1,0:T(8,128)(2,1)S(1)} collective-permute-done((bf16[128,512]{1,0:T(8,128)(2,1)S(1)}, bf16[128,512]{1,0:T(8,128)(2,1)S(1)}, u32[]{:S(2)}, u32[]{:S(2)}) %collective-permute-start.26) | collective-permute-done | bytes 131104 | tf_op jit(solution)/shard_map/ppermute | solution.py:533
  137.1 2.8 %collective-permute-done.27.refs_2_ = bf16[128,512]{1,0:T(8,128)(2,1)S(1)} collective-permute-done((bf16[128,512]{1,0:T(8,128)(2,1)S(1)}, bf16[128,512]{1,0:T(8,128)(2,1)S(1)}, u32[]{:S(2)}, u32[]{:S(2)}) %collective-permute-start.27) | collective-permute-done | bytes 131104 | tf_op jit(solution)/shard_map/ppermute | solution.py:533
  139.8 3.0 %collective-permute-done.28.refs_3_ = bf16[128,512]{1,0:T(8,128)(2,1)S(1)} collective-permute-done((bf16[128,512]{1,0:T(8,128)(2,1)S(1)}, bf16[128,512]{1,0:T(8,128)(2,1)S(1)}, u32[]{:S(2)}, u32[]{:S(2)}) %collective-permute-start.28) | collective-permute-done | bytes 131104 | tf_op jit(solution)/shard_map/ppermute | solution.py:533
  142.8 0.7 midgrad.1
  143.5 3.5 %inputgrad.1 = bf16[128,4096]{1,0:T(8,128)(2,1)} custom-call(bf16[256,256]{1,0:T(8,128)(2,1)S(1)} %copy-done.9, bf16[128,256]{1,0:T(8,128)(2,1)S(1)} %copy-done.10, bf16[128,4096]{1,0:T(8,128)(2,1)S(1)} %get-tuple-element.85.grad_b_ref, bf16[128,4096]{1,0:T(8,128)(2,1)S(1)} %collective-permute-done.24.later_ref, ...), custom_call_target="tpu_custom_call" | custom-call | flops 1073741824 | bytes 8585216 | tf_op jit(solution)/shard_map/inputgrad/pallas_call | solution.py:518
  (55 shorter events, 0.8 us)
Async XLA Ops:
  0.7 1.2 copy-start.8
  1.9 16.9 %copy-start.4 = (bf16[1,128,4096]{2,1,0:T(8,128)(2,1)S(1)}, bf16[1,128,4096]{2,1,0:T(8,128)(2,1)}, u32[]{:S(2)}) copy-start(bf16[1,128,4096]{2,1,0:T(8,128)(2,1)} %param.19) | copy-start | bytes 3145732
  2.6 16.3 %collective-permute-start = (bf16[128,2048]{1,0:T(8,128)(2,1)S(1)}, bf16[128,2048]{1,0:T(8,128)(2,1)S(1)}, u32[]{:S(2)}, u32[]{:S(2)}) collective-permute-start(bf16[128,2048]{1,0:T(8,128)(2,1)S(1)} %get-tuple-element.50), channel_id=1, source_target_pairs={{0,24},{8,0},{16,8},{24,16},{1,25},{9,1},{17,9},{25,17},{2,26},{10... | collective-permute-start | bytes 1572872 | tf_op jit(solution)/shard_map/ppermute | solution.py:20
  6.5 1.2 copy-start
  7.7 1.2 copy-start.5
  9.2 38.8 %copy-start.12 = (bf16[1,512,1024]{2,1,0:T(8,128)(2,1)S(1)}, bf16[1,512,1024]{2,1,0:T(8,128)(2,1)}, u32[]{:S(2)}) copy-start(bf16[1,512,1024]{2,1,0:T(8,128)(2,1)} %param.20) | copy-start | bytes 3145732
  9.2 38.8 %copy-start.13 = (bf16[512,512]{1,0:T(8,128)(2,1)S(1)}, bf16[512,512]{1,0:T(8,128)(2,1)}, u32[]{:S(2)}) copy-start(bf16[512,512]{1,0:T(8,128)(2,1)} %constant.36.clone.fwd_ref) | copy-start | bytes 1572868
  9.2 38.8 %copy-start.14 = (bf16[256,512]{1,0:T(8,128)(2,1)S(1)}, bf16[256,512]{1,0:T(8,128)(2,1)}, u32[]{:S(2)}) copy-start(bf16[256,512]{1,0:T(8,128)(2,1)} %constant.37.clone.inv_ref) | copy-start | bytes 786436
  9.2 51.6 %collective-permute-start.16 = (bf16[128,4096]{1,0:T(8,128)(2,1)S(1)}, bf16[128,4096]{1,0:T(8,128)(2,1)S(1)}, u32[]{:S(2)}, u32[]{:S(2)}) collective-permute-start(bf16[128,4096]{1,0:T(8,128)(2,1)S(1)} %mix.1.mixed_ref), channel_id=1, source_target_pairs={{0,1},{1,2},{2,3},{3,4},{4,5},{5,6},{6,7},{8,9},{9,10},{10,11},{11... | collective-permute-start | bytes 3145736 | tf_op jit(solution)/shard_map/ppermute | solution.py:26
  10.9 18.0 %collective-permute-start.1 = (bf16[128,2048]{1,0:T(8,128)(2,1)S(1)}, bf16[128,2048]{1,0:T(8,128)(2,1)S(1)}, u32[]{:S(2)}, u32[]{:S(2)}) collective-permute-start(bf16[128,2048]{1,0:T(8,128)(2,1)S(1)} %get-tuple-element.51), channel_id=1, source_target_pairs={{0,24},{8,0},{16,8},{24,16},{1,25},{9,1},{17,9},{25,17},{2,26},{10... | collective-permute-start | bytes 1572872 | tf_op jit(solution)/shard_map/ppermute | solution.py:20
  19.6 12.8 %collective-permute-start.2 = (bf16[128,512]{1,0:T(8,128)(2,1)S(1)}, bf16[128,512]{1,0:T(8,128)(2,1)S(1)}, u32[]{:S(2)}, u32[]{:S(2)}) collective-permute-start(bf16[128,512]{1,0:T(8,128)(2,1)S(1)} %get-tuple-element.53), channel_id=1, source_target_pairs={{0,1},{1,0},{2,3},{3,2},{4,5},{5,4},{6,7},{7,6},{8,9},{9,8},{10,11... | collective-permute-start | bytes 393224 | tf_op jit(solution)/shard_map/ppermute | solution.py:533
  19.6 12.7 %collective-permute-start.3 = (bf16[128,512]{1,0:T(8,128)(2,1)S(1)}, bf16[128,512]{1,0:T(8,128)(2,1)S(1)}, u32[]{:S(2)}, u32[]{:S(2)}) collective-permute-start(bf16[128,512]{1,0:T(8,128)(2,1)S(1)} %get-tuple-element.54), channel_id=1, source_target_pairs={{0,2},{1,3},{2,0},{3,1},{4,6},{5,7},{6,4},{7,5},{8,10},{9,11},{10,... | collective-permute-start | bytes 393224 | tf_op jit(solution)/shard_map/ppermute | solution.py:533
  21.3 13.3 %collective-permute-start.4 = (bf16[128,512]{1,0:T(8,128)(2,1)S(1)}, bf16[128,512]{1,0:T(8,128)(2,1)S(1)}, u32[]{:S(2)}, u32[]{:S(2)}) collective-permute-start(bf16[128,512]{1,0:T(8,128)(2,1)S(1)} %get-tuple-element.55), channel_id=1, source_target_pairs={{0,3},{1,2},{2,1},{3,0},{4,7},{5,6},{6,5},{7,4},{8,11},{9,10},{10,... | collective-permute-start | bytes 393224 | tf_op jit(solution)/shard_map/ppermute | solution.py:533
  29.6 17.8 %collective-permute-start.5 = (bf16[128,512]{1,0:T(8,128)(2,1)S(1)}, bf16[128,512]{1,0:T(8,128)(2,1)S(1)}, u32[]{:S(2)}, u32[]{:S(2)}) collective-permute-start(bf16[128,512]{1,0:T(8,128)(2,1)S(1)} %get-tuple-element.56), channel_id=1, source_target_pairs={{0,4},{1,5},{2,6},{3,7},{4,0},{5,1},{6,2},{7,3},{8,12},{9,13},{10,... | collective-permute-start | bytes 393224 | tf_op jit(solution)/shard_map/ppermute | solution.py:533
  32.3 15.7 %collective-permute-start.6 = (bf16[128,512]{1,0:T(8,128)(2,1)S(1)}, bf16[128,512]{1,0:T(8,128)(2,1)S(1)}, u32[]{:S(2)}, u32[]{:S(2)}) collective-permute-start(bf16[128,512]{1,0:T(8,128)(2,1)S(1)} %get-tuple-element.57), channel_id=1, source_target_pairs={{0,5},{1,4},{2,7},{3,6},{4,1},{5,0},{6,3},{7,2},{8,13},{9,12},{10,... | collective-permute-start | bytes 393224 | tf_op jit(solution)/shard_map/ppermute | solution.py:533
  32.3 15.7 %collective-permute-start.7 = (bf16[128,512]{1,0:T(8,128)(2,1)S(1)}, bf16[128,512]{1,0:T(8,128)(2,1)S(1)}, u32[]{:S(2)}, u32[]{:S(2)}) collective-permute-start(bf16[128,512]{1,0:T(8,128)(2,1)S(1)} %get-tuple-element.58), channel_id=1, source_target_pairs={{0,6},{1,7},{2,4},{3,5},{4,2},{5,3},{6,0},{7,1},{8,14},{9,15},{10,... | collective-permute-start | bytes 393224 | tf_op jit(solution)/shard_map/ppermute | solution.py:533
  34.6 13.4 %collective-permute-start.8 = (bf16[128,512]{1,0:T(8,128)(2,1)S(1)}, bf16[128,512]{1,0:T(8,128)(2,1)S(1)}, u32[]{:S(2)}, u32[]{:S(2)}) collective-permute-start(bf16[128,512]{1,0:T(8,128)(2,1)S(1)} %get-tuple-element.59), channel_id=1, source_target_pairs={{0,7},{1,6},{2,5},{3,4},{4,3},{5,2},{6,1},{7,0},{8,15},{9,14},{10,... | collective-permute-start | bytes 393224 | tf_op jit(solution)/shard_map/ppermute | solution.py:533
  48.0 12.8 %copy-start.1 = (bf16[1,128,4096]{2,1,0:T(8,128)(2,1)S(1)}, bf16[1,128,4096]{2,1,0:T(8,128)(2,1)}, u32[]{:S(2)}) copy-start(bf16[1,128,4096]{2,1,0:T(8,128)(2,1)} %param.15) | copy-start | bytes 3145732
  48.1 12.8 %copy-start.2 = (bf16[1,128,4096]{2,1,0:T(8,128)(2,1)S(1)}, bf16[1,128,4096]{2,1,0:T(8,128)(2,1)}, u32[]{:S(2)}) copy-start(bf16[1,128,4096]{2,1,0:T(8,128)(2,1)} %param.18) | copy-start | bytes 3145732
  48.1 12.8 %copy-start.3 = (bf16[1,128,4096]{2,1,0:T(8,128)(2,1)S(1)}, bf16[1,128,4096]{2,1,0:T(8,128)(2,1)}, u32[]{:S(2)}) copy-start(bf16[1,128,4096]{2,1,0:T(8,128)(2,1)} %param.17) | copy-start | bytes 3145732
  48.1 12.8 %copy-start.7 = (bf16[1,128,4096]{2,1,0:T(8,128)(2,1)S(1)}, bf16[1,128,4096]{2,1,0:T(8,128)(2,1)}, u32[]{:S(2)}) copy-start(bf16[1,128,4096]{2,1,0:T(8,128)(2,1)} %param.21) | copy-start | bytes 3145732
  48.1 12.8 %copy-start.9 = (bf16[256,256]{1,0:T(8,128)(2,1)S(1)}, bf16[256,256]{1,0:T(8,128)(2,1)}, u32[]{:S(2)}) copy-start(bf16[256,256]{1,0:T(8,128)(2,1)} %constant.32.clone.fwd_ref) | copy-start | bytes 393220
  48.1 12.8 %copy-start.11 = (bf16[128,256]{1,0:T(8,128)(2,1)S(1)}, bf16[128,256]{1,0:T(8,128)(2,1)}, u32[]{:S(2)}) copy-start(bf16[128,256]{1,0:T(8,128)(2,1)} %constant.33.clone.inv_ref) | copy-start | bytes 196612
  53.4 13.0 %collective-permute-start.9 = (bf16[128,512]{1,0:T(8,128)(2,1)S(1)}, bf16[128,512]{1,0:T(8,128)(2,1)S(1)}, u32[]{:S(2)}, u32[]{:S(2)}) collective-permute-start(bf16[128,512]{1,0:T(8,128)(2,1)S(1)} %get-tuple-element.61), channel_id=1, source_target_pairs={{0,1},{1,0},{2,3},{3,2},{4,5},{5,4},{6,7},{7,6},{8,9},{9,8},{10,11... | collective-permute-start | bytes 393224 | tf_op jit(solution)/shard_map/ppermute | solution.py:533
  55.5 12.9 %collective-permute-start.10 = (bf16[128,512]{1,0:T(8,128)(2,1)S(1)}, bf16[128,512]{1,0:T(8,128)(2,1)S(1)}, u32[]{:S(2)}, u32[]{:S(2)}) collective-permute-start(bf16[128,512]{1,0:T(8,128)(2,1)S(1)} %get-tuple-element.62), channel_id=1, source_target_pairs={{0,2},{1,3},{2,0},{3,1},{4,6},{5,7},{6,4},{7,5},{8,10},{9,11},{10,... | collective-permute-start | bytes 393224 | tf_op jit(solution)/shard_map/ppermute | solution.py:533
  64.5 4.6 %collective-permute-start.17 = (bf16[128,512]{1,0:T(8,128)(2,1)S(1)}, bf16[128,512]{1,0:T(8,128)(2,1)S(1)}, u32[]{:S(2)}, u32[]{:S(2)}) collective-permute-start(bf16[128,512]{1,0:T(8,128)(2,1)S(1)} %get-tuple-element.70), channel_id=1, source_target_pairs={{0,1},{1,0},{2,3},{3,2},{4,5},{5,4},{6,7},{7,6},{8,9},{9,8},{10,11... | collective-permute-start | bytes 393224 | tf_op jit(solution)/shard_map/ppermute | solution.py:533
  64.7 10.7 %collective-permute-start.18 = (bf16[128,512]{1,0:T(8,128)(2,1)S(1)}, bf16[128,512]{1,0:T(8,128)(2,1)S(1)}, u32[]{:S(2)}, u32[]{:S(2)}) collective-permute-start(bf16[128,512]{1,0:T(8,128)(2,1)S(1)} %get-tuple-element.71), channel_id=1, source_target_pairs={{0,2},{1,3},{2,0},{3,1},{4,6},{5,7},{6,4},{7,5},{8,10},{9,11},{10,... | collective-permute-start | bytes 393224 | tf_op jit(solution)/shard_map/ppermute | solution.py:533
  65.0 12.1 %collective-permute-start.19 = (bf16[128,512]{1,0:T(8,128)(2,1)S(1)}, bf16[128,512]{1,0:T(8,128)(2,1)S(1)}, u32[]{:S(2)}, u32[]{:S(2)}) collective-permute-start(bf16[128,512]{1,0:T(8,128)(2,1)S(1)} %get-tuple-element.72), channel_id=1, source_target_pairs={{0,3},{1,2},{2,1},{3,0},{4,7},{5,6},{6,5},{7,4},{8,11},{9,10},{10,... | collective-permute-start | bytes 393224 | tf_op jit(solution)/shard_map/ppermute | solution.py:533
  66.4 10.6 %collective-permute-start.20 = (bf16[128,512]{1,0:T(8,128)(2,1)S(1)}, bf16[128,512]{1,0:T(8,128)(2,1)S(1)}, u32[]{:S(2)}, u32[]{:S(2)}) collective-permute-start(bf16[128,512]{1,0:T(8,128)(2,1)S(1)} %get-tuple-element.73), channel_id=1, source_target_pairs={{0,4},{1,5},{2,6},{3,7},{4,0},{5,1},{6,2},{7,3},{8,12},{9,13},{10,... | collective-permute-start | bytes 393224 | tf_op jit(solution)/shard_map/ppermute | solution.py:533
  68.4 18.5 %collective-permute-start.21 = (bf16[128,512]{1,0:T(8,128)(2,1)S(1)}, bf16[128,512]{1,0:T(8,128)(2,1)S(1)}, u32[]{:S(2)}, u32[]{:S(2)}) collective-permute-start(bf16[128,512]{1,0:T(8,128)(2,1)S(1)} %get-tuple-element.74), channel_id=1, source_target_pairs={{0,5},{1,4},{2,7},{3,6},{4,1},{5,0},{6,3},{7,2},{8,13},{9,12},{10,... | collective-permute-start | bytes 393224 | tf_op jit(solution)/shard_map/ppermute | solution.py:533
  69.1 17.8 %collective-permute-start.22 = (bf16[128,512]{1,0:T(8,128)(2,1)S(1)}, bf16[128,512]{1,0:T(8,128)(2,1)S(1)}, u32[]{:S(2)}, u32[]{:S(2)}) collective-permute-start(bf16[128,512]{1,0:T(8,128)(2,1)S(1)} %get-tuple-element.75), channel_id=1, source_target_pairs={{0,6},{1,7},{2,4},{3,5},{4,2},{5,3},{6,0},{7,1},{8,14},{9,15},{10,... | collective-permute-start | bytes 393224 | tf_op jit(solution)/shard_map/ppermute | solution.py:533
  75.4 20.0 %collective-permute-start.23 = (bf16[128,512]{1,0:T(8,128)(2,1)S(1)}, bf16[128,512]{1,0:T(8,128)(2,1)S(1)}, u32[]{:S(2)}, u32[]{:S(2)}) collective-permute-start(bf16[128,512]{1,0:T(8,128)(2,1)S(1)} %get-tuple-element.76), channel_id=1, source_target_pairs={{0,7},{1,6},{2,5},{3,4},{4,3},{5,2},{6,1},{7,0},{8,15},{9,14},{10,... | collective-permute-start | bytes 393224 | tf_op jit(solution)/shard_map/ppermute | solution.py:533
  77.1 25.2 %collective-permute-start.11 = (bf16[128,512]{1,0:T(8,128)(2,1)S(1)}, bf16[128,512]{1,0:T(8,128)(2,1)S(1)}, u32[]{:S(2)}, u32[]{:S(2)}) collective-permute-start(bf16[128,512]{1,0:T(8,128)(2,1)S(1)} %get-tuple-element.63), channel_id=1, source_target_pairs={{0,3},{1,2},{2,1},{3,0},{4,7},{5,6},{6,5},{7,4},{8,11},{9,10},{10,... | collective-permute-start | bytes 393224 | tf_op jit(solution)/shard_map/ppermute | solution.py:533
  77.1 30.3 %collective-permute-start.12 = (bf16[128,512]{1,0:T(8,128)(2,1)S(1)}, bf16[128,512]{1,0:T(8,128)(2,1)S(1)}, u32[]{:S(2)}, u32[]{:S(2)}) collective-permute-start(bf16[128,512]{1,0:T(8,128)(2,1)S(1)} %get-tuple-element.64), channel_id=1, source_target_pairs={{0,4},{1,5},{2,6},{3,7},{4,0},{5,1},{6,2},{7,3},{8,12},{9,13},{10,... | collective-permute-start | bytes 393224 | tf_op jit(solution)/shard_map/ppermute | solution.py:533
  86.9 22.4 %collective-permute-start.13 = (bf16[128,512]{1,0:T(8,128)(2,1)S(1)}, bf16[128,512]{1,0:T(8,128)(2,1)S(1)}, u32[]{:S(2)}, u32[]{:S(2)}) collective-permute-start(bf16[128,512]{1,0:T(8,128)(2,1)S(1)} %get-tuple-element.65), channel_id=1, source_target_pairs={{0,5},{1,4},{2,7},{3,6},{4,1},{5,0},{6,3},{7,2},{8,13},{9,12},{10,... | collective-permute-start | bytes 393224 | tf_op jit(solution)/shard_map/ppermute | solution.py:533
  86.9 22.4 %collective-permute-start.14 = (bf16[128,512]{1,0:T(8,128)(2,1)S(1)}, bf16[128,512]{1,0:T(8,128)(2,1)S(1)}, u32[]{:S(2)}, u32[]{:S(2)}) collective-permute-start(bf16[128,512]{1,0:T(8,128)(2,1)S(1)} %get-tuple-element.66), channel_id=1, source_target_pairs={{0,6},{1,7},{2,4},{3,5},{4,2},{5,3},{6,0},{7,1},{8,14},{9,15},{10,... | collective-permute-start | bytes 393224 | tf_op jit(solution)/shard_map/ppermute | solution.py:533
  95.4 13.9 %collective-permute-start.15 = (bf16[128,512]{1,0:T(8,128)(2,1)S(1)}, bf16[128,512]{1,0:T(8,128)(2,1)S(1)}, u32[]{:S(2)}, u32[]{:S(2)}) collective-permute-start(bf16[128,512]{1,0:T(8,128)(2,1)S(1)} %get-tuple-element.67), channel_id=1, source_target_pairs={{0,7},{1,6},{2,5},{3,4},{4,3},{5,2},{6,1},{7,0},{8,15},{9,14},{10,... | collective-permute-start | bytes 393224 | tf_op jit(solution)/shard_map/ppermute | solution.py:533
  109.3 2.6 %copy-start.15 = (bf16[128,256]{1,0:T(8,128)(2,1)S(1)}, bf16[128,256]{1,0:T(8,128)(2,1)}, u32[]{:S(2)}) copy-start(bf16[128,256]{1,0:T(8,128)(2,1)} %constant.35.clone.inv_ref) | copy-start | bytes 196612
  110.5 33.0 %collective-permute-start.24 = (bf16[128,4096]{1,0:T(8,128)(2,1)S(1)}, bf16[128,4096]{1,0:T(8,128)(2,1)S(1)}, u32[]{:S(2)}, u32[]{:S(2)}) collective-permute-start(bf16[128,4096]{1,0:T(8,128)(2,1)S(1)} %get-tuple-element.85.grad_b_ref), channel_id=1, source_target_pairs={{1,0},{2,1},{3,2},{4,3},{5,4},{6,5},{7,6},{9,8},{10,9},{11,10},{12... | collective-permute-start | bytes 3145736 | tf_op jit(solution)/shard_map/ppermute | solution.py:26
  112.0 31.5 %copy-start.6 = (bf16[1,128,4096]{2,1,0:T(8,128)(2,1)S(1)}, bf16[1,128,4096]{2,1,0:T(8,128)(2,1)}, u32[]{:S(2)}) copy-start(bf16[1,128,4096]{2,1,0:T(8,128)(2,1)} %param.16) | copy-start | bytes 3145732
  112.0 31.5 %copy-start.10 = (bf16[128,256]{1,0:T(8,128)(2,1)S(1)}, bf16[128,256]{1,0:T(8,128)(2,1)}, u32[]{:S(2)}) copy-start(bf16[128,256]{1,0:T(8,128)(2,1)} %constant.34.clone.inv_ref) | copy-start | bytes 196612
  115.0 3.0 %collective-permute-start.25 = (bf16[4,128,512]{2,1,0:T(8,128)(2,1)S(1)}, bf16[4,128,512]{2,1,0:T(8,128)(2,1)S(1)}, u32[]{:S(2)}, u32[]{:S(2)}) collective-permute-start(bf16[4,128,512]{2,1,0:T(8,128)(2,1)S(1)} %get-tuple-element.88), channel_id=1, source_target_pairs={{0,1},{1,0},{2,3},{3,2},{4,5},{5,4},{6,7},{7,6},{8,9},{9,8},{10,11... | collective-permute-start | bytes 1572872 | tf_op jit(solution)/shard_map/ppermute | solution.py:533
  118.0 19.0 %collective-permute-start.26 = (bf16[128,512]{1,0:T(8,128)(2,1)S(1)}, bf16[128,512]{1,0:T(8,128)(2,1)S(1)}, u32[]{:S(2)}, u32[]{:S(2)}) collective-permute-start(bf16[128,512]{1,0:T(8,128)(2,1)S(1)} %get-tuple-element.94), channel_id=1, source_target_pairs={{0,2},{1,3},{2,0},{3,1},{4,6},{5,7},{6,4},{7,5},{8,10},{9,11},{10,... | collective-permute-start | bytes 393224 | tf_op jit(solution)/shard_map/ppermute | solution.py:533
  124.2 15.6 %collective-permute-start.27 = (bf16[128,512]{1,0:T(8,128)(2,1)S(1)}, bf16[128,512]{1,0:T(8,128)(2,1)S(1)}, u32[]{:S(2)}, u32[]{:S(2)}) collective-permute-start(bf16[128,512]{1,0:T(8,128)(2,1)S(1)} %get-tuple-element.95), channel_id=1, source_target_pairs={{0,4},{1,5},{2,6},{3,7},{4,0},{5,1},{6,2},{7,3},{8,12},{9,13},{10,... | collective-permute-start | bytes 393224 | tf_op jit(solution)/shard_map/ppermute | solution.py:533
  127.4 15.4 %collective-permute-start.28 = (bf16[128,512]{1,0:T(8,128)(2,1)S(1)}, bf16[128,512]{1,0:T(8,128)(2,1)S(1)}, u32[]{:S(2)}, u32[]{:S(2)}) collective-permute-start(bf16[128,512]{1,0:T(8,128)(2,1)S(1)} %get-tuple-element.96), channel_id=1, source_target_pairs={{0,6},{1,7},{2,4},{3,5},{4,2},{5,3},{6,0},{7,1},{8,14},{9,15},{10,... | collective-permute-start | bytes 393224 | tf_op jit(solution)/shard_map/ppermute | solution.py:533

commit v5 on v4

--- a/solution.py
+++ b/solution.py
@@ -370,10 +370,8 @@
     return pl.ds(pl.multiple_of(index * width, width), width)
 
 
-def pick_kernel(me_ref, in_ref, near_ref, far_ref):
-    half, width = me_ref[1], near_ref.shape[1]
-    near_ref[...] = in_ref[:, columns(half, width)]
-    far_ref[...] = in_ref[:, columns(1 - half, width)]
+def pick_kernel(slot, me_ref, in_ref, out_ref):
+    out_ref[...] = in_ref[:, columns(me_ref[slot], out_ref.shape[1])]
 
 
 def pieces_z_kernel(beta, first, me_ref, adjoint_ref, gate_ref, *out_refs):
@@ -420,7 +418,7 @@
 
 
 def pieces_grad_w_kernel(blocks, count, me_ref, fwd_ref, inv_ref, filt_ref, *refs):
-    piece_refs, out_refs = refs[:count], refs[count : 2 * count]
+    piece_refs, out_refs = refs[:count][::-1], refs[count : 2 * count]
     whole_ref, own_ref, other_ref, joint_ref, result_ref = refs[2 * count :]
     rows = piece_refs[0].shape[0]
     size = whole_ref.shape[0] // blocks
@@ -442,7 +440,7 @@
 
 
 def pieces_long_grad_kernel(blocks, scale, count, me_ref, fwd_ref, inv_ref, grad_ref, *refs):
-    piece_refs, out_ref = refs[:count], refs[count]
+    piece_refs, out_ref = refs[:count][::-1], refs[count]
     own_ref, other_ref, joint_ref, whole_ref = refs[count + 1 :]
     rows = piece_refs[0].shape[0]
     size = whole_ref.shape[0] // blocks
@@ -461,7 +459,7 @@
 
 
 def pieces_grad_b_kernel(beta, count, me_ref, near_ref, far_ref, long_ref, mid_ref, *refs):
-    piece_refs, (grad_u_ref, grad_b_ref) = refs[:count], refs[count:]
+    piece_refs, (grad_u_ref, grad_b_ref) = refs[:count][::-1], refs[count:]
     width = piece_refs[0].shape[1]
     half = count // 2
     me = me_ref[0]
@@ -533,10 +531,11 @@
     return lax.ppermute(array, "ctx", [(i, i ^ k) for i in range(count)])
 
 
-def exchanged(pieces, step=1):
-    came = [pieces[0]] + [None] * (len(pieces) - 1)
-    for k in range(len(pieces) - 1, 0, -1):
-        came[k] = swapped(pieces[k], k * step)
+def exchanged(pieces, step=1, first=0):
+    came = list(pieces)
+    for k in range(len(pieces) - 1, -1, -1):
+        if first + k:
+            came[k] = swapped(pieces[k], (first + k) * step)
     return came
 
 
@@ -577,41 +576,50 @@
     few = 4 * tokens * channels
 
     index = lax.axis_index("ctx")
-    me = jnp.stack([index, index // half]).astype(jnp.int32)
+    me = jnp.stack([index, index // half, 1 - index // half]).astype(jnp.int32)
     inputs, gate_pre, gate_mid, gate_long, gate_out = (
         array[0] for array in (layer_input, pre_gate, mid_gate, long_gate, out_gate)
     )
     filter_taps = mid_filter[0]
 
-    near, far = local(pick_kernel, [half_shape] * 2, [me, incoming[0]], few, name="pick")
+    far = local(functools.partial(pick_kernel, 2), [half_shape], [me, incoming[0]], few, name="far")
+    far, inputs, gate_pre = lax.optimization_barrier((far, inputs, gate_pre))
+    mixed_in = local(mix_kernel, [rows_shape], [inputs, gate_pre], few, name="mix")
     far = passed_along(far, "section", -1)
+    earlier = shifted(mixed_in, "ctx", 1)
+    far, sent = lax.optimization_barrier((far, incoming[0]))
+    near = local(functools.partial(pick_kernel, 1), [half_shape], [me, sent], few, name="near")
     near = passed_along(near, "section", -1)
-    mixed_in = local(mix_kernel, [rows_shape], [inputs, gate_pre], few, name="mix")
-    earlier = shifted(mixed_in, "ctx", 1)
     far_z = local(
         functools.partial(pieces_z_kernel, beta, half), [piece] * half, [me, far, gate_out], few, name="farz"
     )
-    near_z = local(
-        functools.partial(pieces_z_kernel, beta, 0), [piece] * half, [me, near, gate_out], few, name="nearz"
-    )
+    far_z, earlier = lax.optimization_barrier((far_z, earlier))
     signal, filt, *pieces_w = local(
         functools.partial(pieces_branch_kernel, beta),
         [((span, channels), BF16)] * 2 + [piece] * devices,
         [me, fwd, inv_conv, earlier, mixed_in, filter_taps, inputs, gate_mid, gate_long], mid_flops,
         name="branch",
     )
-    pieces_z = exchanged(list(near_z) + list(far_z))
-    pieces_w = exchanged(pieces_w)
+    far_z = exchanged(far_z, first=half)
+    far_z, near, pieces_w = lax.optimization_barrier((far_z, near, pieces_w))
+    near_z = local(
+        functools.partial(pieces_z_kernel, beta, 0), [piece] * half, [me, near, gate_out], few, name="nearz"
+    )
+    far_w = exchanged(pieces_w[half:], first=half)
+    near_z = exchanged(near_z)
+    pieces_z = near_z + far_z
     *pieces_g, channel_z = local(
         functools.partial(pieces_grad_w_kernel, blocks, devices),
         [piece] * devices + [((seq_len, owned), BF16)],
-        [me, long_fwd, long_inv, long_filter[0], *pieces_z], long_flops,
+        [me, long_fwd, long_inv, long_filter[0], *pieces_z[::-1]], long_flops,
         [spectrum, spectrum, joint, staged], name="gradw",
     )
-    pieces_g = exchanged(pieces_g)
+    far_w, near_w, pieces_g = lax.optimization_barrier((far_w, pieces_w[:half], pieces_g))
+    pieces_w = exchanged(near_w) + far_w
+    pieces_g = exchanged(pieces_g)[::-1]
     long_grad = local(
         functools.partial(pieces_long_grad_kernel, blocks, scale, devices), [((owned, seq_len), BF16)],
-        [me, long_fwd, long_inv, channel_z, *pieces_w], long_flops,
+        [me, long_fwd, long_inv, channel_z, *pieces_w[::-1]], long_flops,
         [spectrum, spectrum, joint, staged], name="longgrad",
     )
     pieces_g, long_grad = lax.optimization_barrier((pieces_g, long_grad))
@@ -625,12 +633,13 @@
         mid_flops, name="taps",
     )
     sums = local(pair_kernel, [tap_piece] * half, [keep, swapped(send, 1)], few, name="pair")
-    sums = exchanged(list(sums), 2)
-    later, _ = lax.optimization_barrier((later, sums[0]))
+    sums = exchanged(list(sums), 2)[::-1]
+    later, _ = lax.optimization_barrier((later, sums[-1]))
     input_grad = local(
         functools.partial(pieces_input_grad_kernel, 512), [rows_shape],
         [fwd, inv_corr, grad_b, later, filt, grad_u, gate_pre], mid_flops, name="inputgrad",
     )
+    sums, input_grad = lax.optimization_barrier((sums, input_grad))
     mid_grad = local(functools.partial(pieces_total_kernel, scale), [tap_piece], sums, few, name="midgrad")
     return (input_grad[None], long_grad[None], mid_grad[None])
 

time: 147 us -> 137 us (0.932)
  waiting for transfers between devices: 63 us -> 49.1 us
  starting transfers between devices: 53.5 us -> 57.7 us
    ppermute x25, waiting for transfers between devices: 48.2 us -> 36.3 us  [swapped(): return lax.ppermute(array, 'ctx', [(i, i ^ k) for i in range(count)])]
    ppermute x2, starting transfers between devices: 4.53 us -> 6.76 us  [passed_along(): return lax.ppermute(value, axis, pairs)]
    ppermute x2, waiting for transfers between devices: 14.8 us -> 12.8 us  [passed_along(): return lax.ppermute(value, axis, pairs)]
    pallas_call x12 -> x13, Pallas kernels: 25.8 us -> 26.4 us  [local(): pl.pallas_call(body, in_specs=specs, out_specs=[pl.BlockSpec(memory_space...]
  transfers between devices with their start and end apart: 29 -> 29, of which waited for: 13 -> 13; matrix products, arithmetic and copies ran while one was open for 0% -> 0% of each run, Pallas kernels for 14% -> 17%
where the time goes in v5:
time: 137 us
  starting transfers between devices  57.7 us (42%)
  waiting for transfers between devices  49.1 us (36%)
  Pallas kernels  26.4 us (19%)
  local copies, waits for them, and re-layouts  2.59 us (2%)
    ppermute x25, starting transfers between devices, swapped(): return lax.ppermute(array, 'ctx', [(i, i ^ k) for i in range(count)])  46.7 us
    ppermute x25, waiting for transfers between devices, swapped(): return lax.ppermute(array, 'ctx', [(i, i ^ k) for i in range(count)])  36.3 us
    pallas_call x13, Pallas kernels, local(): pl.pallas_call(body, in_specs=specs, out_specs=[pl.BlockSpec(memory_space...  26.4 us
    ppermute x2, waiting for transfers between devices, passed_along(): return lax.ppermute(value, axis, pairs)  12.8 us
    ppermute x2, starting transfers between devices, passed_along(): return lax.ppermute(value, axis, pairs)  6.76 us
    ppermute x2, starting transfers between devices, shifted(): return lax.ppermute(array, axis, pairs)  4.16 us
  transfers between devices with their start and end apart: 29, of which 13 were waited for; matrix products, arithmetic and copies ran while one was open for 0% of the time, Pallas kernels for 17%

profile of v5, /device:TPU:0, one launch (start us, length us, event | category | flops | bytes accessed | tf_op | source)
XLA Modules:
  0.0 136.7 jit_solution(12636987917307674168)
XLA Ops:
  0.7 1.3 copy-done.3
  2.0 0.6 far.1
  2.6 1.2 copy-done.6
  4.1 2.7 %collective-permute-start.1 = (bf16[128,4096]{1,0:T(8,128)(2,1)S(1)}, bf16[128,4096]{1,0:T(8,128)(2,1)S(1)}, u32[]{:S(2)}, u32[]{:S(2)}) collective-permute-start(bf16[128,4096]{1,0:T(8,128)(2,1)S(1)} %mix.1.mixed_ref), channel_id=1, source_target_pairs={{0,1},{1,2},{2,3},{3,4},{4,5},{5,6},{6,7},{8,9},{9,10},{10,11},{11... | collective-permute-start | bytes 3145736 | tf_op jit(solution)/shard_map/ppermute | solution.py:26
  6.8 3.3 %collective-permute-start = (bf16[128,2048]{1,0:T(8,128)(2,1)S(1)}, bf16[128,2048]{1,0:T(8,128)(2,1)S(1)}, u32[]{:S(2)}, u32[]{:S(2)}) collective-permute-start(bf16[128,2048]{1,0:T(8,128)(2,1)S(1)} %far.1), channel_id=1, source_target_pairs={{0,24},{8,0},{16,8},{24,16},{1,25},{9,1},{17,9},{25,17},{2,26},{10... | collective-permute-start | bytes 1572872 | tf_op jit(solution)/shard_map/ppermute | solution.py:20
  10.2 11.5 %collective-permute-done.adjoint_ref.far_ref = bf16[128,2048]{1,0:T(8,128)(2,1)S(1)} collective-permute-done((bf16[128,2048]{1,0:T(8,128)(2,1)S(1)}, bf16[128,2048]{1,0:T(8,128)(2,1)S(1)}, u32[]{:S(2)}, u32[]{:S(2)}) %collective-permute-start) | collective-permute-done | bytes 524320 | tf_op jit(solution)/shard_map/ppermute | solution.py:20
  21.7 0.6 near.1
  22.3 3.4 %collective-permute-start.6 = (bf16[128,2048]{1,0:T(8,128)(2,1)S(1)}, bf16[128,2048]{1,0:T(8,128)(2,1)S(1)}, u32[]{:S(2)}, u32[]{:S(2)}) collective-permute-start(bf16[128,2048]{1,0:T(8,128)(2,1)S(1)} %near.1), channel_id=1, source_target_pairs={{0,24},{8,0},{16,8},{24,16},{1,25},{9,1},{17,9},{25,17},{2,26},{10... | collective-permute-start | bytes 1572872 | tf_op jit(solution)/shard_map/ppermute | solution.py:20
  25.7 0.7 farz.1
  26.4 2.9 %collective-permute-start.2 = (bf16[128,512]{1,0:T(8,128)(2,1)S(1)}, bf16[128,512]{1,0:T(8,128)(2,1)S(1)}, u32[]{:S(2)}, u32[]{:S(2)}) collective-permute-start(bf16[128,512]{1,0:T(8,128)(2,1)S(1)} %get-tuple-element.102), channel_id=1, source_target_pairs={{0,4},{1,5},{2,6},{3,7},{4,0},{5,1},{6,2},{7,3},{8,12},{9,13},{10,... | collective-permute-start | bytes 393224 | tf_op jit(solution)/shard_map/ppermute | solution.py:531
  29.3 1.3 collective-permute-start.4
  30.7 2.0 %collective-permute-start.5 = (bf16[128,512]{1,0:T(8,128)(2,1)S(1)}, bf16[128,512]{1,0:T(8,128)(2,1)S(1)}, u32[]{:S(2)}, u32[]{:S(2)}) collective-permute-start(bf16[128,512]{1,0:T(8,128)(2,1)S(1)} %get-tuple-element.105), channel_id=1, source_target_pairs={{0,7},{1,6},{2,5},{3,4},{4,3},{5,2},{6,1},{7,0},{8,15},{9,14},{10,... | collective-permute-start | bytes 393224 | tf_op jit(solution)/shard_map/ppermute | solution.py:531
  32.7 3.6 %branch.1 = (bf16[256,4096]{1,0:T(8,128)(2,1)S(1)}, bf16[256,4096]{1,0:T(8,128)(2,1)S(1)}, bf16[128,512]{1,0:T(8,128)(2,1)S(1)}, bf16[128,512]{1,0:T(8,128)(2,1)...) custom-call(s32[3]{0:T(128)S(1)} %pad_add_fusion.me_ref, ...), custom_call_target="tpu_custom_call" | custom-call | flops 1073741824 | bytes 11730956 | tf_op jit(solution)/shard_map/branch/pallas_call | solution.py:516
  36.3 1.3 collective-permute-done.6.adjoint_ref.near_ref
  37.7 7.3 %collective-permute-done.2.refs_3_ = bf16[128,512]{1,0:T(8,128)(2,1)S(1)} collective-permute-done((bf16[128,512]{1,0:T(8,128)(2,1)S(1)}, bf16[128,512]{1,0:T(8,128)(2,1)S(1)}, u32[]{:S(2)}, u32[]{:S(2)}) %collective-permute-start.2) | collective-permute-done | bytes 131104 | tf_op jit(solution)/shard_map/ppermute | solution.py:531
  44.9 1.8 %collective-permute-done.3.refs_2_ = bf16[128,512]{1,0:T(8,128)(2,1)S(1)} collective-permute-done((bf16[128,512]{1,0:T(8,128)(2,1)S(1)}, bf16[128,512]{1,0:T(8,128)(2,1)S(1)}, u32[]{:S(2)}, u32[]{:S(2)}) %collective-permute-start.3) | collective-permute-done | bytes 131104 | tf_op jit(solution)/shard_map/ppermute | solution.py:531
  46.8 0.7 nearz.1
  47.5 6.2 %collective-permute-start.11 = (bf16[128,512]{1,0:T(8,128)(2,1)S(1)}, bf16[128,512]{1,0:T(8,128)(2,1)S(1)}, u32[]{:S(2)}, u32[]{:S(2)}) collective-permute-start(bf16[128,512]{1,0:T(8,128)(2,1)S(1)} %get-tuple-element.128), channel_id=1, source_target_pairs={{0,3},{1,2},{2,1},{3,0},{4,7},{5,6},{6,5},{7,4},{8,11},{9,10},{10,... | collective-permute-start | bytes 393224 | tf_op jit(solution)/shard_map/ppermute | solution.py:531
  53.8 2.3 %collective-permute-start.7 = (bf16[128,512]{1,0:T(8,128)(2,1)S(1)}, bf16[128,512]{1,0:T(8,128)(2,1)S(1)}, u32[]{:S(2)}, u32[]{:S(2)}) collective-permute-start(bf16[128,512]{1,0:T(8,128)(2,1)S(1)} %get-tuple-element.116), channel_id=1, source_target_pairs={{0,4},{1,5},{2,6},{3,7},{4,0},{5,1},{6,2},{7,3},{8,12},{9,13},{10,... | collective-permute-start | bytes 393224 | tf_op jit(solution)/shard_map/ppermute | solution.py:531
  56.1 0.4 collective-permute-start.8
  56.5 0.9 collective-permute-done.11.refs_4_
  57.4 2.2 %collective-permute-start.9 = (bf16[128,512]{1,0:T(8,128)(2,1)S(1)}, bf16[128,512]{1,0:T(8,128)(2,1)S(1)}, u32[]{:S(2)}, u32[]{:S(2)}) collective-permute-start(bf16[128,512]{1,0:T(8,128)(2,1)S(1)} %get-tuple-element.118), channel_id=1, source_target_pairs={{0,6},{1,7},{2,4},{3,5},{4,2},{5,3},{6,0},{7,1},{8,14},{9,15},{10,... | collective-permute-start | bytes 393224 | tf_op jit(solution)/shard_map/ppermute | solution.py:531
  59.6 4.8 %collective-permute-done.12.refs_5_ = bf16[128,512]{1,0:T(8,128)(2,1)S(1)} collective-permute-done((bf16[128,512]{1,0:T(8,128)(2,1)S(1)}, bf16[128,512]{1,0:T(8,128)(2,1)S(1)}, u32[]{:S(2)}, u32[]{:S(2)}) %collective-permute-start.12) | collective-permute-done | bytes 131104 | tf_op jit(solution)/shard_map/ppermute | solution.py:531
  64.4 2.2 %collective-permute-start.10 = (bf16[128,512]{1,0:T(8,128)(2,1)S(1)}, bf16[128,512]{1,0:T(8,128)(2,1)S(1)}, u32[]{:S(2)}, u32[]{:S(2)}) collective-permute-start(bf16[128,512]{1,0:T(8,128)(2,1)S(1)} %get-tuple-element.119), channel_id=1, source_target_pairs={{0,7},{1,6},{2,5},{3,4},{4,3},{5,2},{6,1},{7,0},{8,15},{9,14},{10,... | collective-permute-start | bytes 393224 | tf_op jit(solution)/shard_map/ppermute | solution.py:531
  66.5 5.3 %gradw.1 = (bf16[128,512]{1,0:T(8,128)(2,1)S(1)}, bf16[128,512]{1,0:T(8,128)(2,1)S(1)}, bf16[128,512]{1,0:T(8,128)(2,1)S(1)}, bf16[128,512]{1,0:T(8,128)(2,1)S(1...) custom-call(s32[3]{0:T(128)S(1)} %pad_add_fusion.me_ref, ...), custom_call_target="tpu_custom_call" | custom-call | flops 3221225472 | bytes 4980748 | tf_op jit(solution)/shard_map/gradw/pallas_call | solution.py:516
  71.8 2.4 %collective-permute-done.8.refs_2_ = bf16[128,512]{1,0:T(8,128)(2,1)S(1)} collective-permute-done((bf16[128,512]{1,0:T(8,128)(2,1)S(1)}, bf16[128,512]{1,0:T(8,128)(2,1)S(1)}, u32[]{:S(2)}, u32[]{:S(2)}) %collective-permute-start.8) | collective-permute-done | bytes 131104 | tf_op jit(solution)/shard_map/ppermute | solution.py:531
  74.2 2.1 %collective-permute-start.14 = (bf16[128,512]{1,0:T(8,128)(2,1)S(1)}, bf16[128,512]{1,0:T(8,128)(2,1)S(1)}, u32[]{:S(2)}, u32[]{:S(2)}) collective-permute-start(bf16[128,512]{1,0:T(8,128)(2,1)S(1)} %get-tuple-element.140), channel_id=1, source_target_pairs={{0,7},{1,6},{2,5},{3,4},{4,3},{5,2},{6,1},{7,0},{8,15},{9,14},{10,... | collective-permute-start | bytes 393224 | tf_op jit(solution)/shard_map/ppermute | solution.py:531
  76.3 2.1 %collective-permute-start.15 = (bf16[128,512]{1,0:T(8,128)(2,1)S(1)}, bf16[128,512]{1,0:T(8,128)(2,1)S(1)}, u32[]{:S(2)}, u32[]{:S(2)}) collective-permute-start(bf16[128,512]{1,0:T(8,128)(2,1)S(1)} %get-tuple-element.141), channel_id=1, source_target_pairs={{0,6},{1,7},{2,4},{3,5},{4,2},{5,3},{6,0},{7,1},{8,14},{9,15},{10,... | collective-permute-start | bytes 393224 | tf_op jit(solution)/shard_map/ppermute | solution.py:531
  78.4 9.1 %collective-permute-start.21 = (bf16[128,512]{1,0:T(8,128)(2,1)S(1)}, bf16[128,512]{1,0:T(8,128)(2,1)S(1)}, u32[]{:S(2)}, u32[]{:S(2)}) collective-permute-start(bf16[128,512]{1,0:T(8,128)(2,1)S(1)} %get-tuple-element.153), channel_id=1, source_target_pairs={{0,3},{1,2},{2,1},{3,0},{4,7},{5,6},{6,5},{7,4},{8,11},{9,10},{10,... | collective-permute-start | bytes 393224 | tf_op jit(solution)/shard_map/ppermute | solution.py:531
  87.5 0.5 collective-permute-start.22
  88.1 4.2 %collective-permute-start.16 = (bf16[128,512]{1,0:T(8,128)(2,1)S(1)}, bf16[128,512]{1,0:T(8,128)(2,1)S(1)}, u32[]{:S(2)}, u32[]{:S(2)}) collective-permute-start(bf16[128,512]{1,0:T(8,128)(2,1)S(1)} %get-tuple-element.142), channel_id=1, source_target_pairs={{0,5},{1,4},{2,7},{3,6},{4,1},{5,0},{6,3},{7,2},{8,13},{9,12},{10,... | collective-permute-start | bytes 393224 | tf_op jit(solution)/shard_map/ppermute | solution.py:531
  92.2 3.0 %collective-permute-start.17 = (bf16[128,512]{1,0:T(8,128)(2,1)S(1)}, bf16[128,512]{1,0:T(8,128)(2,1)S(1)}, u32[]{:S(2)}, u32[]{:S(2)}) collective-permute-start(bf16[128,512]{1,0:T(8,128)(2,1)S(1)} %get-tuple-element.143), channel_id=1, source_target_pairs={{0,4},{1,5},{2,6},{3,7},{4,0},{5,1},{6,2},{7,3},{8,12},{9,13},{10,... | collective-permute-start | bytes 393224 | tf_op jit(solution)/shard_map/ppermute | solution.py:531
  95.2 1.4 %collective-permute-done.22.refs_5_ = bf16[128,512]{1,0:T(8,128)(2,1)S(1)} collective-permute-done((bf16[128,512]{1,0:T(8,128)(2,1)S(1)}, bf16[128,512]{1,0:T(8,128)(2,1)S(1)}, u32[]{:S(2)}, u32[]{:S(2)}) %collective-permute-start.22) | collective-permute-done | bytes 131104 | tf_op jit(solution)/shard_map/ppermute | solution.py:531
  97.1 6.2 %longgrad.1 = bf16[512,1024]{1,0:T(8,128)(2,1)} custom-call(s32[3]{0:T(128)S(1)} %pad_add_fusion.me_ref, bf16[512,512]{1,0:T(8,128)(2,1)S(1)} %copy-done.13, bf16[256,512]{1,0:T(8,128)(2,1)S(1)} %copy-done.14, bf16[1024,512]{1,0:T(8,128)(2,1)S(1)} %get-tuple-element.148.grad_ref, bf16[128,512]{1,0:T(8,128)(2,1)S(1)} %collective-permute-done.10.refs_0_, ...), custom_call_target="tpu_custom_call" | custom-call | flops 3221225472 | bytes 3932172 | tf_op jit(solution)/shard_map/longgrad/pallas_call | solution.py:516
  103.3 2.2 %collective-permute-done.17.refs_3_ = bf16[128,512]{1,0:T(8,128)(2,1)S(1)} collective-permute-done((bf16[128,512]{1,0:T(8,128)(2,1)S(1)}, bf16[128,512]{1,0:T(8,128)(2,1)S(1)}, u32[]{:S(2)}, u32[]{:S(2)}) %collective-permute-start.17) | collective-permute-done | bytes 131104 | tf_op jit(solution)/shard_map/ppermute | solution.py:531
  105.4 1.0 collective-permute-done.19.refs_5_
  106.4 1.1 gradb.1
  107.6 1.5 %collective-permute-start.28 = (bf16[128,4096]{1,0:T(8,128)(2,1)S(1)}, bf16[128,4096]{1,0:T(8,128)(2,1)S(1)}, u32[]{:S(2)}, u32[]{:S(2)}) collective-permute-start(bf16[128,4096]{1,0:T(8,128)(2,1)S(1)} %get-tuple-element.165.grad_b_ref), channel_id=1, source_target_pairs={{1,0},{2,1},{3,2},{4,3},{5,4},{6,5},{7,6},{9,8},{10,9},{11,10},{12... | collective-permute-start | bytes 3145736 | tf_op jit(solution)/shard_map/ppermute | solution.py:26
  109.1 3.0 %taps.1 = (bf16[4,128,512]{2,1,0:T(8,128)(2,1)S(1)}, bf16[4,128,512]{2,1,0:T(8,128)(2,1)S(1)}) custom-call(s32[3]{0:T(128)S(1)} %pad_add_fusion.me_ref, bf16[256,256]{1,0:T(8,128)(2,1)S(1)} %copy-done.9, bf16[128,256]{1,0:T(8,128)(2,1)S(1)} %copy-done.15, bf16[256,4096]{1,0:T(8,128)(2,1)S(1)} %get-tuple-element.101.signal_ref, ...), custom_call_target="tpu_custom_call" | custom-call | flops 1073741824 | bytes 4390924 | tf_op jit(solution)/shard_map/taps/pallas_call | solution.py:516
  112.0 1.2 collective-permute-start.24
  113.2 1.5 %collective-permute-done.24.came_ref = bf16[4,128,512]{2,1,0:T(8,128)(2,1)S(1)} collective-permute-done((bf16[4,128,512]{2,1,0:T(8,128)(2,1)S(1)}, bf16[4,128,512]{2,1,0:T(8,128)(2,1)S(1)}, u32[]{:S(2)}, u32[]{:S(2)}) %collective-permute-start.24) | collective-permute-done | bytes 524320 | tf_op jit(solution)/shard_map/ppermute | solution.py:531
  114.9 2.7 %collective-permute-start.25 = (bf16[128,512]{1,0:T(8,128)(2,1)S(1)}, bf16[128,512]{1,0:T(8,128)(2,1)S(1)}, u32[]{:S(2)}, u32[]{:S(2)}) collective-permute-start(bf16[128,512]{1,0:T(8,128)(2,1)S(1)} %get-tuple-element.168), channel_id=1, source_target_pairs={{0,6},{1,7},{2,4},{3,5},{4,2},{5,3},{6,0},{7,1},{8,14},{9,15},{10,... | collective-permute-start | bytes 393224 | tf_op jit(solution)/shard_map/ppermute | solution.py:531
  117.6 0.5 collective-permute-start.26
  118.0 1.3 collective-permute-start.27
  119.4 3.5 %inputgrad.1 = bf16[128,4096]{1,0:T(8,128)(2,1)} custom-call(bf16[256,256]{1,0:T(8,128)(2,1)S(1)} %copy-done.9, bf16[128,256]{1,0:T(8,128)(2,1)S(1)} %copy-done.10, bf16[128,4096]{1,0:T(8,128)(2,1)S(1)} %get-tuple-element.165.grad_b_ref, bf16[128,4096]{1,0:T(8,128)(2,1)S(1)} %collective-permute-done.28.later_ref, ...), custom_call_target="tpu_custom_call" | custom-call | flops 1073741824 | bytes 8585216 | tf_op jit(solution)/shard_map/inputgrad/pallas_call | solution.py:516
  122.9 7.8 %collective-permute-done.25.refs_0_ = bf16[128,512]{1,0:T(8,128)(2,1)S(1)} collective-permute-done((bf16[128,512]{1,0:T(8,128)(2,1)S(1)}, bf16[128,512]{1,0:T(8,128)(2,1)S(1)}, u32[]{:S(2)}, u32[]{:S(2)}) %collective-permute-start.25) | collective-permute-done | bytes 131104 | tf_op jit(solution)/shard_map/ppermute | solution.py:531
  130.7 5.2 %collective-permute-done.26.refs_1_ = bf16[128,512]{1,0:T(8,128)(2,1)S(1)} collective-permute-done((bf16[128,512]{1,0:T(8,128)(2,1)S(1)}, bf16[128,512]{1,0:T(8,128)(2,1)S(1)}, u32[]{:S(2)}, u32[]{:S(2)}) %collective-permute-start.26) | collective-permute-done | bytes 131104 | tf_op jit(solution)/shard_map/ppermute | solution.py:531
  135.9 0.7 midgrad.1
  (56 shorter events, 1.3 us)
Async XLA Ops:
  0.6 2.0 %copy-start = (bf16[1,128,4096]{2,1,0:T(8,128)(2,1)S(1)}, bf16[1,128,4096]{2,1,0:T(8,128)(2,1)}, u32[]{:S(2)}) copy-start(bf16[1,128,4096]{2,1,0:T(8,128)(2,1)} %param.15) | copy-start | bytes 3145732
  0.7 1.3 copy-start.3
  2.0 19.7 %copy-start.4 = (bf16[1,128,4096]{2,1,0:T(8,128)(2,1)S(1)}, bf16[1,128,4096]{2,1,0:T(8,128)(2,1)}, u32[]{:S(2)}) copy-start(bf16[1,128,4096]{2,1,0:T(8,128)(2,1)} %param.14) | copy-start | bytes 3145732
  2.6 1.2 copy-start.6
  3.9 21.8 %copy-start.5 = (bf16[1,128,4096]{2,1,0:T(8,128)(2,1)S(1)}, bf16[1,128,4096]{2,1,0:T(8,128)(2,1)}, u32[]{:S(2)}) copy-start(bf16[1,128,4096]{2,1,0:T(8,128)(2,1)} %param.19) | copy-start | bytes 3145732
  3.9 28.8 %copy-start.9 = (bf16[256,256]{1,0:T(8,128)(2,1)S(1)}, bf16[256,256]{1,0:T(8,128)(2,1)}, u32[]{:S(2)}) copy-start(bf16[256,256]{1,0:T(8,128)(2,1)} %constant.35.clone.fwd_ref) | copy-start | bytes 393220
  3.9 28.8 %copy-start.11 = (bf16[128,256]{1,0:T(8,128)(2,1)S(1)}, bf16[128,256]{1,0:T(8,128)(2,1)}, u32[]{:S(2)}) copy-start(bf16[128,256]{1,0:T(8,128)(2,1)} %constant.36.clone.inv_ref) | copy-start | bytes 196612
  4.1 28.6 %copy-start.1 = (bf16[1,128,4096]{2,1,0:T(8,128)(2,1)S(1)}, bf16[1,128,4096]{2,1,0:T(8,128)(2,1)}, u32[]{:S(2)}) copy-start(bf16[1,128,4096]{2,1,0:T(8,128)(2,1)} %param.18) | copy-start | bytes 3145732
  4.1 28.6 %copy-start.2 = (bf16[1,128,4096]{2,1,0:T(8,128)(2,1)S(1)}, bf16[1,128,4096]{2,1,0:T(8,128)(2,1)}, u32[]{:S(2)}) copy-start(bf16[1,128,4096]{2,1,0:T(8,128)(2,1)} %param.17) | copy-start | bytes 3145732
  4.1 28.6 %copy-start.8 = (bf16[1,128,4096]{2,1,0:T(8,128)(2,1)S(1)}, bf16[1,128,4096]{2,1,0:T(8,128)(2,1)}, u32[]{:S(2)}) copy-start(bf16[1,128,4096]{2,1,0:T(8,128)(2,1)} %param.21) | copy-start | bytes 3145732
  4.1 22.3 %collective-permute-start.1 = (bf16[128,4096]{1,0:T(8,128)(2,1)S(1)}, bf16[128,4096]{1,0:T(8,128)(2,1)S(1)}, u32[]{:S(2)}, u32[]{:S(2)}) collective-permute-start(bf16[128,4096]{1,0:T(8,128)(2,1)S(1)} %mix.1.mixed_ref), channel_id=1, source_target_pairs={{0,1},{1,2},{2,3},{3,4},{4,5},{5,6},{6,7},{8,9},{9,10},{10,11},{11... | collective-permute-start | bytes 3145736 | tf_op jit(solution)/shard_map/ppermute | solution.py:26
  6.8 14.8 %collective-permute-start = (bf16[128,2048]{1,0:T(8,128)(2,1)S(1)}, bf16[128,2048]{1,0:T(8,128)(2,1)S(1)}, u32[]{:S(2)}, u32[]{:S(2)}) collective-permute-start(bf16[128,2048]{1,0:T(8,128)(2,1)S(1)} %far.1), channel_id=1, source_target_pairs={{0,24},{8,0},{16,8},{24,16},{1,25},{9,1},{17,9},{25,17},{2,26},{10... | collective-permute-start | bytes 1572872 | tf_op jit(solution)/shard_map/ppermute | solution.py:20
  22.3 15.4 %collective-permute-start.6 = (bf16[128,2048]{1,0:T(8,128)(2,1)S(1)}, bf16[128,2048]{1,0:T(8,128)(2,1)S(1)}, u32[]{:S(2)}, u32[]{:S(2)}) collective-permute-start(bf16[128,2048]{1,0:T(8,128)(2,1)S(1)} %near.1), channel_id=1, source_target_pairs={{0,24},{8,0},{16,8},{24,16},{1,25},{9,1},{17,9},{25,17},{2,26},{10... | collective-permute-start | bytes 1572872 | tf_op jit(solution)/shard_map/ppermute | solution.py:20
  26.4 18.5 %collective-permute-start.2 = (bf16[128,512]{1,0:T(8,128)(2,1)S(1)}, bf16[128,512]{1,0:T(8,128)(2,1)S(1)}, u32[]{:S(2)}, u32[]{:S(2)}) collective-permute-start(bf16[128,512]{1,0:T(8,128)(2,1)S(1)} %get-tuple-element.102), channel_id=1, source_target_pairs={{0,4},{1,5},{2,6},{3,7},{4,0},{5,1},{6,2},{7,3},{8,12},{9,13},{10,... | collective-permute-start | bytes 393224 | tf_op jit(solution)/shard_map/ppermute | solution.py:531
  29.3 17.4 %collective-permute-start.3 = (bf16[128,512]{1,0:T(8,128)(2,1)S(1)}, bf16[128,512]{1,0:T(8,128)(2,1)S(1)}, u32[]{:S(2)}, u32[]{:S(2)}) collective-permute-start(bf16[128,512]{1,0:T(8,128)(2,1)S(1)} %get-tuple-element.103), channel_id=1, source_target_pairs={{0,5},{1,4},{2,7},{3,6},{4,1},{5,0},{6,3},{7,2},{8,13},{9,12},{10,... | collective-permute-start | bytes 393224 | tf_op jit(solution)/shard_map/ppermute | solution.py:531
  29.3 17.4 %collective-permute-start.4 = (bf16[128,512]{1,0:T(8,128)(2,1)S(1)}, bf16[128,512]{1,0:T(8,128)(2,1)S(1)}, u32[]{:S(2)}, u32[]{:S(2)}) collective-permute-start(bf16[128,512]{1,0:T(8,128)(2,1)S(1)} %get-tuple-element.104), channel_id=1, source_target_pairs={{0,6},{1,7},{2,4},{3,5},{4,2},{5,3},{6,0},{7,1},{8,14},{9,15},{10,... | collective-permute-start | bytes 393224 | tf_op jit(solution)/shard_map/ppermute | solution.py:531
  30.7 16.1 %collective-permute-start.5 = (bf16[128,512]{1,0:T(8,128)(2,1)S(1)}, bf16[128,512]{1,0:T(8,128)(2,1)S(1)}, u32[]{:S(2)}, u32[]{:S(2)}) collective-permute-start(bf16[128,512]{1,0:T(8,128)(2,1)S(1)} %get-tuple-element.105), channel_id=1, source_target_pairs={{0,7},{1,6},{2,5},{3,4},{4,3},{5,2},{6,1},{7,0},{8,15},{9,14},{10,... | collective-permute-start | bytes 393224 | tf_op jit(solution)/shard_map/ppermute | solution.py:531
  32.7 33.8 %copy-start.12 = (bf16[1,512,1024]{2,1,0:T(8,128)(2,1)S(1)}, bf16[1,512,1024]{2,1,0:T(8,128)(2,1)}, u32[]{:S(2)}) copy-start(bf16[1,512,1024]{2,1,0:T(8,128)(2,1)} %param.20) | copy-start | bytes 3145732
  32.7 33.8 %copy-start.13 = (bf16[512,512]{1,0:T(8,128)(2,1)S(1)}, bf16[512,512]{1,0:T(8,128)(2,1)}, u32[]{:S(2)}) copy-start(bf16[512,512]{1,0:T(8,128)(2,1)} %constant.39.clone.fwd_ref) | copy-start | bytes 1572868
  32.7 33.8 %copy-start.14 = (bf16[256,512]{1,0:T(8,128)(2,1)S(1)}, bf16[256,512]{1,0:T(8,128)(2,1)}, u32[]{:S(2)}) copy-start(bf16[256,512]{1,0:T(8,128)(2,1)} %constant.40.clone.inv_ref) | copy-start | bytes 786436
  47.5 10.0 %collective-permute-start.11 = (bf16[128,512]{1,0:T(8,128)(2,1)S(1)}, bf16[128,512]{1,0:T(8,128)(2,1)S(1)}, u32[]{:S(2)}, u32[]{:S(2)}) collective-permute-start(bf16[128,512]{1,0:T(8,128)(2,1)S(1)} %get-tuple-element.128), channel_id=1, source_target_pairs={{0,3},{1,2},{2,1},{3,0},{4,7},{5,6},{6,5},{7,4},{8,11},{9,10},{10,... | collective-permute-start | bytes 393224 | tf_op jit(solution)/shard_map/ppermute | solution.py:531
  53.6 10.7 %collective-permute-start.12 = (bf16[128,512]{1,0:T(8,128)(2,1)S(1)}, bf16[128,512]{1,0:T(8,128)(2,1)S(1)}, u32[]{:S(2)}, u32[]{:S(2)}) collective-permute-start(bf16[128,512]{1,0:T(8,128)(2,1)S(1)} %get-tuple-element.129), channel_id=1, source_target_pairs={{0,2},{1,3},{2,0},{3,1},{4,6},{5,7},{6,4},{7,5},{8,10},{9,11},{10,... | collective-permute-start | bytes 393224 | tf_op jit(solution)/shard_map/ppermute | solution.py:531
  53.8 12.7 %collective-permute-start.13 = (bf16[128,512]{1,0:T(8,128)(2,1)S(1)}, bf16[128,512]{1,0:T(8,128)(2,1)S(1)}, u32[]{:S(2)}, u32[]{:S(2)}) collective-permute-start(bf16[128,512]{1,0:T(8,128)(2,1)S(1)} %get-tuple-element.130), channel_id=1, source_target_pairs={{0,1},{1,0},{2,3},{3,2},{4,5},{5,4},{6,7},{7,6},{8,9},{9,8},{10,11... | collective-permute-start | bytes 393224 | tf_op jit(solution)/shard_map/ppermute | solution.py:531
  53.8 18.0 %collective-permute-start.7 = (bf16[128,512]{1,0:T(8,128)(2,1)S(1)}, bf16[128,512]{1,0:T(8,128)(2,1)S(1)}, u32[]{:S(2)}, u32[]{:S(2)}) collective-permute-start(bf16[128,512]{1,0:T(8,128)(2,1)S(1)} %get-tuple-element.116), channel_id=1, source_target_pairs={{0,4},{1,5},{2,6},{3,7},{4,0},{5,1},{6,2},{7,3},{8,12},{9,13},{10,... | collective-permute-start | bytes 393224 | tf_op jit(solution)/shard_map/ppermute | solution.py:531
  56.1 18.1 %collective-permute-start.8 = (bf16[128,512]{1,0:T(8,128)(2,1)S(1)}, bf16[128,512]{1,0:T(8,128)(2,1)S(1)}, u32[]{:S(2)}, u32[]{:S(2)}) collective-permute-start(bf16[128,512]{1,0:T(8,128)(2,1)S(1)} %get-tuple-element.117), channel_id=1, source_target_pairs={{0,5},{1,4},{2,7},{3,6},{4,1},{5,0},{6,3},{7,2},{8,13},{9,12},{10,... | collective-permute-start | bytes 393224 | tf_op jit(solution)/shard_map/ppermute | solution.py:531
  57.4 16.8 %collective-permute-start.9 = (bf16[128,512]{1,0:T(8,128)(2,1)S(1)}, bf16[128,512]{1,0:T(8,128)(2,1)S(1)}, u32[]{:S(2)}, u32[]{:S(2)}) collective-permute-start(bf16[128,512]{1,0:T(8,128)(2,1)S(1)} %get-tuple-element.118), channel_id=1, source_target_pairs={{0,6},{1,7},{2,4},{3,5},{4,2},{5,3},{6,0},{7,1},{8,14},{9,15},{10,... | collective-permute-start | bytes 393224 | tf_op jit(solution)/shard_map/ppermute | solution.py:531
  64.4 9.9 %collective-permute-start.10 = (bf16[128,512]{1,0:T(8,128)(2,1)S(1)}, bf16[128,512]{1,0:T(8,128)(2,1)S(1)}, u32[]{:S(2)}, u32[]{:S(2)}) collective-permute-start(bf16[128,512]{1,0:T(8,128)(2,1)S(1)} %get-tuple-element.119), channel_id=1, source_target_pairs={{0,7},{1,6},{2,5},{3,4},{4,3},{5,2},{6,1},{7,0},{8,15},{9,14},{10,... | collective-permute-start | bytes 393224 | tf_op jit(solution)/shard_map/ppermute | solution.py:531
  74.2 13.8 %collective-permute-start.14 = (bf16[128,512]{1,0:T(8,128)(2,1)S(1)}, bf16[128,512]{1,0:T(8,128)(2,1)S(1)}, u32[]{:S(2)}, u32[]{:S(2)}) collective-permute-start(bf16[128,512]{1,0:T(8,128)(2,1)S(1)} %get-tuple-element.140), channel_id=1, source_target_pairs={{0,7},{1,6},{2,5},{3,4},{4,3},{5,2},{6,1},{7,0},{8,15},{9,14},{10,... | collective-permute-start | bytes 393224 | tf_op jit(solution)/shard_map/ppermute | solution.py:531
  76.3 15.9 %collective-permute-start.15 = (bf16[128,512]{1,0:T(8,128)(2,1)S(1)}, bf16[128,512]{1,0:T(8,128)(2,1)S(1)}, u32[]{:S(2)}, u32[]{:S(2)}) collective-permute-start(bf16[128,512]{1,0:T(8,128)(2,1)S(1)} %get-tuple-element.141), channel_id=1, source_target_pairs={{0,6},{1,7},{2,4},{3,5},{4,2},{5,3},{6,0},{7,1},{8,14},{9,15},{10,... | collective-permute-start | bytes 393224 | tf_op jit(solution)/shard_map/ppermute | solution.py:531
  78.4 16.8 %collective-permute-start.21 = (bf16[128,512]{1,0:T(8,128)(2,1)S(1)}, bf16[128,512]{1,0:T(8,128)(2,1)S(1)}, u32[]{:S(2)}, u32[]{:S(2)}) collective-permute-start(bf16[128,512]{1,0:T(8,128)(2,1)S(1)} %get-tuple-element.153), channel_id=1, source_target_pairs={{0,3},{1,2},{2,1},{3,0},{4,7},{5,6},{6,5},{7,4},{8,11},{9,10},{10,... | collective-permute-start | bytes 393224 | tf_op jit(solution)/shard_map/ppermute | solution.py:531
  87.5 9.1 %collective-permute-start.22 = (bf16[128,512]{1,0:T(8,128)(2,1)S(1)}, bf16[128,512]{1,0:T(8,128)(2,1)S(1)}, u32[]{:S(2)}, u32[]{:S(2)}) collective-permute-start(bf16[128,512]{1,0:T(8,128)(2,1)S(1)} %get-tuple-element.154), channel_id=1, source_target_pairs={{0,2},{1,3},{2,0},{3,1},{4,6},{5,7},{6,4},{7,5},{8,10},{9,11},{10,... | collective-permute-start | bytes 393224 | tf_op jit(solution)/shard_map/ppermute | solution.py:531
  88.0 8.7 %collective-permute-start.23 = (bf16[128,512]{1,0:T(8,128)(2,1)S(1)}, bf16[128,512]{1,0:T(8,128)(2,1)S(1)}, u32[]{:S(2)}, u32[]{:S(2)}) collective-permute-start(bf16[128,512]{1,0:T(8,128)(2,1)S(1)} %get-tuple-element.155), channel_id=1, source_target_pairs={{0,1},{1,0},{2,3},{3,2},{4,5},{5,4},{6,7},{7,6},{8,9},{9,8},{10,11... | collective-permute-start | bytes 393224 | tf_op jit(solution)/shard_map/ppermute | solution.py:531
  88.1 15.2 %collective-permute-start.16 = (bf16[128,512]{1,0:T(8,128)(2,1)S(1)}, bf16[128,512]{1,0:T(8,128)(2,1)S(1)}, u32[]{:S(2)}, u32[]{:S(2)}) collective-permute-start(bf16[128,512]{1,0:T(8,128)(2,1)S(1)} %get-tuple-element.142), channel_id=1, source_target_pairs={{0,5},{1,4},{2,7},{3,6},{4,1},{5,0},{6,3},{7,2},{8,13},{9,12},{10,... | collective-permute-start | bytes 393224 | tf_op jit(solution)/shard_map/ppermute | solution.py:531
  92.2 13.2 %collective-permute-start.17 = (bf16[128,512]{1,0:T(8,128)(2,1)S(1)}, bf16[128,512]{1,0:T(8,128)(2,1)S(1)}, u32[]{:S(2)}, u32[]{:S(2)}) collective-permute-start(bf16[128,512]{1,0:T(8,128)(2,1)S(1)} %get-tuple-element.143), channel_id=1, source_target_pairs={{0,4},{1,5},{2,6},{3,7},{4,0},{5,1},{6,2},{7,3},{8,12},{9,13},{10,... | collective-permute-start | bytes 393224 | tf_op jit(solution)/shard_map/ppermute | solution.py:531
  95.2 10.2 %collective-permute-start.18 = (bf16[128,512]{1,0:T(8,128)(2,1)S(1)}, bf16[128,512]{1,0:T(8,128)(2,1)S(1)}, u32[]{:S(2)}, u32[]{:S(2)}) collective-permute-start(bf16[128,512]{1,0:T(8,128)(2,1)S(1)} %get-tuple-element.144), channel_id=1, source_target_pairs={{0,3},{1,2},{2,1},{3,0},{4,7},{5,6},{6,5},{7,4},{8,11},{9,10},{10,... | collective-permute-start | bytes 393224 | tf_op jit(solution)/shard_map/ppermute | solution.py:531
  96.6 9.8 %collective-permute-start.19 = (bf16[128,512]{1,0:T(8,128)(2,1)S(1)}, bf16[128,512]{1,0:T(8,128)(2,1)S(1)}, u32[]{:S(2)}, u32[]{:S(2)}) collective-permute-start(bf16[128,512]{1,0:T(8,128)(2,1)S(1)} %get-tuple-element.145), channel_id=1, source_target_pairs={{0,2},{1,3},{2,0},{3,1},{4,6},{5,7},{6,4},{7,5},{8,10},{9,11},{10,... | collective-permute-start | bytes 393224 | tf_op jit(solution)/shard_map/ppermute | solution.py:531
  96.7 9.7 %collective-permute-start.20 = (bf16[128,512]{1,0:T(8,128)(2,1)S(1)}, bf16[128,512]{1,0:T(8,128)(2,1)S(1)}, u32[]{:S(2)}, u32[]{:S(2)}) collective-permute-start(bf16[128,512]{1,0:T(8,128)(2,1)S(1)} %get-tuple-element.146), channel_id=1, source_target_pairs={{0,1},{1,0},{2,3},{3,2},{4,5},{5,4},{6,7},{7,6},{8,9},{9,8},{10,11... | collective-permute-start | bytes 393224 | tf_op jit(solution)/shard_map/ppermute | solution.py:531
  103.3 5.8 %copy-start.15 = (bf16[128,256]{1,0:T(8,128)(2,1)S(1)}, bf16[128,256]{1,0:T(8,128)(2,1)}, u32[]{:S(2)}) copy-start(bf16[128,256]{1,0:T(8,128)(2,1)} %constant.38.clone.inv_ref) | copy-start | bytes 196612
  107.6 11.8 %collective-permute-start.28 = (bf16[128,4096]{1,0:T(8,128)(2,1)S(1)}, bf16[128,4096]{1,0:T(8,128)(2,1)S(1)}, u32[]{:S(2)}, u32[]{:S(2)}) collective-permute-start(bf16[128,4096]{1,0:T(8,128)(2,1)S(1)} %get-tuple-element.165.grad_b_ref), channel_id=1, source_target_pairs={{1,0},{2,1},{3,2},{4,3},{5,4},{6,5},{7,6},{9,8},{10,9},{11,10},{12... | collective-permute-start | bytes 3145736 | tf_op jit(solution)/shard_map/ppermute | solution.py:26
  109.0 10.3 %copy-start.7 = (bf16[1,128,4096]{2,1,0:T(8,128)(2,1)S(1)}, bf16[1,128,4096]{2,1,0:T(8,128)(2,1)}, u32[]{:S(2)}) copy-start(bf16[1,128,4096]{2,1,0:T(8,128)(2,1)} %param.16) | copy-start | bytes 3145732
  109.1 10.3 %copy-start.10 = (bf16[128,256]{1,0:T(8,128)(2,1)S(1)}, bf16[128,256]{1,0:T(8,128)(2,1)}, u32[]{:S(2)}) copy-start(bf16[128,256]{1,0:T(8,128)(2,1)} %constant.37.clone.inv_ref) | copy-start | bytes 196612
  112.0 2.7 %collective-permute-start.24 = (bf16[4,128,512]{2,1,0:T(8,128)(2,1)S(1)}, bf16[4,128,512]{2,1,0:T(8,128)(2,1)S(1)}, u32[]{:S(2)}, u32[]{:S(2)}) collective-permute-start(bf16[4,128,512]{2,1,0:T(8,128)(2,1)S(1)} %get-tuple-element.167), channel_id=1, source_target_pairs={{0,1},{1,0},{2,3},{3,2},{4,5},{5,4},{6,7},{7,6},{8,9},{9,8},{10,11... | collective-permute-start | bytes 1572872 | tf_op jit(solution)/shard_map/ppermute | solution.py:531
  114.9 15.9 %collective-permute-start.25 = (bf16[128,512]{1,0:T(8,128)(2,1)S(1)}, bf16[128,512]{1,0:T(8,128)(2,1)S(1)}, u32[]{:S(2)}, u32[]{:S(2)}) collective-permute-start(bf16[128,512]{1,0:T(8,128)(2,1)S(1)} %get-tuple-element.168), channel_id=1, source_target_pairs={{0,6},{1,7},{2,4},{3,5},{4,2},{5,3},{6,0},{7,1},{8,14},{9,15},{10,... | collective-permute-start | bytes 393224 | tf_op jit(solution)/shard_map/ppermute | solution.py:531
  117.6 18.4 %collective-permute-start.26 = (bf16[128,512]{1,0:T(8,128)(2,1)S(1)}, bf16[128,512]{1,0:T(8,128)(2,1)S(1)}, u32[]{:S(2)}, u32[]{:S(2)}) collective-permute-start(bf16[128,512]{1,0:T(8,128)(2,1)S(1)} %get-tuple-element.169), channel_id=1, source_target_pairs={{0,4},{1,5},{2,6},{3,7},{4,0},{5,1},{6,2},{7,3},{8,12},{9,13},{10,... | collective-permute-start | bytes 393224 | tf_op jit(solution)/shard_map/ppermute | solution.py:531
  118.0 17.9 %collective-permute-start.27 = (bf16[128,512]{1,0:T(8,128)(2,1)S(1)}, bf16[128,512]{1,0:T(8,128)(2,1)S(1)}, u32[]{:S(2)}, u32[]{:S(2)}) collective-permute-start(bf16[128,512]{1,0:T(8,128)(2,1)S(1)} %get-tuple-element.170), channel_id=1, source_target_pairs={{0,2},{1,3},{2,0},{3,1},{4,6},{5,7},{6,4},{7,5},{8,10},{9,11},{10,... | collective-permute-start | bytes 393224 | tf_op jit(solution)/shard_map/ppermute | solution.py:531

commit v6 on v5

--- a/solution.py
+++ b/solution.py
@@ -370,8 +370,11 @@
     return pl.ds(pl.multiple_of(index * width, width), width)
 
 
-def pick_kernel(slot, me_ref, in_ref, out_ref):
-    out_ref[...] = in_ref[:, columns(me_ref[slot], out_ref.shape[1])]
+def pick_kernel(firsts, me_ref, in_ref, *out_refs):
+    for first, out_ref in zip(firsts, out_refs):
+        width = out_ref.shape[1]
+        owned = in_ref.shape[1] // 8
+        out_ref[...] = in_ref[:, columns((me_ref[0] ^ first) // (width // owned), width)]
 
 
 def pieces_z_kernel(beta, first, me_ref, adjoint_ref, gate_ref, *out_refs):
@@ -458,19 +461,18 @@
             out_ref[cols, p * size : (p + 1) * size] = lags.astype(BF16)
 
 
-def pieces_grad_b_kernel(beta, count, me_ref, near_ref, far_ref, long_ref, mid_ref, *refs):
+def pieces_grad_b_kernel(beta, count, me_ref, near_ref, mid_ref, far_ref, long_ref, gate_ref, *refs):
     piece_refs, (grad_u_ref, grad_b_ref) = refs[:count][::-1], refs[count:]
     width = piece_refs[0].shape[1]
-    half = count // 2
     me = me_ref[0]
     for k in range(count):
         owner = me ^ k
         cols = columns(owner, width)
-        adjoint_ref = near_ref if k < half else far_ref
-        adjoint = adjoint_ref[:, columns(owner & (half - 1), width)].astype(F32)
+        adjoint_ref = near_ref if k < 4 else mid_ref if k < 6 else far_ref
+        adjoint = adjoint_ref[:, columns(owner & (adjoint_ref.shape[1] // width - 1), width)].astype(F32)
         grad_u = adjoint + piece_refs[k][...].astype(F32) * long_ref[:, cols].astype(F32)
         grad_u_ref[:, cols] = grad_u
-        grad_b_ref[:, cols] = (beta * grad_u * mid_ref[:, cols].astype(F32)).astype(BF16)
+        grad_b_ref[:, cols] = (beta * grad_u * gate_ref[:, cols].astype(F32)).astype(BF16)
 
 
 def pieces_taps_kernel(me_ref, fwd_ref, inv_ref, signal_ref, grad_b_ref, keep_ref, send_ref):
@@ -484,16 +486,22 @@
         (send_ref if k % 2 else keep_ref)[k // 2] = part
 
 
-def pair_kernel(keep_ref, came_ref, *out_refs):
-    for m, out_ref in enumerate(out_refs):
-        out_ref[...] = (keep_ref[m].astype(F32) + came_ref[m].astype(F32)).astype(BF16)
-
-
-def pieces_total_kernel(scale, *refs):
-    total = refs[0][...].astype(F32)
-    for ref in refs[1:-1]:
-        total += ref[...].astype(F32)
-    refs[-1][...] = (total * scale).astype(BF16)
+def pair_kernel(keep_ref, came_ref, kept_ref, sent_ref):
+    for m in range(4):
+        total = keep_ref[m].astype(F32) + came_ref[m].astype(F32)
+        if m % 2:
+            sent_ref[m // 2] = total.astype(BF16)
+        else:
+            kept_ref[m // 2] = total
+
+
+def four_kernel(kept_ref, came_ref, own_ref, sent_ref):
+    own_ref[...] = kept_ref[0] + came_ref[0].astype(F32)
+    sent_ref[...] = (kept_ref[1] + came_ref[1].astype(F32)).astype(BF16)
+
+
+def last_kernel(scale, own_ref, came_ref, out_ref):
+    out_ref[...] = ((own_ref[...] + came_ref[...].astype(F32)) * scale).astype(BF16)
 
 
 def pieces_input_grad_kernel(
@@ -531,12 +539,12 @@
     return lax.ppermute(array, "ctx", [(i, i ^ k) for i in range(count)])
 
 
-def exchanged(pieces, step=1, first=0):
-    came = list(pieces)
-    for k in range(len(pieces) - 1, -1, -1):
-        if first + k:
-            came[k] = swapped(pieces[k], (first + k) * step)
-    return came
+def after(value, *others):
+    return lax.optimization_barrier((value, others))[0]
+
+
+def exchanged(pieces, first=0):
+    return [swapped(piece, first + k) if first + k else piece for k, piece in enumerate(pieces)]
 
 
 def by_permutes(
@@ -569,45 +577,51 @@
 
     rows_shape = ((tokens, channels), BF16)
     half_shape = ((tokens, channels // 2), BF16)
+    quarter_shape = ((tokens, channels // 4), BF16)
     piece = ((tokens, owned), BF16)
     tap_piece = ((taps, owned), BF16)
     mid_flops = 8 * span * tokens * channels
     long_flops = 12 * period * seq_len * owned
     few = 4 * tokens * channels
 
-    index = lax.axis_index("ctx")
-    me = jnp.stack([index, index // half, 1 - index // half]).astype(jnp.int32)
+    me = lax.axis_index("ctx").astype(jnp.int32)[None]
     inputs, gate_pre, gate_mid, gate_long, gate_out = (
         array[0] for array in (layer_input, pre_gate, mid_gate, long_gate, out_gate)
     )
     filter_taps = mid_filter[0]
 
-    far = local(functools.partial(pick_kernel, 2), [half_shape], [me, incoming[0]], few, name="far")
-    far, inputs, gate_pre = lax.optimization_barrier((far, inputs, gate_pre))
+    far = local(functools.partial(pick_kernel, (6,)), [quarter_shape], [me, incoming[0]], few, name="far")
+    far = passed_along(far, "section", -1)
     mixed_in = local(mix_kernel, [rows_shape], [inputs, gate_pre], few, name="mix")
-    far = passed_along(far, "section", -1)
     earlier = shifted(mixed_in, "ctx", 1)
-    far, sent = lax.optimization_barrier((far, incoming[0]))
-    near = local(functools.partial(pick_kernel, 1), [half_shape], [me, sent], few, name="near")
+    sent = after(incoming[0], far)
+    mid, near = local(
+        functools.partial(pick_kernel, (4, 0)), [quarter_shape, half_shape], [me, sent], few, name="near"
+    )
+    mid = passed_along(mid, "section", -1)
     near = passed_along(near, "section", -1)
     far_z = local(
-        functools.partial(pieces_z_kernel, beta, half), [piece] * half, [me, far, gate_out], few, name="farz"
-    )
-    far_z, earlier = lax.optimization_barrier((far_z, earlier))
+        functools.partial(pieces_z_kernel, beta, 6), [piece] * 2, [me, far, gate_out], few, name="farz"
+    )
+    mid = after(mid, far_z)
+    mid_z = local(
+        functools.partial(pieces_z_kernel, beta, 4), [piece] * 2, [me, mid, gate_out], few, name="midz"
+    )
     signal, filt, *pieces_w = local(
         functools.partial(pieces_branch_kernel, beta),
         [((span, channels), BF16)] * 2 + [piece] * devices,
-        [me, fwd, inv_conv, earlier, mixed_in, filter_taps, inputs, gate_mid, gate_long], mid_flops,
-        name="branch",
-    )
-    far_z = exchanged(far_z, first=half)
-    far_z, near, pieces_w = lax.optimization_barrier((far_z, near, pieces_w))
+        [me, fwd, inv_conv, after(earlier, far_z), mixed_in, filter_taps, inputs, gate_mid, gate_long],
+        mid_flops, name="branch",
+    )
+    far_z = exchanged(far_z, 6)
+    near = after(near, mid_z, pieces_w)
+    mid_z = exchanged(mid_z, 4)
     near_z = local(
         functools.partial(pieces_z_kernel, beta, 0), [piece] * half, [me, near, gate_out], few, name="nearz"
     )
-    far_w = exchanged(pieces_w[half:], first=half)
     near_z = exchanged(near_z)
-    pieces_z = near_z + far_z
+    far_w = exchanged(after(pieces_w[half:], far_z, mid_z, near_z), half)
+    pieces_z = near_z + mid_z + far_z
     *pieces_g, channel_z = local(
         functools.partial(pieces_grad_w_kernel, blocks, devices),
         [piece] * devices + [((seq_len, owned), BF16)],
@@ -625,29 +639,35 @@
     pieces_g, long_grad = lax.optimization_barrier((pieces_g, long_grad))
     grad_u, grad_b = local(
         functools.partial(pieces_grad_b_kernel, beta, devices), [((tokens, channels), F32), rows_shape],
-        [me, near, far, gate_long, gate_mid, *pieces_g], few, name="gradb",
+        [me, near, mid, far, gate_long, gate_mid, *pieces_g], few, name="gradb",
     )
     later = shifted(grad_b, "ctx", -1)
     keep, send = local(
         pieces_taps_kernel, [((half, taps, owned), BF16)] * 2, [me, fwd, inv_taps, signal, grad_b],
         mid_flops, name="taps",
     )
-    sums = local(pair_kernel, [tap_piece] * half, [keep, swapped(send, 1)], few, name="pair")
-    sums = exchanged(list(sums), 2)[::-1]
-    later, _ = lax.optimization_barrier((later, sums[-1]))
+    kept, sums = local(
+        pair_kernel, [((2, taps, owned), F32), ((2, taps, owned), BF16)], [keep, swapped(send, 1)], few,
+        name="pair",
+    )
+    own, sums = local(
+        four_kernel, [((taps, owned), F32), tap_piece], [kept, swapped(sums, 2)], few, name="four"
+    )
+    last = swapped(sums, 4)
+    later, _ = lax.optimization_barrier((later, sums))
     input_grad = local(
         functools.partial(pieces_input_grad_kernel, 512), [rows_shape],
         [fwd, inv_corr, grad_b, later, filt, grad_u, gate_pre], mid_flops, name="inputgrad",
     )
-    sums, input_grad = lax.optimization_barrier((sums, input_grad))
-    mid_grad = local(functools.partial(pieces_total_kernel, scale), [tap_piece], sums, few, name="midgrad")
+    last, input_grad = lax.optimization_barrier((last, input_grad))
+    mid_grad = local(functools.partial(last_kernel, scale), [tap_piece], [own, last], few, name="midgrad")
     return (input_grad[None], long_grad[None], mid_grad[None])
 
 
 def per_device(*arrays):
     devices = lax.axis_size("ctx")
     owned = arrays[0].shape[2] // devices
-    if owned % 128 == 0 and devices in (2, 4, 8, 16):
+    if owned % 128 == 0 and devices == 8:
         return by_permutes(*arrays)
     return by_all_to_all(*arrays)
 

time: 137 us -> 140 us (1.022)
  waiting for transfers between devices: 49.1 us -> 63 us
  starting transfers between devices: 57.7 us -> 50.5 us
  Pallas kernels: 26.4 us -> 22.8 us
    ppermute x25 -> x24, starting transfers between devices: 46.7 us -> 38.8 us  [swapped(): return lax.ppermute(array, 'ctx', [(i, i ^ k) for i in range(count)])]
    ppermute x2 -> x3, waiting for transfers between devices: 12.8 us -> 20.5 us  [passed_along(): return lax.ppermute(value, axis, pairs)]
    ppermute x25 -> x24, waiting for transfers between devices: 36.3 us -> 42.5 us  [swapped(): return lax.ppermute(array, 'ctx', [(i, i ^ k) for i in range(count)])]
    pallas_call x13 -> x15, Pallas kernels: 26.4 us -> 22.8 us  [local(): pl.pallas_call(body, in_specs=specs, out_specs=[pl.BlockSpec(memory_space...]
    ppermute x2 -> x3, starting transfers between devices: 6.76 us -> 6.82 us  [passed_along(): return lax.ppermute(value, axis, pairs)]
  transfers between devices with their start and end apart: 29 -> 29, of which waited for: 13 -> 14; matrix products, arithmetic and copies ran while one was open for 0% -> 0% of each run, Pallas kernels for 17% -> 15%
where the time goes in v6:
time: 140 us
  waiting for transfers between devices  63 us (45%)
  starting transfers between devices  50.5 us (36%)
  Pallas kernels  22.8 us (16%)
  local copies, waits for them, and re-layouts  2.52 us (2%)
    ppermute x24, waiting for transfers between devices, swapped(): return lax.ppermute(array, 'ctx', [(i, i ^ k) for i in range(count)])  42.5 us
    ppermute x24, starting transfers between devices, swapped(): return lax.ppermute(array, 'ctx', [(i, i ^ k) for i in range(count)])  38.8 us
    pallas_call x15, Pallas kernels, local(): pl.pallas_call(body, in_specs=specs, out_specs=[pl.BlockSpec(memory_space...  22.8 us
    ppermute x3, waiting for transfers between devices, passed_along(): return lax.ppermute(value, axis, pairs)  20.5 us
    ppermute x3, starting transfers between devices, passed_along(): return lax.ppermute(value, axis, pairs)  6.82 us
    ppermute x2, starting transfers between devices, shifted(): return lax.ppermute(array, axis, pairs)  4.96 us
  transfers between devices with their start and end apart: 29, of which 14 were waited for; matrix products, arithmetic and copies ran while one was open for 0% of the time, Pallas kernels for 15%

profile of v6, /device:TPU:0, one launch (start us, length us, event | category | flops | bytes accessed | tf_op | source)
XLA Modules:
  0.0 139.8 jit_solution(5492380963688791425)
XLA Ops:
  0.6 1.2 copy-done.1
  1.9 1.2 copy-done.6
  3.1 0.2 mix.1.mixed_ref
  3.3 3.5 %collective-permute-start = (bf16[128,4096]{1,0:T(8,128)(2,1)S(1)}, bf16[128,4096]{1,0:T(8,128)(2,1)}, u32[]{:S(2)}, u32[]{:S(2)}) collective-permute-start(bf16[128,4096]{1,0:T(8,128)(2,1)S(1)} %mix.1.mixed_ref), channel_id=1, source_target_pairs={{0,1},{1,2},{2,3},{3,4},{4,5},{5,6},{6,7},{8,9},{9,10},{10,11},{11... | collective-permute-start | bytes 3145736 | tf_op jit(solution)/shard_map/ppermute | solution.py:26
  6.9 3.3 %collective-permute-start.1 = (bf16[128,1024]{1,0:T(8,128)(2,1)S(1)}, bf16[128,1024]{1,0:T(8,128)(2,1)S(1)}, u32[]{:S(2)}, u32[]{:S(2)}) collective-permute-start(bf16[128,1024]{1,0:T(8,128)(2,1)S(1)} %far.1), channel_id=1, source_target_pairs={{0,24},{8,0},{16,8},{24,16},{1,25},{9,1},{17,9},{25,17},{2,26},{10... | collective-permute-start | bytes 786440 | tf_op jit(solution)/shard_map/ppermute | solution.py:20
  10.2 6.6 %collective-permute-done.1.adjoint_ref.far_ref = bf16[128,1024]{1,0:T(8,128)(2,1)S(1)} collective-permute-done((bf16[128,1024]{1,0:T(8,128)(2,1)S(1)}, bf16[128,1024]{1,0:T(8,128)(2,1)S(1)}, u32[]{:S(2)}, u32[]{:S(2)}) %collective-permute-start.1) | collective-permute-done | bytes 262176 | tf_op jit(solution)/shard_map/ppermute | solution.py:20
  16.9 3.4 %collective-permute-start.2 = (bf16[128,2048]{1,0:T(8,128)(2,1)S(1)}, bf16[128,2048]{1,0:T(8,128)(2,1)S(1)}, u32[]{:S(2)}, u32[]{:S(2)}) collective-permute-start(bf16[128,2048]{1,0:T(8,128)(2,1)S(1)} %get-tuple-element.81), channel_id=1, source_target_pairs={{0,24},{8,0},{16,8},{24,16},{1,25},{9,1},{17,9},{25,17},{2,26},{10... | collective-permute-start | bytes 1572872 | tf_op jit(solution)/shard_map/ppermute | solution.py:20
  20.5 1.2 collective-permute-start.4
  21.7 1.8 %collective-permute-start.5 = (bf16[128,512]{1,0:T(8,128)(2,1)S(1)}, bf16[128,512]{1,0:T(8,128)(2,1)S(1)}, u32[]{:S(2)}, u32[]{:S(2)}) collective-permute-start(bf16[128,512]{1,0:T(8,128)(2,1)S(1)} %get-tuple-element.77), channel_id=1, source_target_pairs={{0,7},{1,6},{2,5},{3,4},{4,3},{5,2},{6,1},{7,0},{8,15},{9,14},{10,... | collective-permute-start | bytes 393224 | tf_op jit(solution)/shard_map/ppermute | solution.py:539
  23.5 13.9 %collective-permute-done.3.adjoint_ref.mid_ref = bf16[128,1024]{1,0:T(8,128)(2,1)S(1)} collective-permute-done((bf16[128,1024]{1,0:T(8,128)(2,1)S(1)}, bf16[128,1024]{1,0:T(8,128)(2,1)S(1)}, u32[]{:S(2)}, u32[]{:S(2)}) %collective-permute-start.3) | collective-permute-done | bytes 262176 | tf_op jit(solution)/shard_map/ppermute | solution.py:20
  37.5 1.7 %collective-permute-start.6 = (bf16[128,512]{1,0:T(8,128)(2,1)S(1)}, bf16[128,512]{1,0:T(8,128)(2,1)S(1)}, u32[]{:S(2)}, u32[]{:S(2)}) collective-permute-start(bf16[128,512]{1,0:T(8,128)(2,1)S(1)} %get-tuple-element.84), channel_id=1, source_target_pairs={{0,4},{1,5},{2,6},{3,7},{4,0},{5,1},{6,2},{7,3},{8,12},{9,13},{10,... | collective-permute-start | bytes 393224 | tf_op jit(solution)/shard_map/ppermute | solution.py:539
  39.3 4.4 %branch.1 = (bf16[256,4096]{1,0:T(8,128)(2,1)S(1)}, bf16[256,4096]{1,0:T(8,128)(2,1)S(1)}, bf16[128,512]{1,0:T(8,128)(2,1)S(1)}, bf16[128,512]{1,0:T(8,128)(2,1)...) custom-call(s32[1]{0:T(128)} %bitcast.me_ref, ...), custom_call_target="tpu_custom_call" | custom-call | flops 1073741824 | bytes 11730948 | tf_op jit(solution)/shard_map/branch/pallas_call | solution.py:524
  43.7 0.2 nearz.1
  43.9 1.4 %collective-permute-start.8 = (bf16[128,512]{1,0:T(8,128)(2,1)S(1)}, bf16[128,512]{1,0:T(8,128)(2,1)S(1)}, u32[]{:S(2)}, u32[]{:S(2)}) collective-permute-start(bf16[128,512]{1,0:T(8,128)(2,1)S(1)} %get-tuple-element.96), channel_id=1, source_target_pairs={{0,1},{1,0},{2,3},{3,2},{4,5},{5,4},{6,7},{7,6},{8,9},{9,8},{10,11... | collective-permute-start | bytes 393224 | tf_op jit(solution)/shard_map/ppermute | solution.py:539
  45.3 0.6 collective-permute-start.9
  45.9 0.8 collective-permute-start.10
  46.7 2.8 %collective-permute-done.6.refs_3_ = bf16[128,512]{1,0:T(8,128)(2,1)S(1)} collective-permute-done((bf16[128,512]{1,0:T(8,128)(2,1)S(1)}, bf16[128,512]{1,0:T(8,128)(2,1)S(1)}, u32[]{:S(2)}, u32[]{:S(2)}) %collective-permute-start.6) | collective-permute-done | bytes 131104 | tf_op jit(solution)/shard_map/ppermute | solution.py:539
  49.5 1.5 %collective-permute-done.7.refs_2_ = bf16[128,512]{1,0:T(8,128)(2,1)S(1)} collective-permute-done((bf16[128,512]{1,0:T(8,128)(2,1)S(1)}, bf16[128,512]{1,0:T(8,128)(2,1)S(1)}, u32[]{:S(2)}, u32[]{:S(2)}) %collective-permute-start.7) | collective-permute-done | bytes 131104 | tf_op jit(solution)/shard_map/ppermute | solution.py:539
  51.0 3.5 %collective-permute-done.9.refs_5_ = bf16[128,512]{1,0:T(8,128)(2,1)S(1)} collective-permute-done((bf16[128,512]{1,0:T(8,128)(2,1)S(1)}, bf16[128,512]{1,0:T(8,128)(2,1)S(1)}, u32[]{:S(2)}, u32[]{:S(2)}) %collective-permute-start.9) | collective-permute-done | bytes 131104 | tf_op jit(solution)/shard_map/ppermute | solution.py:539
  54.5 2.6 %collective-permute-done.10.refs_4_ = bf16[128,512]{1,0:T(8,128)(2,1)S(1)} collective-permute-done((bf16[128,512]{1,0:T(8,128)(2,1)S(1)}, bf16[128,512]{1,0:T(8,128)(2,1)S(1)}, u32[]{:S(2)}, u32[]{:S(2)}) %collective-permute-start.10) | collective-permute-done | bytes 131104 | tf_op jit(solution)/shard_map/ppermute | solution.py:539
  57.1 2.4 %collective-permute-start.12 = (bf16[128,512]{1,0:T(8,128)(2,1)S(1)}, bf16[128,512]{1,0:T(8,128)(2,1)S(1)}, u32[]{:S(2)}, u32[]{:S(2)}) collective-permute-start(bf16[128,512]{1,0:T(8,128)(2,1)S(1)} %get-tuple-element.100), channel_id=1, source_target_pairs={{0,5},{1,4},{2,7},{3,6},{4,1},{5,0},{6,3},{7,2},{8,13},{9,12},{10,... | collective-permute-start | bytes 393224 | tf_op jit(solution)/shard_map/ppermute | solution.py:539
  59.5 0.8 collective-permute-start.13
  60.3 3.0 %collective-permute-start.14 = (bf16[128,512]{1,0:T(8,128)(2,1)S(1)}, bf16[128,512]{1,0:T(8,128)(2,1)S(1)}, u32[]{:S(2)}, u32[]{:S(2)}) collective-permute-start(bf16[128,512]{1,0:T(8,128)(2,1)S(1)} %get-tuple-element.102), channel_id=1, source_target_pairs={{0,7},{1,6},{2,5},{3,4},{4,3},{5,2},{6,1},{7,0},{8,15},{9,14},{10,... | collective-permute-start | bytes 393224 | tf_op jit(solution)/shard_map/ppermute | solution.py:539
  63.3 4.7 %gradw.1 = (bf16[128,512]{1,0:T(8,128)(2,1)S(1)}, bf16[128,512]{1,0:T(8,128)(2,1)S(1)}, bf16[128,512]{1,0:T(8,128)(2,1)S(1)}, bf16[128,512]{1,0:T(8,128)(2,1)S(1...) custom-call(s32[1]{0:T(128)} %bitcast.me_ref, ...), custom_call_target="tpu_custom_call" | custom-call | flops 3221225472 | bytes 4980740 | tf_op jit(solution)/shard_map/gradw/pallas_call | solution.py:524
  68.1 5.8 %collective-permute-done.11.refs_3_ = bf16[128,512]{1,0:T(8,128)(2,1)S(1)} collective-permute-done((bf16[128,512]{1,0:T(8,128)(2,1)S(1)}, bf16[128,512]{1,0:T(8,128)(2,1)S(1)}, u32[]{:S(2)}, u32[]{:S(2)}) %collective-permute-start.11) | collective-permute-done | bytes 131104 | tf_op jit(solution)/shard_map/ppermute | solution.py:539
  73.8 2.6 %collective-permute-done.12.refs_2_ = bf16[128,512]{1,0:T(8,128)(2,1)S(1)} collective-permute-done((bf16[128,512]{1,0:T(8,128)(2,1)S(1)}, bf16[128,512]{1,0:T(8,128)(2,1)S(1)}, u32[]{:S(2)}, u32[]{:S(2)}) %collective-permute-start.12) | collective-permute-done | bytes 131104 | tf_op jit(solution)/shard_map/ppermute | solution.py:539
  76.5 1.8 %collective-permute-start.15 = (bf16[128,512]{1,0:T(8,128)(2,1)S(1)}, bf16[128,512]{1,0:T(8,128)(2,1)S(1)}, u32[]{:S(2)}, u32[]{:S(2)}) collective-permute-start(bf16[128,512]{1,0:T(8,128)(2,1)S(1)} %get-tuple-element.111), channel_id=1, source_target_pairs={{0,7},{1,6},{2,5},{3,4},{4,3},{5,2},{6,1},{7,0},{8,15},{9,14},{10,... | collective-permute-start | bytes 393224 | tf_op jit(solution)/shard_map/ppermute | solution.py:539
  78.2 1.8 %collective-permute-start.16 = (bf16[128,512]{1,0:T(8,128)(2,1)S(1)}, bf16[128,512]{1,0:T(8,128)(2,1)S(1)}, u32[]{:S(2)}, u32[]{:S(2)}) collective-permute-start(bf16[128,512]{1,0:T(8,128)(2,1)S(1)} %get-tuple-element.112), channel_id=1, source_target_pairs={{0,6},{1,7},{2,4},{3,5},{4,2},{5,3},{6,0},{7,1},{8,14},{9,15},{10,... | collective-permute-start | bytes 393224 | tf_op jit(solution)/shard_map/ppermute | solution.py:539
  80.0 9.7 %collective-permute-start.22 = (bf16[128,512]{1,0:T(8,128)(2,1)S(1)}, bf16[128,512]{1,0:T(8,128)(2,1)S(1)}, u32[]{:S(2)}, u32[]{:S(2)}) collective-permute-start(bf16[128,512]{1,0:T(8,128)(2,1)S(1)} %get-tuple-element.124), channel_id=1, source_target_pairs={{0,3},{1,2},{2,1},{3,0},{4,7},{5,6},{6,5},{7,4},{8,11},{9,10},{10,... | collective-permute-start | bytes 393224 | tf_op jit(solution)/shard_map/ppermute | solution.py:539
  89.8 0.3 collective-permute-start.23
  90.1 4.0 %collective-permute-start.17 = (bf16[128,512]{1,0:T(8,128)(2,1)S(1)}, bf16[128,512]{1,0:T(8,128)(2,1)S(1)}, u32[]{:S(2)}, u32[]{:S(2)}) collective-permute-start(bf16[128,512]{1,0:T(8,128)(2,1)S(1)} %get-tuple-element.113), channel_id=1, source_target_pairs={{0,5},{1,4},{2,7},{3,6},{4,1},{5,0},{6,3},{7,2},{8,13},{9,12},{10,... | collective-permute-start | bytes 393224 | tf_op jit(solution)/shard_map/ppermute | solution.py:539
  94.2 2.8 %collective-permute-start.18 = (bf16[128,512]{1,0:T(8,128)(2,1)S(1)}, bf16[128,512]{1,0:T(8,128)(2,1)S(1)}, u32[]{:S(2)}, u32[]{:S(2)}) collective-permute-start(bf16[128,512]{1,0:T(8,128)(2,1)S(1)} %get-tuple-element.114), channel_id=1, source_target_pairs={{0,4},{1,5},{2,6},{3,7},{4,0},{5,1},{6,2},{7,3},{8,12},{9,13},{10,... | collective-permute-start | bytes 393224 | tf_op jit(solution)/shard_map/ppermute | solution.py:539
  96.9 1.7 %collective-permute-done.23.refs_5_ = bf16[128,512]{1,0:T(8,128)(2,1)S(1)} collective-permute-done((bf16[128,512]{1,0:T(8,128)(2,1)S(1)}, bf16[128,512]{1,0:T(8,128)(2,1)S(1)}, u32[]{:S(2)}, u32[]{:S(2)}) %collective-permute-start.23) | collective-permute-done | bytes 131104 | tf_op jit(solution)/shard_map/ppermute | solution.py:539
  98.6 0.3 collective-permute-start.20
  98.9 5.7 %longgrad.1 = bf16[512,1024]{1,0:T(8,128)(2,1)} custom-call(s32[1]{0:T(128)} %bitcast.me_ref, bf16[512,512]{1,0:T(8,128)(2,1)S(1)} %copy-done.13, bf16[256,512]{1,0:T(8,128)(2,1)S(1)} %copy-done.14, bf16[1024,512]{1,0:T(8,128)(2,1)S(1)} %get-tuple-element.119.grad_ref, bf16[128,512]{1,0:T(8,128)(2,1)S(1)} %collective-permute-done.14.refs_0_, ...), custom_call_target="tpu_custom_call" | custom-call | flops 3221225472 | bytes 3932164 | tf_op jit(solution)/shard_map/longgrad/pallas_call | solution.py:524
  104.6 3.1 %collective-permute-done.18.refs_3_ = bf16[128,512]{1,0:T(8,128)(2,1)S(1)} collective-permute-done((bf16[128,512]{1,0:T(8,128)(2,1)S(1)}, bf16[128,512]{1,0:T(8,128)(2,1)S(1)}, u32[]{:S(2)}, u32[]{:S(2)}) %collective-permute-start.18) | collective-permute-done | bytes 131104 | tf_op jit(solution)/shard_map/ppermute | solution.py:539
  107.7 1.0 collective-permute-done.20.refs_5_
  108.7 0.6 gradb.1
  109.3 1.5 %collective-permute-start.28 = (bf16[128,4096]{1,0:T(8,128)(2,1)S(1)}, bf16[128,4096]{1,0:T(8,128)(2,1)S(1)}, u32[]{:S(2)}, u32[]{:S(2)}) collective-permute-start(bf16[128,4096]{1,0:T(8,128)(2,1)S(1)} %get-tuple-element.136.grad_b_ref), channel_id=1, source_target_pairs={{1,0},{2,1},{3,2},{4,3},{5,4},{6,5},{7,6},{9,8},{10,9},{11,10},{12... | collective-permute-start | bytes 3145736 | tf_op jit(solution)/shard_map/ppermute | solution.py:26
  110.8 2.4 %taps.1 = (bf16[4,128,512]{2,1,0:T(8,128)(2,1)S(1)}, bf16[4,128,512]{2,1,0:T(8,128)(2,1)S(1)}) custom-call(s32[1]{0:T(128)} %bitcast.me_ref, bf16[256,256]{1,0:T(8,128)(2,1)S(1)} %copy-done.9, bf16[128,256]{1,0:T(8,128)(2,1)S(1)} %copy-done.15, bf16[256,4096]{1,0:T(8,128)(2,1)S(1)} %get-tuple-element.79.signal_ref, ...), custom_call_target="tpu_custom_call" | custom-call | flops 1073741824 | bytes 4390916 | tf_op jit(solution)/shard_map/taps/pallas_call | solution.py:524
  113.2 1.2 collective-permute-start.25
  114.4 1.5 %collective-permute-done.25.came_ref = bf16[4,128,512]{2,1,0:T(8,128)(2,1)S(1)} collective-permute-done((bf16[4,128,512]{2,1,0:T(8,128)(2,1)S(1)}, bf16[4,128,512]{2,1,0:T(8,128)(2,1)S(1)}, u32[]{:S(2)}, u32[]{:S(2)}) %collective-permute-start.25) | collective-permute-done | bytes 524320 | tf_op jit(solution)/shard_map/ppermute | solution.py:539
  116.1 1.7 %collective-permute-start.26 = (bf16[2,128,512]{2,1,0:T(8,128)(2,1)S(1)}, bf16[2,128,512]{2,1,0:T(8,128)(2,1)S(1)}, u32[]{:S(2)}, u32[]{:S(2)}) collective-permute-start(bf16[2,128,512]{2,1,0:T(8,128)(2,1)S(1)} %get-tuple-element.140), channel_id=1, source_target_pairs={{0,2},{1,3},{2,0},{3,1},{4,6},{5,7},{6,4},{7,5},{8,10},{9,11},{10,... | collective-permute-start | bytes 786440 | tf_op jit(solution)/shard_map/ppermute | solution.py:539
  117.7 15.0 %collective-permute-done.26.came_ref = bf16[2,128,512]{2,1,0:T(8,128)(2,1)S(1)} collective-permute-done((bf16[2,128,512]{2,1,0:T(8,128)(2,1)S(1)}, bf16[2,128,512]{2,1,0:T(8,128)(2,1)S(1)}, u32[]{:S(2)}, u32[]{:S(2)}) %collective-permute-start.26) | collective-permute-done | bytes 262176 | tf_op jit(solution)/shard_map/ppermute | solution.py:539
  132.8 1.3 collective-permute-start.27
  134.1 3.5 %inputgrad.1 = bf16[128,4096]{1,0:T(8,128)(2,1)} custom-call(bf16[256,256]{1,0:T(8,128)(2,1)S(1)} %copy-done.9, bf16[128,256]{1,0:T(8,128)(2,1)S(1)} %copy-done.10, bf16[128,4096]{1,0:T(8,128)(2,1)S(1)} %get-tuple-element.136.grad_b_ref, bf16[128,4096]{1,0:T(8,128)(2,1)S(1)} %collective-permute-done.28.later_ref, ...), custom_call_target="tpu_custom_call" | custom-call | flops 1073741824 | bytes 8585216 | tf_op jit(solution)/shard_map/inputgrad/pallas_call | solution.py:524
  137.6 1.5 %collective-permute-done.27.came_ref = bf16[128,512]{1,0:T(8,128)(2,1)S(1)} collective-permute-done((bf16[128,512]{1,0:T(8,128)(2,1)S(1)}, bf16[128,512]{1,0:T(8,128)(2,1)S(1)}, u32[]{:S(2)}, u32[]{:S(2)}) %collective-permute-start.27) | collective-permute-done | bytes 131104 | tf_op jit(solution)/shard_map/ppermute | solution.py:539
  139.1 0.7 midgrad.1
  (57 shorter events, 0.7 us)
Async XLA Ops:
  0.6 1.2 copy-start.1
  1.9 1.2 copy-start.6
  3.1 3.7 %copy-start.5 = (bf16[1,128,4096]{2,1,0:T(8,128)(2,1)S(1)}, bf16[1,128,4096]{2,1,0:T(8,128)(2,1)}, u32[]{:S(2)}) copy-start(bf16[1,128,4096]{2,1,0:T(8,128)(2,1)} %param.14) | copy-start | bytes 3145732
  3.1 17.3 %copy-start = (bf16[1,128,4096]{2,1,0:T(8,128)(2,1)S(1)}, bf16[1,128,4096]{2,1,0:T(8,128)(2,1)}, u32[]{:S(2)}) copy-start(bf16[1,128,4096]{2,1,0:T(8,128)(2,1)} %param.19) | copy-start | bytes 3145732
  3.3 35.9 %collective-permute-start = (bf16[128,4096]{1,0:T(8,128)(2,1)S(1)}, bf16[128,4096]{1,0:T(8,128)(2,1)}, u32[]{:S(2)}, u32[]{:S(2)}) collective-permute-start(bf16[128,4096]{1,0:T(8,128)(2,1)S(1)} %mix.1.mixed_ref), channel_id=1, source_target_pairs={{0,1},{1,2},{2,3},{3,4},{4,5},{5,6},{6,7},{8,9},{9,10},{10,11},{11... | collective-permute-start | bytes 3145736 | tf_op jit(solution)/shard_map/ppermute | solution.py:26
  6.8 32.4 %copy-start.8 = (bf16[1,128,4096]{2,1,0:T(8,128)(2,1)S(1)}, bf16[1,128,4096]{2,1,0:T(8,128)(2,1)}, u32[]{:S(2)}) copy-start(bf16[1,128,4096]{2,1,0:T(8,128)(2,1)} %param.21) | copy-start | bytes 3145732
  6.8 32.4 %copy-start.2 = (bf16[1,128,4096]{2,1,0:T(8,128)(2,1)S(1)}, bf16[1,128,4096]{2,1,0:T(8,128)(2,1)}, u32[]{:S(2)}) copy-start(bf16[1,128,4096]{2,1,0:T(8,128)(2,1)} %param.15) | copy-start | bytes 3145732
  6.9 32.4 %copy-start.3 = (bf16[1,128,4096]{2,1,0:T(8,128)(2,1)S(1)}, bf16[1,128,4096]{2,1,0:T(8,128)(2,1)}, u32[]{:S(2)}) copy-start(bf16[1,128,4096]{2,1,0:T(8,128)(2,1)} %param.18) | copy-start | bytes 3145732
  6.9 32.4 %copy-start.4 = (bf16[1,128,4096]{2,1,0:T(8,128)(2,1)S(1)}, bf16[1,128,4096]{2,1,0:T(8,128)(2,1)}, u32[]{:S(2)}) copy-start(bf16[1,128,4096]{2,1,0:T(8,128)(2,1)} %param.17) | copy-start | bytes 3145732
  6.9 32.4 %copy-start.9 = (bf16[256,256]{1,0:T(8,128)(2,1)S(1)}, bf16[256,256]{1,0:T(8,128)(2,1)}, u32[]{:S(2)}) copy-start(bf16[256,256]{1,0:T(8,128)(2,1)} %constant.16.clone.fwd_ref) | copy-start | bytes 393220
  6.9 32.4 %copy-start.11 = (bf16[128,256]{1,0:T(8,128)(2,1)S(1)}, bf16[128,256]{1,0:T(8,128)(2,1)}, u32[]{:S(2)}) copy-start(bf16[128,256]{1,0:T(8,128)(2,1)} %constant.17.clone.inv_ref) | copy-start | bytes 196612
  6.9 10.0 %collective-permute-start.1 = (bf16[128,1024]{1,0:T(8,128)(2,1)S(1)}, bf16[128,1024]{1,0:T(8,128)(2,1)S(1)}, u32[]{:S(2)}, u32[]{:S(2)}) collective-permute-start(bf16[128,1024]{1,0:T(8,128)(2,1)S(1)} %far.1), channel_id=1, source_target_pairs={{0,24},{8,0},{16,8},{24,16},{1,25},{9,1},{17,9},{25,17},{2,26},{10... | collective-permute-start | bytes 786440 | tf_op jit(solution)/shard_map/ppermute | solution.py:20
  16.9 26.8 %collective-permute-start.2 = (bf16[128,2048]{1,0:T(8,128)(2,1)S(1)}, bf16[128,2048]{1,0:T(8,128)(2,1)S(1)}, u32[]{:S(2)}, u32[]{:S(2)}) collective-permute-start(bf16[128,2048]{1,0:T(8,128)(2,1)S(1)} %get-tuple-element.81), channel_id=1, source_target_pairs={{0,24},{8,0},{16,8},{24,16},{1,25},{9,1},{17,9},{25,17},{2,26},{10... | collective-permute-start | bytes 1572872 | tf_op jit(solution)/shard_map/ppermute | solution.py:20
  20.4 17.0 %collective-permute-start.3 = (bf16[128,1024]{1,0:T(8,128)(2,1)S(1)}, bf16[128,1024]{1,0:T(8,128)(2,1)S(1)}, u32[]{:S(2)}, u32[]{:S(2)}) collective-permute-start(bf16[128,1024]{1,0:T(8,128)(2,1)S(1)} %get-tuple-element.82), channel_id=1, source_target_pairs={{0,24},{8,0},{16,8},{24,16},{1,25},{9,1},{17,9},{25,17},{2,26},{10... | collective-permute-start | bytes 786440 | tf_op jit(solution)/shard_map/ppermute | solution.py:20
  20.5 24.8 %collective-permute-start.4 = (bf16[128,512]{1,0:T(8,128)(2,1)S(1)}, bf16[128,512]{1,0:T(8,128)(2,1)S(1)}, u32[]{:S(2)}, u32[]{:S(2)}) collective-permute-start(bf16[128,512]{1,0:T(8,128)(2,1)S(1)} %get-tuple-element.76), channel_id=1, source_target_pairs={{0,6},{1,7},{2,4},{3,5},{4,2},{5,3},{6,0},{7,1},{8,14},{9,15},{10,... | collective-permute-start | bytes 393224 | tf_op jit(solution)/shard_map/ppermute | solution.py:539
  21.7 24.2 %collective-permute-start.5 = (bf16[128,512]{1,0:T(8,128)(2,1)S(1)}, bf16[128,512]{1,0:T(8,128)(2,1)S(1)}, u32[]{:S(2)}, u32[]{:S(2)}) collective-permute-start(bf16[128,512]{1,0:T(8,128)(2,1)S(1)} %get-tuple-element.77), channel_id=1, source_target_pairs={{0,7},{1,6},{2,5},{3,4},{4,3},{5,2},{6,1},{7,0},{8,15},{9,14},{10,... | collective-permute-start | bytes 393224 | tf_op jit(solution)/shard_map/ppermute | solution.py:539
  37.5 12.1 %collective-permute-start.6 = (bf16[128,512]{1,0:T(8,128)(2,1)S(1)}, bf16[128,512]{1,0:T(8,128)(2,1)S(1)}, u32[]{:S(2)}, u32[]{:S(2)}) collective-permute-start(bf16[128,512]{1,0:T(8,128)(2,1)S(1)} %get-tuple-element.84), channel_id=1, source_target_pairs={{0,4},{1,5},{2,6},{3,7},{4,0},{5,1},{6,2},{7,3},{8,12},{9,13},{10,... | collective-permute-start | bytes 393224 | tf_op jit(solution)/shard_map/ppermute | solution.py:539
  39.2 11.8 %collective-permute-start.7 = (bf16[128,512]{1,0:T(8,128)(2,1)S(1)}, bf16[128,512]{1,0:T(8,128)(2,1)S(1)}, u32[]{:S(2)}, u32[]{:S(2)}) collective-permute-start(bf16[128,512]{1,0:T(8,128)(2,1)S(1)} %get-tuple-element.85), channel_id=1, source_target_pairs={{0,5},{1,4},{2,7},{3,6},{4,1},{5,0},{6,3},{7,2},{8,13},{9,12},{10,... | collective-permute-start | bytes 393224 | tf_op jit(solution)/shard_map/ppermute | solution.py:539
  39.3 24.1 %copy-start.12 = (bf16[1,512,1024]{2,1,0:T(8,128)(2,1)S(1)}, bf16[1,512,1024]{2,1,0:T(8,128)(2,1)}, u32[]{:S(2)}) copy-start(bf16[1,512,1024]{2,1,0:T(8,128)(2,1)} %param.20) | copy-start | bytes 3145732
  39.3 24.1 %copy-start.13 = (bf16[512,512]{1,0:T(8,128)(2,1)S(1)}, bf16[512,512]{1,0:T(8,128)(2,1)}, u32[]{:S(2)}) copy-start(bf16[512,512]{1,0:T(8,128)(2,1)} %constant.20.clone.fwd_ref) | copy-start | bytes 1572868
  39.3 24.1 %copy-start.14 = (bf16[256,512]{1,0:T(8,128)(2,1)S(1)}, bf16[256,512]{1,0:T(8,128)(2,1)}, u32[]{:S(2)}) copy-start(bf16[256,512]{1,0:T(8,128)(2,1)} %constant.21.clone.inv_ref) | copy-start | bytes 786436
  43.9 7.1 %collective-permute-start.8 = (bf16[128,512]{1,0:T(8,128)(2,1)S(1)}, bf16[128,512]{1,0:T(8,128)(2,1)S(1)}, u32[]{:S(2)}, u32[]{:S(2)}) collective-permute-start(bf16[128,512]{1,0:T(8,128)(2,1)S(1)} %get-tuple-element.96), channel_id=1, source_target_pairs={{0,1},{1,0},{2,3},{3,2},{4,5},{5,4},{6,7},{7,6},{8,9},{9,8},{10,11... | collective-permute-start | bytes 393224 | tf_op jit(solution)/shard_map/ppermute | solution.py:539
  45.3 9.2 %collective-permute-start.9 = (bf16[128,512]{1,0:T(8,128)(2,1)S(1)}, bf16[128,512]{1,0:T(8,128)(2,1)S(1)}, u32[]{:S(2)}, u32[]{:S(2)}) collective-permute-start(bf16[128,512]{1,0:T(8,128)(2,1)S(1)} %get-tuple-element.97), channel_id=1, source_target_pairs={{0,2},{1,3},{2,0},{3,1},{4,6},{5,7},{6,4},{7,5},{8,10},{9,11},{10,... | collective-permute-start | bytes 393224 | tf_op jit(solution)/shard_map/ppermute | solution.py:539
  45.9 11.1 %collective-permute-start.10 = (bf16[128,512]{1,0:T(8,128)(2,1)S(1)}, bf16[128,512]{1,0:T(8,128)(2,1)S(1)}, u32[]{:S(2)}, u32[]{:S(2)}) collective-permute-start(bf16[128,512]{1,0:T(8,128)(2,1)S(1)} %get-tuple-element.98), channel_id=1, source_target_pairs={{0,3},{1,2},{2,1},{3,0},{4,7},{5,6},{6,5},{7,4},{8,11},{9,10},{10,... | collective-permute-start | bytes 393224 | tf_op jit(solution)/shard_map/ppermute | solution.py:539
  57.1 16.7 %collective-permute-start.11 = (bf16[128,512]{1,0:T(8,128)(2,1)S(1)}, bf16[128,512]{1,0:T(8,128)(2,1)S(1)}, u32[]{:S(2)}, u32[]{:S(2)}) collective-permute-start(bf16[128,512]{1,0:T(8,128)(2,1)S(1)} %get-tuple-element.99), channel_id=1, source_target_pairs={{0,4},{1,5},{2,6},{3,7},{4,0},{5,1},{6,2},{7,3},{8,12},{9,13},{10,... | collective-permute-start | bytes 393224 | tf_op jit(solution)/shard_map/ppermute | solution.py:539
  57.1 19.4 %collective-permute-start.12 = (bf16[128,512]{1,0:T(8,128)(2,1)S(1)}, bf16[128,512]{1,0:T(8,128)(2,1)S(1)}, u32[]{:S(2)}, u32[]{:S(2)}) collective-permute-start(bf16[128,512]{1,0:T(8,128)(2,1)S(1)} %get-tuple-element.100), channel_id=1, source_target_pairs={{0,5},{1,4},{2,7},{3,6},{4,1},{5,0},{6,3},{7,2},{8,13},{9,12},{10,... | collective-permute-start | bytes 393224 | tf_op jit(solution)/shard_map/ppermute | solution.py:539
  59.5 17.0 %collective-permute-start.13 = (bf16[128,512]{1,0:T(8,128)(2,1)S(1)}, bf16[128,512]{1,0:T(8,128)(2,1)S(1)}, u32[]{:S(2)}, u32[]{:S(2)}) collective-permute-start(bf16[128,512]{1,0:T(8,128)(2,1)S(1)} %get-tuple-element.101), channel_id=1, source_target_pairs={{0,6},{1,7},{2,4},{3,5},{4,2},{5,3},{6,0},{7,1},{8,14},{9,15},{10,... | collective-permute-start | bytes 393224 | tf_op jit(solution)/shard_map/ppermute | solution.py:539
  60.3 16.2 %collective-permute-start.14 = (bf16[128,512]{1,0:T(8,128)(2,1)S(1)}, bf16[128,512]{1,0:T(8,128)(2,1)S(1)}, u32[]{:S(2)}, u32[]{:S(2)}) collective-permute-start(bf16[128,512]{1,0:T(8,128)(2,1)S(1)} %get-tuple-element.102), channel_id=1, source_target_pairs={{0,7},{1,6},{2,5},{3,4},{4,3},{5,2},{6,1},{7,0},{8,15},{9,14},{10,... | collective-permute-start | bytes 393224 | tf_op jit(solution)/shard_map/ppermute | solution.py:539
  76.5 13.7 %collective-permute-start.15 = (bf16[128,512]{1,0:T(8,128)(2,1)S(1)}, bf16[128,512]{1,0:T(8,128)(2,1)S(1)}, u32[]{:S(2)}, u32[]{:S(2)}) collective-permute-start(bf16[128,512]{1,0:T(8,128)(2,1)S(1)} %get-tuple-element.111), channel_id=1, source_target_pairs={{0,7},{1,6},{2,5},{3,4},{4,3},{5,2},{6,1},{7,0},{8,15},{9,14},{10,... | collective-permute-start | bytes 393224 | tf_op jit(solution)/shard_map/ppermute | solution.py:539
  78.2 15.9 %collective-permute-start.16 = (bf16[128,512]{1,0:T(8,128)(2,1)S(1)}, bf16[128,512]{1,0:T(8,128)(2,1)S(1)}, u32[]{:S(2)}, u32[]{:S(2)}) collective-permute-start(bf16[128,512]{1,0:T(8,128)(2,1)S(1)} %get-tuple-element.112), channel_id=1, source_target_pairs={{0,6},{1,7},{2,4},{3,5},{4,2},{5,3},{6,0},{7,1},{8,14},{9,15},{10,... | collective-permute-start | bytes 393224 | tf_op jit(solution)/shard_map/ppermute | solution.py:539
  80.0 16.9 %collective-permute-start.22 = (bf16[128,512]{1,0:T(8,128)(2,1)S(1)}, bf16[128,512]{1,0:T(8,128)(2,1)S(1)}, u32[]{:S(2)}, u32[]{:S(2)}) collective-permute-start(bf16[128,512]{1,0:T(8,128)(2,1)S(1)} %get-tuple-element.124), channel_id=1, source_target_pairs={{0,3},{1,2},{2,1},{3,0},{4,7},{5,6},{6,5},{7,4},{8,11},{9,10},{10,... | collective-permute-start | bytes 393224 | tf_op jit(solution)/shard_map/ppermute | solution.py:539
  89.8 8.8 %collective-permute-start.23 = (bf16[128,512]{1,0:T(8,128)(2,1)S(1)}, bf16[128,512]{1,0:T(8,128)(2,1)S(1)}, u32[]{:S(2)}, u32[]{:S(2)}) collective-permute-start(bf16[128,512]{1,0:T(8,128)(2,1)S(1)} %get-tuple-element.125), channel_id=1, source_target_pairs={{0,2},{1,3},{2,0},{3,1},{4,6},{5,7},{6,4},{7,5},{8,10},{9,11},{10,... | collective-permute-start | bytes 393224 | tf_op jit(solution)/shard_map/ppermute | solution.py:539
  90.0 8.9 %collective-permute-start.24 = (bf16[128,512]{1,0:T(8,128)(2,1)S(1)}, bf16[128,512]{1,0:T(8,128)(2,1)S(1)}, u32[]{:S(2)}, u32[]{:S(2)}) collective-permute-start(bf16[128,512]{1,0:T(8,128)(2,1)S(1)} %get-tuple-element.126), channel_id=1, source_target_pairs={{0,1},{1,0},{2,3},{3,2},{4,5},{5,4},{6,7},{7,6},{8,9},{9,8},{10,11... | collective-permute-start | bytes 393224 | tf_op jit(solution)/shard_map/ppermute | solution.py:539
  90.1 14.5 %collective-permute-start.17 = (bf16[128,512]{1,0:T(8,128)(2,1)S(1)}, bf16[128,512]{1,0:T(8,128)(2,1)S(1)}, u32[]{:S(2)}, u32[]{:S(2)}) collective-permute-start(bf16[128,512]{1,0:T(8,128)(2,1)S(1)} %get-tuple-element.113), channel_id=1, source_target_pairs={{0,5},{1,4},{2,7},{3,6},{4,1},{5,0},{6,3},{7,2},{8,13},{9,12},{10,... | collective-permute-start | bytes 393224 | tf_op jit(solution)/shard_map/ppermute | solution.py:539
  94.2 13.5 %collective-permute-start.18 = (bf16[128,512]{1,0:T(8,128)(2,1)S(1)}, bf16[128,512]{1,0:T(8,128)(2,1)S(1)}, u32[]{:S(2)}, u32[]{:S(2)}) collective-permute-start(bf16[128,512]{1,0:T(8,128)(2,1)S(1)} %get-tuple-element.114), channel_id=1, source_target_pairs={{0,4},{1,5},{2,6},{3,7},{4,0},{5,1},{6,2},{7,3},{8,12},{9,13},{10,... | collective-permute-start | bytes 393224 | tf_op jit(solution)/shard_map/ppermute | solution.py:539
  96.9 10.8 %collective-permute-start.19 = (bf16[128,512]{1,0:T(8,128)(2,1)S(1)}, bf16[128,512]{1,0:T(8,128)(2,1)S(1)}, u32[]{:S(2)}, u32[]{:S(2)}) collective-permute-start(bf16[128,512]{1,0:T(8,128)(2,1)S(1)} %get-tuple-element.115), channel_id=1, source_target_pairs={{0,3},{1,2},{2,1},{3,0},{4,7},{5,6},{6,5},{7,4},{8,11},{9,10},{10,... | collective-permute-start | bytes 393224 | tf_op jit(solution)/shard_map/ppermute | solution.py:539
  98.6 10.1 %collective-permute-start.20 = (bf16[128,512]{1,0:T(8,128)(2,1)S(1)}, bf16[128,512]{1,0:T(8,128)(2,1)S(1)}, u32[]{:S(2)}, u32[]{:S(2)}) collective-permute-start(bf16[128,512]{1,0:T(8,128)(2,1)S(1)} %get-tuple-element.116), channel_id=1, source_target_pairs={{0,2},{1,3},{2,0},{3,1},{4,6},{5,7},{6,4},{7,5},{8,10},{9,11},{10,... | collective-permute-start | bytes 393224 | tf_op jit(solution)/shard_map/ppermute | solution.py:539
  98.9 9.7 %collective-permute-start.21 = (bf16[128,512]{1,0:T(8,128)(2,1)S(1)}, bf16[128,512]{1,0:T(8,128)(2,1)S(1)}, u32[]{:S(2)}, u32[]{:S(2)}) collective-permute-start(bf16[128,512]{1,0:T(8,128)(2,1)S(1)} %get-tuple-element.117), channel_id=1, source_target_pairs={{0,1},{1,0},{2,3},{3,2},{4,5},{5,4},{6,7},{7,6},{8,9},{9,8},{10,11... | collective-permute-start | bytes 393224 | tf_op jit(solution)/shard_map/ppermute | solution.py:539
  104.6 6.2 %copy-start.15 = (bf16[128,256]{1,0:T(8,128)(2,1)S(1)}, bf16[128,256]{1,0:T(8,128)(2,1)}, u32[]{:S(2)}) copy-start(bf16[128,256]{1,0:T(8,128)(2,1)} %constant.19.clone.inv_ref) | copy-start | bytes 196612
  109.3 24.8 %collective-permute-start.28 = (bf16[128,4096]{1,0:T(8,128)(2,1)S(1)}, bf16[128,4096]{1,0:T(8,128)(2,1)S(1)}, u32[]{:S(2)}, u32[]{:S(2)}) collective-permute-start(bf16[128,4096]{1,0:T(8,128)(2,1)S(1)} %get-tuple-element.136.grad_b_ref), channel_id=1, source_target_pairs={{1,0},{2,1},{3,2},{4,3},{5,4},{6,5},{7,6},{9,8},{10,9},{11,10},{12... | collective-permute-start | bytes 3145736 | tf_op jit(solution)/shard_map/ppermute | solution.py:26
  110.8 23.3 %copy-start.7 = (bf16[1,128,4096]{2,1,0:T(8,128)(2,1)S(1)}, bf16[1,128,4096]{2,1,0:T(8,128)(2,1)}, u32[]{:S(2)}) copy-start(bf16[1,128,4096]{2,1,0:T(8,128)(2,1)} %param.16) | copy-start | bytes 3145732
  110.8 23.3 %copy-start.10 = (bf16[128,256]{1,0:T(8,128)(2,1)S(1)}, bf16[128,256]{1,0:T(8,128)(2,1)}, u32[]{:S(2)}) copy-start(bf16[128,256]{1,0:T(8,128)(2,1)} %constant.18.clone.inv_ref) | copy-start | bytes 196612
  113.2 2.7 %collective-permute-start.25 = (bf16[4,128,512]{2,1,0:T(8,128)(2,1)S(1)}, bf16[4,128,512]{2,1,0:T(8,128)(2,1)S(1)}, u32[]{:S(2)}, u32[]{:S(2)}) collective-permute-start(bf16[4,128,512]{2,1,0:T(8,128)(2,1)S(1)} %get-tuple-element.138), channel_id=1, source_target_pairs={{0,1},{1,0},{2,3},{3,2},{4,5},{5,4},{6,7},{7,6},{8,9},{9,8},{10,11... | collective-permute-start | bytes 1572872 | tf_op jit(solution)/shard_map/ppermute | solution.py:539
  116.1 16.6 %collective-permute-start.26 = (bf16[2,128,512]{2,1,0:T(8,128)(2,1)S(1)}, bf16[2,128,512]{2,1,0:T(8,128)(2,1)S(1)}, u32[]{:S(2)}, u32[]{:S(2)}) collective-permute-start(bf16[2,128,512]{2,1,0:T(8,128)(2,1)S(1)} %get-tuple-element.140), channel_id=1, source_target_pairs={{0,2},{1,3},{2,0},{3,1},{4,6},{5,7},{6,4},{7,5},{8,10},{9,11},{10,... | collective-permute-start | bytes 786440 | tf_op jit(solution)/shard_map/ppermute | solution.py:539
  132.8 6.3 %collective-permute-start.27 = (bf16[128,512]{1,0:T(8,128)(2,1)S(1)}, bf16[128,512]{1,0:T(8,128)(2,1)S(1)}, u32[]{:S(2)}, u32[]{:S(2)}) collective-permute-start(bf16[128,512]{1,0:T(8,128)(2,1)S(1)} %get-tuple-element.141), channel_id=1, source_target_pairs={{0,4},{1,5},{2,6},{3,7},{4,0},{5,1},{6,2},{7,3},{8,12},{9,13},{10,... | collective-permute-start | bytes 393224 | tf_op jit(solution)/shard_map/ppermute | solution.py:539

commit v7 on v5

--- a/solution.py
+++ b/solution.py
@@ -370,8 +370,11 @@
     return pl.ds(pl.multiple_of(index * width, width), width)
 
 
-def pick_kernel(slot, me_ref, in_ref, out_ref):
-    out_ref[...] = in_ref[:, columns(me_ref[slot], out_ref.shape[1])]
+def pick_kernel(firsts, me_ref, in_ref, *out_refs):
+    for first, out_ref in zip(firsts, out_refs):
+        width = out_ref.shape[1]
+        owned = in_ref.shape[1] // 8
+        out_ref[...] = in_ref[:, columns((me_ref[0] ^ first) // (width // owned), width)]
 
 
 def pieces_z_kernel(beta, first, me_ref, adjoint_ref, gate_ref, *out_refs):
@@ -458,19 +461,18 @@
             out_ref[cols, p * size : (p + 1) * size] = lags.astype(BF16)
 
 
-def pieces_grad_b_kernel(beta, count, me_ref, near_ref, far_ref, long_ref, mid_ref, *refs):
+def pieces_grad_b_kernel(beta, count, me_ref, near_ref, far_ref, long_ref, gate_ref, *refs):
     piece_refs, (grad_u_ref, grad_b_ref) = refs[:count][::-1], refs[count:]
     width = piece_refs[0].shape[1]
-    half = count // 2
     me = me_ref[0]
     for k in range(count):
         owner = me ^ k
         cols = columns(owner, width)
-        adjoint_ref = near_ref if k < half else far_ref
-        adjoint = adjoint_ref[:, columns(owner & (half - 1), width)].astype(F32)
+        adjoint_ref = near_ref if k < count // 2 else far_ref
+        adjoint = adjoint_ref[:, columns(owner & (adjoint_ref.shape[1] // width - 1), width)].astype(F32)
         grad_u = adjoint + piece_refs[k][...].astype(F32) * long_ref[:, cols].astype(F32)
         grad_u_ref[:, cols] = grad_u
-        grad_b_ref[:, cols] = (beta * grad_u * mid_ref[:, cols].astype(F32)).astype(BF16)
+        grad_b_ref[:, cols] = (beta * grad_u * gate_ref[:, cols].astype(F32)).astype(BF16)
 
 
 def pieces_taps_kernel(me_ref, fwd_ref, inv_ref, signal_ref, grad_b_ref, keep_ref, send_ref):
@@ -531,12 +533,20 @@
     return lax.ppermute(array, "ctx", [(i, i ^ k) for i in range(count)])
 
 
-def exchanged(pieces, step=1, first=0):
-    came = list(pieces)
-    for k in range(len(pieces) - 1, -1, -1):
-        if first + k:
-            came[k] = swapped(pieces[k], (first + k) * step)
-    return came
+def after(value, *others):
+    return lax.optimization_barrier((value, others))[0]
+
+
+def exchanged(pieces, first=0):
+    return [swapped(piece, first + k) if first + k else piece for k, piece in enumerate(pieces)]
+
+
+def in_turn(pieces, *before):
+    came_7 = swapped(after(pieces[3], before[1]), 7)
+    came_6 = swapped(after(pieces[2], before[0]), 6)
+    came_5 = swapped(after(pieces[1], came_7), 5)
+    came_4 = swapped(after(pieces[0], came_6), 4)
+    return [came_4, came_5, came_6, came_7]
 
 
 def by_permutes(
@@ -575,48 +585,46 @@
     long_flops = 12 * period * seq_len * owned
     few = 4 * tokens * channels
 
-    index = lax.axis_index("ctx")
-    me = jnp.stack([index, index // half, 1 - index // half]).astype(jnp.int32)
+    me = lax.axis_index("ctx").astype(jnp.int32)[None]
     inputs, gate_pre, gate_mid, gate_long, gate_out = (
         array[0] for array in (layer_input, pre_gate, mid_gate, long_gate, out_gate)
     )
     filter_taps = mid_filter[0]
 
-    far = local(functools.partial(pick_kernel, 2), [half_shape], [me, incoming[0]], few, name="far")
-    far, inputs, gate_pre = lax.optimization_barrier((far, inputs, gate_pre))
+    far = local(functools.partial(pick_kernel, (4,)), [half_shape], [me, incoming[0]], few, name="far")
+    far = passed_along(far, "section", -1)
     mixed_in = local(mix_kernel, [rows_shape], [inputs, gate_pre], few, name="mix")
-    far = passed_along(far, "section", -1)
     earlier = shifted(mixed_in, "ctx", 1)
-    far, sent = lax.optimization_barrier((far, incoming[0]))
-    near = local(functools.partial(pick_kernel, 1), [half_shape], [me, sent], few, name="near")
+    sent = after(incoming[0], far)
+    near = local(functools.partial(pick_kernel, (0,)), [half_shape], [me, sent], few, name="near")
     near = passed_along(near, "section", -1)
     far_z = local(
         functools.partial(pieces_z_kernel, beta, half), [piece] * half, [me, far, gate_out], few, name="farz"
     )
-    far_z, earlier = lax.optimization_barrier((far_z, earlier))
     signal, filt, *pieces_w = local(
         functools.partial(pieces_branch_kernel, beta),
         [((span, channels), BF16)] * 2 + [piece] * devices,
-        [me, fwd, inv_conv, earlier, mixed_in, filter_taps, inputs, gate_mid, gate_long], mid_flops,
-        name="branch",
-    )
-    far_z = exchanged(far_z, first=half)
-    far_z, near, pieces_w = lax.optimization_barrier((far_z, near, pieces_w))
+        [me, fwd, inv_conv, after(earlier, far_z), mixed_in, filter_taps, inputs, gate_mid, gate_long],
+        mid_flops, name="branch",
+    )
+    far_z = in_turn(far_z, far_z, far_z)
+    near = after(near, pieces_w)
     near_z = local(
         functools.partial(pieces_z_kernel, beta, 0), [piece] * half, [me, near, gate_out], few, name="nearz"
     )
-    far_w = exchanged(pieces_w[half:], first=half)
-    near_z = exchanged(near_z)
-    pieces_z = near_z + far_z
+    far_w = in_turn(pieces_w[half:], far_z[0], far_z[1])
+    pieces_z = exchanged(near_z) + far_z
     *pieces_g, channel_z = local(
         functools.partial(pieces_grad_w_kernel, blocks, devices),
         [piece] * devices + [((seq_len, owned), BF16)],
         [me, long_fwd, long_inv, long_filter[0], *pieces_z[::-1]], long_flops,
         [spectrum, spectrum, joint, staged], name="gradw",
     )
-    far_w, near_w, pieces_g = lax.optimization_barrier((far_w, pieces_w[:half], pieces_g))
+    near_w = after(pieces_w[:half], far_w[2], far_w[3], pieces_g)
     pieces_w = exchanged(near_w) + far_w
-    pieces_g = exchanged(pieces_g)[::-1]
+    far_g = in_turn(pieces_g[half:], far_w[0], far_w[1])
+    near_g = exchanged(after(pieces_g[:half], far_g[2], far_g[3]))
+    pieces_g = far_g[::-1] + near_g[::-1]
     long_grad = local(
         functools.partial(pieces_long_grad_kernel, blocks, scale, devices), [((owned, seq_len), BF16)],
         [me, long_fwd, long_inv, channel_z, *pieces_w[::-1]], long_flops,
@@ -633,8 +641,8 @@
         mid_flops, name="taps",
     )
     sums = local(pair_kernel, [tap_piece] * half, [keep, swapped(send, 1)], few, name="pair")
-    sums = exchanged(list(sums), 2)[::-1]
-    later, _ = lax.optimization_barrier((later, sums[-1]))
+    sums = [swapped(sums[m], 2 * m) for m in (3, 2, 1)] + [sums[0]]
+    later = after(later, sums[-1])
     input_grad = local(
         functools.partial(pieces_input_grad_kernel, 512), [rows_shape],
         [fwd, inv_corr, grad_b, later, filt, grad_u, gate_pre], mid_flops, name="inputgrad",
@@ -647,7 +655,7 @@
 def per_device(*arrays):
     devices = lax.axis_size("ctx")
     owned = arrays[0].shape[2] // devices
-    if owned % 128 == 0 and devices in (2, 4, 8, 16):
+    if owned % 128 == 0 and devices == 8:
         return by_permutes(*arrays)
     return by_all_to_all(*arrays)
 

time: 137 us -> 131 us (0.956)
  starting transfers between devices: 57.7 us -> 47.5 us
  waiting for transfers between devices: 49.1 us -> 56 us
  Pallas kernels: 26.4 us -> 22.8 us
    ppermute x25, starting transfers between devices: 46.7 us -> 35.8 us  [swapped(): return lax.ppermute(array, 'ctx', [(i, i ^ k) for i in range(count)])]
    ppermute x25, waiting for transfers between devices: 36.3 us -> 43.7 us  [swapped(): return lax.ppermute(array, 'ctx', [(i, i ^ k) for i in range(count)])]
    pallas_call x13, Pallas kernels: 26.4 us -> 22.8 us  [local(): pl.pallas_call(body, in_specs=specs, out_specs=[pl.BlockSpec(memory_space...]
  transfers between devices with their start and end apart: 29 -> 29, of which waited for: 13 -> 15; matrix products, arithmetic and copies ran while one was open for 0% -> 0% of each run, Pallas kernels for 17% -> 16%
where the time goes in v7:
time: 131 us
  waiting for transfers between devices  56 us (43%)
  starting transfers between devices  47.5 us (36%)
  Pallas kernels  22.8 us (17%)
  local copies, waits for them, and re-layouts  3.73 us (3%)
    ppermute x25, waiting for transfers between devices, swapped(): return lax.ppermute(array, 'ctx', [(i, i ^ k) for i in range(count)])  43.7 us
    ppermute x25, starting transfers between devices, swapped(): return lax.ppermute(array, 'ctx', [(i, i ^ k) for i in range(count)])  35.8 us
    pallas_call x13, Pallas kernels, local(): pl.pallas_call(body, in_specs=specs, out_specs=[pl.BlockSpec(memory_space...  22.8 us
    ppermute x2, waiting for transfers between devices, passed_along(): return lax.ppermute(value, axis, pairs)  12.3 us
    ppermute x2, starting transfers between devices, passed_along(): return lax.ppermute(value, axis, pairs)  6.74 us
    ppermute x2, starting transfers between devices, shifted(): return lax.ppermute(array, axis, pairs)  4.96 us
    unnamed x32, local copies, waits for them, and re-layouts  3.73 us
  transfers between devices with their start and end apart: 29, of which 15 were waited for; matrix products, arithmetic and copies ran while one was open for 0% of the time, Pallas kernels for 16%

profile of v7, /device:TPU:0, one launch (start us, length us, event | category | flops | bytes accessed | tf_op | source)
XLA Modules:
  0.0 130.9 jit_solution(14861711652458606626)
XLA Ops:
  0.6 1.2 copy-done
  1.9 1.2 copy-done.6
  3.1 0.2 mix.1.mixed_ref
  3.3 3.5 %collective-permute-start = (bf16[128,4096]{1,0:T(8,128)(2,1)S(1)}, bf16[128,4096]{1,0:T(8,128)(2,1)}, u32[]{:S(2)}, u32[]{:S(2)}) collective-permute-start(bf16[128,4096]{1,0:T(8,128)(2,1)S(1)} %mix.1.mixed_ref), channel_id=1, source_target_pairs={{0,1},{1,2},{2,3},{3,4},{4,5},{5,6},{6,7},{8,9},{9,10},{10,11},{11... | collective-permute-start | bytes 3145736 | tf_op jit(solution)/shard_map/ppermute | solution.py:26
  6.9 3.3 %collective-permute-start.1 = (bf16[128,2048]{1,0:T(8,128)(2,1)S(1)}, bf16[128,2048]{1,0:T(8,128)(2,1)S(1)}, u32[]{:S(2)}, u32[]{:S(2)}) collective-permute-start(bf16[128,2048]{1,0:T(8,128)(2,1)S(1)} %far.1), channel_id=1, source_target_pairs={{0,24},{8,0},{16,8},{24,16},{1,25},{9,1},{17,9},{25,17},{2,26},{10... | collective-permute-start | bytes 1572872 | tf_op jit(solution)/shard_map/ppermute | solution.py:20
  10.2 12.3 %collective-permute-done.1.adjoint_ref.far_ref = bf16[128,2048]{1,0:T(8,128)(2,1)S(1)} collective-permute-done((bf16[128,2048]{1,0:T(8,128)(2,1)S(1)}, bf16[128,2048]{1,0:T(8,128)(2,1)S(1)}, u32[]{:S(2)}, u32[]{:S(2)}) %collective-permute-start.1) | collective-permute-done | bytes 524320 | tf_op jit(solution)/shard_map/ppermute | solution.py:20
  22.6 3.4 %collective-permute-start.2 = (bf16[128,2048]{1,0:T(8,128)(2,1)S(1)}, bf16[128,2048]{1,0:T(8,128)(2,1)S(1)}, u32[]{:S(2)}, u32[]{:S(2)}) collective-permute-start(bf16[128,2048]{1,0:T(8,128)(2,1)S(1)} %near.1), channel_id=1, source_target_pairs={{0,24},{8,0},{16,8},{24,16},{1,25},{9,1},{17,9},{25,17},{2,26},{10... | collective-permute-start | bytes 1572872 | tf_op jit(solution)/shard_map/ppermute | solution.py:20
  26.1 1.2 collective-permute-start.4
  27.3 1.8 %collective-permute-start.3 = (bf16[128,512]{1,0:T(8,128)(2,1)S(1)}, bf16[128,512]{1,0:T(8,128)(2,1)S(1)}, u32[]{:S(2)}, u32[]{:S(2)}) collective-permute-start(bf16[128,512]{1,0:T(8,128)(2,1)S(1)} %get-tuple-element.92), channel_id=1, source_target_pairs={{0,7},{1,6},{2,5},{3,4},{4,3},{5,2},{6,1},{7,0},{8,15},{9,14},{10,... | collective-permute-start | bytes 393224 | tf_op jit(solution)/shard_map/ppermute | solution.py:533
  29.1 5.3 %collective-permute-done.4.refs_1_ = bf16[128,512]{1,0:T(8,128)(2,1)S(1)} collective-permute-done((bf16[128,512]{1,0:T(8,128)(2,1)S(1)}, bf16[128,512]{1,0:T(8,128)(2,1)S(1)}, u32[]{:S(2)}, u32[]{:S(2)}) %collective-permute-start.4) | collective-permute-done | bytes 131104 | tf_op jit(solution)/shard_map/ppermute | solution.py:533
  34.4 3.9 %collective-permute-start.6 = (bf16[128,512]{1,0:T(8,128)(2,1)S(1)}, bf16[128,512]{1,0:T(8,128)(2,1)S(1)}, u32[]{:S(2)}, u32[]{:S(2)}) collective-permute-start(bf16[128,512]{1,0:T(8,128)(2,1)S(1)} %get-tuple-element.95), channel_id=1, source_target_pairs={{0,4},{1,5},{2,6},{3,7},{4,0},{5,1},{6,2},{7,3},{8,12},{9,13},{10,... | collective-permute-start | bytes 393224 | tf_op jit(solution)/shard_map/ppermute | solution.py:533
  38.3 2.4 %collective-permute-start.5 = (bf16[128,512]{1,0:T(8,128)(2,1)S(1)}, bf16[128,512]{1,0:T(8,128)(2,1)S(1)}, u32[]{:S(2)}, u32[]{:S(2)}) collective-permute-start(bf16[128,512]{1,0:T(8,128)(2,1)S(1)} %get-tuple-element.94), channel_id=1, source_target_pairs={{0,5},{1,4},{2,7},{3,6},{4,1},{5,0},{6,3},{7,2},{8,13},{9,12},{10,... | collective-permute-start | bytes 393224 | tf_op jit(solution)/shard_map/ppermute | solution.py:533
  40.7 1.2 copy-done.8
  41.9 4.4 %branch.1 = (bf16[256,4096]{1,0:T(8,128)(2,1)S(1)}, bf16[256,4096]{1,0:T(8,128)(2,1)S(1)}, bf16[128,512]{1,0:T(8,128)(2,1)S(1)}, bf16[128,512]{1,0:T(8,128)(2,1)...) custom-call(s32[1]{0:T(128)} %bitcast.me_ref, ...), custom_call_target="tpu_custom_call" | custom-call | flops 1073741824 | bytes 11730948 | tf_op jit(solution)/shard_map/branch/pallas_call | solution.py:518
  46.3 2.7 %collective-permute-done.6.refs_3_ = bf16[128,512]{1,0:T(8,128)(2,1)S(1)} collective-permute-done((bf16[128,512]{1,0:T(8,128)(2,1)S(1)}, bf16[128,512]{1,0:T(8,128)(2,1)S(1)}, u32[]{:S(2)}, u32[]{:S(2)}) %collective-permute-start.6) | collective-permute-done | bytes 131104 | tf_op jit(solution)/shard_map/ppermute | solution.py:533
  49.0 1.4 %collective-permute-done.5.refs_2_ = bf16[128,512]{1,0:T(8,128)(2,1)S(1)} collective-permute-done((bf16[128,512]{1,0:T(8,128)(2,1)S(1)}, bf16[128,512]{1,0:T(8,128)(2,1)S(1)}, u32[]{:S(2)}, u32[]{:S(2)}) %collective-permute-start.5) | collective-permute-done | bytes 131104 | tf_op jit(solution)/shard_map/ppermute | solution.py:533
  50.4 2.2 %collective-permute-start.10 = (bf16[128,512]{1,0:T(8,128)(2,1)S(1)}, bf16[128,512]{1,0:T(8,128)(2,1)S(1)}, u32[]{:S(2)}, u32[]{:S(2)}) collective-permute-start(bf16[128,512]{1,0:T(8,128)(2,1)S(1)} %get-tuple-element.101), channel_id=1, source_target_pairs={{0,7},{1,6},{2,5},{3,4},{4,3},{5,2},{6,1},{7,0},{8,15},{9,14},{10,... | collective-permute-start | bytes 393224 | tf_op jit(solution)/shard_map/ppermute | solution.py:533
  52.6 1.8 %collective-permute-start.13 = (bf16[128,512]{1,0:T(8,128)(2,1)S(1)}, bf16[128,512]{1,0:T(8,128)(2,1)S(1)}, u32[]{:S(2)}, u32[]{:S(2)}) collective-permute-start(bf16[128,512]{1,0:T(8,128)(2,1)S(1)} %get-tuple-element.105), channel_id=1, source_target_pairs={{0,6},{1,7},{2,4},{3,5},{4,2},{5,3},{6,0},{7,1},{8,14},{9,15},{10,... | collective-permute-start | bytes 393224 | tf_op jit(solution)/shard_map/ppermute | solution.py:533
  54.6 1.3 collective-permute-start.8
  55.9 0.5 collective-permute-start.9
  56.5 0.9 collective-permute-done.10.refs_0_
  57.4 4.2 %collective-permute-done.13.refs_1_ = bf16[128,512]{1,0:T(8,128)(2,1)S(1)} collective-permute-done((bf16[128,512]{1,0:T(8,128)(2,1)S(1)}, bf16[128,512]{1,0:T(8,128)(2,1)S(1)}, u32[]{:S(2)}, u32[]{:S(2)}) %collective-permute-start.13) | collective-permute-done | bytes 131104 | tf_op jit(solution)/shard_map/ppermute | solution.py:533
  61.6 2.7 %collective-permute-start.14 = (bf16[128,512]{1,0:T(8,128)(2,1)S(1)}, bf16[128,512]{1,0:T(8,128)(2,1)S(1)}, u32[]{:S(2)}, u32[]{:S(2)}) collective-permute-start(bf16[128,512]{1,0:T(8,128)(2,1)S(1)} %get-tuple-element.106), channel_id=1, source_target_pairs={{0,4},{1,5},{2,6},{3,7},{4,0},{5,1},{6,2},{7,3},{8,12},{9,13},{10,... | collective-permute-start | bytes 393224 | tf_op jit(solution)/shard_map/ppermute | solution.py:533
  64.2 5.0 %collective-permute-done.8.refs_5_ = bf16[128,512]{1,0:T(8,128)(2,1)S(1)} collective-permute-done((bf16[128,512]{1,0:T(8,128)(2,1)S(1)}, bf16[128,512]{1,0:T(8,128)(2,1)S(1)}, u32[]{:S(2)}, u32[]{:S(2)}) %collective-permute-start.8) | collective-permute-done | bytes 131104 | tf_op jit(solution)/shard_map/ppermute | solution.py:533
  69.2 4.7 %gradw.1 = (bf16[128,512]{1,0:T(8,128)(2,1)S(1)}, bf16[128,512]{1,0:T(8,128)(2,1)S(1)}, bf16[128,512]{1,0:T(8,128)(2,1)S(1)}, bf16[128,512]{1,0:T(8,128)(2,1)S(1...) custom-call(s32[1]{0:T(128)} %bitcast.me_ref, ...), custom_call_target="tpu_custom_call" | custom-call | flops 3221225472 | bytes 4980740 | tf_op jit(solution)/shard_map/gradw/pallas_call | solution.py:518
  74.0 1.0 collective-permute-done.14.refs_3_
  75.0 2.1 %collective-permute-start.15 = (bf16[128,512]{1,0:T(8,128)(2,1)S(1)}, bf16[128,512]{1,0:T(8,128)(2,1)S(1)}, u32[]{:S(2)}, u32[]{:S(2)}) collective-permute-start(bf16[128,512]{1,0:T(8,128)(2,1)S(1)} %get-tuple-element.107), channel_id=1, source_target_pairs={{0,6},{1,7},{2,4},{3,5},{4,2},{5,3},{6,0},{7,1},{8,14},{9,15},{10,... | collective-permute-start | bytes 393224 | tf_op jit(solution)/shard_map/ppermute | solution.py:533
  77.1 1.2 collective-permute-start.12
  78.3 2.3 %collective-permute-start.22 = (bf16[128,512]{1,0:T(8,128)(2,1)S(1)}, bf16[128,512]{1,0:T(8,128)(2,1)S(1)}, u32[]{:S(2)}, u32[]{:S(2)}) collective-permute-start(bf16[128,512]{1,0:T(8,128)(2,1)S(1)} %get-tuple-element.122), channel_id=1, source_target_pairs={{0,2},{1,3},{2,0},{3,1},{4,6},{5,7},{6,4},{7,5},{8,10},{9,11},{10,... | collective-permute-start | bytes 393224 | tf_op jit(solution)/shard_map/ppermute | solution.py:533
  80.6 2.4 %collective-permute-done.15.refs_1_ = bf16[128,512]{1,0:T(8,128)(2,1)S(1)} collective-permute-done((bf16[128,512]{1,0:T(8,128)(2,1)S(1)}, bf16[128,512]{1,0:T(8,128)(2,1)S(1)}, u32[]{:S(2)}, u32[]{:S(2)}) %collective-permute-start.15) | collective-permute-done | bytes 131104 | tf_op jit(solution)/shard_map/ppermute | solution.py:533
  82.9 4.1 %collective-permute-start.17 = (bf16[128,512]{1,0:T(8,128)(2,1)S(1)}, bf16[128,512]{1,0:T(8,128)(2,1)S(1)}, u32[]{:S(2)}, u32[]{:S(2)}) collective-permute-start(bf16[128,512]{1,0:T(8,128)(2,1)S(1)} %get-tuple-element.111), channel_id=1, source_target_pairs={{0,4},{1,5},{2,6},{3,7},{4,0},{5,1},{6,2},{7,3},{8,12},{9,13},{10,... | collective-permute-start | bytes 393224 | tf_op jit(solution)/shard_map/ppermute | solution.py:533
  87.1 2.6 %collective-permute-start.16 = (bf16[128,512]{1,0:T(8,128)(2,1)S(1)}, bf16[128,512]{1,0:T(8,128)(2,1)S(1)}, u32[]{:S(2)}, u32[]{:S(2)}) collective-permute-start(bf16[128,512]{1,0:T(8,128)(2,1)S(1)} %get-tuple-element.109), channel_id=1, source_target_pairs={{0,5},{1,4},{2,7},{3,6},{4,1},{5,0},{6,3},{7,2},{8,13},{9,12},{10,... | collective-permute-start | bytes 393224 | tf_op jit(solution)/shard_map/ppermute | solution.py:533
  89.7 1.8 %collective-permute-done.21.refs_4_ = bf16[128,512]{1,0:T(8,128)(2,1)S(1)} collective-permute-done((bf16[128,512]{1,0:T(8,128)(2,1)S(1)}, bf16[128,512]{1,0:T(8,128)(2,1)S(1)}, u32[]{:S(2)}, u32[]{:S(2)}) %collective-permute-start.21) | collective-permute-done | bytes 131104 | tf_op jit(solution)/shard_map/ppermute | solution.py:533
  91.5 2.9 %collective-permute-done.22.refs_5_ = bf16[128,512]{1,0:T(8,128)(2,1)S(1)} collective-permute-done((bf16[128,512]{1,0:T(8,128)(2,1)S(1)}, bf16[128,512]{1,0:T(8,128)(2,1)S(1)}, u32[]{:S(2)}, u32[]{:S(2)}) %collective-permute-start.22) | collective-permute-done | bytes 131104 | tf_op jit(solution)/shard_map/ppermute | solution.py:533
  94.4 5.7 %longgrad.1 = bf16[512,1024]{1,0:T(8,128)(2,1)} custom-call(s32[1]{0:T(128)} %bitcast.me_ref, bf16[512,512]{1,0:T(8,128)(2,1)S(1)} %copy-done.13, bf16[256,512]{1,0:T(8,128)(2,1)S(1)} %copy-done.14, bf16[1024,512]{1,0:T(8,128)(2,1)S(1)} %get-tuple-element.120.grad_ref, bf16[128,512]{1,0:T(8,128)(2,1)S(1)} %collective-permute-done.10.refs_0_, ...), custom_call_target="tpu_custom_call" | custom-call | flops 3221225472 | bytes 3932164 | tf_op jit(solution)/shard_map/longgrad/pallas_call | solution.py:518
  100.1 2.1 %collective-permute-done.19.refs_5_ = bf16[128,512]{1,0:T(8,128)(2,1)S(1)} collective-permute-done((bf16[128,512]{1,0:T(8,128)(2,1)S(1)}, bf16[128,512]{1,0:T(8,128)(2,1)S(1)}, u32[]{:S(2)}, u32[]{:S(2)}) %collective-permute-start.19) | collective-permute-done | bytes 131104 | tf_op jit(solution)/shard_map/ppermute | solution.py:533
  102.2 0.6 gradb.1
  102.8 1.5 %collective-permute-start.28 = (bf16[128,4096]{1,0:T(8,128)(2,1)S(1)}, bf16[128,4096]{1,0:T(8,128)(2,1)S(1)}, u32[]{:S(2)}, u32[]{:S(2)}) collective-permute-start(bf16[128,4096]{1,0:T(8,128)(2,1)S(1)} %get-tuple-element.133.grad_b_ref), channel_id=1, source_target_pairs={{1,0},{2,1},{3,2},{4,3},{5,4},{6,5},{7,6},{9,8},{10,9},{11,10},{12... | collective-permute-start | bytes 3145736 | tf_op jit(solution)/shard_map/ppermute | solution.py:26
  104.3 2.4 %taps.1 = (bf16[4,128,512]{2,1,0:T(8,128)(2,1)S(1)}, bf16[4,128,512]{2,1,0:T(8,128)(2,1)S(1)}) custom-call(s32[1]{0:T(128)} %bitcast.me_ref, bf16[256,256]{1,0:T(8,128)(2,1)S(1)} %copy-done.9, bf16[128,256]{1,0:T(8,128)(2,1)S(1)} %copy-done.15, bf16[256,4096]{1,0:T(8,128)(2,1)S(1)} %get-tuple-element.81.signal_ref, ...), custom_call_target="tpu_custom_call" | custom-call | flops 1073741824 | bytes 4390916 | tf_op jit(solution)/shard_map/taps/pallas_call | solution.py:518
  106.7 1.2 collective-permute-start.24
  107.9 1.5 %collective-permute-done.24.came_ref = bf16[4,128,512]{2,1,0:T(8,128)(2,1)S(1)} collective-permute-done((bf16[4,128,512]{2,1,0:T(8,128)(2,1)S(1)}, bf16[4,128,512]{2,1,0:T(8,128)(2,1)S(1)}, u32[]{:S(2)}, u32[]{:S(2)}) %collective-permute-start.24) | collective-permute-done | bytes 524320 | tf_op jit(solution)/shard_map/ppermute | solution.py:533
  109.6 2.1 %collective-permute-start.25 = (bf16[128,512]{1,0:T(8,128)(2,1)S(1)}, bf16[128,512]{1,0:T(8,128)(2,1)S(1)}, u32[]{:S(2)}, u32[]{:S(2)}) collective-permute-start(bf16[128,512]{1,0:T(8,128)(2,1)S(1)} %get-tuple-element.136), channel_id=1, source_target_pairs={{0,6},{1,7},{2,4},{3,5},{4,2},{5,3},{6,0},{7,1},{8,14},{9,15},{10,... | collective-permute-start | bytes 393224 | tf_op jit(solution)/shard_map/ppermute | solution.py:533
  111.7 0.6 collective-permute-start.26
  112.3 1.7 %collective-permute-start.27 = (bf16[128,512]{1,0:T(8,128)(2,1)S(1)}, bf16[128,512]{1,0:T(8,128)(2,1)S(1)}, u32[]{:S(2)}, u32[]{:S(2)}) collective-permute-start(bf16[128,512]{1,0:T(8,128)(2,1)S(1)} %get-tuple-element.138), channel_id=1, source_target_pairs={{0,2},{1,3},{2,0},{3,1},{4,6},{5,7},{6,4},{7,5},{8,10},{9,11},{10,... | collective-permute-start | bytes 393224 | tf_op jit(solution)/shard_map/ppermute | solution.py:533
  114.1 3.5 %inputgrad.1 = bf16[128,4096]{1,0:T(8,128)(2,1)} custom-call(bf16[256,256]{1,0:T(8,128)(2,1)S(1)} %copy-done.9, bf16[128,256]{1,0:T(8,128)(2,1)S(1)} %copy-done.10, bf16[128,4096]{1,0:T(8,128)(2,1)S(1)} %get-tuple-element.133.grad_b_ref, bf16[128,4096]{1,0:T(8,128)(2,1)S(1)} %collective-permute-done.28.later_ref, ...), custom_call_target="tpu_custom_call" | custom-call | flops 1073741824 | bytes 8585216 | tf_op jit(solution)/shard_map/inputgrad/pallas_call | solution.py:518
  117.6 7.6 %collective-permute-done.25.refs_0_ = bf16[128,512]{1,0:T(8,128)(2,1)S(1)} collective-permute-done((bf16[128,512]{1,0:T(8,128)(2,1)S(1)}, bf16[128,512]{1,0:T(8,128)(2,1)S(1)}, u32[]{:S(2)}, u32[]{:S(2)}) %collective-permute-start.25) | collective-permute-done | bytes 131104 | tf_op jit(solution)/shard_map/ppermute | solution.py:533
  125.2 4.9 %collective-permute-done.26.refs_1_ = bf16[128,512]{1,0:T(8,128)(2,1)S(1)} collective-permute-done((bf16[128,512]{1,0:T(8,128)(2,1)S(1)}, bf16[128,512]{1,0:T(8,128)(2,1)S(1)}, u32[]{:S(2)}, u32[]{:S(2)}) %collective-permute-start.26) | collective-permute-done | bytes 131104 | tf_op jit(solution)/shard_map/ppermute | solution.py:533
  130.2 0.7 midgrad.1
  (55 shorter events, 0.7 us)
Async XLA Ops:
  0.6 1.2 copy-start
  1.9 1.2 copy-start.6
  3.1 3.7 %copy-start.4 = (bf16[1,128,4096]{2,1,0:T(8,128)(2,1)S(1)}, bf16[1,128,4096]{2,1,0:T(8,128)(2,1)}, u32[]{:S(2)}) copy-start(bf16[1,128,4096]{2,1,0:T(8,128)(2,1)} %param.14) | copy-start | bytes 3145732
  3.3 22.7 %copy-start.5 = (bf16[1,128,4096]{2,1,0:T(8,128)(2,1)S(1)}, bf16[1,128,4096]{2,1,0:T(8,128)(2,1)}, u32[]{:S(2)}) copy-start(bf16[1,128,4096]{2,1,0:T(8,128)(2,1)} %param.19) | copy-start | bytes 3145732
  3.3 37.3 %collective-permute-start = (bf16[128,4096]{1,0:T(8,128)(2,1)S(1)}, bf16[128,4096]{1,0:T(8,128)(2,1)}, u32[]{:S(2)}, u32[]{:S(2)}) collective-permute-start(bf16[128,4096]{1,0:T(8,128)(2,1)S(1)} %mix.1.mixed_ref), channel_id=1, source_target_pairs={{0,1},{1,2},{2,3},{3,4},{4,5},{5,6},{6,7},{8,9},{9,10},{10,11},{11... | collective-permute-start | bytes 3145736 | tf_op jit(solution)/shard_map/ppermute | solution.py:26
  6.8 33.8 %copy-start.1 = (bf16[1,128,4096]{2,1,0:T(8,128)(2,1)S(1)}, bf16[1,128,4096]{2,1,0:T(8,128)(2,1)}, u32[]{:S(2)}) copy-start(bf16[1,128,4096]{2,1,0:T(8,128)(2,1)} %param.15) | copy-start | bytes 3145732
  6.8 33.8 %copy-start.2 = (bf16[1,128,4096]{2,1,0:T(8,128)(2,1)S(1)}, bf16[1,128,4096]{2,1,0:T(8,128)(2,1)}, u32[]{:S(2)}) copy-start(bf16[1,128,4096]{2,1,0:T(8,128)(2,1)} %param.18) | copy-start | bytes 3145732
  6.8 33.8 %copy-start.3 = (bf16[1,128,4096]{2,1,0:T(8,128)(2,1)S(1)}, bf16[1,128,4096]{2,1,0:T(8,128)(2,1)}, u32[]{:S(2)}) copy-start(bf16[1,128,4096]{2,1,0:T(8,128)(2,1)} %param.17) | copy-start | bytes 3145732
  6.8 33.8 %copy-start.9 = (bf16[256,256]{1,0:T(8,128)(2,1)S(1)}, bf16[256,256]{1,0:T(8,128)(2,1)}, u32[]{:S(2)}) copy-start(bf16[256,256]{1,0:T(8,128)(2,1)} %constant.16.clone.fwd_ref) | copy-start | bytes 393220
  6.8 33.8 %copy-start.11 = (bf16[128,256]{1,0:T(8,128)(2,1)S(1)}, bf16[128,256]{1,0:T(8,128)(2,1)}, u32[]{:S(2)}) copy-start(bf16[128,256]{1,0:T(8,128)(2,1)} %constant.17.clone.inv_ref) | copy-start | bytes 196612
  6.9 15.6 %collective-permute-start.1 = (bf16[128,2048]{1,0:T(8,128)(2,1)S(1)}, bf16[128,2048]{1,0:T(8,128)(2,1)S(1)}, u32[]{:S(2)}, u32[]{:S(2)}) collective-permute-start(bf16[128,2048]{1,0:T(8,128)(2,1)S(1)} %far.1), channel_id=1, source_target_pairs={{0,24},{8,0},{16,8},{24,16},{1,25},{9,1},{17,9},{25,17},{2,26},{10... | collective-permute-start | bytes 1572872 | tf_op jit(solution)/shard_map/ppermute | solution.py:20
  22.6 27.8 %collective-permute-start.2 = (bf16[128,2048]{1,0:T(8,128)(2,1)S(1)}, bf16[128,2048]{1,0:T(8,128)(2,1)S(1)}, u32[]{:S(2)}, u32[]{:S(2)}) collective-permute-start(bf16[128,2048]{1,0:T(8,128)(2,1)S(1)} %near.1), channel_id=1, source_target_pairs={{0,24},{8,0},{16,8},{24,16},{1,25},{9,1},{17,9},{25,17},{2,26},{10... | collective-permute-start | bytes 1572872 | tf_op jit(solution)/shard_map/ppermute | solution.py:20
  26.1 8.2 %collective-permute-start.4 = (bf16[128,512]{1,0:T(8,128)(2,1)S(1)}, bf16[128,512]{1,0:T(8,128)(2,1)S(1)}, u32[]{:S(2)}, u32[]{:S(2)}) collective-permute-start(bf16[128,512]{1,0:T(8,128)(2,1)S(1)} %get-tuple-element.93), channel_id=1, source_target_pairs={{0,6},{1,7},{2,4},{3,5},{4,2},{5,3},{6,0},{7,1},{8,14},{9,15},{10,... | collective-permute-start | bytes 393224 | tf_op jit(solution)/shard_map/ppermute | solution.py:533
  27.3 10.9 %collective-permute-start.3 = (bf16[128,512]{1,0:T(8,128)(2,1)S(1)}, bf16[128,512]{1,0:T(8,128)(2,1)S(1)}, u32[]{:S(2)}, u32[]{:S(2)}) collective-permute-start(bf16[128,512]{1,0:T(8,128)(2,1)S(1)} %get-tuple-element.92), channel_id=1, source_target_pairs={{0,7},{1,6},{2,5},{3,4},{4,3},{5,2},{6,1},{7,0},{8,15},{9,14},{10,... | collective-permute-start | bytes 393224 | tf_op jit(solution)/shard_map/ppermute | solution.py:533
  34.4 14.6 %collective-permute-start.6 = (bf16[128,512]{1,0:T(8,128)(2,1)S(1)}, bf16[128,512]{1,0:T(8,128)(2,1)S(1)}, u32[]{:S(2)}, u32[]{:S(2)}) collective-permute-start(bf16[128,512]{1,0:T(8,128)(2,1)S(1)} %get-tuple-element.95), channel_id=1, source_target_pairs={{0,4},{1,5},{2,6},{3,7},{4,0},{5,1},{6,2},{7,3},{8,12},{9,13},{10,... | collective-permute-start | bytes 393224 | tf_op jit(solution)/shard_map/ppermute | solution.py:533
  38.3 12.1 %collective-permute-start.5 = (bf16[128,512]{1,0:T(8,128)(2,1)S(1)}, bf16[128,512]{1,0:T(8,128)(2,1)S(1)}, u32[]{:S(2)}, u32[]{:S(2)}) collective-permute-start(bf16[128,512]{1,0:T(8,128)(2,1)S(1)} %get-tuple-element.94), channel_id=1, source_target_pairs={{0,5},{1,4},{2,7},{3,6},{4,1},{5,0},{6,3},{7,2},{8,13},{9,12},{10,... | collective-permute-start | bytes 393224 | tf_op jit(solution)/shard_map/ppermute | solution.py:533
  40.7 1.2 copy-start.8
  41.9 27.3 %copy-start.12 = (bf16[1,512,1024]{2,1,0:T(8,128)(2,1)S(1)}, bf16[1,512,1024]{2,1,0:T(8,128)(2,1)}, u32[]{:S(2)}) copy-start(bf16[1,512,1024]{2,1,0:T(8,128)(2,1)} %param.20) | copy-start | bytes 3145732
  41.9 27.3 %copy-start.13 = (bf16[512,512]{1,0:T(8,128)(2,1)S(1)}, bf16[512,512]{1,0:T(8,128)(2,1)}, u32[]{:S(2)}) copy-start(bf16[512,512]{1,0:T(8,128)(2,1)} %constant.20.clone.fwd_ref) | copy-start | bytes 1572868
  41.9 27.3 %copy-start.14 = (bf16[256,512]{1,0:T(8,128)(2,1)S(1)}, bf16[256,512]{1,0:T(8,128)(2,1)}, u32[]{:S(2)}) copy-start(bf16[256,512]{1,0:T(8,128)(2,1)} %constant.21.clone.inv_ref) | copy-start | bytes 786436
  50.4 7.0 %collective-permute-start.10 = (bf16[128,512]{1,0:T(8,128)(2,1)S(1)}, bf16[128,512]{1,0:T(8,128)(2,1)S(1)}, u32[]{:S(2)}, u32[]{:S(2)}) collective-permute-start(bf16[128,512]{1,0:T(8,128)(2,1)S(1)} %get-tuple-element.101), channel_id=1, source_target_pairs={{0,7},{1,6},{2,5},{3,4},{4,3},{5,2},{6,1},{7,0},{8,15},{9,14},{10,... | collective-permute-start | bytes 393224 | tf_op jit(solution)/shard_map/ppermute | solution.py:533
  52.6 9.0 %collective-permute-start.13 = (bf16[128,512]{1,0:T(8,128)(2,1)S(1)}, bf16[128,512]{1,0:T(8,128)(2,1)S(1)}, u32[]{:S(2)}, u32[]{:S(2)}) collective-permute-start(bf16[128,512]{1,0:T(8,128)(2,1)S(1)} %get-tuple-element.105), channel_id=1, source_target_pairs={{0,6},{1,7},{2,4},{3,5},{4,2},{5,3},{6,0},{7,1},{8,14},{9,15},{10,... | collective-permute-start | bytes 393224 | tf_op jit(solution)/shard_map/ppermute | solution.py:533
  54.5 9.7 %collective-permute-start.7 = (bf16[128,512]{1,0:T(8,128)(2,1)S(1)}, bf16[128,512]{1,0:T(8,128)(2,1)S(1)}, u32[]{:S(2)}, u32[]{:S(2)}) collective-permute-start(bf16[128,512]{1,0:T(8,128)(2,1)S(1)} %get-tuple-element.96), channel_id=1, source_target_pairs={{0,3},{1,2},{2,1},{3,0},{4,7},{5,6},{6,5},{7,4},{8,11},{9,10},{10,... | collective-permute-start | bytes 393224 | tf_op jit(solution)/shard_map/ppermute | solution.py:533
  54.6 14.6 %collective-permute-start.8 = (bf16[128,512]{1,0:T(8,128)(2,1)S(1)}, bf16[128,512]{1,0:T(8,128)(2,1)S(1)}, u32[]{:S(2)}, u32[]{:S(2)}) collective-permute-start(bf16[128,512]{1,0:T(8,128)(2,1)S(1)} %get-tuple-element.97), channel_id=1, source_target_pairs={{0,2},{1,3},{2,0},{3,1},{4,6},{5,7},{6,4},{7,5},{8,10},{9,11},{10,... | collective-permute-start | bytes 393224 | tf_op jit(solution)/shard_map/ppermute | solution.py:533
  55.9 13.3 %collective-permute-start.9 = (bf16[128,512]{1,0:T(8,128)(2,1)S(1)}, bf16[128,512]{1,0:T(8,128)(2,1)S(1)}, u32[]{:S(2)}, u32[]{:S(2)}) collective-permute-start(bf16[128,512]{1,0:T(8,128)(2,1)S(1)} %get-tuple-element.98), channel_id=1, source_target_pairs={{0,1},{1,0},{2,3},{3,2},{4,5},{5,4},{6,7},{7,6},{8,9},{9,8},{10,11... | collective-permute-start | bytes 393224 | tf_op jit(solution)/shard_map/ppermute | solution.py:533
  57.4 16.6 %collective-permute-start.11 = (bf16[128,512]{1,0:T(8,128)(2,1)S(1)}, bf16[128,512]{1,0:T(8,128)(2,1)S(1)}, u32[]{:S(2)}, u32[]{:S(2)}) collective-permute-start(bf16[128,512]{1,0:T(8,128)(2,1)S(1)} %get-tuple-element.102), channel_id=1, source_target_pairs={{0,5},{1,4},{2,7},{3,6},{4,1},{5,0},{6,3},{7,2},{8,13},{9,12},{10,... | collective-permute-start | bytes 393224 | tf_op jit(solution)/shard_map/ppermute | solution.py:533
  61.6 13.4 %collective-permute-start.14 = (bf16[128,512]{1,0:T(8,128)(2,1)S(1)}, bf16[128,512]{1,0:T(8,128)(2,1)S(1)}, u32[]{:S(2)}, u32[]{:S(2)}) collective-permute-start(bf16[128,512]{1,0:T(8,128)(2,1)S(1)} %get-tuple-element.106), channel_id=1, source_target_pairs={{0,4},{1,5},{2,6},{3,7},{4,0},{5,1},{6,2},{7,3},{8,12},{9,13},{10,... | collective-permute-start | bytes 393224 | tf_op jit(solution)/shard_map/ppermute | solution.py:533
  75.0 7.9 %collective-permute-start.15 = (bf16[128,512]{1,0:T(8,128)(2,1)S(1)}, bf16[128,512]{1,0:T(8,128)(2,1)S(1)}, u32[]{:S(2)}, u32[]{:S(2)}) collective-permute-start(bf16[128,512]{1,0:T(8,128)(2,1)S(1)} %get-tuple-element.107), channel_id=1, source_target_pairs={{0,6},{1,7},{2,4},{3,5},{4,2},{5,3},{6,0},{7,1},{8,14},{9,15},{10,... | collective-permute-start | bytes 393224 | tf_op jit(solution)/shard_map/ppermute | solution.py:533
  77.1 10.0 %collective-permute-start.12 = (bf16[128,512]{1,0:T(8,128)(2,1)S(1)}, bf16[128,512]{1,0:T(8,128)(2,1)S(1)}, u32[]{:S(2)}, u32[]{:S(2)}) collective-permute-start(bf16[128,512]{1,0:T(8,128)(2,1)S(1)} %get-tuple-element.103), channel_id=1, source_target_pairs={{0,7},{1,6},{2,5},{3,4},{4,3},{5,2},{6,1},{7,0},{8,15},{9,14},{10,... | collective-permute-start | bytes 393224 | tf_op jit(solution)/shard_map/ppermute | solution.py:533
  78.2 13.2 %collective-permute-start.21 = (bf16[128,512]{1,0:T(8,128)(2,1)S(1)}, bf16[128,512]{1,0:T(8,128)(2,1)S(1)}, u32[]{:S(2)}, u32[]{:S(2)}) collective-permute-start(bf16[128,512]{1,0:T(8,128)(2,1)S(1)} %get-tuple-element.121), channel_id=1, source_target_pairs={{0,3},{1,2},{2,1},{3,0},{4,7},{5,6},{6,5},{7,4},{8,11},{9,10},{10,... | collective-permute-start | bytes 393224 | tf_op jit(solution)/shard_map/ppermute | solution.py:533
  78.3 16.1 %collective-permute-start.22 = (bf16[128,512]{1,0:T(8,128)(2,1)S(1)}, bf16[128,512]{1,0:T(8,128)(2,1)S(1)}, u32[]{:S(2)}, u32[]{:S(2)}) collective-permute-start(bf16[128,512]{1,0:T(8,128)(2,1)S(1)} %get-tuple-element.122), channel_id=1, source_target_pairs={{0,2},{1,3},{2,0},{3,1},{4,6},{5,7},{6,4},{7,5},{8,10},{9,11},{10,... | collective-permute-start | bytes 393224 | tf_op jit(solution)/shard_map/ppermute | solution.py:533
  80.6 13.8 %collective-permute-start.23 = (bf16[128,512]{1,0:T(8,128)(2,1)S(1)}, bf16[128,512]{1,0:T(8,128)(2,1)S(1)}, u32[]{:S(2)}, u32[]{:S(2)}) collective-permute-start(bf16[128,512]{1,0:T(8,128)(2,1)S(1)} %get-tuple-element.123), channel_id=1, source_target_pairs={{0,1},{1,0},{2,3},{3,2},{4,5},{5,4},{6,7},{7,6},{8,9},{9,8},{10,11... | collective-permute-start | bytes 393224 | tf_op jit(solution)/shard_map/ppermute | solution.py:533
  82.9 17.1 %collective-permute-start.17 = (bf16[128,512]{1,0:T(8,128)(2,1)S(1)}, bf16[128,512]{1,0:T(8,128)(2,1)S(1)}, u32[]{:S(2)}, u32[]{:S(2)}) collective-permute-start(bf16[128,512]{1,0:T(8,128)(2,1)S(1)} %get-tuple-element.111), channel_id=1, source_target_pairs={{0,4},{1,5},{2,6},{3,7},{4,0},{5,1},{6,2},{7,3},{8,12},{9,13},{10,... | collective-permute-start | bytes 393224 | tf_op jit(solution)/shard_map/ppermute | solution.py:533
  87.1 13.0 %collective-permute-start.16 = (bf16[128,512]{1,0:T(8,128)(2,1)S(1)}, bf16[128,512]{1,0:T(8,128)(2,1)S(1)}, u32[]{:S(2)}, u32[]{:S(2)}) collective-permute-start(bf16[128,512]{1,0:T(8,128)(2,1)S(1)} %get-tuple-element.109), channel_id=1, source_target_pairs={{0,5},{1,4},{2,7},{3,6},{4,1},{5,0},{6,3},{7,2},{8,13},{9,12},{10,... | collective-permute-start | bytes 393224 | tf_op jit(solution)/shard_map/ppermute | solution.py:533
  91.4 8.6 %collective-permute-start.18 = (bf16[128,512]{1,0:T(8,128)(2,1)S(1)}, bf16[128,512]{1,0:T(8,128)(2,1)S(1)}, u32[]{:S(2)}, u32[]{:S(2)}) collective-permute-start(bf16[128,512]{1,0:T(8,128)(2,1)S(1)} %get-tuple-element.116), channel_id=1, source_target_pairs={{0,3},{1,2},{2,1},{3,0},{4,7},{5,6},{6,5},{7,4},{8,11},{9,10},{10,... | collective-permute-start | bytes 393224 | tf_op jit(solution)/shard_map/ppermute | solution.py:533
  94.3 7.8 %collective-permute-start.19 = (bf16[128,512]{1,0:T(8,128)(2,1)S(1)}, bf16[128,512]{1,0:T(8,128)(2,1)S(1)}, u32[]{:S(2)}, u32[]{:S(2)}) collective-permute-start(bf16[128,512]{1,0:T(8,128)(2,1)S(1)} %get-tuple-element.117), channel_id=1, source_target_pairs={{0,2},{1,3},{2,0},{3,1},{4,6},{5,7},{6,4},{7,5},{8,10},{9,11},{10,... | collective-permute-start | bytes 393224 | tf_op jit(solution)/shard_map/ppermute | solution.py:533
  94.3 7.8 %collective-permute-start.20 = (bf16[128,512]{1,0:T(8,128)(2,1)S(1)}, bf16[128,512]{1,0:T(8,128)(2,1)S(1)}, u32[]{:S(2)}, u32[]{:S(2)}) collective-permute-start(bf16[128,512]{1,0:T(8,128)(2,1)S(1)} %get-tuple-element.118), channel_id=1, source_target_pairs={{0,1},{1,0},{2,3},{3,2},{4,5},{5,4},{6,7},{7,6},{8,9},{9,8},{10,11... | collective-permute-start | bytes 393224 | tf_op jit(solution)/shard_map/ppermute | solution.py:533
  100.0 4.2 %copy-start.15 = (bf16[128,256]{1,0:T(8,128)(2,1)S(1)}, bf16[128,256]{1,0:T(8,128)(2,1)}, u32[]{:S(2)}) copy-start(bf16[128,256]{1,0:T(8,128)(2,1)} %constant.19.clone.inv_ref) | copy-start | bytes 196612
  102.8 11.3 %collective-permute-start.28 = (bf16[128,4096]{1,0:T(8,128)(2,1)S(1)}, bf16[128,4096]{1,0:T(8,128)(2,1)S(1)}, u32[]{:S(2)}, u32[]{:S(2)}) collective-permute-start(bf16[128,4096]{1,0:T(8,128)(2,1)S(1)} %get-tuple-element.133.grad_b_ref), channel_id=1, source_target_pairs={{1,0},{2,1},{3,2},{4,3},{5,4},{6,5},{7,6},{9,8},{10,9},{11,10},{12... | collective-permute-start | bytes 3145736 | tf_op jit(solution)/shard_map/ppermute | solution.py:26
  104.3 9.8 %copy-start.7 = (bf16[1,128,4096]{2,1,0:T(8,128)(2,1)S(1)}, bf16[1,128,4096]{2,1,0:T(8,128)(2,1)}, u32[]{:S(2)}) copy-start(bf16[1,128,4096]{2,1,0:T(8,128)(2,1)} %param.16) | copy-start | bytes 3145732
  104.3 9.8 %copy-start.10 = (bf16[128,256]{1,0:T(8,128)(2,1)S(1)}, bf16[128,256]{1,0:T(8,128)(2,1)}, u32[]{:S(2)}) copy-start(bf16[128,256]{1,0:T(8,128)(2,1)} %constant.18.clone.inv_ref) | copy-start | bytes 196612
  106.7 2.7 %collective-permute-start.24 = (bf16[4,128,512]{2,1,0:T(8,128)(2,1)S(1)}, bf16[4,128,512]{2,1,0:T(8,128)(2,1)S(1)}, u32[]{:S(2)}, u32[]{:S(2)}) collective-permute-start(bf16[4,128,512]{2,1,0:T(8,128)(2,1)S(1)} %get-tuple-element.135), channel_id=1, source_target_pairs={{0,1},{1,0},{2,3},{3,2},{4,5},{5,4},{6,7},{7,6},{8,9},{9,8},{10,11... | collective-permute-start | bytes 1572872 | tf_op jit(solution)/shard_map/ppermute | solution.py:533
  109.6 15.6 %collective-permute-start.25 = (bf16[128,512]{1,0:T(8,128)(2,1)S(1)}, bf16[128,512]{1,0:T(8,128)(2,1)S(1)}, u32[]{:S(2)}, u32[]{:S(2)}) collective-permute-start(bf16[128,512]{1,0:T(8,128)(2,1)S(1)} %get-tuple-element.136), channel_id=1, source_target_pairs={{0,6},{1,7},{2,4},{3,5},{4,2},{5,3},{6,0},{7,1},{8,14},{9,15},{10,... | collective-permute-start | bytes 393224 | tf_op jit(solution)/shard_map/ppermute | solution.py:533
  111.7 18.5 %collective-permute-start.26 = (bf16[128,512]{1,0:T(8,128)(2,1)S(1)}, bf16[128,512]{1,0:T(8,128)(2,1)S(1)}, u32[]{:S(2)}, u32[]{:S(2)}) collective-permute-start(bf16[128,512]{1,0:T(8,128)(2,1)S(1)} %get-tuple-element.137), channel_id=1, source_target_pairs={{0,4},{1,5},{2,6},{3,7},{4,0},{5,1},{6,2},{7,3},{8,12},{9,13},{10,... | collective-permute-start | bytes 393224 | tf_op jit(solution)/shard_map/ppermute | solution.py:533
  112.3 17.8 %collective-permute-start.27 = (bf16[128,512]{1,0:T(8,128)(2,1)S(1)}, bf16[128,512]{1,0:T(8,128)(2,1)S(1)}, u32[]{:S(2)}, u32[]{:S(2)}) collective-permute-start(bf16[128,512]{1,0:T(8,128)(2,1)S(1)} %get-tuple-element.138), channel_id=1, source_target_pairs={{0,2},{1,3},{2,0},{3,1},{4,6},{5,7},{6,4},{7,5},{8,10},{9,11},{10,... | collective-permute-start | bytes 393224 | tf_op jit(solution)/shard_map/ppermute | solution.py:533

commit v8 on v7

--- a/solution.py
+++ b/solution.py
@@ -541,12 +541,10 @@
     return [swapped(piece, first + k) if first + k else piece for k, piece in enumerate(pieces)]
 
 
-def in_turn(pieces, *before):
-    came_7 = swapped(after(pieces[3], before[1]), 7)
-    came_6 = swapped(after(pieces[2], before[0]), 6)
-    came_5 = swapped(after(pieces[1], came_7), 5)
-    came_4 = swapped(after(pieces[0], came_6), 4)
-    return [came_4, came_5, came_6, came_7]
+def far_pair(pieces, first, *before):
+    if before:
+        pieces = [after(piece, other) for piece, other in zip(pieces, before)]
+    return exchanged(pieces, first)
 
 
 def by_permutes(
@@ -601,30 +599,33 @@
     far_z = local(
         functools.partial(pieces_z_kernel, beta, half), [piece] * half, [me, far, gate_out], few, name="farz"
     )
+    near_z = local(
+        functools.partial(pieces_z_kernel, beta, 0), [piece] * half, [me, near, gate_out], few, name="nearz"
+    )
     signal, filt, *pieces_w = local(
         functools.partial(pieces_branch_kernel, beta),
         [((span, channels), BF16)] * 2 + [piece] * devices,
-        [me, fwd, inv_conv, after(earlier, far_z), mixed_in, filter_taps, inputs, gate_mid, gate_long],
+        [me, fwd, inv_conv, after(earlier, near_z), mixed_in, filter_taps, inputs, gate_mid, gate_long],
         mid_flops, name="branch",
     )
-    far_z = in_turn(far_z, far_z, far_z)
-    near = after(near, pieces_w)
-    near_z = local(
-        functools.partial(pieces_z_kernel, beta, 0), [piece] * half, [me, near, gate_out], few, name="nearz"
-    )
-    far_w = in_turn(pieces_w[half:], far_z[0], far_z[1])
-    pieces_z = exchanged(near_z) + far_z
+    z_6, z_7 = far_pair(far_z[2:], 6)
+    z_4, z_5 = far_pair(far_z[:2], 4, z_6, z_7)
+    near_z = exchanged(near_z)
+    pieces_z = near_z + [z_4, z_5, z_6, z_7]
+    w_6, w_7 = far_pair(pieces_w[6:], 6, (z_4, near_z), (z_5, near_z))
+    near_w = exchanged(pieces_w[:half])
     *pieces_g, channel_z = local(
         functools.partial(pieces_grad_w_kernel, blocks, devices),
         [piece] * devices + [((seq_len, owned), BF16)],
         [me, long_fwd, long_inv, long_filter[0], *pieces_z[::-1]], long_flops,
         [spectrum, spectrum, joint, staged], name="gradw",
     )
-    near_w = after(pieces_w[:half], far_w[2], far_w[3], pieces_g)
-    pieces_w = exchanged(near_w) + far_w
-    far_g = in_turn(pieces_g[half:], far_w[0], far_w[1])
-    near_g = exchanged(after(pieces_g[:half], far_g[2], far_g[3]))
-    pieces_g = far_g[::-1] + near_g[::-1]
+    w_4, w_5 = far_pair(pieces_w[4:6], 4, (w_6, near_w, pieces_g[0]), (w_7, near_w, pieces_g[0]))
+    pieces_w = near_w + [w_4, w_5, w_6, w_7]
+    near_g = exchanged(pieces_g[:half])
+    g_6, g_7 = far_pair(pieces_g[6:], 6, (w_4, near_g), (w_5, near_g))
+    g_4, g_5 = far_pair(pieces_g[4:6], 4, g_6, g_7)
+    pieces_g = [g_7, g_6, g_5, g_4] + near_g[::-1]
     long_grad = local(
         functools.partial(pieces_long_grad_kernel, blocks, scale, devices), [((owned, seq_len), BF16)],
         [me, long_fwd, long_inv, channel_z, *pieces_w[::-1]], long_flops,

time: 131 us -> 125 us (0.954)
  waiting for transfers between devices: 56 us -> 50.9 us
    ppermute x2, waiting for transfers between devices: 12.3 us -> 7.85 us  [passed_along(): return lax.ppermute(value, axis, pairs)]
    ppermute x25, starting transfers between devices: 35.8 us -> 37.9 us  [swapped(): return lax.ppermute(array, 'ctx', [(i, i ^ k) for i in range(count)])]
    ppermute x2, starting transfers between devices: 4.96 us -> 3.26 us  [shifted(): return lax.ppermute(array, axis, pairs)]
    pallas_call x13, Pallas kernels: 22.8 us -> 21.5 us  [local(): pl.pallas_call(body, in_specs=specs, out_specs=[pl.BlockSpec(memory_space...]
where the time goes in v8:
time: 125 us; the launch traced here: 124 us
  waiting for transfers between devices  50.9 us (41%)
  starting transfers between devices  48.5 us (39%)
  Pallas kernels  21.5 us (17%)
  local copies, waits for them, and re-layouts  2.61 us (2%)
    ppermute x25, waiting for transfers between devices, swapped(): return lax.ppermute(array, 'ctx', [(i, i ^ k) for i in range(count)])  43 us
    ppermute x25, starting transfers between devices, swapped(): return lax.ppermute(array, 'ctx', [(i, i ^ k) for i in range(count)])  37.9 us
    pallas_call x13, Pallas kernels, local(): pl.pallas_call(body, in_specs=specs, out_specs=[pl.BlockSpec(memory_space...  21.5 us
    ppermute x2, waiting for transfers between devices, passed_along(): return lax.ppermute(value, axis, pairs)  7.85 us
    ppermute x2, starting transfers between devices, passed_along(): return lax.ppermute(value, axis, pairs)  7.38 us
    ppermute x2, starting transfers between devices, shifted(): return lax.ppermute(array, axis, pairs)  3.26 us
    unnamed x32, local copies, waits for them, and re-layouts  2.61 us
  transfers between devices with their start and end apart: 29, of which 15 were waited for; matrix products, arithmetic and copies ran while one was open for 0% of the time, Pallas kernels for 16%

profile of v8, /device:TPU:0, one launch (start us, length us, event | category | flops | bytes accessed | tf_op | source)
XLA Modules:
  0.0 124.3 jit_solution(5917038725142618567)
XLA Ops:
  0.7 1.3 %copy-done.3 = bf16[1,128,4096]{2,1,0:T(8,128)(2,1)S(1)} copy-done((bf16[1,128,4096]{2,1,0:T(8,128)(2,1)S(1)}, bf16[1,128,4096]{2,1,0:T(8,128)(2,1)}, u32[]{:S(2)}) %copy-start.3) | copy-done | bytes 1048600
  2.0 3.9 %collective-permute-start.1 = (bf16[128,2048]{1,0:T(8,128)(2,1)S(1)}, bf16[128,2048]{1,0:T(8,128)(2,1)S(1)}, u32[]{:S(2)}, u32[]{:S(2)}) collective-permute-start(bf16[128,2048]{1,0:T(8,128)(2,1)S(1)} %far.1), channel_id=1, source_target_pairs={{0,24},{8,0},{16,8},{24,16},{1,25},{9,1},{17,9},{25,17},{2,26},{10... | collective-permute-start | bytes 1572872 | tf_op jit(solution)/shard_map/ppermute | solution.py:20
  5.9 1.2 copy-done.6
  7.2 0.2 mix.1.mixed_ref
  7.5 1.8 %collective-permute-start = (bf16[128,4096]{1,0:T(8,128)(2,1)S(1)}, bf16[128,4096]{1,0:T(8,128)(2,1)S(1)}, u32[]{:S(2)}, u32[]{:S(2)}) collective-permute-start(bf16[128,4096]{1,0:T(8,128)(2,1)S(1)} %mix.1.mixed_ref), channel_id=1, source_target_pairs={{0,1},{1,2},{2,3},{3,4},{4,5},{5,6},{6,7},{8,9},{9,10},{10,11},{11... | collective-permute-start | bytes 3145736 | tf_op jit(solution)/shard_map/ppermute | solution.py:26
  9.3 7.9 %collective-permute-done.1.adjoint_ref.far_ref = bf16[128,2048]{1,0:T(8,128)(2,1)S(1)} collective-permute-done((bf16[128,2048]{1,0:T(8,128)(2,1)S(1)}, bf16[128,2048]{1,0:T(8,128)(2,1)S(1)}, u32[]{:S(2)}, u32[]{:S(2)}) %collective-permute-start.1) | collective-permute-done | bytes 524320 | tf_op jit(solution)/shard_map/ppermute | solution.py:20
  17.2 3.4 %collective-permute-start.2 = (bf16[128,2048]{1,0:T(8,128)(2,1)S(1)}, bf16[128,2048]{1,0:T(8,128)(2,1)S(1)}, u32[]{:S(2)}, u32[]{:S(2)}) collective-permute-start(bf16[128,2048]{1,0:T(8,128)(2,1)S(1)} %near.1), channel_id=1, source_target_pairs={{0,24},{8,0},{16,8},{24,16},{1,25},{9,1},{17,9},{25,17},{2,26},{10... | collective-permute-start | bytes 1572872 | tf_op jit(solution)/shard_map/ppermute | solution.py:20
  20.8 3.7 %collective-permute-start.4 = (bf16[128,512]{1,0:T(8,128)(2,1)S(1)}, bf16[128,512]{1,0:T(8,128)(2,1)S(1)}, u32[]{:S(2)}, u32[]{:S(2)}) collective-permute-start(bf16[128,512]{1,0:T(8,128)(2,1)S(1)} %get-tuple-element.73), channel_id=1, source_target_pairs={{0,6},{1,7},{2,4},{3,5},{4,2},{5,3},{6,0},{7,1},{8,14},{9,15},{10,... | collective-permute-start | bytes 393224 | tf_op jit(solution)/shard_map/ppermute | solution.py:533
  24.4 3.5 %collective-permute-done.4.refs_1_ = bf16[128,512]{1,0:T(8,128)(2,1)S(1)} collective-permute-done((bf16[128,512]{1,0:T(8,128)(2,1)S(1)}, bf16[128,512]{1,0:T(8,128)(2,1)S(1)}, u32[]{:S(2)}, u32[]{:S(2)}) %collective-permute-start.4) | collective-permute-done | bytes 131104 | tf_op jit(solution)/shard_map/ppermute | solution.py:533
  28.0 7.2 %collective-permute-start.6 = (bf16[128,512]{1,0:T(8,128)(2,1)S(1)}, bf16[128,512]{1,0:T(8,128)(2,1)S(1)}, u32[]{:S(2)}, u32[]{:S(2)}) collective-permute-start(bf16[128,512]{1,0:T(8,128)(2,1)S(1)} %get-tuple-element.77), channel_id=1, source_target_pairs={{0,4},{1,5},{2,6},{3,7},{4,0},{5,1},{6,2},{7,3},{8,12},{9,13},{10,... | collective-permute-start | bytes 393224 | tf_op jit(solution)/shard_map/ppermute | solution.py:533
  35.2 0.2 nearz.1
  35.4 0.8 collective-permute-start.8
  36.2 1.0 collective-permute-start.9
  37.3 0.2 collective-permute-start.5
  37.5 3.0 %branch.1 = (bf16[256,4096]{1,0:T(8,128)(2,1)S(1)}, bf16[256,4096]{1,0:T(8,128)(2,1)S(1)}, bf16[128,512]{1,0:T(8,128)(2,1)S(1)}, bf16[128,512]{1,0:T(8,128)(2,1)...) custom-call(s32[1]{0:T(128)} %bitcast.me_ref, ...), custom_call_target="tpu_custom_call" | custom-call | flops 1073741824 | bytes 11730948 | tf_op jit(solution)/shard_map/branch/pallas_call | solution.py:518
  40.6 0.6 collective-permute-done.6.refs_3_
  41.2 5.1 %collective-permute-done.7.refs_4_ = bf16[128,512]{1,0:T(8,128)(2,1)S(1)} collective-permute-done((bf16[128,512]{1,0:T(8,128)(2,1)S(1)}, bf16[128,512]{1,0:T(8,128)(2,1)S(1)}, u32[]{:S(2)}, u32[]{:S(2)}) %collective-permute-start.7) | collective-permute-done | bytes 131104 | tf_op jit(solution)/shard_map/ppermute | solution.py:533
  46.3 2.1 %collective-permute-done.8.refs_5_ = bf16[128,512]{1,0:T(8,128)(2,1)S(1)} collective-permute-done((bf16[128,512]{1,0:T(8,128)(2,1)S(1)}, bf16[128,512]{1,0:T(8,128)(2,1)S(1)}, u32[]{:S(2)}, u32[]{:S(2)}) %collective-permute-start.8) | collective-permute-done | bytes 131104 | tf_op jit(solution)/shard_map/ppermute | solution.py:533
  48.4 0.9 collective-permute-start.19
  49.4 2.4 %collective-permute-start.10 = (bf16[128,512]{1,0:T(8,128)(2,1)S(1)}, bf16[128,512]{1,0:T(8,128)(2,1)S(1)}, u32[]{:S(2)}, u32[]{:S(2)}) collective-permute-start(bf16[128,512]{1,0:T(8,128)(2,1)S(1)} %get-tuple-element.81), channel_id=1, source_target_pairs={{0,7},{1,6},{2,5},{3,4},{4,3},{5,2},{6,1},{7,0},{8,15},{9,14},{10,... | collective-permute-start | bytes 393224 | tf_op jit(solution)/shard_map/ppermute | solution.py:533
  51.7 4.7 %gradw.1 = (bf16[128,512]{1,0:T(8,128)(2,1)S(1)}, bf16[128,512]{1,0:T(8,128)(2,1)S(1)}, bf16[128,512]{1,0:T(8,128)(2,1)S(1)}, bf16[128,512]{1,0:T(8,128)(2,1)S(1...) custom-call(s32[1]{0:T(128)} %bitcast.me_ref, ...), custom_call_target="tpu_custom_call" | custom-call | flops 3221225472 | bytes 4980740 | tf_op jit(solution)/shard_map/gradw/pallas_call | solution.py:518
  56.5 0.7 collective-permute-start.15
  57.2 2.6 %collective-permute-done.13.refs_4_ = bf16[128,512]{1,0:T(8,128)(2,1)S(1)} collective-permute-done((bf16[128,512]{1,0:T(8,128)(2,1)S(1)}, bf16[128,512]{1,0:T(8,128)(2,1)S(1)}, u32[]{:S(2)}, u32[]{:S(2)}) %collective-permute-start.13) | collective-permute-done | bytes 131104 | tf_op jit(solution)/shard_map/ppermute | solution.py:533
  59.8 2.2 %collective-permute-start.20 = (bf16[128,512]{1,0:T(8,128)(2,1)S(1)}, bf16[128,512]{1,0:T(8,128)(2,1)S(1)}, u32[]{:S(2)}, u32[]{:S(2)}) collective-permute-start(bf16[128,512]{1,0:T(8,128)(2,1)S(1)} %get-tuple-element.96), channel_id=1, source_target_pairs={{0,4},{1,5},{2,6},{3,7},{4,0},{5,1},{6,2},{7,3},{8,12},{9,13},{10,... | collective-permute-start | bytes 393224 | tf_op jit(solution)/shard_map/ppermute | solution.py:533
  62.0 1.8 %collective-permute-start.14 = (bf16[128,512]{1,0:T(8,128)(2,1)S(1)}, bf16[128,512]{1,0:T(8,128)(2,1)S(1)}, u32[]{:S(2)}, u32[]{:S(2)}) collective-permute-start(bf16[128,512]{1,0:T(8,128)(2,1)S(1)} %get-tuple-element.87), channel_id=1, source_target_pairs={{0,5},{1,4},{2,7},{3,6},{4,1},{5,0},{6,3},{7,2},{8,13},{9,12},{10,... | collective-permute-start | bytes 393224 | tf_op jit(solution)/shard_map/ppermute | solution.py:533
  63.8 2.6 %collective-permute-done.17.refs_4_ = bf16[128,512]{1,0:T(8,128)(2,1)S(1)} collective-permute-done((bf16[128,512]{1,0:T(8,128)(2,1)S(1)}, bf16[128,512]{1,0:T(8,128)(2,1)S(1)}, u32[]{:S(2)}, u32[]{:S(2)}) %collective-permute-start.17) | collective-permute-done | bytes 131104 | tf_op jit(solution)/shard_map/ppermute | solution.py:533
  66.5 6.2 %collective-permute-done.20.refs_3_ = bf16[128,512]{1,0:T(8,128)(2,1)S(1)} collective-permute-done((bf16[128,512]{1,0:T(8,128)(2,1)S(1)}, bf16[128,512]{1,0:T(8,128)(2,1)S(1)}, u32[]{:S(2)}, u32[]{:S(2)}) %collective-permute-start.20) | collective-permute-done | bytes 131104 | tf_op jit(solution)/shard_map/ppermute | solution.py:533
  72.7 1.2 %collective-permute-start.21 = (bf16[128,512]{1,0:T(8,128)(2,1)S(1)}, bf16[128,512]{1,0:T(8,128)(2,1)S(1)}, u32[]{:S(2)}, u32[]{:S(2)}) collective-permute-start(bf16[128,512]{1,0:T(8,128)(2,1)S(1)} %get-tuple-element.97), channel_id=1, source_target_pairs={{0,6},{1,7},{2,4},{3,5},{4,2},{5,3},{6,0},{7,1},{8,14},{9,15},{10,... | collective-permute-start | bytes 393224 | tf_op jit(solution)/shard_map/ppermute | solution.py:533
  73.9 0.7 collective-permute-done.14.refs_2_
  74.6 2.9 %collective-permute-start.18 = (bf16[128,512]{1,0:T(8,128)(2,1)S(1)}, bf16[128,512]{1,0:T(8,128)(2,1)S(1)}, u32[]{:S(2)}, u32[]{:S(2)}) collective-permute-start(bf16[128,512]{1,0:T(8,128)(2,1)S(1)} %get-tuple-element.91), channel_id=1, source_target_pairs={{0,7},{1,6},{2,5},{3,4},{4,3},{5,2},{6,1},{7,0},{8,15},{9,14},{10,... | collective-permute-start | bytes 393224 | tf_op jit(solution)/shard_map/ppermute | solution.py:533
  77.6 1.9 %collective-permute-done.21.refs_1_ = bf16[128,512]{1,0:T(8,128)(2,1)S(1)} collective-permute-done((bf16[128,512]{1,0:T(8,128)(2,1)S(1)}, bf16[128,512]{1,0:T(8,128)(2,1)S(1)}, u32[]{:S(2)}, u32[]{:S(2)}) %collective-permute-start.21) | collective-permute-done | bytes 131104 | tf_op jit(solution)/shard_map/ppermute | solution.py:533
  79.5 4.8 %collective-permute-start.23 = (bf16[128,512]{1,0:T(8,128)(2,1)S(1)}, bf16[128,512]{1,0:T(8,128)(2,1)S(1)}, u32[]{:S(2)}, u32[]{:S(2)}) collective-permute-start(bf16[128,512]{1,0:T(8,128)(2,1)S(1)} %get-tuple-element.101), channel_id=1, source_target_pairs={{0,4},{1,5},{2,6},{3,7},{4,0},{5,1},{6,2},{7,3},{8,12},{9,13},{10,... | collective-permute-start | bytes 393224 | tf_op jit(solution)/shard_map/ppermute | solution.py:533
  84.3 2.3 %collective-permute-start.22 = (bf16[128,512]{1,0:T(8,128)(2,1)S(1)}, bf16[128,512]{1,0:T(8,128)(2,1)S(1)}, u32[]{:S(2)}, u32[]{:S(2)}) collective-permute-start(bf16[128,512]{1,0:T(8,128)(2,1)S(1)} %get-tuple-element.99), channel_id=1, source_target_pairs={{0,5},{1,4},{2,7},{3,6},{4,1},{5,0},{6,3},{7,2},{8,13},{9,12},{10,... | collective-permute-start | bytes 393224 | tf_op jit(solution)/shard_map/ppermute | solution.py:533
  86.5 5.7 %longgrad.1 = bf16[512,1024]{1,0:T(8,128)(2,1)} custom-call(s32[1]{0:T(128)} %bitcast.me_ref, bf16[512,512]{1,0:T(8,128)(2,1)S(1)} %copy-done.13, bf16[256,512]{1,0:T(8,128)(2,1)S(1)} %copy-done.14, bf16[1024,512]{1,0:T(8,128)(2,1)S(1)} %get-tuple-element.102.grad_ref, bf16[128,512]{1,0:T(8,128)(2,1)S(1)} %collective-permute-done.10.refs_0_, ...), custom_call_target="tpu_custom_call" | custom-call | flops 3221225472 | bytes 3932164 | tf_op jit(solution)/shard_map/longgrad/pallas_call | solution.py:518
  92.2 3.0 %collective-permute-done.23.refs_3_ = bf16[128,512]{1,0:T(8,128)(2,1)S(1)} collective-permute-done((bf16[128,512]{1,0:T(8,128)(2,1)S(1)}, bf16[128,512]{1,0:T(8,128)(2,1)S(1)}, u32[]{:S(2)}, u32[]{:S(2)}) %collective-permute-start.23) | collective-permute-done | bytes 131104 | tf_op jit(solution)/shard_map/ppermute | solution.py:533
  95.2 2.0 %collective-permute-done.22.refs_2_ = bf16[128,512]{1,0:T(8,128)(2,1)S(1)} collective-permute-done((bf16[128,512]{1,0:T(8,128)(2,1)S(1)}, bf16[128,512]{1,0:T(8,128)(2,1)S(1)}, u32[]{:S(2)}, u32[]{:S(2)}) %collective-permute-start.22) | collective-permute-done | bytes 131104 | tf_op jit(solution)/shard_map/ppermute | solution.py:533
  97.1 0.6 gradb.1
  97.7 1.5 %collective-permute-start.28 = (bf16[128,4096]{1,0:T(8,128)(2,1)S(1)}, bf16[128,4096]{1,0:T(8,128)(2,1)S(1)}, u32[]{:S(2)}, u32[]{:S(2)}) collective-permute-start(bf16[128,4096]{1,0:T(8,128)(2,1)S(1)} %get-tuple-element.111.grad_b_ref), channel_id=1, source_target_pairs={{1,0},{2,1},{3,2},{4,3},{5,4},{6,5},{7,6},{9,8},{10,9},{11,10},{12... | collective-permute-start | bytes 3145736 | tf_op jit(solution)/shard_map/ppermute | solution.py:26
  99.2 2.4 %taps.1 = (bf16[4,128,512]{2,1,0:T(8,128)(2,1)S(1)}, bf16[4,128,512]{2,1,0:T(8,128)(2,1)S(1)}) custom-call(s32[1]{0:T(128)} %bitcast.me_ref, bf16[256,256]{1,0:T(8,128)(2,1)S(1)} %copy-done.9, bf16[128,256]{1,0:T(8,128)(2,1)S(1)} %copy-done.15, bf16[256,4096]{1,0:T(8,128)(2,1)S(1)} %get-tuple-element.71.signal_ref, ...), custom_call_target="tpu_custom_call" | custom-call | flops 1073741824 | bytes 4390916 | tf_op jit(solution)/shard_map/taps/pallas_call | solution.py:518
  101.7 1.2 collective-permute-start.24
  102.8 1.5 %collective-permute-done.24.came_ref = bf16[4,128,512]{2,1,0:T(8,128)(2,1)S(1)} collective-permute-done((bf16[4,128,512]{2,1,0:T(8,128)(2,1)S(1)}, bf16[4,128,512]{2,1,0:T(8,128)(2,1)S(1)}, u32[]{:S(2)}, u32[]{:S(2)}) %collective-permute-start.24) | collective-permute-done | bytes 524320 | tf_op jit(solution)/shard_map/ppermute | solution.py:533
  104.5 1.3 %collective-permute-start.25 = (bf16[128,512]{1,0:T(8,128)(2,1)S(1)}, bf16[128,512]{1,0:T(8,128)(2,1)S(1)}, u32[]{:S(2)}, u32[]{:S(2)}) collective-permute-start(bf16[128,512]{1,0:T(8,128)(2,1)S(1)} %get-tuple-element.114), channel_id=1, source_target_pairs={{0,6},{1,7},{2,4},{3,5},{4,2},{5,3},{6,0},{7,1},{8,14},{9,15},{10,... | collective-permute-start | bytes 393224 | tf_op jit(solution)/shard_map/ppermute | solution.py:533
  105.8 2.0 %collective-permute-start.26 = (bf16[128,512]{1,0:T(8,128)(2,1)S(1)}, bf16[128,512]{1,0:T(8,128)(2,1)S(1)}, u32[]{:S(2)}, u32[]{:S(2)}) collective-permute-start(bf16[128,512]{1,0:T(8,128)(2,1)S(1)} %get-tuple-element.115), channel_id=1, source_target_pairs={{0,4},{1,5},{2,6},{3,7},{4,0},{5,1},{6,2},{7,3},{8,12},{9,13},{10,... | collective-permute-start | bytes 393224 | tf_op jit(solution)/shard_map/ppermute | solution.py:533
  107.8 1.2 collective-permute-start.27
  109.0 3.5 %inputgrad.1 = bf16[128,4096]{1,0:T(8,128)(2,1)} custom-call(bf16[256,256]{1,0:T(8,128)(2,1)S(1)} %copy-done.9, bf16[128,256]{1,0:T(8,128)(2,1)S(1)} %copy-done.10, bf16[128,4096]{1,0:T(8,128)(2,1)S(1)} %get-tuple-element.111.grad_b_ref, bf16[128,4096]{1,0:T(8,128)(2,1)S(1)} %collective-permute-done.28.later_ref, ...), custom_call_target="tpu_custom_call" | custom-call | flops 1073741824 | bytes 8585216 | tf_op jit(solution)/shard_map/inputgrad/pallas_call | solution.py:518
  112.5 6.8 %collective-permute-done.25.refs_0_ = bf16[128,512]{1,0:T(8,128)(2,1)S(1)} collective-permute-done((bf16[128,512]{1,0:T(8,128)(2,1)S(1)}, bf16[128,512]{1,0:T(8,128)(2,1)S(1)}, u32[]{:S(2)}, u32[]{:S(2)}) %collective-permute-start.25) | collective-permute-done | bytes 131104 | tf_op jit(solution)/shard_map/ppermute | solution.py:533
  119.3 4.3 %collective-permute-done.26.refs_1_ = bf16[128,512]{1,0:T(8,128)(2,1)S(1)} collective-permute-done((bf16[128,512]{1,0:T(8,128)(2,1)S(1)}, bf16[128,512]{1,0:T(8,128)(2,1)S(1)}, u32[]{:S(2)}, u32[]{:S(2)}) %collective-permute-start.26) | collective-permute-done | bytes 131104 | tf_op jit(solution)/shard_map/ppermute | solution.py:533
  123.6 0.7 midgrad.1
  (55 shorter events, 0.6 us)
Async XLA Ops:
  0.6 5.3 %copy-start = (bf16[1,128,4096]{2,1,0:T(8,128)(2,1)S(1)}, bf16[1,128,4096]{2,1,0:T(8,128)(2,1)}, u32[]{:S(2)}) copy-start(bf16[1,128,4096]{2,1,0:T(8,128)(2,1)} %param.15) | copy-start | bytes 3145732
  0.6 1.3 %copy-start.3 = (bf16[1,128,4096]{2,1,0:T(8,128)(2,1)S(1)}, bf16[1,128,4096]{2,1,0:T(8,128)(2,1)}, u32[]{:S(2)}) copy-start(bf16[1,128,4096]{2,1,0:T(8,128)(2,1)} %param.14) | copy-start | bytes 3145732
  2.0 15.2 %copy-start.4 = (bf16[1,128,4096]{2,1,0:T(8,128)(2,1)S(1)}, bf16[1,128,4096]{2,1,0:T(8,128)(2,1)}, u32[]{:S(2)}) copy-start(bf16[1,128,4096]{2,1,0:T(8,128)(2,1)} %param.14) | copy-start | bytes 3145732
  2.0 15.1 %collective-permute-start.1 = (bf16[128,2048]{1,0:T(8,128)(2,1)S(1)}, bf16[128,2048]{1,0:T(8,128)(2,1)S(1)}, u32[]{:S(2)}, u32[]{:S(2)}) collective-permute-start(bf16[128,2048]{1,0:T(8,128)(2,1)S(1)} %far.1), channel_id=1, source_target_pairs={{0,24},{8,0},{16,8},{24,16},{1,25},{9,1},{17,9},{25,17},{2,26},{10... | collective-permute-start | bytes 1572872 | tf_op jit(solution)/shard_map/ppermute | solution.py:20
  5.9 1.2 copy-start.6
  7.2 13.4 %copy-start.5 = (bf16[1,128,4096]{2,1,0:T(8,128)(2,1)S(1)}, bf16[1,128,4096]{2,1,0:T(8,128)(2,1)}, u32[]{:S(2)}) copy-start(bf16[1,128,4096]{2,1,0:T(8,128)(2,1)} %param.19) | copy-start | bytes 3145732
  7.4 30.1 %copy-start.1 = (bf16[1,128,4096]{2,1,0:T(8,128)(2,1)S(1)}, bf16[1,128,4096]{2,1,0:T(8,128)(2,1)}, u32[]{:S(2)}) copy-start(bf16[1,128,4096]{2,1,0:T(8,128)(2,1)} %param.18) | copy-start | bytes 3145732
  7.4 30.1 %copy-start.2 = (bf16[1,128,4096]{2,1,0:T(8,128)(2,1)S(1)}, bf16[1,128,4096]{2,1,0:T(8,128)(2,1)}, u32[]{:S(2)}) copy-start(bf16[1,128,4096]{2,1,0:T(8,128)(2,1)} %param.17) | copy-start | bytes 3145732
  7.4 30.0 %copy-start.8 = (bf16[1,128,4096]{2,1,0:T(8,128)(2,1)S(1)}, bf16[1,128,4096]{2,1,0:T(8,128)(2,1)}, u32[]{:S(2)}) copy-start(bf16[1,128,4096]{2,1,0:T(8,128)(2,1)} %param.21) | copy-start | bytes 3145732
  7.5 30.0 %copy-start.9 = (bf16[256,256]{1,0:T(8,128)(2,1)S(1)}, bf16[256,256]{1,0:T(8,128)(2,1)}, u32[]{:S(2)}) copy-start(bf16[256,256]{1,0:T(8,128)(2,1)} %constant.16.clone.fwd_ref) | copy-start | bytes 393220
  7.5 30.0 %copy-start.11 = (bf16[128,256]{1,0:T(8,128)(2,1)S(1)}, bf16[128,256]{1,0:T(8,128)(2,1)}, u32[]{:S(2)}) copy-start(bf16[128,256]{1,0:T(8,128)(2,1)} %constant.17.clone.inv_ref) | copy-start | bytes 196612
  7.5 29.8 %collective-permute-start = (bf16[128,4096]{1,0:T(8,128)(2,1)S(1)}, bf16[128,4096]{1,0:T(8,128)(2,1)S(1)}, u32[]{:S(2)}, u32[]{:S(2)}) collective-permute-start(bf16[128,4096]{1,0:T(8,128)(2,1)S(1)} %mix.1.mixed_ref), channel_id=1, source_target_pairs={{0,1},{1,2},{2,3},{3,4},{4,5},{5,6},{6,7},{8,9},{9,10},{10,11},{11... | collective-permute-start | bytes 3145736 | tf_op jit(solution)/shard_map/ppermute | solution.py:26
  17.2 18.0 %collective-permute-start.2 = (bf16[128,2048]{1,0:T(8,128)(2,1)S(1)}, bf16[128,2048]{1,0:T(8,128)(2,1)S(1)}, u32[]{:S(2)}, u32[]{:S(2)}) collective-permute-start(bf16[128,2048]{1,0:T(8,128)(2,1)S(1)} %near.1), channel_id=1, source_target_pairs={{0,24},{8,0},{16,8},{24,16},{1,25},{9,1},{17,9},{25,17},{2,26},{10... | collective-permute-start | bytes 1572872 | tf_op jit(solution)/shard_map/ppermute | solution.py:20
  20.8 7.2 %collective-permute-start.4 = (bf16[128,512]{1,0:T(8,128)(2,1)S(1)}, bf16[128,512]{1,0:T(8,128)(2,1)S(1)}, u32[]{:S(2)}, u32[]{:S(2)}) collective-permute-start(bf16[128,512]{1,0:T(8,128)(2,1)S(1)} %get-tuple-element.73), channel_id=1, source_target_pairs={{0,6},{1,7},{2,4},{3,5},{4,2},{5,3},{6,0},{7,1},{8,14},{9,15},{10,... | collective-permute-start | bytes 393224 | tf_op jit(solution)/shard_map/ppermute | solution.py:533
  24.4 11.8 %collective-permute-start.3 = (bf16[128,512]{1,0:T(8,128)(2,1)S(1)}, bf16[128,512]{1,0:T(8,128)(2,1)S(1)}, u32[]{:S(2)}, u32[]{:S(2)}) collective-permute-start(bf16[128,512]{1,0:T(8,128)(2,1)S(1)} %get-tuple-element.72), channel_id=1, source_target_pairs={{0,7},{1,6},{2,5},{3,4},{4,3},{5,2},{6,1},{7,0},{8,15},{9,14},{10,... | collective-permute-start | bytes 393224 | tf_op jit(solution)/shard_map/ppermute | solution.py:533
  28.0 13.2 %collective-permute-start.6 = (bf16[128,512]{1,0:T(8,128)(2,1)S(1)}, bf16[128,512]{1,0:T(8,128)(2,1)S(1)}, u32[]{:S(2)}, u32[]{:S(2)}) collective-permute-start(bf16[128,512]{1,0:T(8,128)(2,1)S(1)} %get-tuple-element.77), channel_id=1, source_target_pairs={{0,4},{1,5},{2,6},{3,7},{4,0},{5,1},{6,2},{7,3},{8,12},{9,13},{10,... | collective-permute-start | bytes 393224 | tf_op jit(solution)/shard_map/ppermute | solution.py:533
  35.4 10.9 %collective-permute-start.7 = (bf16[128,512]{1,0:T(8,128)(2,1)S(1)}, bf16[128,512]{1,0:T(8,128)(2,1)S(1)}, u32[]{:S(2)}, u32[]{:S(2)}) collective-permute-start(bf16[128,512]{1,0:T(8,128)(2,1)S(1)} %get-tuple-element.69), channel_id=1, source_target_pairs={{0,3},{1,2},{2,1},{3,0},{4,7},{5,6},{6,5},{7,4},{8,11},{9,10},{10,... | collective-permute-start | bytes 393224 | tf_op jit(solution)/shard_map/ppermute | solution.py:533
  35.4 13.0 %collective-permute-start.8 = (bf16[128,512]{1,0:T(8,128)(2,1)S(1)}, bf16[128,512]{1,0:T(8,128)(2,1)S(1)}, u32[]{:S(2)}, u32[]{:S(2)}) collective-permute-start(bf16[128,512]{1,0:T(8,128)(2,1)S(1)} %get-tuple-element.68), channel_id=1, source_target_pairs={{0,2},{1,3},{2,0},{3,1},{4,6},{5,7},{6,4},{7,5},{8,10},{9,11},{10,... | collective-permute-start | bytes 393224 | tf_op jit(solution)/shard_map/ppermute | solution.py:533
  36.2 12.2 %collective-permute-start.9 = (bf16[128,512]{1,0:T(8,128)(2,1)S(1)}, bf16[128,512]{1,0:T(8,128)(2,1)S(1)}, u32[]{:S(2)}, u32[]{:S(2)}) collective-permute-start(bf16[128,512]{1,0:T(8,128)(2,1)S(1)} %get-tuple-element.67), channel_id=1, source_target_pairs={{0,1},{1,0},{2,3},{3,2},{4,5},{5,4},{6,7},{7,6},{8,9},{9,8},{10,11... | collective-permute-start | bytes 393224 | tf_op jit(solution)/shard_map/ppermute | solution.py:533
  37.3 12.1 %collective-permute-start.5 = (bf16[128,512]{1,0:T(8,128)(2,1)S(1)}, bf16[128,512]{1,0:T(8,128)(2,1)S(1)}, u32[]{:S(2)}, u32[]{:S(2)}) collective-permute-start(bf16[128,512]{1,0:T(8,128)(2,1)S(1)} %get-tuple-element.75), channel_id=1, source_target_pairs={{0,5},{1,4},{2,7},{3,6},{4,1},{5,0},{6,3},{7,2},{8,13},{9,12},{10,... | collective-permute-start | bytes 393224 | tf_op jit(solution)/shard_map/ppermute | solution.py:533
  37.5 14.2 %copy-start.12 = (bf16[1,512,1024]{2,1,0:T(8,128)(2,1)S(1)}, bf16[1,512,1024]{2,1,0:T(8,128)(2,1)}, u32[]{:S(2)}) copy-start(bf16[1,512,1024]{2,1,0:T(8,128)(2,1)} %param.20) | copy-start | bytes 3145732
  37.5 14.2 %copy-start.13 = (bf16[512,512]{1,0:T(8,128)(2,1)S(1)}, bf16[512,512]{1,0:T(8,128)(2,1)}, u32[]{:S(2)}) copy-start(bf16[512,512]{1,0:T(8,128)(2,1)} %constant.20.clone.fwd_ref) | copy-start | bytes 1572868
  37.5 14.2 %copy-start.14 = (bf16[256,512]{1,0:T(8,128)(2,1)S(1)}, bf16[256,512]{1,0:T(8,128)(2,1)}, u32[]{:S(2)}) copy-start(bf16[256,512]{1,0:T(8,128)(2,1)} %constant.21.clone.inv_ref) | copy-start | bytes 786436
  41.2 15.3 %collective-permute-start.11 = (bf16[128,512]{1,0:T(8,128)(2,1)S(1)}, bf16[128,512]{1,0:T(8,128)(2,1)S(1)}, u32[]{:S(2)}, u32[]{:S(2)}) collective-permute-start(bf16[128,512]{1,0:T(8,128)(2,1)S(1)} %get-tuple-element.83), channel_id=1, source_target_pairs={{0,1},{1,0},{2,3},{3,2},{4,5},{5,4},{6,7},{7,6},{8,9},{9,8},{10,11... | collective-permute-start | bytes 393224 | tf_op jit(solution)/shard_map/ppermute | solution.py:533
  46.3 10.9 %collective-permute-start.12 = (bf16[128,512]{1,0:T(8,128)(2,1)S(1)}, bf16[128,512]{1,0:T(8,128)(2,1)S(1)}, u32[]{:S(2)}, u32[]{:S(2)}) collective-permute-start(bf16[128,512]{1,0:T(8,128)(2,1)S(1)} %get-tuple-element.84), channel_id=1, source_target_pairs={{0,2},{1,3},{2,0},{3,1},{4,6},{5,7},{6,4},{7,5},{8,10},{9,11},{10,... | collective-permute-start | bytes 393224 | tf_op jit(solution)/shard_map/ppermute | solution.py:533
  48.4 11.4 %collective-permute-start.13 = (bf16[128,512]{1,0:T(8,128)(2,1)S(1)}, bf16[128,512]{1,0:T(8,128)(2,1)S(1)}, u32[]{:S(2)}, u32[]{:S(2)}) collective-permute-start(bf16[128,512]{1,0:T(8,128)(2,1)S(1)} %get-tuple-element.85), channel_id=1, source_target_pairs={{0,3},{1,2},{2,1},{3,0},{4,7},{5,6},{6,5},{7,4},{8,11},{9,10},{10,... | collective-permute-start | bytes 393224 | tf_op jit(solution)/shard_map/ppermute | solution.py:533
  48.4 11.4 %collective-permute-start.19 = (bf16[128,512]{1,0:T(8,128)(2,1)S(1)}, bf16[128,512]{1,0:T(8,128)(2,1)S(1)}, u32[]{:S(2)}, u32[]{:S(2)}) collective-permute-start(bf16[128,512]{1,0:T(8,128)(2,1)S(1)} %get-tuple-element.95), channel_id=1, source_target_pairs={{0,6},{1,7},{2,4},{3,5},{4,2},{5,3},{6,0},{7,1},{8,14},{9,15},{10,... | collective-permute-start | bytes 393224 | tf_op jit(solution)/shard_map/ppermute | solution.py:533
  49.4 12.7 %collective-permute-start.10 = (bf16[128,512]{1,0:T(8,128)(2,1)S(1)}, bf16[128,512]{1,0:T(8,128)(2,1)S(1)}, u32[]{:S(2)}, u32[]{:S(2)}) collective-permute-start(bf16[128,512]{1,0:T(8,128)(2,1)S(1)} %get-tuple-element.81), channel_id=1, source_target_pairs={{0,7},{1,6},{2,5},{3,4},{4,3},{5,2},{6,1},{7,0},{8,15},{9,14},{10,... | collective-permute-start | bytes 393224 | tf_op jit(solution)/shard_map/ppermute | solution.py:533
  56.5 7.4 %collective-permute-start.15 = (bf16[128,512]{1,0:T(8,128)(2,1)S(1)}, bf16[128,512]{1,0:T(8,128)(2,1)S(1)}, u32[]{:S(2)}, u32[]{:S(2)}) collective-permute-start(bf16[128,512]{1,0:T(8,128)(2,1)S(1)} %get-tuple-element.88), channel_id=1, source_target_pairs={{0,1},{1,0},{2,3},{3,2},{4,5},{5,4},{6,7},{7,6},{8,9},{9,8},{10,11... | collective-permute-start | bytes 393224 | tf_op jit(solution)/shard_map/ppermute | solution.py:533
  57.2 6.7 %collective-permute-start.16 = (bf16[128,512]{1,0:T(8,128)(2,1)S(1)}, bf16[128,512]{1,0:T(8,128)(2,1)S(1)}, u32[]{:S(2)}, u32[]{:S(2)}) collective-permute-start(bf16[128,512]{1,0:T(8,128)(2,1)S(1)} %get-tuple-element.89), channel_id=1, source_target_pairs={{0,2},{1,3},{2,0},{3,1},{4,6},{5,7},{6,4},{7,5},{8,10},{9,11},{10,... | collective-permute-start | bytes 393224 | tf_op jit(solution)/shard_map/ppermute | solution.py:533
  59.8 6.7 %collective-permute-start.17 = (bf16[128,512]{1,0:T(8,128)(2,1)S(1)}, bf16[128,512]{1,0:T(8,128)(2,1)S(1)}, u32[]{:S(2)}, u32[]{:S(2)}) collective-permute-start(bf16[128,512]{1,0:T(8,128)(2,1)S(1)} %get-tuple-element.90), channel_id=1, source_target_pairs={{0,3},{1,2},{2,1},{3,0},{4,7},{5,6},{6,5},{7,4},{8,11},{9,10},{10,... | collective-permute-start | bytes 393224 | tf_op jit(solution)/shard_map/ppermute | solution.py:533
  59.8 12.9 %collective-permute-start.20 = (bf16[128,512]{1,0:T(8,128)(2,1)S(1)}, bf16[128,512]{1,0:T(8,128)(2,1)S(1)}, u32[]{:S(2)}, u32[]{:S(2)}) collective-permute-start(bf16[128,512]{1,0:T(8,128)(2,1)S(1)} %get-tuple-element.96), channel_id=1, source_target_pairs={{0,4},{1,5},{2,6},{3,7},{4,0},{5,1},{6,2},{7,3},{8,12},{9,13},{10,... | collective-permute-start | bytes 393224 | tf_op jit(solution)/shard_map/ppermute | solution.py:533
  62.0 12.6 %collective-permute-start.14 = (bf16[128,512]{1,0:T(8,128)(2,1)S(1)}, bf16[128,512]{1,0:T(8,128)(2,1)S(1)}, u32[]{:S(2)}, u32[]{:S(2)}) collective-permute-start(bf16[128,512]{1,0:T(8,128)(2,1)S(1)} %get-tuple-element.87), channel_id=1, source_target_pairs={{0,5},{1,4},{2,7},{3,6},{4,1},{5,0},{6,3},{7,2},{8,13},{9,12},{10,... | collective-permute-start | bytes 393224 | tf_op jit(solution)/shard_map/ppermute | solution.py:533
  72.7 6.8 %collective-permute-start.21 = (bf16[128,512]{1,0:T(8,128)(2,1)S(1)}, bf16[128,512]{1,0:T(8,128)(2,1)S(1)}, u32[]{:S(2)}, u32[]{:S(2)}) collective-permute-start(bf16[128,512]{1,0:T(8,128)(2,1)S(1)} %get-tuple-element.97), channel_id=1, source_target_pairs={{0,6},{1,7},{2,4},{3,5},{4,2},{5,3},{6,0},{7,1},{8,14},{9,15},{10,... | collective-permute-start | bytes 393224 | tf_op jit(solution)/shard_map/ppermute | solution.py:533
  74.6 9.6 %collective-permute-start.18 = (bf16[128,512]{1,0:T(8,128)(2,1)S(1)}, bf16[128,512]{1,0:T(8,128)(2,1)S(1)}, u32[]{:S(2)}, u32[]{:S(2)}) collective-permute-start(bf16[128,512]{1,0:T(8,128)(2,1)S(1)} %get-tuple-element.91), channel_id=1, source_target_pairs={{0,7},{1,6},{2,5},{3,4},{4,3},{5,2},{6,1},{7,0},{8,15},{9,14},{10,... | collective-permute-start | bytes 393224 | tf_op jit(solution)/shard_map/ppermute | solution.py:533
  79.5 15.7 %collective-permute-start.23 = (bf16[128,512]{1,0:T(8,128)(2,1)S(1)}, bf16[128,512]{1,0:T(8,128)(2,1)S(1)}, u32[]{:S(2)}, u32[]{:S(2)}) collective-permute-start(bf16[128,512]{1,0:T(8,128)(2,1)S(1)} %get-tuple-element.101), channel_id=1, source_target_pairs={{0,4},{1,5},{2,6},{3,7},{4,0},{5,1},{6,2},{7,3},{8,12},{9,13},{10,... | collective-permute-start | bytes 393224 | tf_op jit(solution)/shard_map/ppermute | solution.py:533
  84.3 12.8 %collective-permute-start.22 = (bf16[128,512]{1,0:T(8,128)(2,1)S(1)}, bf16[128,512]{1,0:T(8,128)(2,1)S(1)}, u32[]{:S(2)}, u32[]{:S(2)}) collective-permute-start(bf16[128,512]{1,0:T(8,128)(2,1)S(1)} %get-tuple-element.99), channel_id=1, source_target_pairs={{0,5},{1,4},{2,7},{3,6},{4,1},{5,0},{6,3},{7,2},{8,13},{9,12},{10,... | collective-permute-start | bytes 393224 | tf_op jit(solution)/shard_map/ppermute | solution.py:533
  92.2 7.0 %copy-start.15 = (bf16[128,256]{1,0:T(8,128)(2,1)S(1)}, bf16[128,256]{1,0:T(8,128)(2,1)}, u32[]{:S(2)}) copy-start(bf16[128,256]{1,0:T(8,128)(2,1)} %constant.19.clone.inv_ref) | copy-start | bytes 196612
  97.7 11.3 %collective-permute-start.28 = (bf16[128,4096]{1,0:T(8,128)(2,1)S(1)}, bf16[128,4096]{1,0:T(8,128)(2,1)S(1)}, u32[]{:S(2)}, u32[]{:S(2)}) collective-permute-start(bf16[128,4096]{1,0:T(8,128)(2,1)S(1)} %get-tuple-element.111.grad_b_ref), channel_id=1, source_target_pairs={{1,0},{2,1},{3,2},{4,3},{5,4},{6,5},{7,6},{9,8},{10,9},{11,10},{12... | collective-permute-start | bytes 3145736 | tf_op jit(solution)/shard_map/ppermute | solution.py:26
  99.2 9.8 %copy-start.7 = (bf16[1,128,4096]{2,1,0:T(8,128)(2,1)S(1)}, bf16[1,128,4096]{2,1,0:T(8,128)(2,1)}, u32[]{:S(2)}) copy-start(bf16[1,128,4096]{2,1,0:T(8,128)(2,1)} %param.16) | copy-start | bytes 3145732
  99.2 9.8 %copy-start.10 = (bf16[128,256]{1,0:T(8,128)(2,1)S(1)}, bf16[128,256]{1,0:T(8,128)(2,1)}, u32[]{:S(2)}) copy-start(bf16[128,256]{1,0:T(8,128)(2,1)} %constant.18.clone.inv_ref) | copy-start | bytes 196612
  101.7 2.7 %collective-permute-start.24 = (bf16[4,128,512]{2,1,0:T(8,128)(2,1)S(1)}, bf16[4,128,512]{2,1,0:T(8,128)(2,1)S(1)}, u32[]{:S(2)}, u32[]{:S(2)}) collective-permute-start(bf16[4,128,512]{2,1,0:T(8,128)(2,1)S(1)} %get-tuple-element.113), channel_id=1, source_target_pairs={{0,1},{1,0},{2,3},{3,2},{4,5},{5,4},{6,7},{7,6},{8,9},{9,8},{10,11... | collective-permute-start | bytes 1572872 | tf_op jit(solution)/shard_map/ppermute | solution.py:533
  104.5 14.8 %collective-permute-start.25 = (bf16[128,512]{1,0:T(8,128)(2,1)S(1)}, bf16[128,512]{1,0:T(8,128)(2,1)S(1)}, u32[]{:S(2)}, u32[]{:S(2)}) collective-permute-start(bf16[128,512]{1,0:T(8,128)(2,1)S(1)} %get-tuple-element.114), channel_id=1, source_target_pairs={{0,6},{1,7},{2,4},{3,5},{4,2},{5,3},{6,0},{7,1},{8,14},{9,15},{10,... | collective-permute-start | bytes 393224 | tf_op jit(solution)/shard_map/ppermute | solution.py:533
  105.8 17.8 %collective-permute-start.26 = (bf16[128,512]{1,0:T(8,128)(2,1)S(1)}, bf16[128,512]{1,0:T(8,128)(2,1)S(1)}, u32[]{:S(2)}, u32[]{:S(2)}) collective-permute-start(bf16[128,512]{1,0:T(8,128)(2,1)S(1)} %get-tuple-element.115), channel_id=1, source_target_pairs={{0,4},{1,5},{2,6},{3,7},{4,0},{5,1},{6,2},{7,3},{8,12},{9,13},{10,... | collective-permute-start | bytes 393224 | tf_op jit(solution)/shard_map/ppermute | solution.py:533
  107.8 15.8 %collective-permute-start.27 = (bf16[128,512]{1,0:T(8,128)(2,1)S(1)}, bf16[128,512]{1,0:T(8,128)(2,1)S(1)}, u32[]{:S(2)}, u32[]{:S(2)}) collective-permute-start(bf16[128,512]{1,0:T(8,128)(2,1)S(1)} %get-tuple-element.116), channel_id=1, source_target_pairs={{0,2},{1,3},{2,0},{3,1},{4,6},{5,7},{6,4},{7,5},{8,10},{9,11},{10,... | collective-permute-start | bytes 393224 | tf_op jit(solution)/shard_map/ppermute | solution.py:533

commit v9 on v8

--- a/solution.py
+++ b/solution.py
@@ -599,28 +599,29 @@
     far_z = local(
         functools.partial(pieces_z_kernel, beta, half), [piece] * half, [me, far, gate_out], few, name="farz"
     )
-    near_z = local(
-        functools.partial(pieces_z_kernel, beta, 0), [piece] * half, [me, near, gate_out], few, name="nearz"
-    )
     signal, filt, *pieces_w = local(
         functools.partial(pieces_branch_kernel, beta),
         [((span, channels), BF16)] * 2 + [piece] * devices,
-        [me, fwd, inv_conv, after(earlier, near_z), mixed_in, filter_taps, inputs, gate_mid, gate_long],
+        [me, fwd, inv_conv, after(earlier, far_z), mixed_in, filter_taps, inputs, gate_mid, gate_long],
         mid_flops, name="branch",
     )
     z_6, z_7 = far_pair(far_z[2:], 6)
     z_4, z_5 = far_pair(far_z[:2], 4, z_6, z_7)
+    near_w = exchanged(pieces_w[:half])
+    near_z = local(
+        functools.partial(pieces_z_kernel, beta, 0), [piece] * half,
+        [me, after(near, near_w, z_7), gate_out], few, name="nearz",
+    )
     near_z = exchanged(near_z)
     pieces_z = near_z + [z_4, z_5, z_6, z_7]
     w_6, w_7 = far_pair(pieces_w[6:], 6, (z_4, near_z), (z_5, near_z))
-    near_w = exchanged(pieces_w[:half])
     *pieces_g, channel_z = local(
         functools.partial(pieces_grad_w_kernel, blocks, devices),
         [piece] * devices + [((seq_len, owned), BF16)],
         [me, long_fwd, long_inv, long_filter[0], *pieces_z[::-1]], long_flops,
         [spectrum, spectrum, joint, staged], name="gradw",
     )
-    w_4, w_5 = far_pair(pieces_w[4:6], 4, (w_6, near_w, pieces_g[0]), (w_7, near_w, pieces_g[0]))
+    w_4, w_5 = far_pair(pieces_w[4:6], 4, (w_6, pieces_g[0]), (w_7, pieces_g[0]))
     pieces_w = near_w + [w_4, w_5, w_6, w_7]
     near_g = exchanged(pieces_g[:half])
     g_6, g_7 = far_pair(pieces_g[6:], 6, (w_4, near_g), (w_5, near_g))
@@ -644,9 +645,14 @@
     sums = local(pair_kernel, [tap_piece] * half, [keep, swapped(send, 1)], few, name="pair")
     sums = [swapped(sums[m], 2 * m) for m in (3, 2, 1)] + [sums[0]]
     later = after(later, sums[-1])
-    input_grad = local(
-        functools.partial(pieces_input_grad_kernel, 512), [rows_shape],
-        [fwd, inv_corr, grad_b, later, filt, grad_u, gate_pre], mid_flops, name="inputgrad",
+    wide = channels // 4
+    rows_spec = pl.BlockSpec((tokens, wide), lambda i: (0, i))
+    filt_spec = pl.BlockSpec((span, wide), lambda i: (0, i))
+    input_grad = call(
+        functools.partial(pieces_input_grad_kernel, 512), (4,),
+        [whole_spec(fwd), whole_spec(inv_corr), rows_spec, rows_spec, filt_spec, rows_spec, rows_spec],
+        [(*rows_shape, rows_spec)], [fwd, inv_corr, grad_b, later, filt, grad_u, gate_pre], mid_flops,
+        name="inputgrad",
     )
     sums, input_grad = lax.optimization_barrier((sums, input_grad))
     mid_grad = local(functools.partial(pieces_total_kernel, scale), [tap_piece], sums, few, name="midgrad")

time: 125 us -> 133 us (1.064)
  starting transfers between devices: 48.5 us -> 59.5 us
  waiting for transfers between devices: 50.9 us -> 44.7 us
  Pallas kernels: 21.5 us -> 23.6 us
    ppermute x25, waiting for transfers between devices: 43 us -> 32.4 us  [swapped(): return lax.ppermute(array, 'ctx', [(i, i ^ k) for i in range(count)])]
    ppermute x25, starting transfers between devices: 37.9 us -> 47.8 us  [swapped(): return lax.ppermute(array, 'ctx', [(i, i ^ k) for i in range(count)])]
    ppermute x2, waiting for transfers between devices: 7.85 us -> 12.3 us  [passed_along(): return lax.ppermute(value, axis, pairs)]
    pallas_call x0 -> x1, Pallas kernels: none -> 4.32 us  [call(): pl.pallas_call(body, grid=grid, in_specs=ins, out_specs=[spec for _, _, s...]
    pallas_call x13 -> x12, Pallas kernels: 21.5 us -> 19.3 us  [local(): pl.pallas_call(body, in_specs=specs, out_specs=[pl.BlockSpec(memory_space...]
    ppermute x2, starting transfers between devices: 3.26 us -> 4.96 us  [shifted(): return lax.ppermute(array, axis, pairs)]
  transfers between devices with their start and end apart: 29 -> 29, of which waited for: 15 -> 12; matrix products, arithmetic and copies ran while one was open for 0% -> 0% of each run, Pallas kernels for 16% -> 17%
where the time goes in v9:
time: 133 us; the launch traced here: 132 us
  starting transfers between devices  59.5 us (45%)
  waiting for transfers between devices  44.7 us (34%)
  Pallas kernels  23.6 us (18%)
  local copies, waits for them, and re-layouts  3.73 us (3%)
    ppermute x25, starting transfers between devices, swapped(): return lax.ppermute(array, 'ctx', [(i, i ^ k) for i in range(count)])  47.8 us
    ppermute x25, waiting for transfers between devices, swapped(): return lax.ppermute(array, 'ctx', [(i, i ^ k) for i in range(count)])  32.4 us
    pallas_call x12, Pallas kernels, local(): pl.pallas_call(body, in_specs=specs, out_specs=[pl.BlockSpec(memory_space...  19.3 us
    ppermute x2, waiting for transfers between devices, passed_along(): return lax.ppermute(value, axis, pairs)  12.3 us
    ppermute x2, starting transfers between devices, passed_along(): return lax.ppermute(value, axis, pairs)  6.74 us
    ppermute x2, starting transfers between devices, shifted(): return lax.ppermute(array, axis, pairs)  4.96 us
    pallas_call x1, Pallas kernels, call(): pl.pallas_call(body, grid=grid, in_specs=ins, out_specs=[spec for _, _, s...  4.32 us
    unnamed x32, local copies, waits for them, and re-layouts  3.73 us
  transfers between devices with their start and end apart: 29, of which 12 were waited for; matrix products, arithmetic and copies ran while one was open for 0% of the time, Pallas kernels for 17%

profile of v9, /device:TPU:0, one launch (start us, length us, event | category | flops | bytes accessed | tf_op | source)
XLA Modules:
  0.0 132.3 jit_solution(3962406842338702916)
XLA Ops:
  0.6 1.2 copy-done
  1.9 1.2 copy-done.6
  3.1 0.2 mix.1.mixed_ref
  3.3 3.5 %collective-permute-start = (bf16[128,4096]{1,0:T(8,128)(2,1)S(1)}, bf16[128,4096]{1,0:T(8,128)(2,1)}, u32[]{:S(2)}, u32[]{:S(2)}) collective-permute-start(bf16[128,4096]{1,0:T(8,128)(2,1)S(1)} %mix.1.mixed_ref), channel_id=1, source_target_pairs={{0,1},{1,2},{2,3},{3,4},{4,5},{5,6},{6,7},{8,9},{9,10},{10,11},{11... | collective-permute-start | bytes 3145736 | tf_op jit(solution)/shard_map/ppermute | solution.py:26
  6.9 3.3 %collective-permute-start.1 = (bf16[128,2048]{1,0:T(8,128)(2,1)S(1)}, bf16[128,2048]{1,0:T(8,128)(2,1)S(1)}, u32[]{:S(2)}, u32[]{:S(2)}) collective-permute-start(bf16[128,2048]{1,0:T(8,128)(2,1)S(1)} %far.1), channel_id=1, source_target_pairs={{0,24},{8,0},{16,8},{24,16},{1,25},{9,1},{17,9},{25,17},{2,26},{10... | collective-permute-start | bytes 1572872 | tf_op jit(solution)/shard_map/ppermute | solution.py:20
  10.2 12.3 %collective-permute-done.1.adjoint_ref.far_ref = bf16[128,2048]{1,0:T(8,128)(2,1)S(1)} collective-permute-done((bf16[128,2048]{1,0:T(8,128)(2,1)S(1)}, bf16[128,2048]{1,0:T(8,128)(2,1)S(1)}, u32[]{:S(2)}, u32[]{:S(2)}) %collective-permute-start.1) | collective-permute-done | bytes 524320 | tf_op jit(solution)/shard_map/ppermute | solution.py:20
  22.6 3.4 %collective-permute-start.2 = (bf16[128,2048]{1,0:T(8,128)(2,1)S(1)}, bf16[128,2048]{1,0:T(8,128)(2,1)S(1)}, u32[]{:S(2)}, u32[]{:S(2)}) collective-permute-start(bf16[128,2048]{1,0:T(8,128)(2,1)S(1)} %near.1), channel_id=1, source_target_pairs={{0,24},{8,0},{16,8},{24,16},{1,25},{9,1},{17,9},{25,17},{2,26},{10... | collective-permute-start | bytes 1572872 | tf_op jit(solution)/shard_map/ppermute | solution.py:20
  26.0 0.2 farz.1
  26.1 1.2 collective-permute-start.4
  27.3 1.8 %collective-permute-start.3 = (bf16[128,512]{1,0:T(8,128)(2,1)S(1)}, bf16[128,512]{1,0:T(8,128)(2,1)S(1)}, u32[]{:S(2)}, u32[]{:S(2)}) collective-permute-start(bf16[128,512]{1,0:T(8,128)(2,1)S(1)} %get-tuple-element.69), channel_id=1, source_target_pairs={{0,7},{1,6},{2,5},{3,4},{4,3},{5,2},{6,1},{7,0},{8,15},{9,14},{10,... | collective-permute-start | bytes 393224 | tf_op jit(solution)/shard_map/ppermute | solution.py:533
  29.2 1.2 copy-done.8
  30.4 4.4 %branch.1 = (bf16[256,4096]{1,0:T(8,128)(2,1)S(1)}, bf16[256,4096]{1,0:T(8,128)(2,1)S(1)}, bf16[128,512]{1,0:T(8,128)(2,1)S(1)}, bf16[128,512]{1,0:T(8,128)(2,1)...) custom-call(s32[1]{0:T(128)} %bitcast.me_ref, ...), custom_call_target="tpu_custom_call" | custom-call | flops 1073741824 | bytes 11730948 | tf_op jit(solution)/shard_map/branch/pallas_call | solution.py:518
  34.8 1.1 collective-permute-start.7
  35.9 1.4 %collective-permute-start.9 = (bf16[128,512]{1,0:T(8,128)(2,1)S(1)}, bf16[128,512]{1,0:T(8,128)(2,1)S(1)}, u32[]{:S(2)}, u32[]{:S(2)}) collective-permute-start(bf16[128,512]{1,0:T(8,128)(2,1)S(1)} %get-tuple-element.78), channel_id=1, source_target_pairs={{0,3},{1,2},{2,1},{3,0},{4,7},{5,6},{6,5},{7,4},{8,11},{9,10},{10,... | collective-permute-start | bytes 393224 | tf_op jit(solution)/shard_map/ppermute | solution.py:533
  37.3 3.6 %collective-permute-start.6 = (bf16[128,512]{1,0:T(8,128)(2,1)S(1)}, bf16[128,512]{1,0:T(8,128)(2,1)S(1)}, u32[]{:S(2)}, u32[]{:S(2)}) collective-permute-start(bf16[128,512]{1,0:T(8,128)(2,1)S(1)} %get-tuple-element.74), channel_id=1, source_target_pairs={{0,4},{1,5},{2,6},{3,7},{4,0},{5,1},{6,2},{7,3},{8,12},{9,13},{10,... | collective-permute-start | bytes 393224 | tf_op jit(solution)/shard_map/ppermute | solution.py:533
  40.9 3.0 %collective-permute-done.8.refs_5_ = bf16[128,512]{1,0:T(8,128)(2,1)S(1)} collective-permute-done((bf16[128,512]{1,0:T(8,128)(2,1)S(1)}, bf16[128,512]{1,0:T(8,128)(2,1)S(1)}, u32[]{:S(2)}, u32[]{:S(2)}) %collective-permute-start.8) | collective-permute-done | bytes 131104 | tf_op jit(solution)/shard_map/ppermute | solution.py:533
  43.9 1.1 collective-permute-done.9.refs_4_
  45.2 2.6 %collective-permute-start.11 = (bf16[128,512]{1,0:T(8,128)(2,1)S(1)}, bf16[128,512]{1,0:T(8,128)(2,1)S(1)}, u32[]{:S(2)}, u32[]{:S(2)}) collective-permute-start(bf16[128,512]{1,0:T(8,128)(2,1)S(1)} %get-tuple-element.81), channel_id=1, source_target_pairs={{0,2},{1,3},{2,0},{3,1},{4,6},{5,7},{6,4},{7,5},{8,10},{9,11},{10,... | collective-permute-start | bytes 393224 | tf_op jit(solution)/shard_map/ppermute | solution.py:533
  47.8 0.7 collective-permute-start.5
  48.5 1.3 collective-permute-done.10.refs_4_
  49.8 6.7 %collective-permute-done.11.refs_5_ = bf16[128,512]{1,0:T(8,128)(2,1)S(1)} collective-permute-done((bf16[128,512]{1,0:T(8,128)(2,1)S(1)}, bf16[128,512]{1,0:T(8,128)(2,1)S(1)}, u32[]{:S(2)}, u32[]{:S(2)}) %collective-permute-start.11) | collective-permute-done | bytes 131104 | tf_op jit(solution)/shard_map/ppermute | solution.py:533
  56.5 2.3 %collective-permute-start.13 = (bf16[128,512]{1,0:T(8,128)(2,1)S(1)}, bf16[128,512]{1,0:T(8,128)(2,1)S(1)}, u32[]{:S(2)}, u32[]{:S(2)}) collective-permute-start(bf16[128,512]{1,0:T(8,128)(2,1)S(1)} %get-tuple-element.87), channel_id=1, source_target_pairs={{0,7},{1,6},{2,5},{3,4},{4,3},{5,2},{6,1},{7,0},{8,15},{9,14},{10,... | collective-permute-start | bytes 393224 | tf_op jit(solution)/shard_map/ppermute | solution.py:533
  58.8 1.8 %collective-permute-start.19 = (bf16[128,512]{1,0:T(8,128)(2,1)S(1)}, bf16[128,512]{1,0:T(8,128)(2,1)S(1)}, u32[]{:S(2)}, u32[]{:S(2)}) collective-permute-start(bf16[128,512]{1,0:T(8,128)(2,1)S(1)} %get-tuple-element.97), channel_id=1, source_target_pairs={{0,6},{1,7},{2,4},{3,5},{4,2},{5,3},{6,0},{7,1},{8,14},{9,15},{10,... | collective-permute-start | bytes 393224 | tf_op jit(solution)/shard_map/ppermute | solution.py:533
  60.6 4.7 %gradw.1 = (bf16[128,512]{1,0:T(8,128)(2,1)S(1)}, bf16[128,512]{1,0:T(8,128)(2,1)S(1)}, bf16[128,512]{1,0:T(8,128)(2,1)S(1)}, bf16[128,512]{1,0:T(8,128)(2,1)S(1...) custom-call(s32[1]{0:T(128)} %bitcast.me_ref, ...), custom_call_target="tpu_custom_call" | custom-call | flops 3221225472 | bytes 4980740 | tf_op jit(solution)/shard_map/gradw/pallas_call | solution.py:518
  65.5 1.8 %collective-permute-start.17 = (bf16[128,512]{1,0:T(8,128)(2,1)S(1)}, bf16[128,512]{1,0:T(8,128)(2,1)S(1)}, u32[]{:S(2)}, u32[]{:S(2)}) collective-permute-start(bf16[128,512]{1,0:T(8,128)(2,1)S(1)} %get-tuple-element.92), channel_id=1, source_target_pairs={{0,3},{1,2},{2,1},{3,0},{4,7},{5,6},{6,5},{7,4},{8,11},{9,10},{10,... | collective-permute-start | bytes 393224 | tf_op jit(solution)/shard_map/ppermute | solution.py:533
  67.3 2.1 %collective-permute-start.14 = (bf16[128,512]{1,0:T(8,128)(2,1)S(1)}, bf16[128,512]{1,0:T(8,128)(2,1)S(1)}, u32[]{:S(2)}, u32[]{:S(2)}) collective-permute-start(bf16[128,512]{1,0:T(8,128)(2,1)S(1)} %get-tuple-element.89), channel_id=1, source_target_pairs={{0,5},{1,4},{2,7},{3,6},{4,1},{5,0},{6,3},{7,2},{8,13},{9,12},{10,... | collective-permute-start | bytes 393224 | tf_op jit(solution)/shard_map/ppermute | solution.py:533
  69.4 3.0 %collective-permute-start.20 = (bf16[128,512]{1,0:T(8,128)(2,1)S(1)}, bf16[128,512]{1,0:T(8,128)(2,1)S(1)}, u32[]{:S(2)}, u32[]{:S(2)}) collective-permute-start(bf16[128,512]{1,0:T(8,128)(2,1)S(1)} %get-tuple-element.98), channel_id=1, source_target_pairs={{0,4},{1,5},{2,6},{3,7},{4,0},{5,1},{6,2},{7,3},{8,12},{9,13},{10,... | collective-permute-start | bytes 393224 | tf_op jit(solution)/shard_map/ppermute | solution.py:533
  72.4 2.2 %collective-permute-done.16.refs_5_ = bf16[128,512]{1,0:T(8,128)(2,1)S(1)} collective-permute-done((bf16[128,512]{1,0:T(8,128)(2,1)S(1)}, bf16[128,512]{1,0:T(8,128)(2,1)S(1)}, u32[]{:S(2)}, u32[]{:S(2)}) %collective-permute-start.16) | collective-permute-done | bytes 131104 | tf_op jit(solution)/shard_map/ppermute | solution.py:533
  74.6 2.0 %collective-permute-done.17.refs_4_ = bf16[128,512]{1,0:T(8,128)(2,1)S(1)} collective-permute-done((bf16[128,512]{1,0:T(8,128)(2,1)S(1)}, bf16[128,512]{1,0:T(8,128)(2,1)S(1)}, u32[]{:S(2)}, u32[]{:S(2)}) %collective-permute-start.17) | collective-permute-done | bytes 131104 | tf_op jit(solution)/shard_map/ppermute | solution.py:533
  76.6 4.9 %collective-permute-start.18 = (bf16[128,512]{1,0:T(8,128)(2,1)S(1)}, bf16[128,512]{1,0:T(8,128)(2,1)S(1)}, u32[]{:S(2)}, u32[]{:S(2)}) collective-permute-start(bf16[128,512]{1,0:T(8,128)(2,1)S(1)} %get-tuple-element.93), channel_id=1, source_target_pairs={{0,7},{1,6},{2,5},{3,4},{4,3},{5,2},{6,1},{7,0},{8,15},{9,14},{10,... | collective-permute-start | bytes 393224 | tf_op jit(solution)/shard_map/ppermute | solution.py:533
  81.6 2.9 %collective-permute-done.20.refs_3_ = bf16[128,512]{1,0:T(8,128)(2,1)S(1)} collective-permute-done((bf16[128,512]{1,0:T(8,128)(2,1)S(1)}, bf16[128,512]{1,0:T(8,128)(2,1)S(1)}, u32[]{:S(2)}, u32[]{:S(2)}) %collective-permute-start.20) | collective-permute-done | bytes 131104 | tf_op jit(solution)/shard_map/ppermute | solution.py:533
  84.4 1.9 %collective-permute-start.21 = (bf16[128,512]{1,0:T(8,128)(2,1)S(1)}, bf16[128,512]{1,0:T(8,128)(2,1)S(1)}, u32[]{:S(2)}, u32[]{:S(2)}) collective-permute-start(bf16[128,512]{1,0:T(8,128)(2,1)S(1)} %get-tuple-element.99), channel_id=1, source_target_pairs={{0,6},{1,7},{2,4},{3,5},{4,2},{5,3},{6,0},{7,1},{8,14},{9,15},{10,... | collective-permute-start | bytes 393224 | tf_op jit(solution)/shard_map/ppermute | solution.py:533
  86.3 5.5 %collective-permute-start.22 = (bf16[128,512]{1,0:T(8,128)(2,1)S(1)}, bf16[128,512]{1,0:T(8,128)(2,1)S(1)}, u32[]{:S(2)}, u32[]{:S(2)}) collective-permute-start(bf16[128,512]{1,0:T(8,128)(2,1)S(1)} %get-tuple-element.101), channel_id=1, source_target_pairs={{0,5},{1,4},{2,7},{3,6},{4,1},{5,0},{6,3},{7,2},{8,13},{9,12},{10,... | collective-permute-start | bytes 393224 | tf_op jit(solution)/shard_map/ppermute | solution.py:533
  91.9 6.2 %collective-permute-start.23 = (bf16[128,512]{1,0:T(8,128)(2,1)S(1)}, bf16[128,512]{1,0:T(8,128)(2,1)S(1)}, u32[]{:S(2)}, u32[]{:S(2)}) collective-permute-start(bf16[128,512]{1,0:T(8,128)(2,1)S(1)} %get-tuple-element.103), channel_id=1, source_target_pairs={{0,4},{1,5},{2,6},{3,7},{4,0},{5,1},{6,2},{7,3},{8,12},{9,13},{10,... | collective-permute-start | bytes 393224 | tf_op jit(solution)/shard_map/ppermute | solution.py:533
  98.1 5.7 %longgrad.1 = bf16[512,1024]{1,0:T(8,128)(2,1)} custom-call(s32[1]{0:T(128)} %bitcast.me_ref, bf16[512,512]{1,0:T(8,128)(2,1)S(1)} %copy-done.13, bf16[256,512]{1,0:T(8,128)(2,1)S(1)} %copy-done.14, bf16[1024,512]{1,0:T(8,128)(2,1)S(1)} %get-tuple-element.104.grad_ref, bf16[128,512]{1,0:T(8,128)(2,1)S(1)} %collective-permute-done.13.refs_0_, ...), custom_call_target="tpu_custom_call" | custom-call | flops 3221225472 | bytes 3932164 | tf_op jit(solution)/shard_map/longgrad/pallas_call | solution.py:518
  103.7 1.5 %collective-permute-done.23.refs_3_ = bf16[128,512]{1,0:T(8,128)(2,1)S(1)} collective-permute-done((bf16[128,512]{1,0:T(8,128)(2,1)S(1)}, bf16[128,512]{1,0:T(8,128)(2,1)S(1)}, u32[]{:S(2)}, u32[]{:S(2)}) %collective-permute-start.23) | collective-permute-done | bytes 131104 | tf_op jit(solution)/shard_map/ppermute | solution.py:533
  105.3 0.6 gradb.1
  105.9 1.5 %collective-permute-start.28 = (bf16[128,4096]{1,0:T(8,128)(2,1)S(1)}, bf16[128,4096]{1,0:T(8,128)(2,1)S(1)}, u32[]{:S(2)}, u32[]{:S(2)}) collective-permute-start(bf16[128,4096]{1,0:T(8,128)(2,1)S(1)} %get-tuple-element.113.grad_b_ref), channel_id=1, source_target_pairs={{1,0},{2,1},{3,2},{4,3},{5,4},{6,5},{7,6},{9,8},{10,9},{11,10},{12... | collective-permute-start | bytes 3145736 | tf_op jit(solution)/shard_map/ppermute | solution.py:26
  107.4 2.4 %taps.1 = (bf16[4,128,512]{2,1,0:T(8,128)(2,1)S(1)}, bf16[4,128,512]{2,1,0:T(8,128)(2,1)S(1)}) custom-call(s32[1]{0:T(128)} %bitcast.me_ref, bf16[256,256]{1,0:T(8,128)(2,1)S(1)} %copy-done.9, bf16[128,256]{1,0:T(8,128)(2,1)S(1)} %copy-done.15, bf16[256,4096]{1,0:T(8,128)(2,1)S(1)} %get-tuple-element.71.signal_ref, ...), custom_call_target="tpu_custom_call" | custom-call | flops 1073741824 | bytes 4390916 | tf_op jit(solution)/shard_map/taps/pallas_call | solution.py:518
  109.8 1.2 collective-permute-start.24
  111.0 1.5 %collective-permute-done.24.came_ref = bf16[4,128,512]{2,1,0:T(8,128)(2,1)S(1)} collective-permute-done((bf16[4,128,512]{2,1,0:T(8,128)(2,1)S(1)}, bf16[4,128,512]{2,1,0:T(8,128)(2,1)S(1)}, u32[]{:S(2)}, u32[]{:S(2)}) %collective-permute-start.24) | collective-permute-done | bytes 524320 | tf_op jit(solution)/shard_map/ppermute | solution.py:533
  112.7 1.9 %collective-permute-start.25 = (bf16[128,512]{1,0:T(8,128)(2,1)S(1)}, bf16[128,512]{1,0:T(8,128)(2,1)S(1)}, u32[]{:S(2)}, u32[]{:S(2)}) collective-permute-start(bf16[128,512]{1,0:T(8,128)(2,1)S(1)} %get-tuple-element.116), channel_id=1, source_target_pairs={{0,6},{1,7},{2,4},{3,5},{4,2},{5,3},{6,0},{7,1},{8,14},{9,15},{10,... | collective-permute-start | bytes 393224 | tf_op jit(solution)/shard_map/ppermute | solution.py:533
  114.6 0.9 collective-permute-start.26
  115.5 1.6 %collective-permute-start.27 = (bf16[128,512]{1,0:T(8,128)(2,1)S(1)}, bf16[128,512]{1,0:T(8,128)(2,1)S(1)}, u32[]{:S(2)}, u32[]{:S(2)}) collective-permute-start(bf16[128,512]{1,0:T(8,128)(2,1)S(1)} %get-tuple-element.118), channel_id=1, source_target_pairs={{0,2},{1,3},{2,0},{3,1},{4,6},{5,7},{6,4},{7,5},{8,10},{9,11},{10,... | collective-permute-start | bytes 393224 | tf_op jit(solution)/shard_map/ppermute | solution.py:533
  117.1 4.3 %inputgrad.1 = bf16[128,4096]{1,0:T(8,128)(2,1)} custom-call(bf16[256,256]{1,0:T(8,128)(2,1)S(1)} %copy-done.9, bf16[128,256]{1,0:T(8,128)(2,1)S(1)} %copy-done.10, bf16[128,4096]{1,0:T(8,128)(2,1)S(1)} %get-tuple-element.113.grad_b_ref, bf16[128,4096]{1,0:T(8,128)(2,1)S(1)} %collective-permute-done.28.later_ref, ...), custom_call_target="tpu_custom_call" | custom-call | flops 1073741824 | bytes 8585216 | tf_op jit(solution)/shard_map/inputgrad/pallas_call | solution.py:222
  121.5 6.7 %collective-permute-done.25.refs_0_ = bf16[128,512]{1,0:T(8,128)(2,1)S(1)} collective-permute-done((bf16[128,512]{1,0:T(8,128)(2,1)S(1)}, bf16[128,512]{1,0:T(8,128)(2,1)S(1)}, u32[]{:S(2)}, u32[]{:S(2)}) %collective-permute-start.25) | collective-permute-done | bytes 131104 | tf_op jit(solution)/shard_map/ppermute | solution.py:533
  128.1 3.5 %collective-permute-done.26.refs_1_ = bf16[128,512]{1,0:T(8,128)(2,1)S(1)} collective-permute-done((bf16[128,512]{1,0:T(8,128)(2,1)S(1)}, bf16[128,512]{1,0:T(8,128)(2,1)S(1)}, u32[]{:S(2)}, u32[]{:S(2)}) %collective-permute-start.26) | collective-permute-done | bytes 131104 | tf_op jit(solution)/shard_map/ppermute | solution.py:533
  131.6 0.7 midgrad.1
  (55 shorter events, 0.7 us)
Async XLA Ops:
  0.6 1.2 copy-start
  1.9 1.2 copy-start.6
  3.1 3.7 %copy-start.4 = (bf16[1,128,4096]{2,1,0:T(8,128)(2,1)S(1)}, bf16[1,128,4096]{2,1,0:T(8,128)(2,1)}, u32[]{:S(2)}) copy-start(bf16[1,128,4096]{2,1,0:T(8,128)(2,1)} %param.14) | copy-start | bytes 3145732
  3.3 22.7 %copy-start.5 = (bf16[1,128,4096]{2,1,0:T(8,128)(2,1)S(1)}, bf16[1,128,4096]{2,1,0:T(8,128)(2,1)}, u32[]{:S(2)}) copy-start(bf16[1,128,4096]{2,1,0:T(8,128)(2,1)} %param.19) | copy-start | bytes 3145732
  3.3 25.8 %collective-permute-start = (bf16[128,4096]{1,0:T(8,128)(2,1)S(1)}, bf16[128,4096]{1,0:T(8,128)(2,1)}, u32[]{:S(2)}, u32[]{:S(2)}) collective-permute-start(bf16[128,4096]{1,0:T(8,128)(2,1)S(1)} %mix.1.mixed_ref), channel_id=1, source_target_pairs={{0,1},{1,2},{2,3},{3,4},{4,5},{5,6},{6,7},{8,9},{9,10},{10,11},{11... | collective-permute-start | bytes 3145736 | tf_op jit(solution)/shard_map/ppermute | solution.py:26
  6.8 22.3 %copy-start.1 = (bf16[1,128,4096]{2,1,0:T(8,128)(2,1)S(1)}, bf16[1,128,4096]{2,1,0:T(8,128)(2,1)}, u32[]{:S(2)}) copy-start(bf16[1,128,4096]{2,1,0:T(8,128)(2,1)} %param.15) | copy-start | bytes 3145732
  6.8 22.3 %copy-start.2 = (bf16[1,128,4096]{2,1,0:T(8,128)(2,1)S(1)}, bf16[1,128,4096]{2,1,0:T(8,128)(2,1)}, u32[]{:S(2)}) copy-start(bf16[1,128,4096]{2,1,0:T(8,128)(2,1)} %param.18) | copy-start | bytes 3145732
  6.8 22.3 %copy-start.3 = (bf16[1,128,4096]{2,1,0:T(8,128)(2,1)S(1)}, bf16[1,128,4096]{2,1,0:T(8,128)(2,1)}, u32[]{:S(2)}) copy-start(bf16[1,128,4096]{2,1,0:T(8,128)(2,1)} %param.17) | copy-start | bytes 3145732
  6.8 22.3 %copy-start.9 = (bf16[256,256]{1,0:T(8,128)(2,1)S(1)}, bf16[256,256]{1,0:T(8,128)(2,1)}, u32[]{:S(2)}) copy-start(bf16[256,256]{1,0:T(8,128)(2,1)} %constant.16.clone.fwd_ref) | copy-start | bytes 393220
  6.8 22.3 %copy-start.11 = (bf16[128,256]{1,0:T(8,128)(2,1)S(1)}, bf16[128,256]{1,0:T(8,128)(2,1)}, u32[]{:S(2)}) copy-start(bf16[128,256]{1,0:T(8,128)(2,1)} %constant.17.clone.inv_ref) | copy-start | bytes 196612
  6.9 15.6 %collective-permute-start.1 = (bf16[128,2048]{1,0:T(8,128)(2,1)S(1)}, bf16[128,2048]{1,0:T(8,128)(2,1)S(1)}, u32[]{:S(2)}, u32[]{:S(2)}) collective-permute-start(bf16[128,2048]{1,0:T(8,128)(2,1)S(1)} %far.1), channel_id=1, source_target_pairs={{0,24},{8,0},{16,8},{24,16},{1,25},{9,1},{17,9},{25,17},{2,26},{10... | collective-permute-start | bytes 1572872 | tf_op jit(solution)/shard_map/ppermute | solution.py:20
  22.6 18.4 %collective-permute-start.2 = (bf16[128,2048]{1,0:T(8,128)(2,1)S(1)}, bf16[128,2048]{1,0:T(8,128)(2,1)S(1)}, u32[]{:S(2)}, u32[]{:S(2)}) collective-permute-start(bf16[128,2048]{1,0:T(8,128)(2,1)S(1)} %near.1), channel_id=1, source_target_pairs={{0,24},{8,0},{16,8},{24,16},{1,25},{9,1},{17,9},{25,17},{2,26},{10... | collective-permute-start | bytes 1572872 | tf_op jit(solution)/shard_map/ppermute | solution.py:20
  26.1 9.8 %collective-permute-start.4 = (bf16[128,512]{1,0:T(8,128)(2,1)S(1)}, bf16[128,512]{1,0:T(8,128)(2,1)S(1)}, u32[]{:S(2)}, u32[]{:S(2)}) collective-permute-start(bf16[128,512]{1,0:T(8,128)(2,1)S(1)} %get-tuple-element.68), channel_id=1, source_target_pairs={{0,6},{1,7},{2,4},{3,5},{4,2},{5,3},{6,0},{7,1},{8,14},{9,15},{10,... | collective-permute-start | bytes 393224 | tf_op jit(solution)/shard_map/ppermute | solution.py:533
  27.3 10.0 %collective-permute-start.3 = (bf16[128,512]{1,0:T(8,128)(2,1)S(1)}, bf16[128,512]{1,0:T(8,128)(2,1)S(1)}, u32[]{:S(2)}, u32[]{:S(2)}) collective-permute-start(bf16[128,512]{1,0:T(8,128)(2,1)S(1)} %get-tuple-element.69), channel_id=1, source_target_pairs={{0,7},{1,6},{2,5},{3,4},{4,3},{5,2},{6,1},{7,0},{8,15},{9,14},{10,... | collective-permute-start | bytes 393224 | tf_op jit(solution)/shard_map/ppermute | solution.py:533
  29.2 1.2 copy-start.8
  30.4 30.2 %copy-start.12 = (bf16[1,512,1024]{2,1,0:T(8,128)(2,1)S(1)}, bf16[1,512,1024]{2,1,0:T(8,128)(2,1)}, u32[]{:S(2)}) copy-start(bf16[1,512,1024]{2,1,0:T(8,128)(2,1)} %param.20) | copy-start | bytes 3145732
  30.4 30.2 %copy-start.13 = (bf16[512,512]{1,0:T(8,128)(2,1)S(1)}, bf16[512,512]{1,0:T(8,128)(2,1)}, u32[]{:S(2)}) copy-start(bf16[512,512]{1,0:T(8,128)(2,1)} %constant.20.clone.fwd_ref) | copy-start | bytes 1572868
  30.4 30.2 %copy-start.14 = (bf16[256,512]{1,0:T(8,128)(2,1)S(1)}, bf16[256,512]{1,0:T(8,128)(2,1)}, u32[]{:S(2)}) copy-start(bf16[256,512]{1,0:T(8,128)(2,1)} %constant.21.clone.inv_ref) | copy-start | bytes 786436
  34.8 6.1 %collective-permute-start.7 = (bf16[128,512]{1,0:T(8,128)(2,1)S(1)}, bf16[128,512]{1,0:T(8,128)(2,1)S(1)}, u32[]{:S(2)}, u32[]{:S(2)}) collective-permute-start(bf16[128,512]{1,0:T(8,128)(2,1)S(1)} %get-tuple-element.76), channel_id=1, source_target_pairs={{0,1},{1,0},{2,3},{3,2},{4,5},{5,4},{6,7},{7,6},{8,9},{9,8},{10,11... | collective-permute-start | bytes 393224 | tf_op jit(solution)/shard_map/ppermute | solution.py:533
  35.9 8.0 %collective-permute-start.8 = (bf16[128,512]{1,0:T(8,128)(2,1)S(1)}, bf16[128,512]{1,0:T(8,128)(2,1)S(1)}, u32[]{:S(2)}, u32[]{:S(2)}) collective-permute-start(bf16[128,512]{1,0:T(8,128)(2,1)S(1)} %get-tuple-element.77), channel_id=1, source_target_pairs={{0,2},{1,3},{2,0},{3,1},{4,6},{5,7},{6,4},{7,5},{8,10},{9,11},{10,... | collective-permute-start | bytes 393224 | tf_op jit(solution)/shard_map/ppermute | solution.py:533
  35.9 9.1 %collective-permute-start.9 = (bf16[128,512]{1,0:T(8,128)(2,1)S(1)}, bf16[128,512]{1,0:T(8,128)(2,1)S(1)}, u32[]{:S(2)}, u32[]{:S(2)}) collective-permute-start(bf16[128,512]{1,0:T(8,128)(2,1)S(1)} %get-tuple-element.78), channel_id=1, source_target_pairs={{0,3},{1,2},{2,1},{3,0},{4,7},{5,6},{6,5},{7,4},{8,11},{9,10},{10,... | collective-permute-start | bytes 393224 | tf_op jit(solution)/shard_map/ppermute | solution.py:533
  37.3 11.2 %collective-permute-start.6 = (bf16[128,512]{1,0:T(8,128)(2,1)S(1)}, bf16[128,512]{1,0:T(8,128)(2,1)S(1)}, u32[]{:S(2)}, u32[]{:S(2)}) collective-permute-start(bf16[128,512]{1,0:T(8,128)(2,1)S(1)} %get-tuple-element.74), channel_id=1, source_target_pairs={{0,4},{1,5},{2,6},{3,7},{4,0},{5,1},{6,2},{7,3},{8,12},{9,13},{10,... | collective-permute-start | bytes 393224 | tf_op jit(solution)/shard_map/ppermute | solution.py:533
  45.1 4.7 %collective-permute-start.10 = (bf16[128,512]{1,0:T(8,128)(2,1)S(1)}, bf16[128,512]{1,0:T(8,128)(2,1)S(1)}, u32[]{:S(2)}, u32[]{:S(2)}) collective-permute-start(bf16[128,512]{1,0:T(8,128)(2,1)S(1)} %get-tuple-element.80), channel_id=1, source_target_pairs={{0,3},{1,2},{2,1},{3,0},{4,7},{5,6},{6,5},{7,4},{8,11},{9,10},{10,... | collective-permute-start | bytes 393224 | tf_op jit(solution)/shard_map/ppermute | solution.py:533
  45.2 11.3 %collective-permute-start.11 = (bf16[128,512]{1,0:T(8,128)(2,1)S(1)}, bf16[128,512]{1,0:T(8,128)(2,1)S(1)}, u32[]{:S(2)}, u32[]{:S(2)}) collective-permute-start(bf16[128,512]{1,0:T(8,128)(2,1)S(1)} %get-tuple-element.81), channel_id=1, source_target_pairs={{0,2},{1,3},{2,0},{3,1},{4,6},{5,7},{6,4},{7,5},{8,10},{9,11},{10,... | collective-permute-start | bytes 393224 | tf_op jit(solution)/shard_map/ppermute | solution.py:533
  47.8 8.7 %collective-permute-start.12 = (bf16[128,512]{1,0:T(8,128)(2,1)S(1)}, bf16[128,512]{1,0:T(8,128)(2,1)S(1)}, u32[]{:S(2)}, u32[]{:S(2)}) collective-permute-start(bf16[128,512]{1,0:T(8,128)(2,1)S(1)} %get-tuple-element.82), channel_id=1, source_target_pairs={{0,1},{1,0},{2,3},{3,2},{4,5},{5,4},{6,7},{7,6},{8,9},{9,8},{10,11... | collective-permute-start | bytes 393224 | tf_op jit(solution)/shard_map/ppermute | solution.py:533
  47.8 8.7 %collective-permute-start.5 = (bf16[128,512]{1,0:T(8,128)(2,1)S(1)}, bf16[128,512]{1,0:T(8,128)(2,1)S(1)}, u32[]{:S(2)}, u32[]{:S(2)}) collective-permute-start(bf16[128,512]{1,0:T(8,128)(2,1)S(1)} %get-tuple-element.73), channel_id=1, source_target_pairs={{0,5},{1,4},{2,7},{3,6},{4,1},{5,0},{6,3},{7,2},{8,13},{9,12},{10,... | collective-permute-start | bytes 393224 | tf_op jit(solution)/shard_map/ppermute | solution.py:533
  56.5 10.8 %collective-permute-start.13 = (bf16[128,512]{1,0:T(8,128)(2,1)S(1)}, bf16[128,512]{1,0:T(8,128)(2,1)S(1)}, u32[]{:S(2)}, u32[]{:S(2)}) collective-permute-start(bf16[128,512]{1,0:T(8,128)(2,1)S(1)} %get-tuple-element.87), channel_id=1, source_target_pairs={{0,7},{1,6},{2,5},{3,4},{4,3},{5,2},{6,1},{7,0},{8,15},{9,14},{10,... | collective-permute-start | bytes 393224 | tf_op jit(solution)/shard_map/ppermute | solution.py:533
  58.8 10.6 %collective-permute-start.19 = (bf16[128,512]{1,0:T(8,128)(2,1)S(1)}, bf16[128,512]{1,0:T(8,128)(2,1)S(1)}, u32[]{:S(2)}, u32[]{:S(2)}) collective-permute-start(bf16[128,512]{1,0:T(8,128)(2,1)S(1)} %get-tuple-element.97), channel_id=1, source_target_pairs={{0,6},{1,7},{2,4},{3,5},{4,2},{5,3},{6,0},{7,1},{8,14},{9,15},{10,... | collective-permute-start | bytes 393224 | tf_op jit(solution)/shard_map/ppermute | solution.py:533
  65.3 7.1 %collective-permute-start.15 = (bf16[128,512]{1,0:T(8,128)(2,1)S(1)}, bf16[128,512]{1,0:T(8,128)(2,1)S(1)}, u32[]{:S(2)}, u32[]{:S(2)}) collective-permute-start(bf16[128,512]{1,0:T(8,128)(2,1)S(1)} %get-tuple-element.90), channel_id=1, source_target_pairs={{0,1},{1,0},{2,3},{3,2},{4,5},{5,4},{6,7},{7,6},{8,9},{9,8},{10,11... | collective-permute-start | bytes 393224 | tf_op jit(solution)/shard_map/ppermute | solution.py:533
  65.4 9.2 %collective-permute-start.16 = (bf16[128,512]{1,0:T(8,128)(2,1)S(1)}, bf16[128,512]{1,0:T(8,128)(2,1)S(1)}, u32[]{:S(2)}, u32[]{:S(2)}) collective-permute-start(bf16[128,512]{1,0:T(8,128)(2,1)S(1)} %get-tuple-element.91), channel_id=1, source_target_pairs={{0,2},{1,3},{2,0},{3,1},{4,6},{5,7},{6,4},{7,5},{8,10},{9,11},{10,... | collective-permute-start | bytes 393224 | tf_op jit(solution)/shard_map/ppermute | solution.py:533
  65.5 11.1 %collective-permute-start.17 = (bf16[128,512]{1,0:T(8,128)(2,1)S(1)}, bf16[128,512]{1,0:T(8,128)(2,1)S(1)}, u32[]{:S(2)}, u32[]{:S(2)}) collective-permute-start(bf16[128,512]{1,0:T(8,128)(2,1)S(1)} %get-tuple-element.92), channel_id=1, source_target_pairs={{0,3},{1,2},{2,1},{3,0},{4,7},{5,6},{6,5},{7,4},{8,11},{9,10},{10,... | collective-permute-start | bytes 393224 | tf_op jit(solution)/shard_map/ppermute | solution.py:533
  67.3 9.4 %collective-permute-start.14 = (bf16[128,512]{1,0:T(8,128)(2,1)S(1)}, bf16[128,512]{1,0:T(8,128)(2,1)S(1)}, u32[]{:S(2)}, u32[]{:S(2)}) collective-permute-start(bf16[128,512]{1,0:T(8,128)(2,1)S(1)} %get-tuple-element.89), channel_id=1, source_target_pairs={{0,5},{1,4},{2,7},{3,6},{4,1},{5,0},{6,3},{7,2},{8,13},{9,12},{10,... | collective-permute-start | bytes 393224 | tf_op jit(solution)/shard_map/ppermute | solution.py:533
  69.4 15.0 %collective-permute-start.20 = (bf16[128,512]{1,0:T(8,128)(2,1)S(1)}, bf16[128,512]{1,0:T(8,128)(2,1)S(1)}, u32[]{:S(2)}, u32[]{:S(2)}) collective-permute-start(bf16[128,512]{1,0:T(8,128)(2,1)S(1)} %get-tuple-element.98), channel_id=1, source_target_pairs={{0,4},{1,5},{2,6},{3,7},{4,0},{5,1},{6,2},{7,3},{8,12},{9,13},{10,... | collective-permute-start | bytes 393224 | tf_op jit(solution)/shard_map/ppermute | solution.py:533
  76.6 9.7 %collective-permute-start.18 = (bf16[128,512]{1,0:T(8,128)(2,1)S(1)}, bf16[128,512]{1,0:T(8,128)(2,1)S(1)}, u32[]{:S(2)}, u32[]{:S(2)}) collective-permute-start(bf16[128,512]{1,0:T(8,128)(2,1)S(1)} %get-tuple-element.93), channel_id=1, source_target_pairs={{0,7},{1,6},{2,5},{3,4},{4,3},{5,2},{6,1},{7,0},{8,15},{9,14},{10,... | collective-permute-start | bytes 393224 | tf_op jit(solution)/shard_map/ppermute | solution.py:533
  84.4 7.4 %collective-permute-start.21 = (bf16[128,512]{1,0:T(8,128)(2,1)S(1)}, bf16[128,512]{1,0:T(8,128)(2,1)S(1)}, u32[]{:S(2)}, u32[]{:S(2)}) collective-permute-start(bf16[128,512]{1,0:T(8,128)(2,1)S(1)} %get-tuple-element.99), channel_id=1, source_target_pairs={{0,6},{1,7},{2,4},{3,5},{4,2},{5,3},{6,0},{7,1},{8,14},{9,15},{10,... | collective-permute-start | bytes 393224 | tf_op jit(solution)/shard_map/ppermute | solution.py:533
  86.3 17.4 %collective-permute-start.22 = (bf16[128,512]{1,0:T(8,128)(2,1)S(1)}, bf16[128,512]{1,0:T(8,128)(2,1)S(1)}, u32[]{:S(2)}, u32[]{:S(2)}) collective-permute-start(bf16[128,512]{1,0:T(8,128)(2,1)S(1)} %get-tuple-element.101), channel_id=1, source_target_pairs={{0,5},{1,4},{2,7},{3,6},{4,1},{5,0},{6,3},{7,2},{8,13},{9,12},{10,... | collective-permute-start | bytes 393224 | tf_op jit(solution)/shard_map/ppermute | solution.py:533
  91.9 13.4 %collective-permute-start.23 = (bf16[128,512]{1,0:T(8,128)(2,1)S(1)}, bf16[128,512]{1,0:T(8,128)(2,1)S(1)}, u32[]{:S(2)}, u32[]{:S(2)}) collective-permute-start(bf16[128,512]{1,0:T(8,128)(2,1)S(1)} %get-tuple-element.103), channel_id=1, source_target_pairs={{0,4},{1,5},{2,6},{3,7},{4,0},{5,1},{6,2},{7,3},{8,12},{9,13},{10,... | collective-permute-start | bytes 393224 | tf_op jit(solution)/shard_map/ppermute | solution.py:533
  103.7 3.6 %copy-start.15 = (bf16[128,256]{1,0:T(8,128)(2,1)S(1)}, bf16[128,256]{1,0:T(8,128)(2,1)}, u32[]{:S(2)}) copy-start(bf16[128,256]{1,0:T(8,128)(2,1)} %constant.19.clone.inv_ref) | copy-start | bytes 196612
  105.9 11.3 %collective-permute-start.28 = (bf16[128,4096]{1,0:T(8,128)(2,1)S(1)}, bf16[128,4096]{1,0:T(8,128)(2,1)S(1)}, u32[]{:S(2)}, u32[]{:S(2)}) collective-permute-start(bf16[128,4096]{1,0:T(8,128)(2,1)S(1)} %get-tuple-element.113.grad_b_ref), channel_id=1, source_target_pairs={{1,0},{2,1},{3,2},{4,3},{5,4},{6,5},{7,6},{9,8},{10,9},{11,10},{12... | collective-permute-start | bytes 3145736 | tf_op jit(solution)/shard_map/ppermute | solution.py:26
  107.4 9.8 %copy-start.7 = (bf16[1,128,4096]{2,1,0:T(8,128)(2,1)S(1)}, bf16[1,128,4096]{2,1,0:T(8,128)(2,1)}, u32[]{:S(2)}) copy-start(bf16[1,128,4096]{2,1,0:T(8,128)(2,1)} %param.16) | copy-start | bytes 3145732
  107.4 9.8 %copy-start.10 = (bf16[128,256]{1,0:T(8,128)(2,1)S(1)}, bf16[128,256]{1,0:T(8,128)(2,1)}, u32[]{:S(2)}) copy-start(bf16[128,256]{1,0:T(8,128)(2,1)} %constant.18.clone.inv_ref) | copy-start | bytes 196612
  109.8 2.7 %collective-permute-start.24 = (bf16[4,128,512]{2,1,0:T(8,128)(2,1)S(1)}, bf16[4,128,512]{2,1,0:T(8,128)(2,1)S(1)}, u32[]{:S(2)}, u32[]{:S(2)}) collective-permute-start(bf16[4,128,512]{2,1,0:T(8,128)(2,1)S(1)} %get-tuple-element.115), channel_id=1, source_target_pairs={{0,1},{1,0},{2,3},{3,2},{4,5},{5,4},{6,7},{7,6},{8,9},{9,8},{10,11... | collective-permute-start | bytes 1572872 | tf_op jit(solution)/shard_map/ppermute | solution.py:533
  112.7 15.5 %collective-permute-start.25 = (bf16[128,512]{1,0:T(8,128)(2,1)S(1)}, bf16[128,512]{1,0:T(8,128)(2,1)S(1)}, u32[]{:S(2)}, u32[]{:S(2)}) collective-permute-start(bf16[128,512]{1,0:T(8,128)(2,1)S(1)} %get-tuple-element.116), channel_id=1, source_target_pairs={{0,6},{1,7},{2,4},{3,5},{4,2},{5,3},{6,0},{7,1},{8,14},{9,15},{10,... | collective-permute-start | bytes 393224 | tf_op jit(solution)/shard_map/ppermute | solution.py:533
  114.6 17.0 %collective-permute-start.26 = (bf16[128,512]{1,0:T(8,128)(2,1)S(1)}, bf16[128,512]{1,0:T(8,128)(2,1)S(1)}, u32[]{:S(2)}, u32[]{:S(2)}) collective-permute-start(bf16[128,512]{1,0:T(8,128)(2,1)S(1)} %get-tuple-element.117), channel_id=1, source_target_pairs={{0,4},{1,5},{2,6},{3,7},{4,0},{5,1},{6,2},{7,3},{8,12},{9,13},{10,... | collective-permute-start | bytes 393224 | tf_op jit(solution)/shard_map/ppermute | solution.py:533
  115.5 16.0 %collective-permute-start.27 = (bf16[128,512]{1,0:T(8,128)(2,1)S(1)}, bf16[128,512]{1,0:T(8,128)(2,1)S(1)}, u32[]{:S(2)}, u32[]{:S(2)}) collective-permute-start(bf16[128,512]{1,0:T(8,128)(2,1)S(1)} %get-tuple-element.118), channel_id=1, source_target_pairs={{0,2},{1,3},{2,0},{3,1},{4,6},{5,7},{6,4},{7,5},{8,10},{9,11},{10,... | collective-permute-start | bytes 393224 | tf_op jit(solution)/shard_map/ppermute | solution.py:533

commit v10 on v8

--- a/solution.py
+++ b/solution.py
@@ -599,6 +599,10 @@
     far_z = local(
         functools.partial(pieces_z_kernel, beta, half), [piece] * half, [me, far, gate_out], few, name="farz"
     )
+    z_6, z_7 = far_pair(far_z[2:], 6)
+    z_5 = swapped(far_z[1], 5)
+    z_4 = swapped(after(far_z[0], z_6), 4)
+    near = after(near, z_5, z_6, z_7)
     near_z = local(
         functools.partial(pieces_z_kernel, beta, 0), [piece] * half, [me, near, gate_out], few, name="nearz"
     )
@@ -608,8 +612,6 @@
         [me, fwd, inv_conv, after(earlier, near_z), mixed_in, filter_taps, inputs, gate_mid, gate_long],
         mid_flops, name="branch",
     )
-    z_6, z_7 = far_pair(far_z[2:], 6)
-    z_4, z_5 = far_pair(far_z[:2], 4, z_6, z_7)
     near_z = exchanged(near_z)
     pieces_z = near_z + [z_4, z_5, z_6, z_7]
     w_6, w_7 = far_pair(pieces_w[6:], 6, (z_4, near_z), (z_5, near_z))

time: 125 us -> 129 us (1.032)
  starting transfers between devices: 48.5 us -> 64.1 us
  waiting for transfers between devices: 50.9 us -> 39.7 us
    ppermute x25, starting transfers between devices: 37.9 us -> 53.5 us  [swapped(): return lax.ppermute(array, 'ctx', [(i, i ^ k) for i in range(count)])]
    ppermute x25, waiting for transfers between devices: 43 us -> 31.9 us  [swapped(): return lax.ppermute(array, 'ctx', [(i, i ^ k) for i in range(count)])]
  transfers between devices with their start and end apart: 29 -> 29, of which waited for: 15 -> 14; matrix products, arithmetic and copies ran while one was open for 0% -> 0% of each run, Pallas kernels for 16% -> 16%
where the time goes in v10:
time: 129 us
  starting transfers between devices  64.1 us (50%)
  waiting for transfers between devices  39.7 us (31%)
  Pallas kernels  21.5 us (17%)
  local copies, waits for them, and re-layouts  2.61 us (2%)
    ppermute x25, starting transfers between devices, swapped(): return lax.ppermute(array, 'ctx', [(i, i ^ k) for i in range(count)])  53.5 us
    ppermute x25, waiting for transfers between devices, swapped(): return lax.ppermute(array, 'ctx', [(i, i ^ k) for i in range(count)])  31.9 us
    pallas_call x13, Pallas kernels, local(): pl.pallas_call(body, in_specs=specs, out_specs=[pl.BlockSpec(memory_space...  21.5 us
    ppermute x2, waiting for transfers between devices, passed_along(): return lax.ppermute(value, axis, pairs)  7.85 us
    ppermute x2, starting transfers between devices, passed_along(): return lax.ppermute(value, axis, pairs)  7.38 us
    ppermute x2, starting transfers between devices, shifted(): return lax.ppermute(array, axis, pairs)  3.26 us
    unnamed x32, local copies, waits for them, and re-layouts  2.61 us
  transfers between devices with their start and end apart: 29, of which 14 were waited for; matrix products, arithmetic and copies ran while one was open for 0% of the time, Pallas kernels for 16%

profile of v10, /device:TPU:0, one launch (start us, length us, event | category | flops | bytes accessed | tf_op | source)
XLA Modules:
  0.0 128.8 jit_solution(7622512181879926566)
XLA Ops:
  0.7 1.3 %copy-done.3 = bf16[1,128,4096]{2,1,0:T(8,128)(2,1)S(1)} copy-done((bf16[1,128,4096]{2,1,0:T(8,128)(2,1)S(1)}, bf16[1,128,4096]{2,1,0:T(8,128)(2,1)}, u32[]{:S(2)}) %copy-start.3) | copy-done | bytes 1048600
  2.0 3.9 %collective-permute-start.1 = (bf16[128,2048]{1,0:T(8,128)(2,1)S(1)}, bf16[128,2048]{1,0:T(8,128)(2,1)S(1)}, u32[]{:S(2)}, u32[]{:S(2)}) collective-permute-start(bf16[128,2048]{1,0:T(8,128)(2,1)S(1)} %far.1), channel_id=1, source_target_pairs={{0,24},{8,0},{16,8},{24,16},{1,25},{9,1},{17,9},{25,17},{2,26},{10... | collective-permute-start | bytes 1572872 | tf_op jit(solution)/shard_map/ppermute | solution.py:20
  5.9 1.2 copy-done.6
  7.2 0.2 mix.1.mixed_ref
  7.5 1.8 %collective-permute-start = (bf16[128,4096]{1,0:T(8,128)(2,1)S(1)}, bf16[128,4096]{1,0:T(8,128)(2,1)S(1)}, u32[]{:S(2)}, u32[]{:S(2)}) collective-permute-start(bf16[128,4096]{1,0:T(8,128)(2,1)S(1)} %mix.1.mixed_ref), channel_id=1, source_target_pairs={{0,1},{1,2},{2,3},{3,4},{4,5},{5,6},{6,7},{8,9},{9,10},{10,11},{11... | collective-permute-start | bytes 3145736 | tf_op jit(solution)/shard_map/ppermute | solution.py:26
  9.3 7.9 %collective-permute-done.1.adjoint_ref.far_ref = bf16[128,2048]{1,0:T(8,128)(2,1)S(1)} collective-permute-done((bf16[128,2048]{1,0:T(8,128)(2,1)S(1)}, bf16[128,2048]{1,0:T(8,128)(2,1)S(1)}, u32[]{:S(2)}, u32[]{:S(2)}) %collective-permute-start.1) | collective-permute-done | bytes 524320 | tf_op jit(solution)/shard_map/ppermute | solution.py:20
  17.2 3.4 %collective-permute-start.2 = (bf16[128,2048]{1,0:T(8,128)(2,1)S(1)}, bf16[128,2048]{1,0:T(8,128)(2,1)S(1)}, u32[]{:S(2)}, u32[]{:S(2)}) collective-permute-start(bf16[128,2048]{1,0:T(8,128)(2,1)S(1)} %near.1), channel_id=1, source_target_pairs={{0,24},{8,0},{16,8},{24,16},{1,25},{9,1},{17,9},{25,17},{2,26},{10... | collective-permute-start | bytes 1572872 | tf_op jit(solution)/shard_map/ppermute | solution.py:20
  20.8 3.7 %collective-permute-start.4 = (bf16[128,512]{1,0:T(8,128)(2,1)S(1)}, bf16[128,512]{1,0:T(8,128)(2,1)S(1)}, u32[]{:S(2)}, u32[]{:S(2)}) collective-permute-start(bf16[128,512]{1,0:T(8,128)(2,1)S(1)} %get-tuple-element.67), channel_id=1, source_target_pairs={{0,6},{1,7},{2,4},{3,5},{4,2},{5,3},{6,0},{7,1},{8,14},{9,15},{10,... | collective-permute-start | bytes 393224 | tf_op jit(solution)/shard_map/ppermute | solution.py:533
  24.4 1.6 %collective-permute-start.5 = (bf16[128,512]{1,0:T(8,128)(2,1)S(1)}, bf16[128,512]{1,0:T(8,128)(2,1)S(1)}, u32[]{:S(2)}, u32[]{:S(2)}) collective-permute-start(bf16[128,512]{1,0:T(8,128)(2,1)S(1)} %get-tuple-element.68), channel_id=1, source_target_pairs={{0,7},{1,6},{2,5},{3,4},{4,3},{5,2},{6,1},{7,0},{8,15},{9,14},{10,... | collective-permute-start | bytes 393224 | tf_op jit(solution)/shard_map/ppermute | solution.py:533
  26.1 2.3 %collective-permute-done.4.refs_1_ = bf16[128,512]{1,0:T(8,128)(2,1)S(1)} collective-permute-done((bf16[128,512]{1,0:T(8,128)(2,1)S(1)}, bf16[128,512]{1,0:T(8,128)(2,1)S(1)}, u32[]{:S(2)}, u32[]{:S(2)}) %collective-permute-start.4) | collective-permute-done | bytes 131104 | tf_op jit(solution)/shard_map/ppermute | solution.py:533
  28.4 9.6 %collective-permute-start.6 = (bf16[128,512]{1,0:T(8,128)(2,1)S(1)}, bf16[128,512]{1,0:T(8,128)(2,1)S(1)}, u32[]{:S(2)}, u32[]{:S(2)}) collective-permute-start(bf16[128,512]{1,0:T(8,128)(2,1)S(1)} %get-tuple-element.77), channel_id=1, source_target_pairs={{0,4},{1,5},{2,6},{3,7},{4,0},{5,1},{6,2},{7,3},{8,12},{9,13},{10,... | collective-permute-start | bytes 393224 | tf_op jit(solution)/shard_map/ppermute | solution.py:533
  38.2 5.8 %collective-permute-start.7 = (bf16[128,512]{1,0:T(8,128)(2,1)S(1)}, bf16[128,512]{1,0:T(8,128)(2,1)S(1)}, u32[]{:S(2)}, u32[]{:S(2)}) collective-permute-start(bf16[128,512]{1,0:T(8,128)(2,1)S(1)} %get-tuple-element.73), channel_id=1, source_target_pairs={{0,3},{1,2},{2,1},{3,0},{4,7},{5,6},{6,5},{7,4},{8,11},{9,10},{10,... | collective-permute-start | bytes 393224 | tf_op jit(solution)/shard_map/ppermute | solution.py:533
  44.0 0.8 collective-permute-start.8
  44.9 3.0 %branch.1 = (bf16[256,4096]{1,0:T(8,128)(2,1)S(1)}, bf16[256,4096]{1,0:T(8,128)(2,1)S(1)}, bf16[128,512]{1,0:T(8,128)(2,1)S(1)}, bf16[128,512]{1,0:T(8,128)(2,1)...) custom-call(s32[1]{0:T(128)} %bitcast.me_ref, ...), custom_call_target="tpu_custom_call" | custom-call | flops 1073741824 | bytes 11730948 | tf_op jit(solution)/shard_map/branch/pallas_call | solution.py:518
  48.0 0.5 collective-permute-start.11
  48.5 1.4 %collective-permute-start.12 = (bf16[128,512]{1,0:T(8,128)(2,1)S(1)}, bf16[128,512]{1,0:T(8,128)(2,1)S(1)}, u32[]{:S(2)}, u32[]{:S(2)}) collective-permute-start(bf16[128,512]{1,0:T(8,128)(2,1)S(1)} %get-tuple-element.84), channel_id=1, source_target_pairs={{0,2},{1,3},{2,0},{3,1},{4,6},{5,7},{6,4},{7,5},{8,10},{9,11},{10,... | collective-permute-start | bytes 393224 | tf_op jit(solution)/shard_map/ppermute | solution.py:533
  50.0 1.2 collective-permute-done.8.refs_5_
  51.2 4.2 %collective-permute-start.19 = (bf16[128,512]{1,0:T(8,128)(2,1)S(1)}, bf16[128,512]{1,0:T(8,128)(2,1)S(1)}, u32[]{:S(2)}, u32[]{:S(2)}) collective-permute-start(bf16[128,512]{1,0:T(8,128)(2,1)S(1)} %get-tuple-element.95), channel_id=1, source_target_pairs={{0,6},{1,7},{2,4},{3,5},{4,2},{5,3},{6,0},{7,1},{8,14},{9,15},{10,... | collective-permute-start | bytes 393224 | tf_op jit(solution)/shard_map/ppermute | solution.py:533
  55.5 4.7 %gradw.1 = (bf16[128,512]{1,0:T(8,128)(2,1)S(1)}, bf16[128,512]{1,0:T(8,128)(2,1)S(1)}, bf16[128,512]{1,0:T(8,128)(2,1)S(1)}, bf16[128,512]{1,0:T(8,128)(2,1)S(1...) custom-call(s32[1]{0:T(128)} %bitcast.me_ref, ...), custom_call_target="tpu_custom_call" | custom-call | flops 3221225472 | bytes 4980740 | tf_op jit(solution)/shard_map/gradw/pallas_call | solution.py:518
  60.2 0.2 collective-permute-start.15
  60.4 1.7 %collective-permute-start.17 = (bf16[128,512]{1,0:T(8,128)(2,1)S(1)}, bf16[128,512]{1,0:T(8,128)(2,1)S(1)}, u32[]{:S(2)}, u32[]{:S(2)}) collective-permute-start(bf16[128,512]{1,0:T(8,128)(2,1)S(1)} %get-tuple-element.90), channel_id=1, source_target_pairs={{0,3},{1,2},{2,1},{3,0},{4,7},{5,6},{6,5},{7,4},{8,11},{9,10},{10,... | collective-permute-start | bytes 393224 | tf_op jit(solution)/shard_map/ppermute | solution.py:533
  62.2 1.2 collective-permute-done.19.refs_1_
  63.3 3.6 %collective-permute-start.20 = (bf16[128,512]{1,0:T(8,128)(2,1)S(1)}, bf16[128,512]{1,0:T(8,128)(2,1)S(1)}, u32[]{:S(2)}, u32[]{:S(2)}) collective-permute-start(bf16[128,512]{1,0:T(8,128)(2,1)S(1)} %get-tuple-element.96), channel_id=1, source_target_pairs={{0,4},{1,5},{2,6},{3,7},{4,0},{5,1},{6,2},{7,3},{8,12},{9,13},{10,... | collective-permute-start | bytes 393224 | tf_op jit(solution)/shard_map/ppermute | solution.py:533
  66.9 0.8 collective-permute-start.14
  67.7 0.6 collective-permute-done.16.refs_5_
  68.3 5.5 %collective-permute-done.17.refs_4_ = bf16[128,512]{1,0:T(8,128)(2,1)S(1)} collective-permute-done((bf16[128,512]{1,0:T(8,128)(2,1)S(1)}, bf16[128,512]{1,0:T(8,128)(2,1)S(1)}, u32[]{:S(2)}, u32[]{:S(2)}) %collective-permute-start.17) | collective-permute-done | bytes 131104 | tf_op jit(solution)/shard_map/ppermute | solution.py:533
  73.8 3.2 %collective-permute-done.20.refs_3_ = bf16[128,512]{1,0:T(8,128)(2,1)S(1)} collective-permute-done((bf16[128,512]{1,0:T(8,128)(2,1)S(1)}, bf16[128,512]{1,0:T(8,128)(2,1)S(1)}, u32[]{:S(2)}, u32[]{:S(2)}) %collective-permute-start.20) | collective-permute-done | bytes 131104 | tf_op jit(solution)/shard_map/ppermute | solution.py:533
  76.9 2.6 %collective-permute-start.21 = (bf16[128,512]{1,0:T(8,128)(2,1)S(1)}, bf16[128,512]{1,0:T(8,128)(2,1)S(1)}, u32[]{:S(2)}, u32[]{:S(2)}) collective-permute-start(bf16[128,512]{1,0:T(8,128)(2,1)S(1)} %get-tuple-element.97), channel_id=1, source_target_pairs={{0,6},{1,7},{2,4},{3,5},{4,2},{5,3},{6,0},{7,1},{8,14},{9,15},{10,... | collective-permute-start | bytes 393224 | tf_op jit(solution)/shard_map/ppermute | solution.py:533
  79.6 1.0 collective-permute-done.14.refs_2_
  80.6 1.2 collective-permute-start.18
  81.8 2.0 %collective-permute-done.21.refs_1_ = bf16[128,512]{1,0:T(8,128)(2,1)S(1)} collective-permute-done((bf16[128,512]{1,0:T(8,128)(2,1)S(1)}, bf16[128,512]{1,0:T(8,128)(2,1)S(1)}, u32[]{:S(2)}, u32[]{:S(2)}) %collective-permute-start.21) | collective-permute-done | bytes 131104 | tf_op jit(solution)/shard_map/ppermute | solution.py:533
  83.8 7.5 %collective-permute-start.23 = (bf16[128,512]{1,0:T(8,128)(2,1)S(1)}, bf16[128,512]{1,0:T(8,128)(2,1)S(1)}, u32[]{:S(2)}, u32[]{:S(2)}) collective-permute-start(bf16[128,512]{1,0:T(8,128)(2,1)S(1)} %get-tuple-element.101), channel_id=1, source_target_pairs={{0,4},{1,5},{2,6},{3,7},{4,0},{5,1},{6,2},{7,3},{8,12},{9,13},{10,... | collective-permute-start | bytes 393224 | tf_op jit(solution)/shard_map/ppermute | solution.py:533
  91.3 2.2 %collective-permute-start.22 = (bf16[128,512]{1,0:T(8,128)(2,1)S(1)}, bf16[128,512]{1,0:T(8,128)(2,1)S(1)}, u32[]{:S(2)}, u32[]{:S(2)}) collective-permute-start(bf16[128,512]{1,0:T(8,128)(2,1)S(1)} %get-tuple-element.99), channel_id=1, source_target_pairs={{0,5},{1,4},{2,7},{3,6},{4,1},{5,0},{6,3},{7,2},{8,13},{9,12},{10,... | collective-permute-start | bytes 393224 | tf_op jit(solution)/shard_map/ppermute | solution.py:533
  93.5 5.6 %longgrad.1 = bf16[512,1024]{1,0:T(8,128)(2,1)} custom-call(s32[1]{0:T(128)} %bitcast.me_ref, bf16[512,512]{1,0:T(8,128)(2,1)S(1)} %copy-done.13, bf16[256,512]{1,0:T(8,128)(2,1)S(1)} %copy-done.14, bf16[1024,512]{1,0:T(8,128)(2,1)S(1)} %get-tuple-element.102.grad_ref, bf16[128,512]{1,0:T(8,128)(2,1)S(1)} %collective-permute-done.10.refs_0_, ...), custom_call_target="tpu_custom_call" | custom-call | flops 3221225472 | bytes 3932164 | tf_op jit(solution)/shard_map/longgrad/pallas_call | solution.py:518
  99.2 0.7 collective-permute-done.23.refs_3_
  99.9 1.2 collective-permute-done.22.refs_2_
  101.1 0.6 gradb.1
  101.7 1.5 %collective-permute-start.28 = (bf16[128,4096]{1,0:T(8,128)(2,1)S(1)}, bf16[128,4096]{1,0:T(8,128)(2,1)S(1)}, u32[]{:S(2)}, u32[]{:S(2)}) collective-permute-start(bf16[128,4096]{1,0:T(8,128)(2,1)S(1)} %get-tuple-element.111.grad_b_ref), channel_id=1, source_target_pairs={{1,0},{2,1},{3,2},{4,3},{5,4},{6,5},{7,6},{9,8},{10,9},{11,10},{12... | collective-permute-start | bytes 3145736 | tf_op jit(solution)/shard_map/ppermute | solution.py:26
  103.2 2.4 %taps.1 = (bf16[4,128,512]{2,1,0:T(8,128)(2,1)S(1)}, bf16[4,128,512]{2,1,0:T(8,128)(2,1)S(1)}) custom-call(s32[1]{0:T(128)} %bitcast.me_ref, bf16[256,256]{1,0:T(8,128)(2,1)S(1)} %copy-done.9, bf16[128,256]{1,0:T(8,128)(2,1)S(1)} %copy-done.15, bf16[256,4096]{1,0:T(8,128)(2,1)S(1)} %get-tuple-element.75.signal_ref, ...), custom_call_target="tpu_custom_call" | custom-call | flops 1073741824 | bytes 4390916 | tf_op jit(solution)/shard_map/taps/pallas_call | solution.py:518
  105.7 1.3 %collective-permute-start.24 = (bf16[4,128,512]{2,1,0:T(8,128)(2,1)S(1)}, bf16[4,128,512]{2,1,0:T(8,128)(2,1)S(1)}, u32[]{:S(2)}, u32[]{:S(2)}) collective-permute-start(bf16[4,128,512]{2,1,0:T(8,128)(2,1)S(1)} %get-tuple-element.113), channel_id=1, source_target_pairs={{0,1},{1,0},{2,3},{3,2},{4,5},{5,4},{6,7},{7,6},{8,9},{9,8},{10,11... | collective-permute-start | bytes 1572872 | tf_op jit(solution)/shard_map/ppermute | solution.py:533
  107.0 1.5 %collective-permute-done.24.came_ref = bf16[4,128,512]{2,1,0:T(8,128)(2,1)S(1)} collective-permute-done((bf16[4,128,512]{2,1,0:T(8,128)(2,1)S(1)}, bf16[4,128,512]{2,1,0:T(8,128)(2,1)S(1)}, u32[]{:S(2)}, u32[]{:S(2)}) %collective-permute-start.24) | collective-permute-done | bytes 524320 | tf_op jit(solution)/shard_map/ppermute | solution.py:533
  108.7 2.1 %collective-permute-start.25 = (bf16[128,512]{1,0:T(8,128)(2,1)S(1)}, bf16[128,512]{1,0:T(8,128)(2,1)S(1)}, u32[]{:S(2)}, u32[]{:S(2)}) collective-permute-start(bf16[128,512]{1,0:T(8,128)(2,1)S(1)} %get-tuple-element.114), channel_id=1, source_target_pairs={{0,6},{1,7},{2,4},{3,5},{4,2},{5,3},{6,0},{7,1},{8,14},{9,15},{10,... | collective-permute-start | bytes 393224 | tf_op jit(solution)/shard_map/ppermute | solution.py:533
  110.7 1.5 %collective-permute-start.26 = (bf16[128,512]{1,0:T(8,128)(2,1)S(1)}, bf16[128,512]{1,0:T(8,128)(2,1)S(1)}, u32[]{:S(2)}, u32[]{:S(2)}) collective-permute-start(bf16[128,512]{1,0:T(8,128)(2,1)S(1)} %get-tuple-element.115), channel_id=1, source_target_pairs={{0,4},{1,5},{2,6},{3,7},{4,0},{5,1},{6,2},{7,3},{8,12},{9,13},{10,... | collective-permute-start | bytes 393224 | tf_op jit(solution)/shard_map/ppermute | solution.py:533
  112.2 0.9 collective-permute-start.27
  113.1 3.5 %inputgrad.1 = bf16[128,4096]{1,0:T(8,128)(2,1)} custom-call(bf16[256,256]{1,0:T(8,128)(2,1)S(1)} %copy-done.9, bf16[128,256]{1,0:T(8,128)(2,1)S(1)} %copy-done.10, bf16[128,4096]{1,0:T(8,128)(2,1)S(1)} %get-tuple-element.111.grad_b_ref, bf16[128,4096]{1,0:T(8,128)(2,1)S(1)} %collective-permute-done.28.later_ref, ...), custom_call_target="tpu_custom_call" | custom-call | flops 1073741824 | bytes 8585216 | tf_op jit(solution)/shard_map/inputgrad/pallas_call | solution.py:518
  116.7 7.6 %collective-permute-done.25.refs_0_ = bf16[128,512]{1,0:T(8,128)(2,1)S(1)} collective-permute-done((bf16[128,512]{1,0:T(8,128)(2,1)S(1)}, bf16[128,512]{1,0:T(8,128)(2,1)S(1)}, u32[]{:S(2)}, u32[]{:S(2)}) %collective-permute-start.25) | collective-permute-done | bytes 131104 | tf_op jit(solution)/shard_map/ppermute | solution.py:533
  124.2 3.8 %collective-permute-done.26.refs_1_ = bf16[128,512]{1,0:T(8,128)(2,1)S(1)} collective-permute-done((bf16[128,512]{1,0:T(8,128)(2,1)S(1)}, bf16[128,512]{1,0:T(8,128)(2,1)S(1)}, u32[]{:S(2)}, u32[]{:S(2)}) %collective-permute-start.26) | collective-permute-done | bytes 131104 | tf_op jit(solution)/shard_map/ppermute | solution.py:533
  128.1 0.7 midgrad.1
  (55 shorter events, 0.8 us)
Async XLA Ops:
  0.6 5.3 %copy-start = (bf16[1,128,4096]{2,1,0:T(8,128)(2,1)S(1)}, bf16[1,128,4096]{2,1,0:T(8,128)(2,1)}, u32[]{:S(2)}) copy-start(bf16[1,128,4096]{2,1,0:T(8,128)(2,1)} %param.15) | copy-start | bytes 3145732
  0.6 1.3 %copy-start.3 = (bf16[1,128,4096]{2,1,0:T(8,128)(2,1)S(1)}, bf16[1,128,4096]{2,1,0:T(8,128)(2,1)}, u32[]{:S(2)}) copy-start(bf16[1,128,4096]{2,1,0:T(8,128)(2,1)} %param.14) | copy-start | bytes 3145732
  2.0 15.2 %copy-start.4 = (bf16[1,128,4096]{2,1,0:T(8,128)(2,1)S(1)}, bf16[1,128,4096]{2,1,0:T(8,128)(2,1)}, u32[]{:S(2)}) copy-start(bf16[1,128,4096]{2,1,0:T(8,128)(2,1)} %param.14) | copy-start | bytes 3145732
  2.0 15.1 %collective-permute-start.1 = (bf16[128,2048]{1,0:T(8,128)(2,1)S(1)}, bf16[128,2048]{1,0:T(8,128)(2,1)S(1)}, u32[]{:S(2)}, u32[]{:S(2)}) collective-permute-start(bf16[128,2048]{1,0:T(8,128)(2,1)S(1)} %far.1), channel_id=1, source_target_pairs={{0,24},{8,0},{16,8},{24,16},{1,25},{9,1},{17,9},{25,17},{2,26},{10... | collective-permute-start | bytes 1572872 | tf_op jit(solution)/shard_map/ppermute | solution.py:20
  5.9 1.2 copy-start.6
  7.2 13.4 %copy-start.5 = (bf16[1,128,4096]{2,1,0:T(8,128)(2,1)S(1)}, bf16[1,128,4096]{2,1,0:T(8,128)(2,1)}, u32[]{:S(2)}) copy-start(bf16[1,128,4096]{2,1,0:T(8,128)(2,1)} %param.19) | copy-start | bytes 3145732
  7.4 37.4 %copy-start.1 = (bf16[1,128,4096]{2,1,0:T(8,128)(2,1)S(1)}, bf16[1,128,4096]{2,1,0:T(8,128)(2,1)}, u32[]{:S(2)}) copy-start(bf16[1,128,4096]{2,1,0:T(8,128)(2,1)} %param.18) | copy-start | bytes 3145732
  7.4 37.4 %copy-start.2 = (bf16[1,128,4096]{2,1,0:T(8,128)(2,1)S(1)}, bf16[1,128,4096]{2,1,0:T(8,128)(2,1)}, u32[]{:S(2)}) copy-start(bf16[1,128,4096]{2,1,0:T(8,128)(2,1)} %param.17) | copy-start | bytes 3145732
  7.4 37.4 %copy-start.8 = (bf16[1,128,4096]{2,1,0:T(8,128)(2,1)S(1)}, bf16[1,128,4096]{2,1,0:T(8,128)(2,1)}, u32[]{:S(2)}) copy-start(bf16[1,128,4096]{2,1,0:T(8,128)(2,1)} %param.21) | copy-start | bytes 3145732
  7.5 37.4 %copy-start.9 = (bf16[256,256]{1,0:T(8,128)(2,1)S(1)}, bf16[256,256]{1,0:T(8,128)(2,1)}, u32[]{:S(2)}) copy-start(bf16[256,256]{1,0:T(8,128)(2,1)} %constant.16.clone.fwd_ref) | copy-start | bytes 393220
  7.5 37.4 %copy-start.11 = (bf16[128,256]{1,0:T(8,128)(2,1)S(1)}, bf16[128,256]{1,0:T(8,128)(2,1)}, u32[]{:S(2)}) copy-start(bf16[128,256]{1,0:T(8,128)(2,1)} %constant.17.clone.inv_ref) | copy-start | bytes 196612
  7.5 37.4 %collective-permute-start = (bf16[128,4096]{1,0:T(8,128)(2,1)S(1)}, bf16[128,4096]{1,0:T(8,128)(2,1)S(1)}, u32[]{:S(2)}, u32[]{:S(2)}) collective-permute-start(bf16[128,4096]{1,0:T(8,128)(2,1)S(1)} %mix.1.mixed_ref), channel_id=1, source_target_pairs={{0,1},{1,2},{2,3},{3,4},{4,5},{5,6},{6,7},{8,9},{9,10},{10,11},{11... | collective-permute-start | bytes 3145736 | tf_op jit(solution)/shard_map/ppermute | solution.py:26
  17.2 20.8 %collective-permute-start.2 = (bf16[128,2048]{1,0:T(8,128)(2,1)S(1)}, bf16[128,2048]{1,0:T(8,128)(2,1)S(1)}, u32[]{:S(2)}, u32[]{:S(2)}) collective-permute-start(bf16[128,2048]{1,0:T(8,128)(2,1)S(1)} %near.1), channel_id=1, source_target_pairs={{0,24},{8,0},{16,8},{24,16},{1,25},{9,1},{17,9},{25,17},{2,26},{10... | collective-permute-start | bytes 1572872 | tf_op jit(solution)/shard_map/ppermute | solution.py:20
  20.8 7.6 %collective-permute-start.4 = (bf16[128,512]{1,0:T(8,128)(2,1)S(1)}, bf16[128,512]{1,0:T(8,128)(2,1)S(1)}, u32[]{:S(2)}, u32[]{:S(2)}) collective-permute-start(bf16[128,512]{1,0:T(8,128)(2,1)S(1)} %get-tuple-element.67), channel_id=1, source_target_pairs={{0,6},{1,7},{2,4},{3,5},{4,2},{5,3},{6,0},{7,1},{8,14},{9,15},{10,... | collective-permute-start | bytes 393224 | tf_op jit(solution)/shard_map/ppermute | solution.py:533
  24.4 13.6 %collective-permute-start.3 = (bf16[128,512]{1,0:T(8,128)(2,1)S(1)}, bf16[128,512]{1,0:T(8,128)(2,1)S(1)}, u32[]{:S(2)}, u32[]{:S(2)}) collective-permute-start(bf16[128,512]{1,0:T(8,128)(2,1)S(1)} %get-tuple-element.66), channel_id=1, source_target_pairs={{0,5},{1,4},{2,7},{3,6},{4,1},{5,0},{6,3},{7,2},{8,13},{9,12},{10,... | collective-permute-start | bytes 393224 | tf_op jit(solution)/shard_map/ppermute | solution.py:533
  24.4 13.6 %collective-permute-start.5 = (bf16[128,512]{1,0:T(8,128)(2,1)S(1)}, bf16[128,512]{1,0:T(8,128)(2,1)S(1)}, u32[]{:S(2)}, u32[]{:S(2)}) collective-permute-start(bf16[128,512]{1,0:T(8,128)(2,1)S(1)} %get-tuple-element.68), channel_id=1, source_target_pairs={{0,7},{1,6},{2,5},{3,4},{4,3},{5,2},{6,1},{7,0},{8,15},{9,14},{10,... | collective-permute-start | bytes 393224 | tf_op jit(solution)/shard_map/ppermute | solution.py:533
  28.4 20.1 %collective-permute-start.6 = (bf16[128,512]{1,0:T(8,128)(2,1)S(1)}, bf16[128,512]{1,0:T(8,128)(2,1)S(1)}, u32[]{:S(2)}, u32[]{:S(2)}) collective-permute-start(bf16[128,512]{1,0:T(8,128)(2,1)S(1)} %get-tuple-element.77), channel_id=1, source_target_pairs={{0,4},{1,5},{2,6},{3,7},{4,0},{5,1},{6,2},{7,3},{8,12},{9,13},{10,... | collective-permute-start | bytes 393224 | tf_op jit(solution)/shard_map/ppermute | solution.py:533
  38.2 11.7 %collective-permute-start.7 = (bf16[128,512]{1,0:T(8,128)(2,1)S(1)}, bf16[128,512]{1,0:T(8,128)(2,1)S(1)}, u32[]{:S(2)}, u32[]{:S(2)}) collective-permute-start(bf16[128,512]{1,0:T(8,128)(2,1)S(1)} %get-tuple-element.73), channel_id=1, source_target_pairs={{0,3},{1,2},{2,1},{3,0},{4,7},{5,6},{6,5},{7,4},{8,11},{9,10},{10,... | collective-permute-start | bytes 393224 | tf_op jit(solution)/shard_map/ppermute | solution.py:533
  44.0 7.2 %collective-permute-start.8 = (bf16[128,512]{1,0:T(8,128)(2,1)S(1)}, bf16[128,512]{1,0:T(8,128)(2,1)S(1)}, u32[]{:S(2)}, u32[]{:S(2)}) collective-permute-start(bf16[128,512]{1,0:T(8,128)(2,1)S(1)} %get-tuple-element.72), channel_id=1, source_target_pairs={{0,2},{1,3},{2,0},{3,1},{4,6},{5,7},{6,4},{7,5},{8,10},{9,11},{10,... | collective-permute-start | bytes 393224 | tf_op jit(solution)/shard_map/ppermute | solution.py:533
  44.8 6.4 %collective-permute-start.9 = (bf16[128,512]{1,0:T(8,128)(2,1)S(1)}, bf16[128,512]{1,0:T(8,128)(2,1)S(1)}, u32[]{:S(2)}, u32[]{:S(2)}) collective-permute-start(bf16[128,512]{1,0:T(8,128)(2,1)S(1)} %get-tuple-element.71), channel_id=1, source_target_pairs={{0,1},{1,0},{2,3},{3,2},{4,5},{5,4},{6,7},{7,6},{8,9},{9,8},{10,11... | collective-permute-start | bytes 393224 | tf_op jit(solution)/shard_map/ppermute | solution.py:533
  44.9 10.6 %copy-start.12 = (bf16[1,512,1024]{2,1,0:T(8,128)(2,1)S(1)}, bf16[1,512,1024]{2,1,0:T(8,128)(2,1)}, u32[]{:S(2)}) copy-start(bf16[1,512,1024]{2,1,0:T(8,128)(2,1)} %param.20) | copy-start | bytes 3145732
  44.9 10.6 %copy-start.13 = (bf16[512,512]{1,0:T(8,128)(2,1)S(1)}, bf16[512,512]{1,0:T(8,128)(2,1)}, u32[]{:S(2)}) copy-start(bf16[512,512]{1,0:T(8,128)(2,1)} %constant.20.clone.fwd_ref) | copy-start | bytes 1572868
  44.9 10.5 %copy-start.14 = (bf16[256,512]{1,0:T(8,128)(2,1)S(1)}, bf16[256,512]{1,0:T(8,128)(2,1)}, u32[]{:S(2)}) copy-start(bf16[256,512]{1,0:T(8,128)(2,1)} %constant.21.clone.inv_ref) | copy-start | bytes 786436
  48.0 12.2 %collective-permute-start.11 = (bf16[128,512]{1,0:T(8,128)(2,1)S(1)}, bf16[128,512]{1,0:T(8,128)(2,1)S(1)}, u32[]{:S(2)}, u32[]{:S(2)}) collective-permute-start(bf16[128,512]{1,0:T(8,128)(2,1)S(1)} %get-tuple-element.83), channel_id=1, source_target_pairs={{0,1},{1,0},{2,3},{3,2},{4,5},{5,4},{6,7},{7,6},{8,9},{9,8},{10,11... | collective-permute-start | bytes 393224 | tf_op jit(solution)/shard_map/ppermute | solution.py:533
  48.5 11.9 %collective-permute-start.12 = (bf16[128,512]{1,0:T(8,128)(2,1)S(1)}, bf16[128,512]{1,0:T(8,128)(2,1)S(1)}, u32[]{:S(2)}, u32[]{:S(2)}) collective-permute-start(bf16[128,512]{1,0:T(8,128)(2,1)S(1)} %get-tuple-element.84), channel_id=1, source_target_pairs={{0,2},{1,3},{2,0},{3,1},{4,6},{5,7},{6,4},{7,5},{8,10},{9,11},{10,... | collective-permute-start | bytes 393224 | tf_op jit(solution)/shard_map/ppermute | solution.py:533
  49.9 10.5 %collective-permute-start.13 = (bf16[128,512]{1,0:T(8,128)(2,1)S(1)}, bf16[128,512]{1,0:T(8,128)(2,1)S(1)}, u32[]{:S(2)}, u32[]{:S(2)}) collective-permute-start(bf16[128,512]{1,0:T(8,128)(2,1)S(1)} %get-tuple-element.85), channel_id=1, source_target_pairs={{0,3},{1,2},{2,1},{3,0},{4,7},{5,6},{6,5},{7,4},{8,11},{9,10},{10,... | collective-permute-start | bytes 393224 | tf_op jit(solution)/shard_map/ppermute | solution.py:533
  51.2 12.1 %collective-permute-start.19 = (bf16[128,512]{1,0:T(8,128)(2,1)S(1)}, bf16[128,512]{1,0:T(8,128)(2,1)S(1)}, u32[]{:S(2)}, u32[]{:S(2)}) collective-permute-start(bf16[128,512]{1,0:T(8,128)(2,1)S(1)} %get-tuple-element.95), channel_id=1, source_target_pairs={{0,6},{1,7},{2,4},{3,5},{4,2},{5,3},{6,0},{7,1},{8,14},{9,15},{10,... | collective-permute-start | bytes 393224 | tf_op jit(solution)/shard_map/ppermute | solution.py:533
  55.5 11.5 %collective-permute-start.10 = (bf16[128,512]{1,0:T(8,128)(2,1)S(1)}, bf16[128,512]{1,0:T(8,128)(2,1)S(1)}, u32[]{:S(2)}, u32[]{:S(2)}) collective-permute-start(bf16[128,512]{1,0:T(8,128)(2,1)S(1)} %get-tuple-element.81), channel_id=1, source_target_pairs={{0,7},{1,6},{2,5},{3,4},{4,3},{5,2},{6,1},{7,0},{8,15},{9,14},{10,... | collective-permute-start | bytes 393224 | tf_op jit(solution)/shard_map/ppermute | solution.py:533
  60.2 7.5 %collective-permute-start.15 = (bf16[128,512]{1,0:T(8,128)(2,1)S(1)}, bf16[128,512]{1,0:T(8,128)(2,1)S(1)}, u32[]{:S(2)}, u32[]{:S(2)}) collective-permute-start(bf16[128,512]{1,0:T(8,128)(2,1)S(1)} %get-tuple-element.88), channel_id=1, source_target_pairs={{0,1},{1,0},{2,3},{3,2},{4,5},{5,4},{6,7},{7,6},{8,9},{9,8},{10,11... | collective-permute-start | bytes 393224 | tf_op jit(solution)/shard_map/ppermute | solution.py:533
  60.4 7.9 %collective-permute-start.16 = (bf16[128,512]{1,0:T(8,128)(2,1)S(1)}, bf16[128,512]{1,0:T(8,128)(2,1)S(1)}, u32[]{:S(2)}, u32[]{:S(2)}) collective-permute-start(bf16[128,512]{1,0:T(8,128)(2,1)S(1)} %get-tuple-element.89), channel_id=1, source_target_pairs={{0,2},{1,3},{2,0},{3,1},{4,6},{5,7},{6,4},{7,5},{8,10},{9,11},{10,... | collective-permute-start | bytes 393224 | tf_op jit(solution)/shard_map/ppermute | solution.py:533
  60.4 13.4 %collective-permute-start.17 = (bf16[128,512]{1,0:T(8,128)(2,1)S(1)}, bf16[128,512]{1,0:T(8,128)(2,1)S(1)}, u32[]{:S(2)}, u32[]{:S(2)}) collective-permute-start(bf16[128,512]{1,0:T(8,128)(2,1)S(1)} %get-tuple-element.90), channel_id=1, source_target_pairs={{0,3},{1,2},{2,1},{3,0},{4,7},{5,6},{6,5},{7,4},{8,11},{9,10},{10,... | collective-permute-start | bytes 393224 | tf_op jit(solution)/shard_map/ppermute | solution.py:533
  63.3 13.6 %collective-permute-start.20 = (bf16[128,512]{1,0:T(8,128)(2,1)S(1)}, bf16[128,512]{1,0:T(8,128)(2,1)S(1)}, u32[]{:S(2)}, u32[]{:S(2)}) collective-permute-start(bf16[128,512]{1,0:T(8,128)(2,1)S(1)} %get-tuple-element.96), channel_id=1, source_target_pairs={{0,4},{1,5},{2,6},{3,7},{4,0},{5,1},{6,2},{7,3},{8,12},{9,13},{10,... | collective-permute-start | bytes 393224 | tf_op jit(solution)/shard_map/ppermute | solution.py:533
  66.9 13.6 %collective-permute-start.14 = (bf16[128,512]{1,0:T(8,128)(2,1)S(1)}, bf16[128,512]{1,0:T(8,128)(2,1)S(1)}, u32[]{:S(2)}, u32[]{:S(2)}) collective-permute-start(bf16[128,512]{1,0:T(8,128)(2,1)S(1)} %get-tuple-element.87), channel_id=1, source_target_pairs={{0,5},{1,4},{2,7},{3,6},{4,1},{5,0},{6,3},{7,2},{8,13},{9,12},{10,... | collective-permute-start | bytes 393224 | tf_op jit(solution)/shard_map/ppermute | solution.py:533
  76.9 6.9 %collective-permute-start.21 = (bf16[128,512]{1,0:T(8,128)(2,1)S(1)}, bf16[128,512]{1,0:T(8,128)(2,1)S(1)}, u32[]{:S(2)}, u32[]{:S(2)}) collective-permute-start(bf16[128,512]{1,0:T(8,128)(2,1)S(1)} %get-tuple-element.97), channel_id=1, source_target_pairs={{0,6},{1,7},{2,4},{3,5},{4,2},{5,3},{6,0},{7,1},{8,14},{9,15},{10,... | collective-permute-start | bytes 393224 | tf_op jit(solution)/shard_map/ppermute | solution.py:533
  80.6 10.7 %collective-permute-start.18 = (bf16[128,512]{1,0:T(8,128)(2,1)S(1)}, bf16[128,512]{1,0:T(8,128)(2,1)S(1)}, u32[]{:S(2)}, u32[]{:S(2)}) collective-permute-start(bf16[128,512]{1,0:T(8,128)(2,1)S(1)} %get-tuple-element.91), channel_id=1, source_target_pairs={{0,7},{1,6},{2,5},{3,4},{4,3},{5,2},{6,1},{7,0},{8,15},{9,14},{10,... | collective-permute-start | bytes 393224 | tf_op jit(solution)/shard_map/ppermute | solution.py:533
  83.8 16.1 %collective-permute-start.23 = (bf16[128,512]{1,0:T(8,128)(2,1)S(1)}, bf16[128,512]{1,0:T(8,128)(2,1)S(1)}, u32[]{:S(2)}, u32[]{:S(2)}) collective-permute-start(bf16[128,512]{1,0:T(8,128)(2,1)S(1)} %get-tuple-element.101), channel_id=1, source_target_pairs={{0,4},{1,5},{2,6},{3,7},{4,0},{5,1},{6,2},{7,3},{8,12},{9,13},{10,... | collective-permute-start | bytes 393224 | tf_op jit(solution)/shard_map/ppermute | solution.py:533
  91.3 9.8 %collective-permute-start.22 = (bf16[128,512]{1,0:T(8,128)(2,1)S(1)}, bf16[128,512]{1,0:T(8,128)(2,1)S(1)}, u32[]{:S(2)}, u32[]{:S(2)}) collective-permute-start(bf16[128,512]{1,0:T(8,128)(2,1)S(1)} %get-tuple-element.99), channel_id=1, source_target_pairs={{0,5},{1,4},{2,7},{3,6},{4,1},{5,0},{6,3},{7,2},{8,13},{9,12},{10,... | collective-permute-start | bytes 393224 | tf_op jit(solution)/shard_map/ppermute | solution.py:533
  99.2 4.0 %copy-start.15 = (bf16[128,256]{1,0:T(8,128)(2,1)S(1)}, bf16[128,256]{1,0:T(8,128)(2,1)}, u32[]{:S(2)}) copy-start(bf16[128,256]{1,0:T(8,128)(2,1)} %constant.19.clone.inv_ref) | copy-start | bytes 196612
  101.7 11.4 %collective-permute-start.28 = (bf16[128,4096]{1,0:T(8,128)(2,1)S(1)}, bf16[128,4096]{1,0:T(8,128)(2,1)S(1)}, u32[]{:S(2)}, u32[]{:S(2)}) collective-permute-start(bf16[128,4096]{1,0:T(8,128)(2,1)S(1)} %get-tuple-element.111.grad_b_ref), channel_id=1, source_target_pairs={{1,0},{2,1},{3,2},{4,3},{5,4},{6,5},{7,6},{9,8},{10,9},{11,10},{12... | collective-permute-start | bytes 3145736 | tf_op jit(solution)/shard_map/ppermute | solution.py:26
  103.2 9.9 %copy-start.7 = (bf16[1,128,4096]{2,1,0:T(8,128)(2,1)S(1)}, bf16[1,128,4096]{2,1,0:T(8,128)(2,1)}, u32[]{:S(2)}) copy-start(bf16[1,128,4096]{2,1,0:T(8,128)(2,1)} %param.16) | copy-start | bytes 3145732
  103.2 9.9 %copy-start.10 = (bf16[128,256]{1,0:T(8,128)(2,1)S(1)}, bf16[128,256]{1,0:T(8,128)(2,1)}, u32[]{:S(2)}) copy-start(bf16[128,256]{1,0:T(8,128)(2,1)} %constant.18.clone.inv_ref) | copy-start | bytes 196612
  105.7 2.9 %collective-permute-start.24 = (bf16[4,128,512]{2,1,0:T(8,128)(2,1)S(1)}, bf16[4,128,512]{2,1,0:T(8,128)(2,1)S(1)}, u32[]{:S(2)}, u32[]{:S(2)}) collective-permute-start(bf16[4,128,512]{2,1,0:T(8,128)(2,1)S(1)} %get-tuple-element.113), channel_id=1, source_target_pairs={{0,1},{1,0},{2,3},{3,2},{4,5},{5,4},{6,7},{7,6},{8,9},{9,8},{10,11... | collective-permute-start | bytes 1572872 | tf_op jit(solution)/shard_map/ppermute | solution.py:533
  108.7 15.6 %collective-permute-start.25 = (bf16[128,512]{1,0:T(8,128)(2,1)S(1)}, bf16[128,512]{1,0:T(8,128)(2,1)S(1)}, u32[]{:S(2)}, u32[]{:S(2)}) collective-permute-start(bf16[128,512]{1,0:T(8,128)(2,1)S(1)} %get-tuple-element.114), channel_id=1, source_target_pairs={{0,6},{1,7},{2,4},{3,5},{4,2},{5,3},{6,0},{7,1},{8,14},{9,15},{10,... | collective-permute-start | bytes 393224 | tf_op jit(solution)/shard_map/ppermute | solution.py:533
  110.7 17.3 %collective-permute-start.26 = (bf16[128,512]{1,0:T(8,128)(2,1)S(1)}, bf16[128,512]{1,0:T(8,128)(2,1)S(1)}, u32[]{:S(2)}, u32[]{:S(2)}) collective-permute-start(bf16[128,512]{1,0:T(8,128)(2,1)S(1)} %get-tuple-element.115), channel_id=1, source_target_pairs={{0,4},{1,5},{2,6},{3,7},{4,0},{5,1},{6,2},{7,3},{8,12},{9,13},{10,... | collective-permute-start | bytes 393224 | tf_op jit(solution)/shard_map/ppermute | solution.py:533
  112.2 15.9 %collective-permute-start.27 = (bf16[128,512]{1,0:T(8,128)(2,1)S(1)}, bf16[128,512]{1,0:T(8,128)(2,1)S(1)}, u32[]{:S(2)}, u32[]{:S(2)}) collective-permute-start(bf16[128,512]{1,0:T(8,128)(2,1)S(1)} %get-tuple-element.116), channel_id=1, source_target_pairs={{0,2},{1,3},{2,0},{3,1},{4,6},{5,7},{6,4},{7,5},{8,10},{9,11},{10,... | collective-permute-start | bytes 393224 | tf_op jit(solution)/shard_map/ppermute | solution.py:533

commit v11 on v8

--- a/solution.py
+++ b/solution.py
@@ -612,7 +612,7 @@
     z_4, z_5 = far_pair(far_z[:2], 4, z_6, z_7)
     near_z = exchanged(near_z)
     pieces_z = near_z + [z_4, z_5, z_6, z_7]
-    w_6, w_7 = far_pair(pieces_w[6:], 6, (z_4, near_z), (z_5, near_z))
+    w_6, w_7 = far_pair(pieces_w[6:], 6, z_4, z_5)
     near_w = exchanged(pieces_w[:half])
     *pieces_g, channel_z = local(
         functools.partial(pieces_grad_w_kernel, blocks, devices),

time: 125 us -> 129 us (1.032)
  starting transfers between devices: 48.5 us -> 57.8 us
  waiting for transfers between devices: 50.9 us -> 45.5 us
    ppermute x25, starting transfers between devices: 37.9 us -> 47.2 us  [swapped(): return lax.ppermute(array, 'ctx', [(i, i ^ k) for i in range(count)])]
    ppermute x25, waiting for transfers between devices: 43 us -> 37.6 us  [swapped(): return lax.ppermute(array, 'ctx', [(i, i ^ k) for i in range(count)])]
  transfers between devices with their start and end apart: 29 -> 29, of which waited for: 15 -> 12; matrix products, arithmetic and copies ran while one was open for 0% -> 0% of each run, Pallas kernels for 16% -> 16%
where the time goes in v11:
time: 129 us; the launch traced here: 128 us
  starting transfers between devices  57.8 us (45%)
  waiting for transfers between devices  45.5 us (35%)
  Pallas kernels  21.5 us (17%)
  local copies, waits for them, and re-layouts  2.61 us (2%)
    ppermute x25, starting transfers between devices, swapped(): return lax.ppermute(array, 'ctx', [(i, i ^ k) for i in range(count)])  47.2 us
    ppermute x25, waiting for transfers between devices, swapped(): return lax.ppermute(array, 'ctx', [(i, i ^ k) for i in range(count)])  37.6 us
    pallas_call x13, Pallas kernels, local(): pl.pallas_call(body, in_specs=specs, out_specs=[pl.BlockSpec(memory_space...  21.5 us
    ppermute x2, waiting for transfers between devices, passed_along(): return lax.ppermute(value, axis, pairs)  7.85 us
    ppermute x2, starting transfers between devices, passed_along(): return lax.ppermute(value, axis, pairs)  7.38 us
    ppermute x2, starting transfers between devices, shifted(): return lax.ppermute(array, axis, pairs)  3.26 us
    unnamed x32, local copies, waits for them, and re-layouts  2.61 us
  transfers between devices with their start and end apart: 29, of which 12 were waited for; matrix products, arithmetic and copies ran while one was open for 0% of the time, Pallas kernels for 16%

profile of v11, /device:TPU:0, one launch (start us, length us, event | category | flops | bytes accessed | tf_op | source)
XLA Modules:
  0.0 128.3 jit_solution(7035052174431104648)
XLA Ops:
  0.7 1.3 %copy-done.3 = bf16[1,128,4096]{2,1,0:T(8,128)(2,1)S(1)} copy-done((bf16[1,128,4096]{2,1,0:T(8,128)(2,1)S(1)}, bf16[1,128,4096]{2,1,0:T(8,128)(2,1)}, u32[]{:S(2)}) %copy-start.3) | copy-done | bytes 1048600
  2.0 3.9 %collective-permute-start.1 = (bf16[128,2048]{1,0:T(8,128)(2,1)S(1)}, bf16[128,2048]{1,0:T(8,128)(2,1)S(1)}, u32[]{:S(2)}, u32[]{:S(2)}) collective-permute-start(bf16[128,2048]{1,0:T(8,128)(2,1)S(1)} %far.1), channel_id=1, source_target_pairs={{0,24},{8,0},{16,8},{24,16},{1,25},{9,1},{17,9},{25,17},{2,26},{10... | collective-permute-start | bytes 1572872 | tf_op jit(solution)/shard_map/ppermute | solution.py:20
  5.9 1.2 copy-done.6
  7.2 0.2 mix.1.mixed_ref
  7.5 1.8 %collective-permute-start = (bf16[128,4096]{1,0:T(8,128)(2,1)S(1)}, bf16[128,4096]{1,0:T(8,128)(2,1)S(1)}, u32[]{:S(2)}, u32[]{:S(2)}) collective-permute-start(bf16[128,4096]{1,0:T(8,128)(2,1)S(1)} %mix.1.mixed_ref), channel_id=1, source_target_pairs={{0,1},{1,2},{2,3},{3,4},{4,5},{5,6},{6,7},{8,9},{9,10},{10,11},{11... | collective-permute-start | bytes 3145736 | tf_op jit(solution)/shard_map/ppermute | solution.py:26
  9.3 7.9 %collective-permute-done.1.adjoint_ref.far_ref = bf16[128,2048]{1,0:T(8,128)(2,1)S(1)} collective-permute-done((bf16[128,2048]{1,0:T(8,128)(2,1)S(1)}, bf16[128,2048]{1,0:T(8,128)(2,1)S(1)}, u32[]{:S(2)}, u32[]{:S(2)}) %collective-permute-start.1) | collective-permute-done | bytes 524320 | tf_op jit(solution)/shard_map/ppermute | solution.py:20
  17.2 3.4 %collective-permute-start.2 = (bf16[128,2048]{1,0:T(8,128)(2,1)S(1)}, bf16[128,2048]{1,0:T(8,128)(2,1)S(1)}, u32[]{:S(2)}, u32[]{:S(2)}) collective-permute-start(bf16[128,2048]{1,0:T(8,128)(2,1)S(1)} %near.1), channel_id=1, source_target_pairs={{0,24},{8,0},{16,8},{24,16},{1,25},{9,1},{17,9},{25,17},{2,26},{10... | collective-permute-start | bytes 1572872 | tf_op jit(solution)/shard_map/ppermute | solution.py:20
  20.6 0.2 farz.1
  20.8 2.0 %collective-permute-start.3 = (bf16[128,512]{1,0:T(8,128)(2,1)S(1)}, bf16[128,512]{1,0:T(8,128)(2,1)S(1)}, u32[]{:S(2)}, u32[]{:S(2)}) collective-permute-start(bf16[128,512]{1,0:T(8,128)(2,1)S(1)} %get-tuple-element.72), channel_id=1, source_target_pairs={{0,7},{1,6},{2,5},{3,4},{4,3},{5,2},{6,1},{7,0},{8,15},{9,14},{10,... | collective-permute-start | bytes 393224 | tf_op jit(solution)/shard_map/ppermute | solution.py:533
  22.7 1.8 %collective-permute-start.4 = (bf16[128,512]{1,0:T(8,128)(2,1)S(1)}, bf16[128,512]{1,0:T(8,128)(2,1)S(1)}, u32[]{:S(2)}, u32[]{:S(2)}) collective-permute-start(bf16[128,512]{1,0:T(8,128)(2,1)S(1)} %get-tuple-element.73), channel_id=1, source_target_pairs={{0,6},{1,7},{2,4},{3,5},{4,2},{5,3},{6,0},{7,1},{8,14},{9,15},{10,... | collective-permute-start | bytes 393224 | tf_op jit(solution)/shard_map/ppermute | solution.py:533
  24.5 3.7 %collective-permute-done.3.refs_0_ = bf16[128,512]{1,0:T(8,128)(2,1)S(1)} collective-permute-done((bf16[128,512]{1,0:T(8,128)(2,1)S(1)}, bf16[128,512]{1,0:T(8,128)(2,1)S(1)}, u32[]{:S(2)}, u32[]{:S(2)}) %collective-permute-start.3) | collective-permute-done | bytes 131104 | tf_op jit(solution)/shard_map/ppermute | solution.py:533
  28.3 5.4 %collective-permute-start.5 = (bf16[128,512]{1,0:T(8,128)(2,1)S(1)}, bf16[128,512]{1,0:T(8,128)(2,1)S(1)}, u32[]{:S(2)}, u32[]{:S(2)}) collective-permute-start(bf16[128,512]{1,0:T(8,128)(2,1)S(1)} %get-tuple-element.75), channel_id=1, source_target_pairs={{0,5},{1,4},{2,7},{3,6},{4,1},{5,0},{6,3},{7,2},{8,13},{9,12},{10,... | collective-permute-start | bytes 393224 | tf_op jit(solution)/shard_map/ppermute | solution.py:533
  33.6 3.1 %collective-permute-start.6 = (bf16[128,512]{1,0:T(8,128)(2,1)S(1)}, bf16[128,512]{1,0:T(8,128)(2,1)S(1)}, u32[]{:S(2)}, u32[]{:S(2)}) collective-permute-start(bf16[128,512]{1,0:T(8,128)(2,1)S(1)} %get-tuple-element.77), channel_id=1, source_target_pairs={{0,4},{1,5},{2,6},{3,7},{4,0},{5,1},{6,2},{7,3},{8,12},{9,13},{10,... | collective-permute-start | bytes 393224 | tf_op jit(solution)/shard_map/ppermute | solution.py:533
  36.9 1.1 collective-permute-start.7
  38.0 6.3 %collective-permute-start.8 = (bf16[128,512]{1,0:T(8,128)(2,1)S(1)}, bf16[128,512]{1,0:T(8,128)(2,1)S(1)}, u32[]{:S(2)}, u32[]{:S(2)}) collective-permute-start(bf16[128,512]{1,0:T(8,128)(2,1)S(1)} %get-tuple-element.68), channel_id=1, source_target_pairs={{0,2},{1,3},{2,0},{3,1},{4,6},{5,7},{6,4},{7,5},{8,10},{9,11},{10,... | collective-permute-start | bytes 393224 | tf_op jit(solution)/shard_map/ppermute | solution.py:533
  44.4 3.1 %branch.1 = (bf16[256,4096]{1,0:T(8,128)(2,1)S(1)}, bf16[256,4096]{1,0:T(8,128)(2,1)S(1)}, bf16[128,512]{1,0:T(8,128)(2,1)S(1)}, bf16[128,512]{1,0:T(8,128)(2,1)...) custom-call(s32[1]{0:T(128)} %bitcast.me_ref, ...), custom_call_target="tpu_custom_call" | custom-call | flops 1073741824 | bytes 11730948 | tf_op jit(solution)/shard_map/branch/pallas_call | solution.py:518
  47.5 0.5 collective-permute-start.11
  48.1 1.6 %collective-permute-start.12 = (bf16[128,512]{1,0:T(8,128)(2,1)S(1)}, bf16[128,512]{1,0:T(8,128)(2,1)S(1)}, u32[]{:S(2)}, u32[]{:S(2)}) collective-permute-start(bf16[128,512]{1,0:T(8,128)(2,1)S(1)} %get-tuple-element.84), channel_id=1, source_target_pairs={{0,2},{1,3},{2,0},{3,1},{4,6},{5,7},{6,4},{7,5},{8,10},{9,11},{10,... | collective-permute-start | bytes 393224 | tf_op jit(solution)/shard_map/ppermute | solution.py:533
  49.7 1.8 %collective-permute-done.8.refs_5_ = bf16[128,512]{1,0:T(8,128)(2,1)S(1)} collective-permute-done((bf16[128,512]{1,0:T(8,128)(2,1)S(1)}, bf16[128,512]{1,0:T(8,128)(2,1)S(1)}, u32[]{:S(2)}, u32[]{:S(2)}) %collective-permute-start.8) | collective-permute-done | bytes 131104 | tf_op jit(solution)/shard_map/ppermute | solution.py:533
  51.5 5.1 %collective-permute-start.19 = (bf16[128,512]{1,0:T(8,128)(2,1)S(1)}, bf16[128,512]{1,0:T(8,128)(2,1)S(1)}, u32[]{:S(2)}, u32[]{:S(2)}) collective-permute-start(bf16[128,512]{1,0:T(8,128)(2,1)S(1)} %get-tuple-element.95), channel_id=1, source_target_pairs={{0,6},{1,7},{2,4},{3,5},{4,2},{5,3},{6,0},{7,1},{8,14},{9,15},{10,... | collective-permute-start | bytes 393224 | tf_op jit(solution)/shard_map/ppermute | solution.py:533
  56.6 4.7 %gradw.1 = (bf16[128,512]{1,0:T(8,128)(2,1)S(1)}, bf16[128,512]{1,0:T(8,128)(2,1)S(1)}, bf16[128,512]{1,0:T(8,128)(2,1)S(1)}, bf16[128,512]{1,0:T(8,128)(2,1)S(1...) custom-call(s32[1]{0:T(128)} %bitcast.me_ref, ...), custom_call_target="tpu_custom_call" | custom-call | flops 3221225472 | bytes 4980740 | tf_op jit(solution)/shard_map/gradw/pallas_call | solution.py:518
  61.3 0.4 collective-permute-start.14
  61.7 1.7 %collective-permute-start.15 = (bf16[128,512]{1,0:T(8,128)(2,1)S(1)}, bf16[128,512]{1,0:T(8,128)(2,1)S(1)}, u32[]{:S(2)}, u32[]{:S(2)}) collective-permute-start(bf16[128,512]{1,0:T(8,128)(2,1)S(1)} %get-tuple-element.88), channel_id=1, source_target_pairs={{0,1},{1,0},{2,3},{3,2},{4,5},{5,4},{6,7},{7,6},{8,9},{9,8},{10,11... | collective-permute-start | bytes 393224 | tf_op jit(solution)/shard_map/ppermute | solution.py:533
  63.4 1.8 %collective-permute-start.16 = (bf16[128,512]{1,0:T(8,128)(2,1)S(1)}, bf16[128,512]{1,0:T(8,128)(2,1)S(1)}, u32[]{:S(2)}, u32[]{:S(2)}) collective-permute-start(bf16[128,512]{1,0:T(8,128)(2,1)S(1)} %get-tuple-element.89), channel_id=1, source_target_pairs={{0,2},{1,3},{2,0},{3,1},{4,6},{5,7},{6,4},{7,5},{8,10},{9,11},{10,... | collective-permute-start | bytes 393224 | tf_op jit(solution)/shard_map/ppermute | solution.py:533
  65.3 0.7 collective-permute-start.20
  66.0 4.7 %collective-permute-done.14.refs_2_ = bf16[128,512]{1,0:T(8,128)(2,1)S(1)} collective-permute-done((bf16[128,512]{1,0:T(8,128)(2,1)S(1)}, bf16[128,512]{1,0:T(8,128)(2,1)S(1)}, u32[]{:S(2)}, u32[]{:S(2)}) %collective-permute-start.14) | collective-permute-done | bytes 131104 | tf_op jit(solution)/shard_map/ppermute | solution.py:533
  70.7 3.8 %collective-permute-done.16.refs_5_ = bf16[128,512]{1,0:T(8,128)(2,1)S(1)} collective-permute-done((bf16[128,512]{1,0:T(8,128)(2,1)S(1)}, bf16[128,512]{1,0:T(8,128)(2,1)S(1)}, u32[]{:S(2)}, u32[]{:S(2)}) %collective-permute-start.16) | collective-permute-done | bytes 131104 | tf_op jit(solution)/shard_map/ppermute | solution.py:533
  74.5 2.1 %collective-permute-done.17.refs_4_ = bf16[128,512]{1,0:T(8,128)(2,1)S(1)} collective-permute-done((bf16[128,512]{1,0:T(8,128)(2,1)S(1)}, bf16[128,512]{1,0:T(8,128)(2,1)S(1)}, u32[]{:S(2)}, u32[]{:S(2)}) %collective-permute-start.17) | collective-permute-done | bytes 131104 | tf_op jit(solution)/shard_map/ppermute | solution.py:533
  76.7 1.7 %collective-permute-start.18 = (bf16[128,512]{1,0:T(8,128)(2,1)S(1)}, bf16[128,512]{1,0:T(8,128)(2,1)S(1)}, u32[]{:S(2)}, u32[]{:S(2)}) collective-permute-start(bf16[128,512]{1,0:T(8,128)(2,1)S(1)} %get-tuple-element.91), channel_id=1, source_target_pairs={{0,7},{1,6},{2,5},{3,4},{4,3},{5,2},{6,1},{7,0},{8,15},{9,14},{10,... | collective-permute-start | bytes 393224 | tf_op jit(solution)/shard_map/ppermute | solution.py:533
  78.4 1.9 %collective-permute-start.21 = (bf16[128,512]{1,0:T(8,128)(2,1)S(1)}, bf16[128,512]{1,0:T(8,128)(2,1)S(1)}, u32[]{:S(2)}, u32[]{:S(2)}) collective-permute-start(bf16[128,512]{1,0:T(8,128)(2,1)S(1)} %get-tuple-element.97), channel_id=1, source_target_pairs={{0,6},{1,7},{2,4},{3,5},{4,2},{5,3},{6,0},{7,1},{8,14},{9,15},{10,... | collective-permute-start | bytes 393224 | tf_op jit(solution)/shard_map/ppermute | solution.py:533
  80.3 3.8 %collective-permute-done.18.refs_0_ = bf16[128,512]{1,0:T(8,128)(2,1)S(1)} collective-permute-done((bf16[128,512]{1,0:T(8,128)(2,1)S(1)}, bf16[128,512]{1,0:T(8,128)(2,1)S(1)}, u32[]{:S(2)}, u32[]{:S(2)}) %collective-permute-start.18) | collective-permute-done | bytes 131104 | tf_op jit(solution)/shard_map/ppermute | solution.py:533
  84.0 3.3 %collective-permute-start.22 = (bf16[128,512]{1,0:T(8,128)(2,1)S(1)}, bf16[128,512]{1,0:T(8,128)(2,1)S(1)}, u32[]{:S(2)}, u32[]{:S(2)}) collective-permute-start(bf16[128,512]{1,0:T(8,128)(2,1)S(1)} %get-tuple-element.99), channel_id=1, source_target_pairs={{0,5},{1,4},{2,7},{3,6},{4,1},{5,0},{6,3},{7,2},{8,13},{9,12},{10,... | collective-permute-start | bytes 393224 | tf_op jit(solution)/shard_map/ppermute | solution.py:533
  87.3 3.1 %collective-permute-start.23 = (bf16[128,512]{1,0:T(8,128)(2,1)S(1)}, bf16[128,512]{1,0:T(8,128)(2,1)S(1)}, u32[]{:S(2)}, u32[]{:S(2)}) collective-permute-start(bf16[128,512]{1,0:T(8,128)(2,1)S(1)} %get-tuple-element.101), channel_id=1, source_target_pairs={{0,4},{1,5},{2,6},{3,7},{4,0},{5,1},{6,2},{7,3},{8,12},{9,13},{10,... | collective-permute-start | bytes 393224 | tf_op jit(solution)/shard_map/ppermute | solution.py:533
  90.4 5.7 %longgrad.1 = bf16[512,1024]{1,0:T(8,128)(2,1)} custom-call(s32[1]{0:T(128)} %bitcast.me_ref, bf16[512,512]{1,0:T(8,128)(2,1)S(1)} %copy-done.13, bf16[256,512]{1,0:T(8,128)(2,1)S(1)} %copy-done.14, bf16[1024,512]{1,0:T(8,128)(2,1)S(1)} %get-tuple-element.102.grad_ref, bf16[128,512]{1,0:T(8,128)(2,1)S(1)} %collective-permute-done.10.refs_0_, ...), custom_call_target="tpu_custom_call" | custom-call | flops 3221225472 | bytes 3932164 | tf_op jit(solution)/shard_map/longgrad/pallas_call | solution.py:518
  96.1 2.6 %collective-permute-done.22.refs_2_ = bf16[128,512]{1,0:T(8,128)(2,1)S(1)} collective-permute-done((bf16[128,512]{1,0:T(8,128)(2,1)S(1)}, bf16[128,512]{1,0:T(8,128)(2,1)S(1)}, u32[]{:S(2)}, u32[]{:S(2)}) %collective-permute-start.22) | collective-permute-done | bytes 131104 | tf_op jit(solution)/shard_map/ppermute | solution.py:533
  98.6 2.7 %collective-permute-done.23.refs_3_ = bf16[128,512]{1,0:T(8,128)(2,1)S(1)} collective-permute-done((bf16[128,512]{1,0:T(8,128)(2,1)S(1)}, bf16[128,512]{1,0:T(8,128)(2,1)S(1)}, u32[]{:S(2)}, u32[]{:S(2)}) %collective-permute-start.23) | collective-permute-done | bytes 131104 | tf_op jit(solution)/shard_map/ppermute | solution.py:533
  101.4 0.6 gradb.1
  102.0 1.5 %collective-permute-start.28 = (bf16[128,4096]{1,0:T(8,128)(2,1)S(1)}, bf16[128,4096]{1,0:T(8,128)(2,1)S(1)}, u32[]{:S(2)}, u32[]{:S(2)}) collective-permute-start(bf16[128,4096]{1,0:T(8,128)(2,1)S(1)} %get-tuple-element.111.grad_b_ref), channel_id=1, source_target_pairs={{1,0},{2,1},{3,2},{4,3},{5,4},{6,5},{7,6},{9,8},{10,9},{11,10},{12... | collective-permute-start | bytes 3145736 | tf_op jit(solution)/shard_map/ppermute | solution.py:26
  103.5 2.4 %taps.1 = (bf16[4,128,512]{2,1,0:T(8,128)(2,1)S(1)}, bf16[4,128,512]{2,1,0:T(8,128)(2,1)S(1)}) custom-call(s32[1]{0:T(128)} %bitcast.me_ref, bf16[256,256]{1,0:T(8,128)(2,1)S(1)} %copy-done.9, bf16[128,256]{1,0:T(8,128)(2,1)S(1)} %copy-done.15, bf16[256,4096]{1,0:T(8,128)(2,1)S(1)} %get-tuple-element.71.signal_ref, ...), custom_call_target="tpu_custom_call" | custom-call | flops 1073741824 | bytes 4390916 | tf_op jit(solution)/shard_map/taps/pallas_call | solution.py:518
  105.9 1.2 collective-permute-start.24
  107.1 1.5 %collective-permute-done.24.came_ref = bf16[4,128,512]{2,1,0:T(8,128)(2,1)S(1)} collective-permute-done((bf16[4,128,512]{2,1,0:T(8,128)(2,1)S(1)}, bf16[4,128,512]{2,1,0:T(8,128)(2,1)S(1)}, u32[]{:S(2)}, u32[]{:S(2)}) %collective-permute-start.24) | collective-permute-done | bytes 524320 | tf_op jit(solution)/shard_map/ppermute | solution.py:533
  108.8 1.7 %collective-permute-start.25 = (bf16[128,512]{1,0:T(8,128)(2,1)S(1)}, bf16[128,512]{1,0:T(8,128)(2,1)S(1)}, u32[]{:S(2)}, u32[]{:S(2)}) collective-permute-start(bf16[128,512]{1,0:T(8,128)(2,1)S(1)} %get-tuple-element.114), channel_id=1, source_target_pairs={{0,6},{1,7},{2,4},{3,5},{4,2},{5,3},{6,0},{7,1},{8,14},{9,15},{10,... | collective-permute-start | bytes 393224 | tf_op jit(solution)/shard_map/ppermute | solution.py:533
  110.5 1.4 %collective-permute-start.26 = (bf16[128,512]{1,0:T(8,128)(2,1)S(1)}, bf16[128,512]{1,0:T(8,128)(2,1)S(1)}, u32[]{:S(2)}, u32[]{:S(2)}) collective-permute-start(bf16[128,512]{1,0:T(8,128)(2,1)S(1)} %get-tuple-element.115), channel_id=1, source_target_pairs={{0,4},{1,5},{2,6},{3,7},{4,0},{5,1},{6,2},{7,3},{8,12},{9,13},{10,... | collective-permute-start | bytes 393224 | tf_op jit(solution)/shard_map/ppermute | solution.py:533
  111.9 1.3 %collective-permute-start.27 = (bf16[128,512]{1,0:T(8,128)(2,1)S(1)}, bf16[128,512]{1,0:T(8,128)(2,1)S(1)}, u32[]{:S(2)}, u32[]{:S(2)}) collective-permute-start(bf16[128,512]{1,0:T(8,128)(2,1)S(1)} %get-tuple-element.116), channel_id=1, source_target_pairs={{0,2},{1,3},{2,0},{3,1},{4,6},{5,7},{6,4},{7,5},{8,10},{9,11},{10,... | collective-permute-start | bytes 393224 | tf_op jit(solution)/shard_map/ppermute | solution.py:533
  113.3 3.5 %inputgrad.1 = bf16[128,4096]{1,0:T(8,128)(2,1)} custom-call(bf16[256,256]{1,0:T(8,128)(2,1)S(1)} %copy-done.9, bf16[128,256]{1,0:T(8,128)(2,1)S(1)} %copy-done.10, bf16[128,4096]{1,0:T(8,128)(2,1)S(1)} %get-tuple-element.111.grad_b_ref, bf16[128,4096]{1,0:T(8,128)(2,1)S(1)} %collective-permute-done.28.later_ref, ...), custom_call_target="tpu_custom_call" | custom-call | flops 1073741824 | bytes 8585216 | tf_op jit(solution)/shard_map/inputgrad/pallas_call | solution.py:518
  116.8 7.2 %collective-permute-done.25.refs_0_ = bf16[128,512]{1,0:T(8,128)(2,1)S(1)} collective-permute-done((bf16[128,512]{1,0:T(8,128)(2,1)S(1)}, bf16[128,512]{1,0:T(8,128)(2,1)S(1)}, u32[]{:S(2)}, u32[]{:S(2)}) %collective-permute-start.25) | collective-permute-done | bytes 131104 | tf_op jit(solution)/shard_map/ppermute | solution.py:533
  124.0 3.6 %collective-permute-done.26.refs_1_ = bf16[128,512]{1,0:T(8,128)(2,1)S(1)} collective-permute-done((bf16[128,512]{1,0:T(8,128)(2,1)S(1)}, bf16[128,512]{1,0:T(8,128)(2,1)S(1)}, u32[]{:S(2)}, u32[]{:S(2)}) %collective-permute-start.26) | collective-permute-done | bytes 131104 | tf_op jit(solution)/shard_map/ppermute | solution.py:533
  127.6 0.7 midgrad.1
  (55 shorter events, 0.7 us)
Async XLA Ops:
  0.6 5.3 %copy-start = (bf16[1,128,4096]{2,1,0:T(8,128)(2,1)S(1)}, bf16[1,128,4096]{2,1,0:T(8,128)(2,1)}, u32[]{:S(2)}) copy-start(bf16[1,128,4096]{2,1,0:T(8,128)(2,1)} %param.15) | copy-start | bytes 3145732
  0.6 1.3 %copy-start.3 = (bf16[1,128,4096]{2,1,0:T(8,128)(2,1)S(1)}, bf16[1,128,4096]{2,1,0:T(8,128)(2,1)}, u32[]{:S(2)}) copy-start(bf16[1,128,4096]{2,1,0:T(8,128)(2,1)} %param.14) | copy-start | bytes 3145732
  2.0 15.2 %copy-start.4 = (bf16[1,128,4096]{2,1,0:T(8,128)(2,1)S(1)}, bf16[1,128,4096]{2,1,0:T(8,128)(2,1)}, u32[]{:S(2)}) copy-start(bf16[1,128,4096]{2,1,0:T(8,128)(2,1)} %param.14) | copy-start | bytes 3145732
  2.0 15.1 %collective-permute-start.1 = (bf16[128,2048]{1,0:T(8,128)(2,1)S(1)}, bf16[128,2048]{1,0:T(8,128)(2,1)S(1)}, u32[]{:S(2)}, u32[]{:S(2)}) collective-permute-start(bf16[128,2048]{1,0:T(8,128)(2,1)S(1)} %far.1), channel_id=1, source_target_pairs={{0,24},{8,0},{16,8},{24,16},{1,25},{9,1},{17,9},{25,17},{2,26},{10... | collective-permute-start | bytes 1572872 | tf_op jit(solution)/shard_map/ppermute | solution.py:20
  5.9 1.2 copy-start.6
  7.2 13.4 %copy-start.5 = (bf16[1,128,4096]{2,1,0:T(8,128)(2,1)S(1)}, bf16[1,128,4096]{2,1,0:T(8,128)(2,1)}, u32[]{:S(2)}) copy-start(bf16[1,128,4096]{2,1,0:T(8,128)(2,1)} %param.19) | copy-start | bytes 3145732
  7.4 36.9 %copy-start.1 = (bf16[1,128,4096]{2,1,0:T(8,128)(2,1)S(1)}, bf16[1,128,4096]{2,1,0:T(8,128)(2,1)}, u32[]{:S(2)}) copy-start(bf16[1,128,4096]{2,1,0:T(8,128)(2,1)} %param.18) | copy-start | bytes 3145732
  7.4 36.9 %copy-start.2 = (bf16[1,128,4096]{2,1,0:T(8,128)(2,1)S(1)}, bf16[1,128,4096]{2,1,0:T(8,128)(2,1)}, u32[]{:S(2)}) copy-start(bf16[1,128,4096]{2,1,0:T(8,128)(2,1)} %param.17) | copy-start | bytes 3145732
  7.4 36.9 %copy-start.8 = (bf16[1,128,4096]{2,1,0:T(8,128)(2,1)S(1)}, bf16[1,128,4096]{2,1,0:T(8,128)(2,1)}, u32[]{:S(2)}) copy-start(bf16[1,128,4096]{2,1,0:T(8,128)(2,1)} %param.21) | copy-start | bytes 3145732
  7.5 36.9 %copy-start.9 = (bf16[256,256]{1,0:T(8,128)(2,1)S(1)}, bf16[256,256]{1,0:T(8,128)(2,1)}, u32[]{:S(2)}) copy-start(bf16[256,256]{1,0:T(8,128)(2,1)} %constant.16.clone.fwd_ref) | copy-start | bytes 393220
  7.5 36.8 %copy-start.11 = (bf16[128,256]{1,0:T(8,128)(2,1)S(1)}, bf16[128,256]{1,0:T(8,128)(2,1)}, u32[]{:S(2)}) copy-start(bf16[128,256]{1,0:T(8,128)(2,1)} %constant.17.clone.inv_ref) | copy-start | bytes 196612
  7.5 36.8 %collective-permute-start = (bf16[128,4096]{1,0:T(8,128)(2,1)S(1)}, bf16[128,4096]{1,0:T(8,128)(2,1)S(1)}, u32[]{:S(2)}, u32[]{:S(2)}) collective-permute-start(bf16[128,4096]{1,0:T(8,128)(2,1)S(1)} %mix.1.mixed_ref), channel_id=1, source_target_pairs={{0,1},{1,2},{2,3},{3,4},{4,5},{5,6},{6,7},{8,9},{9,10},{10,11},{11... | collective-permute-start | bytes 3145736 | tf_op jit(solution)/shard_map/ppermute | solution.py:26
  17.2 19.5 %collective-permute-start.2 = (bf16[128,2048]{1,0:T(8,128)(2,1)S(1)}, bf16[128,2048]{1,0:T(8,128)(2,1)S(1)}, u32[]{:S(2)}, u32[]{:S(2)}) collective-permute-start(bf16[128,2048]{1,0:T(8,128)(2,1)S(1)} %near.1), channel_id=1, source_target_pairs={{0,24},{8,0},{16,8},{24,16},{1,25},{9,1},{17,9},{25,17},{2,26},{10... | collective-permute-start | bytes 1572872 | tf_op jit(solution)/shard_map/ppermute | solution.py:20
  20.8 7.5 %collective-permute-start.3 = (bf16[128,512]{1,0:T(8,128)(2,1)S(1)}, bf16[128,512]{1,0:T(8,128)(2,1)S(1)}, u32[]{:S(2)}, u32[]{:S(2)}) collective-permute-start(bf16[128,512]{1,0:T(8,128)(2,1)S(1)} %get-tuple-element.72), channel_id=1, source_target_pairs={{0,7},{1,6},{2,5},{3,4},{4,3},{5,2},{6,1},{7,0},{8,15},{9,14},{10,... | collective-permute-start | bytes 393224 | tf_op jit(solution)/shard_map/ppermute | solution.py:533
  22.7 10.9 %collective-permute-start.4 = (bf16[128,512]{1,0:T(8,128)(2,1)S(1)}, bf16[128,512]{1,0:T(8,128)(2,1)S(1)}, u32[]{:S(2)}, u32[]{:S(2)}) collective-permute-start(bf16[128,512]{1,0:T(8,128)(2,1)S(1)} %get-tuple-element.73), channel_id=1, source_target_pairs={{0,6},{1,7},{2,4},{3,5},{4,2},{5,3},{6,0},{7,1},{8,14},{9,15},{10,... | collective-permute-start | bytes 393224 | tf_op jit(solution)/shard_map/ppermute | solution.py:533
  28.3 19.2 %collective-permute-start.5 = (bf16[128,512]{1,0:T(8,128)(2,1)S(1)}, bf16[128,512]{1,0:T(8,128)(2,1)S(1)}, u32[]{:S(2)}, u32[]{:S(2)}) collective-permute-start(bf16[128,512]{1,0:T(8,128)(2,1)S(1)} %get-tuple-element.75), channel_id=1, source_target_pairs={{0,5},{1,4},{2,7},{3,6},{4,1},{5,0},{6,3},{7,2},{8,13},{9,12},{10,... | collective-permute-start | bytes 393224 | tf_op jit(solution)/shard_map/ppermute | solution.py:533
  33.6 13.9 %collective-permute-start.6 = (bf16[128,512]{1,0:T(8,128)(2,1)S(1)}, bf16[128,512]{1,0:T(8,128)(2,1)S(1)}, u32[]{:S(2)}, u32[]{:S(2)}) collective-permute-start(bf16[128,512]{1,0:T(8,128)(2,1)S(1)} %get-tuple-element.77), channel_id=1, source_target_pairs={{0,4},{1,5},{2,6},{3,7},{4,0},{5,1},{6,2},{7,3},{8,12},{9,13},{10,... | collective-permute-start | bytes 393224 | tf_op jit(solution)/shard_map/ppermute | solution.py:533
  36.9 11.2 %collective-permute-start.7 = (bf16[128,512]{1,0:T(8,128)(2,1)S(1)}, bf16[128,512]{1,0:T(8,128)(2,1)S(1)}, u32[]{:S(2)}, u32[]{:S(2)}) collective-permute-start(bf16[128,512]{1,0:T(8,128)(2,1)S(1)} %get-tuple-element.69), channel_id=1, source_target_pairs={{0,3},{1,2},{2,1},{3,0},{4,7},{5,6},{6,5},{7,4},{8,11},{9,10},{10,... | collective-permute-start | bytes 393224 | tf_op jit(solution)/shard_map/ppermute | solution.py:533
  38.0 13.6 %collective-permute-start.8 = (bf16[128,512]{1,0:T(8,128)(2,1)S(1)}, bf16[128,512]{1,0:T(8,128)(2,1)S(1)}, u32[]{:S(2)}, u32[]{:S(2)}) collective-permute-start(bf16[128,512]{1,0:T(8,128)(2,1)S(1)} %get-tuple-element.68), channel_id=1, source_target_pairs={{0,2},{1,3},{2,0},{3,1},{4,6},{5,7},{6,4},{7,5},{8,10},{9,11},{10,... | collective-permute-start | bytes 393224 | tf_op jit(solution)/shard_map/ppermute | solution.py:533
  44.3 7.2 %collective-permute-start.9 = (bf16[128,512]{1,0:T(8,128)(2,1)S(1)}, bf16[128,512]{1,0:T(8,128)(2,1)S(1)}, u32[]{:S(2)}, u32[]{:S(2)}) collective-permute-start(bf16[128,512]{1,0:T(8,128)(2,1)S(1)} %get-tuple-element.67), channel_id=1, source_target_pairs={{0,1},{1,0},{2,3},{3,2},{4,5},{5,4},{6,7},{7,6},{8,9},{9,8},{10,11... | collective-permute-start | bytes 393224 | tf_op jit(solution)/shard_map/ppermute | solution.py:533
  44.3 12.3 %copy-start.12 = (bf16[1,512,1024]{2,1,0:T(8,128)(2,1)S(1)}, bf16[1,512,1024]{2,1,0:T(8,128)(2,1)}, u32[]{:S(2)}) copy-start(bf16[1,512,1024]{2,1,0:T(8,128)(2,1)} %param.20) | copy-start | bytes 3145732
  44.3 12.2 %copy-start.13 = (bf16[512,512]{1,0:T(8,128)(2,1)S(1)}, bf16[512,512]{1,0:T(8,128)(2,1)}, u32[]{:S(2)}) copy-start(bf16[512,512]{1,0:T(8,128)(2,1)} %constant.20.clone.fwd_ref) | copy-start | bytes 1572868
  44.3 12.2 %copy-start.14 = (bf16[256,512]{1,0:T(8,128)(2,1)S(1)}, bf16[256,512]{1,0:T(8,128)(2,1)}, u32[]{:S(2)}) copy-start(bf16[256,512]{1,0:T(8,128)(2,1)} %constant.21.clone.inv_ref) | copy-start | bytes 786436
  47.4 13.9 %collective-permute-start.10 = (bf16[128,512]{1,0:T(8,128)(2,1)S(1)}, bf16[128,512]{1,0:T(8,128)(2,1)S(1)}, u32[]{:S(2)}, u32[]{:S(2)}) collective-permute-start(bf16[128,512]{1,0:T(8,128)(2,1)S(1)} %get-tuple-element.81), channel_id=1, source_target_pairs={{0,7},{1,6},{2,5},{3,4},{4,3},{5,2},{6,1},{7,0},{8,15},{9,14},{10,... | collective-permute-start | bytes 393224 | tf_op jit(solution)/shard_map/ppermute | solution.py:533
  47.5 13.8 %collective-permute-start.11 = (bf16[128,512]{1,0:T(8,128)(2,1)S(1)}, bf16[128,512]{1,0:T(8,128)(2,1)S(1)}, u32[]{:S(2)}, u32[]{:S(2)}) collective-permute-start(bf16[128,512]{1,0:T(8,128)(2,1)S(1)} %get-tuple-element.83), channel_id=1, source_target_pairs={{0,1},{1,0},{2,3},{3,2},{4,5},{5,4},{6,7},{7,6},{8,9},{9,8},{10,11... | collective-permute-start | bytes 393224 | tf_op jit(solution)/shard_map/ppermute | solution.py:533
  48.1 13.3 %collective-permute-start.12 = (bf16[128,512]{1,0:T(8,128)(2,1)S(1)}, bf16[128,512]{1,0:T(8,128)(2,1)S(1)}, u32[]{:S(2)}, u32[]{:S(2)}) collective-permute-start(bf16[128,512]{1,0:T(8,128)(2,1)S(1)} %get-tuple-element.84), channel_id=1, source_target_pairs={{0,2},{1,3},{2,0},{3,1},{4,6},{5,7},{6,4},{7,5},{8,10},{9,11},{10,... | collective-permute-start | bytes 393224 | tf_op jit(solution)/shard_map/ppermute | solution.py:533
  51.5 9.8 %collective-permute-start.13 = (bf16[128,512]{1,0:T(8,128)(2,1)S(1)}, bf16[128,512]{1,0:T(8,128)(2,1)S(1)}, u32[]{:S(2)}, u32[]{:S(2)}) collective-permute-start(bf16[128,512]{1,0:T(8,128)(2,1)S(1)} %get-tuple-element.85), channel_id=1, source_target_pairs={{0,3},{1,2},{2,1},{3,0},{4,7},{5,6},{6,5},{7,4},{8,11},{9,10},{10,... | collective-permute-start | bytes 393224 | tf_op jit(solution)/shard_map/ppermute | solution.py:533
  51.5 13.8 %collective-permute-start.19 = (bf16[128,512]{1,0:T(8,128)(2,1)S(1)}, bf16[128,512]{1,0:T(8,128)(2,1)S(1)}, u32[]{:S(2)}, u32[]{:S(2)}) collective-permute-start(bf16[128,512]{1,0:T(8,128)(2,1)S(1)} %get-tuple-element.95), channel_id=1, source_target_pairs={{0,6},{1,7},{2,4},{3,5},{4,2},{5,3},{6,0},{7,1},{8,14},{9,15},{10,... | collective-permute-start | bytes 393224 | tf_op jit(solution)/shard_map/ppermute | solution.py:533
  61.3 9.4 %collective-permute-start.14 = (bf16[128,512]{1,0:T(8,128)(2,1)S(1)}, bf16[128,512]{1,0:T(8,128)(2,1)S(1)}, u32[]{:S(2)}, u32[]{:S(2)}) collective-permute-start(bf16[128,512]{1,0:T(8,128)(2,1)S(1)} %get-tuple-element.87), channel_id=1, source_target_pairs={{0,5},{1,4},{2,7},{3,6},{4,1},{5,0},{6,3},{7,2},{8,13},{9,12},{10,... | collective-permute-start | bytes 393224 | tf_op jit(solution)/shard_map/ppermute | solution.py:533
  61.7 9.0 %collective-permute-start.15 = (bf16[128,512]{1,0:T(8,128)(2,1)S(1)}, bf16[128,512]{1,0:T(8,128)(2,1)S(1)}, u32[]{:S(2)}, u32[]{:S(2)}) collective-permute-start(bf16[128,512]{1,0:T(8,128)(2,1)S(1)} %get-tuple-element.88), channel_id=1, source_target_pairs={{0,1},{1,0},{2,3},{3,2},{4,5},{5,4},{6,7},{7,6},{8,9},{9,8},{10,11... | collective-permute-start | bytes 393224 | tf_op jit(solution)/shard_map/ppermute | solution.py:533
  63.4 11.2 %collective-permute-start.16 = (bf16[128,512]{1,0:T(8,128)(2,1)S(1)}, bf16[128,512]{1,0:T(8,128)(2,1)S(1)}, u32[]{:S(2)}, u32[]{:S(2)}) collective-permute-start(bf16[128,512]{1,0:T(8,128)(2,1)S(1)} %get-tuple-element.89), channel_id=1, source_target_pairs={{0,2},{1,3},{2,0},{3,1},{4,6},{5,7},{6,4},{7,5},{8,10},{9,11},{10,... | collective-permute-start | bytes 393224 | tf_op jit(solution)/shard_map/ppermute | solution.py:533
  65.2 11.5 %collective-permute-start.17 = (bf16[128,512]{1,0:T(8,128)(2,1)S(1)}, bf16[128,512]{1,0:T(8,128)(2,1)S(1)}, u32[]{:S(2)}, u32[]{:S(2)}) collective-permute-start(bf16[128,512]{1,0:T(8,128)(2,1)S(1)} %get-tuple-element.90), channel_id=1, source_target_pairs={{0,3},{1,2},{2,1},{3,0},{4,7},{5,6},{6,5},{7,4},{8,11},{9,10},{10,... | collective-permute-start | bytes 393224 | tf_op jit(solution)/shard_map/ppermute | solution.py:533
  65.3 13.0 %collective-permute-start.20 = (bf16[128,512]{1,0:T(8,128)(2,1)S(1)}, bf16[128,512]{1,0:T(8,128)(2,1)S(1)}, u32[]{:S(2)}, u32[]{:S(2)}) collective-permute-start(bf16[128,512]{1,0:T(8,128)(2,1)S(1)} %get-tuple-element.96), channel_id=1, source_target_pairs={{0,4},{1,5},{2,6},{3,7},{4,0},{5,1},{6,2},{7,3},{8,12},{9,13},{10,... | collective-permute-start | bytes 393224 | tf_op jit(solution)/shard_map/ppermute | solution.py:533
  76.7 7.4 %collective-permute-start.18 = (bf16[128,512]{1,0:T(8,128)(2,1)S(1)}, bf16[128,512]{1,0:T(8,128)(2,1)S(1)}, u32[]{:S(2)}, u32[]{:S(2)}) collective-permute-start(bf16[128,512]{1,0:T(8,128)(2,1)S(1)} %get-tuple-element.91), channel_id=1, source_target_pairs={{0,7},{1,6},{2,5},{3,4},{4,3},{5,2},{6,1},{7,0},{8,15},{9,14},{10,... | collective-permute-start | bytes 393224 | tf_op jit(solution)/shard_map/ppermute | solution.py:533
  78.4 9.0 %collective-permute-start.21 = (bf16[128,512]{1,0:T(8,128)(2,1)S(1)}, bf16[128,512]{1,0:T(8,128)(2,1)S(1)}, u32[]{:S(2)}, u32[]{:S(2)}) collective-permute-start(bf16[128,512]{1,0:T(8,128)(2,1)S(1)} %get-tuple-element.97), channel_id=1, source_target_pairs={{0,6},{1,7},{2,4},{3,5},{4,2},{5,3},{6,0},{7,1},{8,14},{9,15},{10,... | collective-permute-start | bytes 393224 | tf_op jit(solution)/shard_map/ppermute | solution.py:533
  84.0 14.6 %collective-permute-start.22 = (bf16[128,512]{1,0:T(8,128)(2,1)S(1)}, bf16[128,512]{1,0:T(8,128)(2,1)S(1)}, u32[]{:S(2)}, u32[]{:S(2)}) collective-permute-start(bf16[128,512]{1,0:T(8,128)(2,1)S(1)} %get-tuple-element.99), channel_id=1, source_target_pairs={{0,5},{1,4},{2,7},{3,6},{4,1},{5,0},{6,3},{7,2},{8,13},{9,12},{10,... | collective-permute-start | bytes 393224 | tf_op jit(solution)/shard_map/ppermute | solution.py:533
  87.3 14.0 %collective-permute-start.23 = (bf16[128,512]{1,0:T(8,128)(2,1)S(1)}, bf16[128,512]{1,0:T(8,128)(2,1)S(1)}, u32[]{:S(2)}, u32[]{:S(2)}) collective-permute-start(bf16[128,512]{1,0:T(8,128)(2,1)S(1)} %get-tuple-element.101), channel_id=1, source_target_pairs={{0,4},{1,5},{2,6},{3,7},{4,0},{5,1},{6,2},{7,3},{8,12},{9,13},{10,... | collective-permute-start | bytes 393224 | tf_op jit(solution)/shard_map/ppermute | solution.py:533
  96.1 7.4 %copy-start.15 = (bf16[128,256]{1,0:T(8,128)(2,1)S(1)}, bf16[128,256]{1,0:T(8,128)(2,1)}, u32[]{:S(2)}) copy-start(bf16[128,256]{1,0:T(8,128)(2,1)} %constant.19.clone.inv_ref) | copy-start | bytes 196612
  102.0 11.3 %collective-permute-start.28 = (bf16[128,4096]{1,0:T(8,128)(2,1)S(1)}, bf16[128,4096]{1,0:T(8,128)(2,1)S(1)}, u32[]{:S(2)}, u32[]{:S(2)}) collective-permute-start(bf16[128,4096]{1,0:T(8,128)(2,1)S(1)} %get-tuple-element.111.grad_b_ref), channel_id=1, source_target_pairs={{1,0},{2,1},{3,2},{4,3},{5,4},{6,5},{7,6},{9,8},{10,9},{11,10},{12... | collective-permute-start | bytes 3145736 | tf_op jit(solution)/shard_map/ppermute | solution.py:26
  103.5 9.8 %copy-start.7 = (bf16[1,128,4096]{2,1,0:T(8,128)(2,1)S(1)}, bf16[1,128,4096]{2,1,0:T(8,128)(2,1)}, u32[]{:S(2)}) copy-start(bf16[1,128,4096]{2,1,0:T(8,128)(2,1)} %param.16) | copy-start | bytes 3145732
  103.5 9.8 %copy-start.10 = (bf16[128,256]{1,0:T(8,128)(2,1)S(1)}, bf16[128,256]{1,0:T(8,128)(2,1)}, u32[]{:S(2)}) copy-start(bf16[128,256]{1,0:T(8,128)(2,1)} %constant.18.clone.inv_ref) | copy-start | bytes 196612
  105.9 2.7 %collective-permute-start.24 = (bf16[4,128,512]{2,1,0:T(8,128)(2,1)S(1)}, bf16[4,128,512]{2,1,0:T(8,128)(2,1)S(1)}, u32[]{:S(2)}, u32[]{:S(2)}) collective-permute-start(bf16[4,128,512]{2,1,0:T(8,128)(2,1)S(1)} %get-tuple-element.113), channel_id=1, source_target_pairs={{0,1},{1,0},{2,3},{3,2},{4,5},{5,4},{6,7},{7,6},{8,9},{9,8},{10,11... | collective-permute-start | bytes 1572872 | tf_op jit(solution)/shard_map/ppermute | solution.py:533
  108.8 15.2 %collective-permute-start.25 = (bf16[128,512]{1,0:T(8,128)(2,1)S(1)}, bf16[128,512]{1,0:T(8,128)(2,1)S(1)}, u32[]{:S(2)}, u32[]{:S(2)}) collective-permute-start(bf16[128,512]{1,0:T(8,128)(2,1)S(1)} %get-tuple-element.114), channel_id=1, source_target_pairs={{0,6},{1,7},{2,4},{3,5},{4,2},{5,3},{6,0},{7,1},{8,14},{9,15},{10,... | collective-permute-start | bytes 393224 | tf_op jit(solution)/shard_map/ppermute | solution.py:533
  110.5 17.1 %collective-permute-start.26 = (bf16[128,512]{1,0:T(8,128)(2,1)S(1)}, bf16[128,512]{1,0:T(8,128)(2,1)S(1)}, u32[]{:S(2)}, u32[]{:S(2)}) collective-permute-start(bf16[128,512]{1,0:T(8,128)(2,1)S(1)} %get-tuple-element.115), channel_id=1, source_target_pairs={{0,4},{1,5},{2,6},{3,7},{4,0},{5,1},{6,2},{7,3},{8,12},{9,13},{10,... | collective-permute-start | bytes 393224 | tf_op jit(solution)/shard_map/ppermute | solution.py:533
  111.9 15.7 %collective-permute-start.27 = (bf16[128,512]{1,0:T(8,128)(2,1)S(1)}, bf16[128,512]{1,0:T(8,128)(2,1)S(1)}, u32[]{:S(2)}, u32[]{:S(2)}) collective-permute-start(bf16[128,512]{1,0:T(8,128)(2,1)S(1)} %get-tuple-element.116), channel_id=1, source_target_pairs={{0,2},{1,3},{2,0},{3,1},{4,6},{5,7},{6,4},{7,5},{8,10},{9,11},{10,... | collective-permute-start | bytes 393224 | tf_op jit(solution)/shard_map/ppermute | solution.py:533

commit v12 on v11

--- a/solution.py
+++ b/solution.py
@@ -612,7 +612,7 @@
     z_4, z_5 = far_pair(far_z[:2], 4, z_6, z_7)
     near_z = exchanged(near_z)
     pieces_z = near_z + [z_4, z_5, z_6, z_7]
-    w_6, w_7 = far_pair(pieces_w[6:], 6, z_4, z_5)
+    w_6, w_7 = far_pair(pieces_w[6:], 6, z_4, (z_5, near_z))
     near_w = exchanged(pieces_w[:half])
     *pieces_g, channel_z = local(
         functools.partial(pieces_grad_w_kernel, blocks, devices),

time: 129 us -> 127 us (0.984)
  starting transfers between devices: 57.8 us -> 51.3 us
  waiting for transfers between devices: 45.5 us -> 50.3 us
    ppermute x25, starting transfers between devices: 47.2 us -> 40.7 us  [swapped(): return lax.ppermute(array, 'ctx', [(i, i ^ k) for i in range(count)])]
    ppermute x25, waiting for transfers between devices: 37.6 us -> 42.5 us  [swapped(): return lax.ppermute(array, 'ctx', [(i, i ^ k) for i in range(count)])]
  transfers between devices with their start and end apart: 29 -> 29, of which waited for: 12 -> 14; matrix products, arithmetic and copies ran while one was open for 0% -> 0% of each run, Pallas kernels for 16% -> 16%
where the time goes in v12:
time: 127 us
  starting transfers between devices  51.3 us (40%)
  waiting for transfers between devices  50.3 us (40%)
  Pallas kernels  21.5 us (17%)
  local copies, waits for them, and re-layouts  2.61 us (2%)
    ppermute x25, waiting for transfers between devices, swapped(): return lax.ppermute(array, 'ctx', [(i, i ^ k) for i in range(count)])  42.5 us
    ppermute x25, starting transfers between devices, swapped(): return lax.ppermute(array, 'ctx', [(i, i ^ k) for i in range(count)])  40.7 us
    pallas_call x13, Pallas kernels, local(): pl.pallas_call(body, in_specs=specs, out_specs=[pl.BlockSpec(memory_space...  21.5 us
    ppermute x2, waiting for transfers between devices, passed_along(): return lax.ppermute(value, axis, pairs)  7.85 us
    ppermute x2, starting transfers between devices, passed_along(): return lax.ppermute(value, axis, pairs)  7.38 us
    ppermute x2, starting transfers between devices, shifted(): return lax.ppermute(array, axis, pairs)  3.26 us
    unnamed x32, local copies, waits for them, and re-layouts  2.61 us
  transfers between devices with their start and end apart: 29, of which 14 were waited for; matrix products, arithmetic and copies ran while one was open for 0% of the time, Pallas kernels for 16%

profile of v12, /device:TPU:0, one launch (start us, length us, event | category | flops | bytes accessed | tf_op | source)
XLA Modules:
  0.0 126.6 jit_solution(4504965608636593273)
XLA Ops:
  0.7 1.3 %copy-done.3 = bf16[1,128,4096]{2,1,0:T(8,128)(2,1)S(1)} copy-done((bf16[1,128,4096]{2,1,0:T(8,128)(2,1)S(1)}, bf16[1,128,4096]{2,1,0:T(8,128)(2,1)}, u32[]{:S(2)}) %copy-start.3) | copy-done | bytes 1048600
  2.0 3.9 %collective-permute-start.1 = (bf16[128,2048]{1,0:T(8,128)(2,1)S(1)}, bf16[128,2048]{1,0:T(8,128)(2,1)S(1)}, u32[]{:S(2)}, u32[]{:S(2)}) collective-permute-start(bf16[128,2048]{1,0:T(8,128)(2,1)S(1)} %far.1), channel_id=1, source_target_pairs={{0,24},{8,0},{16,8},{24,16},{1,25},{9,1},{17,9},{25,17},{2,26},{10... | collective-permute-start | bytes 1572872 | tf_op jit(solution)/shard_map/ppermute | solution.py:20
  5.9 1.2 copy-done.6
  7.2 0.2 mix.1.mixed_ref
  7.5 1.8 %collective-permute-start = (bf16[128,4096]{1,0:T(8,128)(2,1)S(1)}, bf16[128,4096]{1,0:T(8,128)(2,1)S(1)}, u32[]{:S(2)}, u32[]{:S(2)}) collective-permute-start(bf16[128,4096]{1,0:T(8,128)(2,1)S(1)} %mix.1.mixed_ref), channel_id=1, source_target_pairs={{0,1},{1,2},{2,3},{3,4},{4,5},{5,6},{6,7},{8,9},{9,10},{10,11},{11... | collective-permute-start | bytes 3145736 | tf_op jit(solution)/shard_map/ppermute | solution.py:26
  9.3 7.9 %collective-permute-done.1.adjoint_ref.far_ref = bf16[128,2048]{1,0:T(8,128)(2,1)S(1)} collective-permute-done((bf16[128,2048]{1,0:T(8,128)(2,1)S(1)}, bf16[128,2048]{1,0:T(8,128)(2,1)S(1)}, u32[]{:S(2)}, u32[]{:S(2)}) %collective-permute-start.1) | collective-permute-done | bytes 524320 | tf_op jit(solution)/shard_map/ppermute | solution.py:20
  17.2 3.4 %collective-permute-start.2 = (bf16[128,2048]{1,0:T(8,128)(2,1)S(1)}, bf16[128,2048]{1,0:T(8,128)(2,1)S(1)}, u32[]{:S(2)}, u32[]{:S(2)}) collective-permute-start(bf16[128,2048]{1,0:T(8,128)(2,1)S(1)} %near.1), channel_id=1, source_target_pairs={{0,24},{8,0},{16,8},{24,16},{1,25},{9,1},{17,9},{25,17},{2,26},{10... | collective-permute-start | bytes 1572872 | tf_op jit(solution)/shard_map/ppermute | solution.py:20
  20.6 0.2 farz.1
  20.8 2.0 %collective-permute-start.3 = (bf16[128,512]{1,0:T(8,128)(2,1)S(1)}, bf16[128,512]{1,0:T(8,128)(2,1)S(1)}, u32[]{:S(2)}, u32[]{:S(2)}) collective-permute-start(bf16[128,512]{1,0:T(8,128)(2,1)S(1)} %get-tuple-element.72), channel_id=1, source_target_pairs={{0,7},{1,6},{2,5},{3,4},{4,3},{5,2},{6,1},{7,0},{8,15},{9,14},{10,... | collective-permute-start | bytes 393224 | tf_op jit(solution)/shard_map/ppermute | solution.py:533
  22.7 1.8 %collective-permute-start.4 = (bf16[128,512]{1,0:T(8,128)(2,1)S(1)}, bf16[128,512]{1,0:T(8,128)(2,1)S(1)}, u32[]{:S(2)}, u32[]{:S(2)}) collective-permute-start(bf16[128,512]{1,0:T(8,128)(2,1)S(1)} %get-tuple-element.73), channel_id=1, source_target_pairs={{0,6},{1,7},{2,4},{3,5},{4,2},{5,3},{6,0},{7,1},{8,14},{9,15},{10,... | collective-permute-start | bytes 393224 | tf_op jit(solution)/shard_map/ppermute | solution.py:533
  24.5 3.7 %collective-permute-done.3.refs_0_ = bf16[128,512]{1,0:T(8,128)(2,1)S(1)} collective-permute-done((bf16[128,512]{1,0:T(8,128)(2,1)S(1)}, bf16[128,512]{1,0:T(8,128)(2,1)S(1)}, u32[]{:S(2)}, u32[]{:S(2)}) %collective-permute-start.3) | collective-permute-done | bytes 131104 | tf_op jit(solution)/shard_map/ppermute | solution.py:533
  28.3 2.5 %collective-permute-done.4.refs_1_ = bf16[128,512]{1,0:T(8,128)(2,1)S(1)} collective-permute-done((bf16[128,512]{1,0:T(8,128)(2,1)S(1)}, bf16[128,512]{1,0:T(8,128)(2,1)S(1)}, u32[]{:S(2)}, u32[]{:S(2)}) %collective-permute-start.4) | collective-permute-done | bytes 131104 | tf_op jit(solution)/shard_map/ppermute | solution.py:533
  30.8 5.9 %collective-permute-start.6 = (bf16[128,512]{1,0:T(8,128)(2,1)S(1)}, bf16[128,512]{1,0:T(8,128)(2,1)S(1)}, u32[]{:S(2)}, u32[]{:S(2)}) collective-permute-start(bf16[128,512]{1,0:T(8,128)(2,1)S(1)} %get-tuple-element.77), channel_id=1, source_target_pairs={{0,4},{1,5},{2,6},{3,7},{4,0},{5,1},{6,2},{7,3},{8,12},{9,13},{10,... | collective-permute-start | bytes 393224 | tf_op jit(solution)/shard_map/ppermute | solution.py:533
  36.7 0.4 collective-permute-start.5
  37.3 2.2 %collective-permute-start.7 = (bf16[128,512]{1,0:T(8,128)(2,1)S(1)}, bf16[128,512]{1,0:T(8,128)(2,1)S(1)}, u32[]{:S(2)}, u32[]{:S(2)}) collective-permute-start(bf16[128,512]{1,0:T(8,128)(2,1)S(1)} %get-tuple-element.69), channel_id=1, source_target_pairs={{0,3},{1,2},{2,1},{3,0},{4,7},{5,6},{6,5},{7,4},{8,11},{9,10},{10,... | collective-permute-start | bytes 393224 | tf_op jit(solution)/shard_map/ppermute | solution.py:533
  39.5 0.2 collective-permute-start.9
  39.8 3.1 %branch.1 = (bf16[256,4096]{1,0:T(8,128)(2,1)S(1)}, bf16[256,4096]{1,0:T(8,128)(2,1)S(1)}, bf16[128,512]{1,0:T(8,128)(2,1)S(1)}, bf16[128,512]{1,0:T(8,128)(2,1)...) custom-call(s32[1]{0:T(128)} %bitcast.me_ref, ...), custom_call_target="tpu_custom_call" | custom-call | flops 1073741824 | bytes 11730948 | tf_op jit(solution)/shard_map/branch/pallas_call | solution.py:518
  42.8 3.8 %collective-permute-done.6.refs_3_ = bf16[128,512]{1,0:T(8,128)(2,1)S(1)} collective-permute-done((bf16[128,512]{1,0:T(8,128)(2,1)S(1)}, bf16[128,512]{1,0:T(8,128)(2,1)S(1)}, u32[]{:S(2)}, u32[]{:S(2)}) %collective-permute-start.6) | collective-permute-done | bytes 131104 | tf_op jit(solution)/shard_map/ppermute | solution.py:533
  46.7 2.9 %collective-permute-done.5.refs_2_ = bf16[128,512]{1,0:T(8,128)(2,1)S(1)} collective-permute-done((bf16[128,512]{1,0:T(8,128)(2,1)S(1)}, bf16[128,512]{1,0:T(8,128)(2,1)S(1)}, u32[]{:S(2)}, u32[]{:S(2)}) %collective-permute-start.5) | collective-permute-done | bytes 131104 | tf_op jit(solution)/shard_map/ppermute | solution.py:533
  49.6 1.3 %collective-permute-start.13 = (bf16[128,512]{1,0:T(8,128)(2,1)S(1)}, bf16[128,512]{1,0:T(8,128)(2,1)S(1)}, u32[]{:S(2)}, u32[]{:S(2)}) collective-permute-start(bf16[128,512]{1,0:T(8,128)(2,1)S(1)} %get-tuple-element.85), channel_id=1, source_target_pairs={{0,3},{1,2},{2,1},{3,0},{4,7},{5,6},{6,5},{7,4},{8,11},{9,10},{10,... | collective-permute-start | bytes 393224 | tf_op jit(solution)/shard_map/ppermute | solution.py:533
  50.9 1.5 %collective-permute-start.19 = (bf16[128,512]{1,0:T(8,128)(2,1)S(1)}, bf16[128,512]{1,0:T(8,128)(2,1)S(1)}, u32[]{:S(2)}, u32[]{:S(2)}) collective-permute-start(bf16[128,512]{1,0:T(8,128)(2,1)S(1)} %get-tuple-element.95), channel_id=1, source_target_pairs={{0,6},{1,7},{2,4},{3,5},{4,2},{5,3},{6,0},{7,1},{8,14},{9,15},{10,... | collective-permute-start | bytes 393224 | tf_op jit(solution)/shard_map/ppermute | solution.py:533
  52.4 2.5 %collective-permute-start.10 = (bf16[128,512]{1,0:T(8,128)(2,1)S(1)}, bf16[128,512]{1,0:T(8,128)(2,1)S(1)}, u32[]{:S(2)}, u32[]{:S(2)}) collective-permute-start(bf16[128,512]{1,0:T(8,128)(2,1)S(1)} %get-tuple-element.81), channel_id=1, source_target_pairs={{0,7},{1,6},{2,5},{3,4},{4,3},{5,2},{6,1},{7,0},{8,15},{9,14},{10,... | collective-permute-start | bytes 393224 | tf_op jit(solution)/shard_map/ppermute | solution.py:533
  54.9 4.7 %gradw.1 = (bf16[128,512]{1,0:T(8,128)(2,1)S(1)}, bf16[128,512]{1,0:T(8,128)(2,1)S(1)}, bf16[128,512]{1,0:T(8,128)(2,1)S(1)}, bf16[128,512]{1,0:T(8,128)(2,1)S(1...) custom-call(s32[1]{0:T(128)} %bitcast.me_ref, ...), custom_call_target="tpu_custom_call" | custom-call | flops 3221225472 | bytes 4980740 | tf_op jit(solution)/shard_map/gradw/pallas_call | solution.py:518
  59.8 1.8 %collective-permute-start.17 = (bf16[128,512]{1,0:T(8,128)(2,1)S(1)}, bf16[128,512]{1,0:T(8,128)(2,1)S(1)}, u32[]{:S(2)}, u32[]{:S(2)}) collective-permute-start(bf16[128,512]{1,0:T(8,128)(2,1)S(1)} %get-tuple-element.90), channel_id=1, source_target_pairs={{0,3},{1,2},{2,1},{3,0},{4,7},{5,6},{6,5},{7,4},{8,11},{9,10},{10,... | collective-permute-start | bytes 393224 | tf_op jit(solution)/shard_map/ppermute | solution.py:533
  61.6 0.2 collective-permute-start.20
  61.8 1.1 collective-permute-done.10.refs_0_
  62.9 2.6 %collective-permute-start.14 = (bf16[128,512]{1,0:T(8,128)(2,1)S(1)}, bf16[128,512]{1,0:T(8,128)(2,1)S(1)}, u32[]{:S(2)}, u32[]{:S(2)}) collective-permute-start(bf16[128,512]{1,0:T(8,128)(2,1)S(1)} %get-tuple-element.87), channel_id=1, source_target_pairs={{0,5},{1,4},{2,7},{3,6},{4,1},{5,0},{6,3},{7,2},{8,13},{9,12},{10,... | collective-permute-start | bytes 393224 | tf_op jit(solution)/shard_map/ppermute | solution.py:533
  65.5 3.2 %collective-permute-done.16.refs_5_ = bf16[128,512]{1,0:T(8,128)(2,1)S(1)} collective-permute-done((bf16[128,512]{1,0:T(8,128)(2,1)S(1)}, bf16[128,512]{1,0:T(8,128)(2,1)S(1)}, u32[]{:S(2)}, u32[]{:S(2)}) %collective-permute-start.16) | collective-permute-done | bytes 131104 | tf_op jit(solution)/shard_map/ppermute | solution.py:533
  68.7 2.9 %collective-permute-done.17.refs_4_ = bf16[128,512]{1,0:T(8,128)(2,1)S(1)} collective-permute-done((bf16[128,512]{1,0:T(8,128)(2,1)S(1)}, bf16[128,512]{1,0:T(8,128)(2,1)S(1)}, u32[]{:S(2)}, u32[]{:S(2)}) %collective-permute-start.17) | collective-permute-done | bytes 131104 | tf_op jit(solution)/shard_map/ppermute | solution.py:533
  71.6 3.2 %collective-permute-start.21 = (bf16[128,512]{1,0:T(8,128)(2,1)S(1)}, bf16[128,512]{1,0:T(8,128)(2,1)S(1)}, u32[]{:S(2)}, u32[]{:S(2)}) collective-permute-start(bf16[128,512]{1,0:T(8,128)(2,1)S(1)} %get-tuple-element.97), channel_id=1, source_target_pairs={{0,6},{1,7},{2,4},{3,5},{4,2},{5,3},{6,0},{7,1},{8,14},{9,15},{10,... | collective-permute-start | bytes 393224 | tf_op jit(solution)/shard_map/ppermute | solution.py:533
  74.9 4.6 %collective-permute-done.14.refs_2_ = bf16[128,512]{1,0:T(8,128)(2,1)S(1)} collective-permute-done((bf16[128,512]{1,0:T(8,128)(2,1)S(1)}, bf16[128,512]{1,0:T(8,128)(2,1)S(1)}, u32[]{:S(2)}, u32[]{:S(2)}) %collective-permute-start.14) | collective-permute-done | bytes 131104 | tf_op jit(solution)/shard_map/ppermute | solution.py:533
  79.4 3.7 %collective-permute-start.23 = (bf16[128,512]{1,0:T(8,128)(2,1)S(1)}, bf16[128,512]{1,0:T(8,128)(2,1)S(1)}, u32[]{:S(2)}, u32[]{:S(2)}) collective-permute-start(bf16[128,512]{1,0:T(8,128)(2,1)S(1)} %get-tuple-element.101), channel_id=1, source_target_pairs={{0,4},{1,5},{2,6},{3,7},{4,0},{5,1},{6,2},{7,3},{8,12},{9,13},{10,... | collective-permute-start | bytes 393224 | tf_op jit(solution)/shard_map/ppermute | solution.py:533
  83.1 2.6 %collective-permute-done.18.refs_0_ = bf16[128,512]{1,0:T(8,128)(2,1)S(1)} collective-permute-done((bf16[128,512]{1,0:T(8,128)(2,1)S(1)}, bf16[128,512]{1,0:T(8,128)(2,1)S(1)}, u32[]{:S(2)}, u32[]{:S(2)}) %collective-permute-start.18) | collective-permute-done | bytes 131104 | tf_op jit(solution)/shard_map/ppermute | solution.py:533
  85.7 5.6 %collective-permute-start.22 = (bf16[128,512]{1,0:T(8,128)(2,1)S(1)}, bf16[128,512]{1,0:T(8,128)(2,1)S(1)}, u32[]{:S(2)}, u32[]{:S(2)}) collective-permute-start(bf16[128,512]{1,0:T(8,128)(2,1)S(1)} %get-tuple-element.99), channel_id=1, source_target_pairs={{0,5},{1,4},{2,7},{3,6},{4,1},{5,0},{6,3},{7,2},{8,13},{9,12},{10,... | collective-permute-start | bytes 393224 | tf_op jit(solution)/shard_map/ppermute | solution.py:533
  91.3 5.6 %longgrad.1 = bf16[512,1024]{1,0:T(8,128)(2,1)} custom-call(s32[1]{0:T(128)} %bitcast.me_ref, bf16[512,512]{1,0:T(8,128)(2,1)S(1)} %copy-done.13, bf16[256,512]{1,0:T(8,128)(2,1)S(1)} %copy-done.14, bf16[1024,512]{1,0:T(8,128)(2,1)S(1)} %get-tuple-element.102.grad_ref, bf16[128,512]{1,0:T(8,128)(2,1)S(1)} %collective-permute-done.10.refs_0_, ...), custom_call_target="tpu_custom_call" | custom-call | flops 3221225472 | bytes 3932164 | tf_op jit(solution)/shard_map/longgrad/pallas_call | solution.py:518
  97.0 2.8 %collective-permute-done.22.refs_2_ = bf16[128,512]{1,0:T(8,128)(2,1)S(1)} collective-permute-done((bf16[128,512]{1,0:T(8,128)(2,1)S(1)}, bf16[128,512]{1,0:T(8,128)(2,1)S(1)}, u32[]{:S(2)}, u32[]{:S(2)}) %collective-permute-start.22) | collective-permute-done | bytes 131104 | tf_op jit(solution)/shard_map/ppermute | solution.py:533
  99.8 0.6 gradb.1
  100.4 1.5 %collective-permute-start.28 = (bf16[128,4096]{1,0:T(8,128)(2,1)S(1)}, bf16[128,4096]{1,0:T(8,128)(2,1)S(1)}, u32[]{:S(2)}, u32[]{:S(2)}) collective-permute-start(bf16[128,4096]{1,0:T(8,128)(2,1)S(1)} %get-tuple-element.111.grad_b_ref), channel_id=1, source_target_pairs={{1,0},{2,1},{3,2},{4,3},{5,4},{6,5},{7,6},{9,8},{10,9},{11,10},{12... | collective-permute-start | bytes 3145736 | tf_op jit(solution)/shard_map/ppermute | solution.py:26
  101.9 2.4 %taps.1 = (bf16[4,128,512]{2,1,0:T(8,128)(2,1)S(1)}, bf16[4,128,512]{2,1,0:T(8,128)(2,1)S(1)}) custom-call(s32[1]{0:T(128)} %bitcast.me_ref, bf16[256,256]{1,0:T(8,128)(2,1)S(1)} %copy-done.9, bf16[128,256]{1,0:T(8,128)(2,1)S(1)} %copy-done.15, bf16[256,4096]{1,0:T(8,128)(2,1)S(1)} %get-tuple-element.71.signal_ref, ...), custom_call_target="tpu_custom_call" | custom-call | flops 1073741824 | bytes 4390916 | tf_op jit(solution)/shard_map/taps/pallas_call | solution.py:518
  104.4 1.2 collective-permute-start.24
  105.5 1.5 %collective-permute-done.24.came_ref = bf16[4,128,512]{2,1,0:T(8,128)(2,1)S(1)} collective-permute-done((bf16[4,128,512]{2,1,0:T(8,128)(2,1)S(1)}, bf16[4,128,512]{2,1,0:T(8,128)(2,1)S(1)}, u32[]{:S(2)}, u32[]{:S(2)}) %collective-permute-start.24) | collective-permute-done | bytes 524320 | tf_op jit(solution)/shard_map/ppermute | solution.py:533
  107.2 0.7 collective-permute-start.25
  107.9 2.4 %collective-permute-start.26 = (bf16[128,512]{1,0:T(8,128)(2,1)S(1)}, bf16[128,512]{1,0:T(8,128)(2,1)S(1)}, u32[]{:S(2)}, u32[]{:S(2)}) collective-permute-start(bf16[128,512]{1,0:T(8,128)(2,1)S(1)} %get-tuple-element.115), channel_id=1, source_target_pairs={{0,4},{1,5},{2,6},{3,7},{4,0},{5,1},{6,2},{7,3},{8,12},{9,13},{10,... | collective-permute-start | bytes 393224 | tf_op jit(solution)/shard_map/ppermute | solution.py:533
  110.3 1.4 %collective-permute-start.27 = (bf16[128,512]{1,0:T(8,128)(2,1)S(1)}, bf16[128,512]{1,0:T(8,128)(2,1)S(1)}, u32[]{:S(2)}, u32[]{:S(2)}) collective-permute-start(bf16[128,512]{1,0:T(8,128)(2,1)S(1)} %get-tuple-element.116), channel_id=1, source_target_pairs={{0,2},{1,3},{2,0},{3,1},{4,6},{5,7},{6,4},{7,5},{8,10},{9,11},{10,... | collective-permute-start | bytes 393224 | tf_op jit(solution)/shard_map/ppermute | solution.py:533
  111.7 3.5 %inputgrad.1 = bf16[128,4096]{1,0:T(8,128)(2,1)} custom-call(bf16[256,256]{1,0:T(8,128)(2,1)S(1)} %copy-done.9, bf16[128,256]{1,0:T(8,128)(2,1)S(1)} %copy-done.10, bf16[128,4096]{1,0:T(8,128)(2,1)S(1)} %get-tuple-element.111.grad_b_ref, bf16[128,4096]{1,0:T(8,128)(2,1)S(1)} %collective-permute-done.28.later_ref, ...), custom_call_target="tpu_custom_call" | custom-call | flops 1073741824 | bytes 8585216 | tf_op jit(solution)/shard_map/inputgrad/pallas_call | solution.py:518
  115.2 6.4 %collective-permute-done.25.refs_0_ = bf16[128,512]{1,0:T(8,128)(2,1)S(1)} collective-permute-done((bf16[128,512]{1,0:T(8,128)(2,1)S(1)}, bf16[128,512]{1,0:T(8,128)(2,1)S(1)}, u32[]{:S(2)}, u32[]{:S(2)}) %collective-permute-start.25) | collective-permute-done | bytes 131104 | tf_op jit(solution)/shard_map/ppermute | solution.py:533
  121.6 4.2 %collective-permute-done.26.refs_1_ = bf16[128,512]{1,0:T(8,128)(2,1)S(1)} collective-permute-done((bf16[128,512]{1,0:T(8,128)(2,1)S(1)}, bf16[128,512]{1,0:T(8,128)(2,1)S(1)}, u32[]{:S(2)}, u32[]{:S(2)}) %collective-permute-start.26) | collective-permute-done | bytes 131104 | tf_op jit(solution)/shard_map/ppermute | solution.py:533
  125.8 0.7 midgrad.1
  (55 shorter events, 0.7 us)
Async XLA Ops:
  0.6 5.3 %copy-start = (bf16[1,128,4096]{2,1,0:T(8,128)(2,1)S(1)}, bf16[1,128,4096]{2,1,0:T(8,128)(2,1)}, u32[]{:S(2)}) copy-start(bf16[1,128,4096]{2,1,0:T(8,128)(2,1)} %param.15) | copy-start | bytes 3145732
  0.6 1.3 %copy-start.3 = (bf16[1,128,4096]{2,1,0:T(8,128)(2,1)S(1)}, bf16[1,128,4096]{2,1,0:T(8,128)(2,1)}, u32[]{:S(2)}) copy-start(bf16[1,128,4096]{2,1,0:T(8,128)(2,1)} %param.14) | copy-start | bytes 3145732
  2.0 15.2 %copy-start.4 = (bf16[1,128,4096]{2,1,0:T(8,128)(2,1)S(1)}, bf16[1,128,4096]{2,1,0:T(8,128)(2,1)}, u32[]{:S(2)}) copy-start(bf16[1,128,4096]{2,1,0:T(8,128)(2,1)} %param.14) | copy-start | bytes 3145732
  2.0 15.1 %collective-permute-start.1 = (bf16[128,2048]{1,0:T(8,128)(2,1)S(1)}, bf16[128,2048]{1,0:T(8,128)(2,1)S(1)}, u32[]{:S(2)}, u32[]{:S(2)}) collective-permute-start(bf16[128,2048]{1,0:T(8,128)(2,1)S(1)} %far.1), channel_id=1, source_target_pairs={{0,24},{8,0},{16,8},{24,16},{1,25},{9,1},{17,9},{25,17},{2,26},{10... | collective-permute-start | bytes 1572872 | tf_op jit(solution)/shard_map/ppermute | solution.py:20
  5.9 1.2 copy-start.6
  7.2 13.4 %copy-start.5 = (bf16[1,128,4096]{2,1,0:T(8,128)(2,1)S(1)}, bf16[1,128,4096]{2,1,0:T(8,128)(2,1)}, u32[]{:S(2)}) copy-start(bf16[1,128,4096]{2,1,0:T(8,128)(2,1)} %param.19) | copy-start | bytes 3145732
  7.4 32.3 %copy-start.1 = (bf16[1,128,4096]{2,1,0:T(8,128)(2,1)S(1)}, bf16[1,128,4096]{2,1,0:T(8,128)(2,1)}, u32[]{:S(2)}) copy-start(bf16[1,128,4096]{2,1,0:T(8,128)(2,1)} %param.18) | copy-start | bytes 3145732
  7.4 32.3 %copy-start.2 = (bf16[1,128,4096]{2,1,0:T(8,128)(2,1)S(1)}, bf16[1,128,4096]{2,1,0:T(8,128)(2,1)}, u32[]{:S(2)}) copy-start(bf16[1,128,4096]{2,1,0:T(8,128)(2,1)} %param.17) | copy-start | bytes 3145732
  7.4 32.3 %copy-start.8 = (bf16[1,128,4096]{2,1,0:T(8,128)(2,1)S(1)}, bf16[1,128,4096]{2,1,0:T(8,128)(2,1)}, u32[]{:S(2)}) copy-start(bf16[1,128,4096]{2,1,0:T(8,128)(2,1)} %param.21) | copy-start | bytes 3145732
  7.5 32.3 %copy-start.9 = (bf16[256,256]{1,0:T(8,128)(2,1)S(1)}, bf16[256,256]{1,0:T(8,128)(2,1)}, u32[]{:S(2)}) copy-start(bf16[256,256]{1,0:T(8,128)(2,1)} %constant.16.clone.fwd_ref) | copy-start | bytes 393220
  7.5 32.3 %copy-start.11 = (bf16[128,256]{1,0:T(8,128)(2,1)S(1)}, bf16[128,256]{1,0:T(8,128)(2,1)}, u32[]{:S(2)}) copy-start(bf16[128,256]{1,0:T(8,128)(2,1)} %constant.17.clone.inv_ref) | copy-start | bytes 196612
  7.5 32.0 %collective-permute-start = (bf16[128,4096]{1,0:T(8,128)(2,1)S(1)}, bf16[128,4096]{1,0:T(8,128)(2,1)S(1)}, u32[]{:S(2)}, u32[]{:S(2)}) collective-permute-start(bf16[128,4096]{1,0:T(8,128)(2,1)S(1)} %mix.1.mixed_ref), channel_id=1, source_target_pairs={{0,1},{1,2},{2,3},{3,4},{4,5},{5,6},{6,7},{8,9},{9,10},{10,11},{11... | collective-permute-start | bytes 3145736 | tf_op jit(solution)/shard_map/ppermute | solution.py:26
  17.2 20.0 %collective-permute-start.2 = (bf16[128,2048]{1,0:T(8,128)(2,1)S(1)}, bf16[128,2048]{1,0:T(8,128)(2,1)S(1)}, u32[]{:S(2)}, u32[]{:S(2)}) collective-permute-start(bf16[128,2048]{1,0:T(8,128)(2,1)S(1)} %near.1), channel_id=1, source_target_pairs={{0,24},{8,0},{16,8},{24,16},{1,25},{9,1},{17,9},{25,17},{2,26},{10... | collective-permute-start | bytes 1572872 | tf_op jit(solution)/shard_map/ppermute | solution.py:20
  20.8 7.5 %collective-permute-start.3 = (bf16[128,512]{1,0:T(8,128)(2,1)S(1)}, bf16[128,512]{1,0:T(8,128)(2,1)S(1)}, u32[]{:S(2)}, u32[]{:S(2)}) collective-permute-start(bf16[128,512]{1,0:T(8,128)(2,1)S(1)} %get-tuple-element.72), channel_id=1, source_target_pairs={{0,7},{1,6},{2,5},{3,4},{4,3},{5,2},{6,1},{7,0},{8,15},{9,14},{10,... | collective-permute-start | bytes 393224 | tf_op jit(solution)/shard_map/ppermute | solution.py:533
  22.7 8.1 %collective-permute-start.4 = (bf16[128,512]{1,0:T(8,128)(2,1)S(1)}, bf16[128,512]{1,0:T(8,128)(2,1)S(1)}, u32[]{:S(2)}, u32[]{:S(2)}) collective-permute-start(bf16[128,512]{1,0:T(8,128)(2,1)S(1)} %get-tuple-element.73), channel_id=1, source_target_pairs={{0,6},{1,7},{2,4},{3,5},{4,2},{5,3},{6,0},{7,1},{8,14},{9,15},{10,... | collective-permute-start | bytes 393224 | tf_op jit(solution)/shard_map/ppermute | solution.py:533
  30.8 15.9 %collective-permute-start.6 = (bf16[128,512]{1,0:T(8,128)(2,1)S(1)}, bf16[128,512]{1,0:T(8,128)(2,1)S(1)}, u32[]{:S(2)}, u32[]{:S(2)}) collective-permute-start(bf16[128,512]{1,0:T(8,128)(2,1)S(1)} %get-tuple-element.77), channel_id=1, source_target_pairs={{0,4},{1,5},{2,6},{3,7},{4,0},{5,1},{6,2},{7,3},{8,12},{9,13},{10,... | collective-permute-start | bytes 393224 | tf_op jit(solution)/shard_map/ppermute | solution.py:533
  36.7 12.9 %collective-permute-start.5 = (bf16[128,512]{1,0:T(8,128)(2,1)S(1)}, bf16[128,512]{1,0:T(8,128)(2,1)S(1)}, u32[]{:S(2)}, u32[]{:S(2)}) collective-permute-start(bf16[128,512]{1,0:T(8,128)(2,1)S(1)} %get-tuple-element.75), channel_id=1, source_target_pairs={{0,5},{1,4},{2,7},{3,6},{4,1},{5,0},{6,3},{7,2},{8,13},{9,12},{10,... | collective-permute-start | bytes 393224 | tf_op jit(solution)/shard_map/ppermute | solution.py:533
  37.3 12.3 %collective-permute-start.7 = (bf16[128,512]{1,0:T(8,128)(2,1)S(1)}, bf16[128,512]{1,0:T(8,128)(2,1)S(1)}, u32[]{:S(2)}, u32[]{:S(2)}) collective-permute-start(bf16[128,512]{1,0:T(8,128)(2,1)S(1)} %get-tuple-element.69), channel_id=1, source_target_pairs={{0,3},{1,2},{2,1},{3,0},{4,7},{5,6},{6,5},{7,4},{8,11},{9,10},{10,... | collective-permute-start | bytes 393224 | tf_op jit(solution)/shard_map/ppermute | solution.py:533
  39.5 11.4 %collective-permute-start.8 = (bf16[128,512]{1,0:T(8,128)(2,1)S(1)}, bf16[128,512]{1,0:T(8,128)(2,1)S(1)}, u32[]{:S(2)}, u32[]{:S(2)}) collective-permute-start(bf16[128,512]{1,0:T(8,128)(2,1)S(1)} %get-tuple-element.68), channel_id=1, source_target_pairs={{0,2},{1,3},{2,0},{3,1},{4,6},{5,7},{6,4},{7,5},{8,10},{9,11},{10,... | collective-permute-start | bytes 393224 | tf_op jit(solution)/shard_map/ppermute | solution.py:533
  39.5 12.9 %collective-permute-start.9 = (bf16[128,512]{1,0:T(8,128)(2,1)S(1)}, bf16[128,512]{1,0:T(8,128)(2,1)S(1)}, u32[]{:S(2)}, u32[]{:S(2)}) collective-permute-start(bf16[128,512]{1,0:T(8,128)(2,1)S(1)} %get-tuple-element.67), channel_id=1, source_target_pairs={{0,1},{1,0},{2,3},{3,2},{4,5},{5,4},{6,7},{7,6},{8,9},{9,8},{10,11... | collective-permute-start | bytes 393224 | tf_op jit(solution)/shard_map/ppermute | solution.py:533
  39.7 15.2 %copy-start.12 = (bf16[1,512,1024]{2,1,0:T(8,128)(2,1)S(1)}, bf16[1,512,1024]{2,1,0:T(8,128)(2,1)}, u32[]{:S(2)}) copy-start(bf16[1,512,1024]{2,1,0:T(8,128)(2,1)} %param.20) | copy-start | bytes 3145732
  39.7 15.2 %copy-start.13 = (bf16[512,512]{1,0:T(8,128)(2,1)S(1)}, bf16[512,512]{1,0:T(8,128)(2,1)}, u32[]{:S(2)}) copy-start(bf16[512,512]{1,0:T(8,128)(2,1)} %constant.20.clone.fwd_ref) | copy-start | bytes 1572868
  39.7 15.2 %copy-start.14 = (bf16[256,512]{1,0:T(8,128)(2,1)S(1)}, bf16[256,512]{1,0:T(8,128)(2,1)}, u32[]{:S(2)}) copy-start(bf16[256,512]{1,0:T(8,128)(2,1)} %constant.21.clone.inv_ref) | copy-start | bytes 786436
  46.7 13.0 %collective-permute-start.11 = (bf16[128,512]{1,0:T(8,128)(2,1)S(1)}, bf16[128,512]{1,0:T(8,128)(2,1)S(1)}, u32[]{:S(2)}, u32[]{:S(2)}) collective-permute-start(bf16[128,512]{1,0:T(8,128)(2,1)S(1)} %get-tuple-element.83), channel_id=1, source_target_pairs={{0,1},{1,0},{2,3},{3,2},{4,5},{5,4},{6,7},{7,6},{8,9},{9,8},{10,11... | collective-permute-start | bytes 393224 | tf_op jit(solution)/shard_map/ppermute | solution.py:533
  49.6 10.1 %collective-permute-start.12 = (bf16[128,512]{1,0:T(8,128)(2,1)S(1)}, bf16[128,512]{1,0:T(8,128)(2,1)S(1)}, u32[]{:S(2)}, u32[]{:S(2)}) collective-permute-start(bf16[128,512]{1,0:T(8,128)(2,1)S(1)} %get-tuple-element.84), channel_id=1, source_target_pairs={{0,2},{1,3},{2,0},{3,1},{4,6},{5,7},{6,4},{7,5},{8,10},{9,11},{10,... | collective-permute-start | bytes 393224 | tf_op jit(solution)/shard_map/ppermute | solution.py:533
  49.6 10.2 %collective-permute-start.13 = (bf16[128,512]{1,0:T(8,128)(2,1)S(1)}, bf16[128,512]{1,0:T(8,128)(2,1)S(1)}, u32[]{:S(2)}, u32[]{:S(2)}) collective-permute-start(bf16[128,512]{1,0:T(8,128)(2,1)S(1)} %get-tuple-element.85), channel_id=1, source_target_pairs={{0,3},{1,2},{2,1},{3,0},{4,7},{5,6},{6,5},{7,4},{8,11},{9,10},{10,... | collective-permute-start | bytes 393224 | tf_op jit(solution)/shard_map/ppermute | solution.py:533
  50.9 10.7 %collective-permute-start.19 = (bf16[128,512]{1,0:T(8,128)(2,1)S(1)}, bf16[128,512]{1,0:T(8,128)(2,1)S(1)}, u32[]{:S(2)}, u32[]{:S(2)}) collective-permute-start(bf16[128,512]{1,0:T(8,128)(2,1)S(1)} %get-tuple-element.95), channel_id=1, source_target_pairs={{0,6},{1,7},{2,4},{3,5},{4,2},{5,3},{6,0},{7,1},{8,14},{9,15},{10,... | collective-permute-start | bytes 393224 | tf_op jit(solution)/shard_map/ppermute | solution.py:533
  52.4 10.5 %collective-permute-start.10 = (bf16[128,512]{1,0:T(8,128)(2,1)S(1)}, bf16[128,512]{1,0:T(8,128)(2,1)S(1)}, u32[]{:S(2)}, u32[]{:S(2)}) collective-permute-start(bf16[128,512]{1,0:T(8,128)(2,1)S(1)} %get-tuple-element.81), channel_id=1, source_target_pairs={{0,7},{1,6},{2,5},{3,4},{4,3},{5,2},{6,1},{7,0},{8,15},{9,14},{10,... | collective-permute-start | bytes 393224 | tf_op jit(solution)/shard_map/ppermute | solution.py:533
  59.6 5.9 %collective-permute-start.15 = (bf16[128,512]{1,0:T(8,128)(2,1)S(1)}, bf16[128,512]{1,0:T(8,128)(2,1)S(1)}, u32[]{:S(2)}, u32[]{:S(2)}) collective-permute-start(bf16[128,512]{1,0:T(8,128)(2,1)S(1)} %get-tuple-element.88), channel_id=1, source_target_pairs={{0,1},{1,0},{2,3},{3,2},{4,5},{5,4},{6,7},{7,6},{8,9},{9,8},{10,11... | collective-permute-start | bytes 393224 | tf_op jit(solution)/shard_map/ppermute | solution.py:533
  59.7 9.0 %collective-permute-start.16 = (bf16[128,512]{1,0:T(8,128)(2,1)S(1)}, bf16[128,512]{1,0:T(8,128)(2,1)S(1)}, u32[]{:S(2)}, u32[]{:S(2)}) collective-permute-start(bf16[128,512]{1,0:T(8,128)(2,1)S(1)} %get-tuple-element.89), channel_id=1, source_target_pairs={{0,2},{1,3},{2,0},{3,1},{4,6},{5,7},{6,4},{7,5},{8,10},{9,11},{10,... | collective-permute-start | bytes 393224 | tf_op jit(solution)/shard_map/ppermute | solution.py:533
  59.8 11.8 %collective-permute-start.17 = (bf16[128,512]{1,0:T(8,128)(2,1)S(1)}, bf16[128,512]{1,0:T(8,128)(2,1)S(1)}, u32[]{:S(2)}, u32[]{:S(2)}) collective-permute-start(bf16[128,512]{1,0:T(8,128)(2,1)S(1)} %get-tuple-element.90), channel_id=1, source_target_pairs={{0,3},{1,2},{2,1},{3,0},{4,7},{5,6},{6,5},{7,4},{8,11},{9,10},{10,... | collective-permute-start | bytes 393224 | tf_op jit(solution)/shard_map/ppermute | solution.py:533
  61.6 10.1 %collective-permute-start.20 = (bf16[128,512]{1,0:T(8,128)(2,1)S(1)}, bf16[128,512]{1,0:T(8,128)(2,1)S(1)}, u32[]{:S(2)}, u32[]{:S(2)}) collective-permute-start(bf16[128,512]{1,0:T(8,128)(2,1)S(1)} %get-tuple-element.96), channel_id=1, source_target_pairs={{0,4},{1,5},{2,6},{3,7},{4,0},{5,1},{6,2},{7,3},{8,12},{9,13},{10,... | collective-permute-start | bytes 393224 | tf_op jit(solution)/shard_map/ppermute | solution.py:533
  62.9 16.5 %collective-permute-start.14 = (bf16[128,512]{1,0:T(8,128)(2,1)S(1)}, bf16[128,512]{1,0:T(8,128)(2,1)S(1)}, u32[]{:S(2)}, u32[]{:S(2)}) collective-permute-start(bf16[128,512]{1,0:T(8,128)(2,1)S(1)} %get-tuple-element.87), channel_id=1, source_target_pairs={{0,5},{1,4},{2,7},{3,6},{4,1},{5,0},{6,3},{7,2},{8,13},{9,12},{10,... | collective-permute-start | bytes 393224 | tf_op jit(solution)/shard_map/ppermute | solution.py:533
  71.6 7.8 %collective-permute-start.21 = (bf16[128,512]{1,0:T(8,128)(2,1)S(1)}, bf16[128,512]{1,0:T(8,128)(2,1)S(1)}, u32[]{:S(2)}, u32[]{:S(2)}) collective-permute-start(bf16[128,512]{1,0:T(8,128)(2,1)S(1)} %get-tuple-element.97), channel_id=1, source_target_pairs={{0,6},{1,7},{2,4},{3,5},{4,2},{5,3},{6,0},{7,1},{8,14},{9,15},{10,... | collective-permute-start | bytes 393224 | tf_op jit(solution)/shard_map/ppermute | solution.py:533
  79.4 6.3 %collective-permute-start.18 = (bf16[128,512]{1,0:T(8,128)(2,1)S(1)}, bf16[128,512]{1,0:T(8,128)(2,1)S(1)}, u32[]{:S(2)}, u32[]{:S(2)}) collective-permute-start(bf16[128,512]{1,0:T(8,128)(2,1)S(1)} %get-tuple-element.91), channel_id=1, source_target_pairs={{0,7},{1,6},{2,5},{3,4},{4,3},{5,2},{6,1},{7,0},{8,15},{9,14},{10,... | collective-permute-start | bytes 393224 | tf_op jit(solution)/shard_map/ppermute | solution.py:533
  79.4 17.6 %collective-permute-start.23 = (bf16[128,512]{1,0:T(8,128)(2,1)S(1)}, bf16[128,512]{1,0:T(8,128)(2,1)S(1)}, u32[]{:S(2)}, u32[]{:S(2)}) collective-permute-start(bf16[128,512]{1,0:T(8,128)(2,1)S(1)} %get-tuple-element.101), channel_id=1, source_target_pairs={{0,4},{1,5},{2,6},{3,7},{4,0},{5,1},{6,2},{7,3},{8,12},{9,13},{10,... | collective-permute-start | bytes 393224 | tf_op jit(solution)/shard_map/ppermute | solution.py:533
  85.7 14.1 %collective-permute-start.22 = (bf16[128,512]{1,0:T(8,128)(2,1)S(1)}, bf16[128,512]{1,0:T(8,128)(2,1)S(1)}, u32[]{:S(2)}, u32[]{:S(2)}) collective-permute-start(bf16[128,512]{1,0:T(8,128)(2,1)S(1)} %get-tuple-element.99), channel_id=1, source_target_pairs={{0,5},{1,4},{2,7},{3,6},{4,1},{5,0},{6,3},{7,2},{8,13},{9,12},{10,... | collective-permute-start | bytes 393224 | tf_op jit(solution)/shard_map/ppermute | solution.py:533
  97.0 4.9 %copy-start.15 = (bf16[128,256]{1,0:T(8,128)(2,1)S(1)}, bf16[128,256]{1,0:T(8,128)(2,1)}, u32[]{:S(2)}) copy-start(bf16[128,256]{1,0:T(8,128)(2,1)} %constant.19.clone.inv_ref) | copy-start | bytes 196612
  100.4 11.3 %collective-permute-start.28 = (bf16[128,4096]{1,0:T(8,128)(2,1)S(1)}, bf16[128,4096]{1,0:T(8,128)(2,1)S(1)}, u32[]{:S(2)}, u32[]{:S(2)}) collective-permute-start(bf16[128,4096]{1,0:T(8,128)(2,1)S(1)} %get-tuple-element.111.grad_b_ref), channel_id=1, source_target_pairs={{1,0},{2,1},{3,2},{4,3},{5,4},{6,5},{7,6},{9,8},{10,9},{11,10},{12... | collective-permute-start | bytes 3145736 | tf_op jit(solution)/shard_map/ppermute | solution.py:26
  101.9 9.8 %copy-start.7 = (bf16[1,128,4096]{2,1,0:T(8,128)(2,1)S(1)}, bf16[1,128,4096]{2,1,0:T(8,128)(2,1)}, u32[]{:S(2)}) copy-start(bf16[1,128,4096]{2,1,0:T(8,128)(2,1)} %param.16) | copy-start | bytes 3145732
  101.9 9.8 %copy-start.10 = (bf16[128,256]{1,0:T(8,128)(2,1)S(1)}, bf16[128,256]{1,0:T(8,128)(2,1)}, u32[]{:S(2)}) copy-start(bf16[128,256]{1,0:T(8,128)(2,1)} %constant.18.clone.inv_ref) | copy-start | bytes 196612
  104.4 2.7 %collective-permute-start.24 = (bf16[4,128,512]{2,1,0:T(8,128)(2,1)S(1)}, bf16[4,128,512]{2,1,0:T(8,128)(2,1)S(1)}, u32[]{:S(2)}, u32[]{:S(2)}) collective-permute-start(bf16[4,128,512]{2,1,0:T(8,128)(2,1)S(1)} %get-tuple-element.113), channel_id=1, source_target_pairs={{0,1},{1,0},{2,3},{3,2},{4,5},{5,4},{6,7},{7,6},{8,9},{9,8},{10,11... | collective-permute-start | bytes 1572872 | tf_op jit(solution)/shard_map/ppermute | solution.py:533
  107.2 14.4 %collective-permute-start.25 = (bf16[128,512]{1,0:T(8,128)(2,1)S(1)}, bf16[128,512]{1,0:T(8,128)(2,1)S(1)}, u32[]{:S(2)}, u32[]{:S(2)}) collective-permute-start(bf16[128,512]{1,0:T(8,128)(2,1)S(1)} %get-tuple-element.114), channel_id=1, source_target_pairs={{0,6},{1,7},{2,4},{3,5},{4,2},{5,3},{6,0},{7,1},{8,14},{9,15},{10,... | collective-permute-start | bytes 393224 | tf_op jit(solution)/shard_map/ppermute | solution.py:533
  107.9 18.0 %collective-permute-start.26 = (bf16[128,512]{1,0:T(8,128)(2,1)S(1)}, bf16[128,512]{1,0:T(8,128)(2,1)S(1)}, u32[]{:S(2)}, u32[]{:S(2)}) collective-permute-start(bf16[128,512]{1,0:T(8,128)(2,1)S(1)} %get-tuple-element.115), channel_id=1, source_target_pairs={{0,4},{1,5},{2,6},{3,7},{4,0},{5,1},{6,2},{7,3},{8,12},{9,13},{10,... | collective-permute-start | bytes 393224 | tf_op jit(solution)/shard_map/ppermute | solution.py:533
  110.3 15.5 %collective-permute-start.27 = (bf16[128,512]{1,0:T(8,128)(2,1)S(1)}, bf16[128,512]{1,0:T(8,128)(2,1)S(1)}, u32[]{:S(2)}, u32[]{:S(2)}) collective-permute-start(bf16[128,512]{1,0:T(8,128)(2,1)S(1)} %get-tuple-element.116), channel_id=1, source_target_pairs={{0,2},{1,3},{2,0},{3,1},{4,6},{5,7},{6,4},{7,5},{8,10},{9,11},{10,... | collective-permute-start | bytes 393224 | tf_op jit(solution)/shard_map/ppermute | solution.py:533
